TPU v7x, 32 devices: a whole 2x2x4 slice. The times are simulated.
32 devices in a mesh: groups: 2 (over x), row: 16 (over z, y, core).
Axes of the slice: x: 2, y: 2, z: 4, core: 2. Of those that a mesh axis runs over, the one named last changes fastest.
Arguments:
- alignment_embedding: bfloat16 [256, 256, 256], P(('groups', 'row')), parts along dimension 0, may hold values from -6 to 6
- rescaling_factor: float32 [256], replicated, may hold values from 0.1 to 1.9
- recentering_offset: float32 [256], replicated, may hold values from -3 to 3
- first_side_coefficients: bfloat16 [256, 32], replicated, may hold values from -0.375 to 0.375
- first_side_offset: float32 [32], replicated, may hold values from -2 to 2
- second_side_coefficients: bfloat16 [256, 32], replicated, may hold values from -0.375 to 0.375
- second_side_offset: float32 [32], replicated, may hold values from -2 to 2
- final_projector_coefficients: bfloat16 [1024, 128], replicated, may hold values from -2 to 2
- final_projector_offset: float32 [128], replicated, may hold values from -2 to 2
Outputs:
- pair_update: bfloat16 [512, 256, 128], P(('groups', 'row')), parts along dimension 0
There are 2 independent parts, one for each index of `groups`. A program takes and returns all parts, laid end to end along the dimension named above; an argument that names none is the same for every part. Nothing has to cross between parts.
All inputs are finite; a program needn't handle non-finite values.
Results may differ from a plain program's by a relative error of at most 0.0053.
Values may be sent and summed in bfloat16 or wider, within the bound.
No kernel may reach another device: no remote copies, remote signals or barrier semaphores. Data moves between devices by JAX's collectives and lax.ppermute only.
A program may use at most 192 MiB of HBM per device.

v0:
```python
import jax
import jax.numpy as jnp
from jax import lax
from jax.sharding import PartitionSpec as P


def standardize_embedding(values, rescaling_factor, recentering_offset):
    values = values.astype(jnp.float32)
    center = jnp.mean(values, axis=-1, keepdims=True)
    spread = jnp.mean(jnp.square(values - center), axis=-1, keepdims=True)
    return (
        (values - center) * lax.rsqrt(spread + 1e-05) * rescaling_factor + recentering_offset
    ).astype(jnp.bfloat16)


def project(standardized_alignment, weight, bias):
    unrolled_lines = standardized_alignment.reshape(-1, standardized_alignment.shape[2])
    result = jnp.dot(unrolled_lines, weight, preferred_element_type=jnp.float32) + bias
    return result.astype(jnp.bfloat16).reshape(
        standardized_alignment.shape[0], standardized_alignment.shape[1], weight.shape[1]
    )


def pair_block(left_tile, fetched, final_projector_coefficients, final_projector_offset):
    samples, rows_here, hidden = left_tile.shape
    cols_here = fetched.shape[1]
    summed = lax.dot_general(
        left_tile.reshape(samples, rows_here * hidden),
        fetched.reshape(samples, cols_here * hidden),
        (((0,), (0,)), ((), ())),
        preferred_element_type=jnp.float32,
    )
    outer = (summed / samples).astype(jnp.bfloat16).reshape(rows_here, hidden, cols_here, hidden)
    weight_grid = final_projector_coefficients.reshape(
        hidden, hidden, final_projector_coefficients.shape[1]
    )
    result = (
        lax.dot_general(
            outer, weight_grid, (((1, 3), (0, 1)), ((), ())), preferred_element_type=jnp.float32
        )
        + final_projector_offset
    )
    return result.astype(jnp.bfloat16)


def pair_tile(left_tile, right_all, final_projector_coefficients, final_projector_offset):
    rows_total = left_tile.shape[1]
    cols_total = right_all.shape[1]
    row_block = 16
    col_block = 128
    col_count = cols_total // col_block
    total_count = rows_total // row_block * col_count
    initial = jnp.zeros(
        (rows_total, cols_total, final_projector_coefficients.shape[1]), jnp.bfloat16
    )

    def one_block(index, result):
        row_start = index // col_count * row_block
        col_start = index % col_count * col_block
        right_part = lax.dynamic_slice_in_dim(right_all, col_start, col_block, 1)
        produced = pair_block(
            left_tile, right_part, final_projector_coefficients, final_projector_offset
        )
        return lax.dynamic_update_slice(
            result, produced, (row_start, col_start, jnp.zeros((), jnp.int32))
        )

    return lax.fori_loop(0, total_count, one_block, initial)


def per_device(
    alignment_embedding,
    rescaling_factor,
    recentering_offset,
    first_side_coefficients,
    first_side_offset,
    second_side_coefficients,
    second_side_offset,
    final_projector_coefficients,
    final_projector_offset,
):
    standardized_alignment = standardize_embedding(
        alignment_embedding, rescaling_factor, recentering_offset
    )
    left_proj = project(standardized_alignment, first_side_coefficients, first_side_offset)
    right_proj = project(standardized_alignment, second_side_coefficients, second_side_offset)
    left_tile = lax.all_to_all(left_proj, "row", split_axis=1, concat_axis=0, tiled=True)
    right_all = lax.all_gather(right_proj, "row", axis=0, tiled=True)
    return pair_tile(left_tile, right_all, final_projector_coefficients, final_projector_offset)


def solution(mesh):
    return jax.shard_map(
        per_device,
        mesh=mesh,
        in_specs=(P(("groups", "row"), None, None), P(), P(), P(), P(), P(), P(), P(), P()),
        out_specs=P(("groups", "row"), None, None),
        check_vma=False,
    )
```

profile of v0, /device:TPU:0, one launch (start us, length us, event | category | flops | bytes accessed | tf_op | source)
XLA Modules:
  0.0 193.0 jit_solution(15801531075971331851)
XLA Ops:
  6.6 1.6 convert_reduce_fusion
  8.3 1.9 fusion.8
  10.2 0.7 fusion.11
  11.4 0.7 copy.41
  12.1 0.4 fusion.7
  12.9 1.2 reshape.73
  14.1 7.4 %all-to-all-start = ((bf16[16,2,2048]{2,1,0:T(2,128)(2,1)}), bf16[16,2,2048]{2,1,0:T(2,128)(2,1)S(1)}, u32[]{:S(2)}, u32[]{:S(2)}) async-start(bf16[16,2,2048]{2,1,0:T(2,128)(2,1)} %reshape.73), calls=%async_computation | async-start | bytes 262144 | tf_op jit(solution)/shard_map/all_to_all | solution.py:87
  21.5 9.4 %all-to-all-done = bf16[16,2,2048]{2,1,0:T(2,128)(2,1)S(1)} async-done(((bf16[16,2,2048]{2,1,0:T(2,128)(2,1)}), bf16[16,2,2048]{2,1,0:T(2,128)(2,1)S(1)}, u32[]{:S(2)}, u32[]{:S(2)}) %all-to-all-start) | async-done | bytes 131104 | tf_op jit(solution)/shard_map/all_to_all | solution.py:87
  31.3 0.4 copy.30
  31.7 26.1 %all-gather.2.cloned.1.call-done = bf16[128,256,32]{1,2,0:T(8,128)(2,1)} async-done(((bf16[8,256,32]{1,2,0:T(8,128)(2,1)}), bf16[128,256,32]{1,2,0:T(8,128)(2,1)}) %all-gather.2.cloned.1.call-update) | async-done | bytes 2097168 | tf_op jit(solution)/shard_map/all_gather | solution.py:88
  58.0 127.2 %while.15 = (s32[]{:T(128)}, bf16[16,256,128]{2,1,0:T(8,128)(2,1)S(1)}, bf16[128,256,32]{1,2,0:T(8,128)(2,1)}, bf16[128,16,32]{0,2,1:T(8,128)(2,1)S(1)}, bf16[10...) while((s32[]{:T(128)}, ...), condition=%wide.region_3.4_spmd, body=%wide.region_2.3_spmd.sunk | while | flops 1078460416 | bytes 31329016 | solution.py:68
  58.0 1.3 constant_dynamic-slice_fusion.2
  59.3 1.5 copy.44
  60.8 3.2 %fusion.30 = bf16[512,4096]{0,1:T(8,128)(2,1)} fusion(bf16[128,4096]{0,1:T(8,128)(2,1)S(1)} %bitcast.59, bf16[128,512]{0,1:T(8,128)(2,1)S(1)} %bitcast.62), kind=kOutput, calls=%fused_computation.1.clone.1 | convolution fusion | flops 541065216 | bytes 5373952 | tf_op jit(solution)/shard_map/while/body/eval_jaxpr/dot_general | solution.py:27
  64.0 19.1 %reshape.76 = bf16[16,32,128,32]{1,0,3,2:T(8,128)(2,1)} reshape(bf16[512,4096]{0,1:T(8,128)(2,1)} %fusion.30) | data formatting | bytes 8388608 | tf_op jit(solution)/shard_map/while/body/eval_jaxpr/reshape | solution.py:33
  83.2 29.2 %copy.45 = bf16[16,32,128,32]{3,2,1,0:T(8,128)(2,1)} copy(bf16[16,32,128,32]{1,0,3,2:T(8,128)(2,1)} %reshape.76) | data formatting | bytes 8388608 | tf_op jit(solution)/shard_map/while/body/eval_jaxpr/reshape | solution.py:33
  112.3 9.3 %fusion.31 = bf16[16,256,128]{2,1,0:T(8,128)(2,1)S(1)} fusion(bf16[16,256,128]{2,1,0:T(8,128)(2,1)S(1)} %get-tuple-element.234, s32[]{:T(128)S(6)} %select_n.42, bf16[16,32,128,32]{3,2,1,0:T(8,128)(2,1)} %copy.45, bf16[32,32,128,1]{2,1,0,3:T(8,128)(2,1)S(1)} %bitcast.70, f32[128]{0:T(128)S(1)} %copy-done.9), kind=kOutput, calls=%fused_computation.5.clone.1 | convolution fusion | flops 537395200 | bytes 4981252 | tf_op jit(solution)/shard_map/while/body/eval_jaxpr/dot_general | solution.py:38
  121.6 1.3 constant_dynamic-slice_fusion.2
  122.9 1.5 copy.44
  124.4 3.2 %fusion.30 = bf16[512,4096]{0,1:T(8,128)(2,1)} fusion(bf16[128,4096]{0,1:T(8,128)(2,1)S(1)} %bitcast.59, bf16[128,512]{0,1:T(8,128)(2,1)S(1)} %bitcast.62), kind=kOutput, calls=%fused_computation.1.clone.1 | convolution fusion | flops 541065216 | bytes 5373952 | tf_op jit(solution)/shard_map/while/body/eval_jaxpr/dot_general | solution.py:27
  127.6 19.1 %reshape.76 = bf16[16,32,128,32]{1,0,3,2:T(8,128)(2,1)} reshape(bf16[512,4096]{0,1:T(8,128)(2,1)} %fusion.30) | data formatting | bytes 8388608 | tf_op jit(solution)/shard_map/while/body/eval_jaxpr/reshape | solution.py:33
  146.8 29.2 %copy.45 = bf16[16,32,128,32]{3,2,1,0:T(8,128)(2,1)} copy(bf16[16,32,128,32]{1,0,3,2:T(8,128)(2,1)} %reshape.76) | data formatting | bytes 8388608 | tf_op jit(solution)/shard_map/while/body/eval_jaxpr/reshape | solution.py:33
  175.9 9.3 %fusion.31 = bf16[16,256,128]{2,1,0:T(8,128)(2,1)S(1)} fusion(bf16[16,256,128]{2,1,0:T(8,128)(2,1)S(1)} %get-tuple-element.234, s32[]{:T(128)S(6)} %select_n.42, bf16[16,32,128,32]{3,2,1,0:T(8,128)(2,1)} %copy.45, bf16[32,32,128,1]{2,1,0,3:T(8,128)(2,1)S(1)} %bitcast.70, f32[128]{0:T(128)S(1)} %copy-done.9), kind=kOutput, calls=%fused_computation.5.clone.1 | convolution fusion | flops 537395200 | bytes 4981252 | tf_op jit(solution)/shard_map/while/body/eval_jaxpr/dot_general | solution.py:38
  185.2 1.0 copy-done.2
  (31 shorter events, 1.5 us)
Async XLA Ops:
  6.5 4.4 %copy-start = (bf16[256,32]{0,1:T(8,128)(2,1)S(1)}, bf16[256,32]{0,1:T(8,128)(2,1)}, u32[]{:S(2)}) copy-start(bf16[256,32]{0,1:T(8,128)(2,1)} %param.16) | copy-start | bytes 49156
  6.5 3.6 %copy-start.1 = (bf16[8,256,256]{2,1,0:T(8,128)(2,1)S(1)}, bf16[8,256,256]{2,1,0:T(8,128)(2,1)}, u32[]{:S(2)}) copy-start(bf16[8,256,256]{2,1,0:T(8,128)(2,1)} %param.11) | copy-start | bytes 3145732
  6.5 3.6 %copy-start.4 = (f32[256]{0:T(256)S(1)}, f32[256]{0:T(256)}, u32[]{:S(2)}) copy-start(f32[256]{0:T(256)} %param.13) | copy-start | bytes 3076
  6.5 3.7 %copy-start.5 = (f32[256]{0:T(256)S(1)}, f32[256]{0:T(256)}, u32[]{:S(2)}) copy-start(f32[256]{0:T(256)} %param.12) | copy-start | bytes 3076
  6.5 4.4 %copy-start.6 = (f32[32]{0:T(128)S(1)}, f32[32]{0:T(128)}, u32[]{:S(2)}) copy-start(f32[32]{0:T(128)} %param.17) | copy-start | bytes 388
  6.5 51.2 %all-gather.2.cloned.1.call-start = ((), (), s32[]{:S(2)}) async-start(), calls=%async_computation.1 | async-start | bytes 2228224 | tf_op jit(solution)/shard_map/all_gather | solution.py:88
  10.1 1.9 copy-start.3
  10.1 1.9 copy-start.7
  12.9 45.1 %copy-start.8 = (bf16[1024,128]{1,0:T(8,128)(2,1)S(1)}, bf16[1024,128]{1,0:T(8,128)(2,1)}, u32[]{:S(2)}) copy-start(bf16[1024,128]{1,0:T(8,128)(2,1)} %param.18) | copy-start | bytes 786436
  14.1 16.8 %all-to-all-start = ((bf16[16,2,2048]{2,1,0:T(2,128)(2,1)}), bf16[16,2,2048]{2,1,0:T(2,128)(2,1)S(1)}, u32[]{:S(2)}, u32[]{:S(2)}) async-start(bf16[16,2,2048]{2,1,0:T(2,128)(2,1)} %reshape.73), calls=%async_computation | async-start | bytes 262144 | tf_op jit(solution)/shard_map/all_to_all | solution.py:87
  83.2 29.2 %copy-start.9 = (f32[128]{0:T(128)S(1)}, f32[128]{0:T(128)}, u32[]{:S(2)}) copy-start(f32[128]{0:T(128)} %get-tuple-element.249) | copy-start | bytes 1540 | tf_op jit(solution)/shard_map/while
  146.8 29.2 %copy-start.9 = (f32[128]{0:T(128)S(1)}, f32[128]{0:T(128)}, u32[]{:S(2)}) copy-start(f32[128]{0:T(128)} %get-tuple-element.249) | copy-start | bytes 1540 | tf_op jit(solution)/shard_map/while
  185.2 1.0 copy-start.2
Sparse Core Ops, SparseCore 0:
  12.2 45.5 all-gather.1
where the time goes:
time: 196 us; the launch traced here: 193 us
  local copies, waits for them, and re-layouts  106 us (54%)
  waiting for transfers between devices  35.5 us (18%)
  matrix products  25.7 us (13%)
  between operations  13.6 us (7%)
  starting transfers between devices  7.42 us (4%)
  other arithmetic  4.25 us (2%)
    reshape x4, local copies, waits for them, and re-layouts, pair_block(): (summed / samples).astype(jnp.bfloat16)  96.5 us
    all_gather x1, waiting for transfers between devices, per_device(): right_all = lax.all_gather(right_proj, 'row', axis=0, tiled=True)  26.1 us
    dot_general x2, matrix products, pair_block(): lax.dot_general(outer, weight_grid, (((1, 3), (0, 1)), ((), ())), preferr...  18.5 us
    all_to_all x1, waiting for transfers between devices, per_device(): lax.all_to_all(left_proj, 'row', split_axis=1, concat_axis=0, tiled=True)  9.41 us
    all_to_all x1, starting transfers between devices, per_device(): lax.all_to_all(left_proj, 'row', split_axis=1, concat_axis=0, tiled=True)  7.38 us
    dot_general x2, matrix products, pair_block(): lax.dot_general(left_tile.reshape(samples, rows_here * hidden), fetched.r...  6.41 us
    dynamic_slice x4, local copies, waits for them, and re-layouts, one_block(): right_part = lax.dynamic_slice_in_dim(right_all, col_start, col_block, 1)  5.67 us
  transfers between devices with their start and end apart: 2, of which 2 were waited for; matrix products, arithmetic and copies ran while one was open for 1% of the time, Pallas kernels for 0%

commit v1 on v0

v1 whole, which is shorter than its diff:
```python
import functools

import jax
import jax.numpy as jnp
from jax import lax
from jax.experimental import pallas as pl
from jax.experimental.pallas import tpu as pltpu
from jax.sharding import PartitionSpec as P

VMEM_LIMIT = 48 * 1024 * 1024


def repeat_rows(values, times):
    rows, cols = values.shape
    return jnp.broadcast_to(values[:, None, :], (rows, times, cols)).reshape(rows * times, cols)


def project_kernel(
    rows_here,
    x_ref,
    gain_ref,
    shift_ref,
    first_ref,
    first_offset_ref,
    second_ref,
    second_offset_ref,
    *refs,
):
    messages, left_ref = refs[:-1], refs[-1]
    samples, residues, _ = x_ref.shape
    hidden = first_ref.shape[0]
    width = samples * hidden
    first = jnp.concatenate([first_ref[...].astype(jnp.float32)] * samples, axis=0)
    second = repeat_rows(second_ref[...].astype(jnp.float32), samples)
    row = lax.broadcasted_iota(jnp.int32, (width, 1), 0)
    spot = lax.broadcasted_iota(jnp.int32, (hidden, width), 1)
    channel = lax.broadcasted_iota(jnp.int32, (hidden, width), 0)

    def spread(offset_ref, owner):
        return jnp.dot(
            offset_ref[...],
            (owner == channel).astype(jnp.float32),
            precision=lax.Precision.HIGHEST,
            preferred_element_type=jnp.float32,
        )

    left = jnp.zeros((residues, width), jnp.float32)
    right = jnp.zeros((residues, width), jnp.float32)
    for s in range(samples):
        values = x_ref[s].astype(jnp.float32)
        center = jnp.mean(values, axis=-1, keepdims=True)
        values = values - center
        spread_of = jnp.mean(jnp.square(values), axis=-1, keepdims=True)
        normed = (values * lax.rsqrt(spread_of + 1e-05) * gain_ref[...] + shift_ref[...]).astype(
            jnp.bfloat16
        )
        first_here = jnp.where(row // hidden == s, first, 0.0).astype(jnp.bfloat16)
        second_here = jnp.where(row % samples == s, second, 0.0).astype(jnp.bfloat16)
        dims = (((1,), (1,)), ((), ()))
        left += lax.dot_general(normed, first_here, dims, preferred_element_type=jnp.float32)
        right += lax.dot_general(normed, second_here, dims, preferred_element_type=jnp.float32)
    left_ref[...] = (left + spread(first_offset_ref, spot % hidden)).astype(jnp.bfloat16)
    right = (right + spread(second_offset_ref, spot // samples)).astype(jnp.bfloat16)

    blocks = len(messages)
    here = lax.axis_index("row") * rows_here * blocks // residues
    for step, message in enumerate(messages):
        start = lax.rem(here + step, blocks) * (residues // blocks)
        start = pl.multiple_of(start, residues // blocks)
        message[:residues, :] = right
        message[residues:, :] = left_ref[pl.ds(start, residues // blocks), :]


def pair_kernel(count, rows_here, samples, begins, ends, *refs):
    refs = list(refs)
    messages = [refs.pop(0) for _ in range(count)]
    weight_ref = refs.pop(0)
    offset_ref = refs.pop(0)
    total_ref = None if begins else refs.pop(0)
    out_ref, mixed_ref = refs
    width, columns = weight_ref.shape
    channels = offset_ref.shape[1]
    hidden = columns // channels
    here = width // hidden
    extra, residues = None, None
    residues = out_ref.shape[1] if ends else out_ref.shape[0]
    extra = messages[0].shape[0] - residues
    slot = lax.rem(lax.axis_index("row"), extra // rows_here)
    start = pl.multiple_of(residues + slot * rows_here, rows_here)

    row = lax.broadcasted_iota(jnp.int32, (rows_here * here, width), 0)
    lane = lax.broadcasted_iota(jnp.int32, (rows_here * here, width), 1)
    keep = lane // hidden == row % here
    picked = []
    for message in messages:
        left = message[pl.ds(start, rows_here), :].astype(jnp.float32)
        picked.append(jnp.where(keep, repeat_rows(left, here), 0.0).astype(jnp.bfloat16))
    picked = jnp.concatenate(picked, axis=0)

    group = 8
    for chunk in range(hidden // group):
        mixed = jnp.dot(
            picked,
            weight_ref[:, chunk * group * channels : (chunk + 1) * group * channels],
            preferred_element_type=jnp.float32,
        )
        for n in range(count):
            for i in range(rows_here):
                top = (n * rows_here + i) * here
                piece = jnp.concatenate(
                    [mixed[top : top + here, e * channels : (e + 1) * channels] for e in range(group)],
                    axis=0,
                )
                low = n * width + chunk * group * here
                mixed_ref[low : low + group * here, i * channels : (i + 1) * channels] = piece.astype(
                    jnp.bfloat16
                )

    right = jnp.concatenate([message[:residues, :] for message in messages], axis=1)
    pair = 2
    for i in range(0, rows_here, pair):
        cols = slice(i * channels, (i + pair) * channels)
        value = jnp.dot(right, mixed_ref[:, cols], preferred_element_type=jnp.float32)
        if not begins:
            value = value + total_ref[:, cols]
        if ends:
            for k in range(pair):
                part = value[:, k * channels : (k + 1) * channels]
                out_ref[i + k] = (part * (1.0 / samples) + offset_ref[...]).astype(jnp.bfloat16)
        else:
            out_ref[:, cols] = value


def per_device(
    size,
    alignment_embedding,
    rescaling_factor,
    recentering_offset,
    first_side_coefficients,
    first_side_offset,
    second_side_coefficients,
    second_side_offset,
    final_projector_coefficients,
    final_projector_offset,
):
    here, residues, features = alignment_embedding.shape
    hidden = first_side_coefficients.shape[1]
    channels = final_projector_coefficients.shape[1]
    width = here * hidden
    samples = here * size
    rows_here = residues // size
    near = 4
    blocks = size // near
    message = jax.ShapeDtypeStruct((residues + residues // blocks, width), jnp.bfloat16)

    vmem = pl.BlockSpec(memory_space=pltpu.VMEM)
    messages = pl.pallas_call(
        functools.partial(project_kernel, rows_here),
        out_shape=[message] * blocks,
        in_specs=[vmem] * 7,
        out_specs=[vmem] * blocks,
        scratch_shapes=[pltpu.VMEM((residues, width), jnp.bfloat16)],
        compiler_params=pltpu.CompilerParams(vmem_limit_bytes=VMEM_LIMIT),
    )(
        alignment_embedding,
        rescaling_factor.reshape(1, features),
        recentering_offset.reshape(1, features),
        first_side_coefficients.T,
        first_side_offset.reshape(1, hidden),
        second_side_coefficients.T,
        second_side_offset.reshape(1, hidden),
    )

    def send(value, target):
        return lax.ppermute(value, "row", [(r, target(r)) for r in range(size)])

    weight = jnp.tile(final_projector_coefficients.reshape(hidden, hidden * channels), (here, 1))
    offset = final_projector_offset.reshape(1, channels)
    total = None
    for step in range(blocks):
        one = messages[0] if step == 0 else send(messages[step], lambda r: (r + near * step) % size)
        two = send(one, lambda r: r ^ 2)
        group = [one, two, send(one, lambda r: r ^ 1), send(two, lambda r: r ^ 1)]
        begins, ends = step == 0, step == blocks - 1
        operands = group + [weight, offset] + ([] if begins else [total])
        if ends:
            result = jax.ShapeDtypeStruct((rows_here, residues, channels), jnp.bfloat16)
        else:
            result = jax.ShapeDtypeStruct((residues, rows_here * channels), jnp.float32)
        total = pl.pallas_call(
            functools.partial(pair_kernel, len(group), rows_here, samples, begins, ends),
            out_shape=result,
            in_specs=[vmem] * len(operands),
            out_specs=vmem,
            scratch_shapes=[pltpu.VMEM((len(group) * width, rows_here * channels), jnp.bfloat16)],
            compiler_params=pltpu.CompilerParams(vmem_limit_bytes=VMEM_LIMIT),
        )(*operands)
    return total


def solution(mesh):
    return jax.shard_map(
        functools.partial(per_device, mesh.shape["row"]),
        mesh=mesh,
        in_specs=(P(("groups", "row"), None, None), P(), P(), P(), P(), P(), P(), P(), P()),
        out_specs=P(("groups", "row"), None, None),
        check_vma=False,
    )
```

time: 196 us -> 52.7 us (0.27); the launches traced: 193 us -> 52 us
  local copies, waits for them, and re-layouts: 106 us -> 9.29 us
  matrix products: 25.7 us -> 0 us
  waiting for transfers between devices: 35.5 us -> 15.1 us
  Pallas kernels: 0 us -> 15.4 us
  between operations: 13.6 us -> 0.11 us
  starting transfers between devices: 7.42 us -> 12.2 us
  other arithmetic: 4.25 us -> 0 us
    reshape x6 -> x0, local copies, waits for them, and re-layouts: 97.6 us -> none  [the longest x4 96.5 us: pair_block(): (summed / samples).astype(jnp.bfloat16)]
    all_gather x1 -> x0, waiting for transfers between devices: 26.1 us -> none  [per_device(): right_all = lax.all_gather(right_proj, 'row', axis=0, tiled=True)]
    dot_general x6 -> x0, matrix products: 25.7 us -> none  [the longest x2 18.5 us: pair_block(): lax.dot_general(outer, weight_grid, (((1, 3), (0, 1)), ((), ())), preferr...]
    pallas_call x0 -> x5, Pallas kernels: none -> 15.4 us  [the longest x4 13.8 us: per_device(): pl.pallas_call(functools.partial(pair_kernel, len(group), rows_here, samp...]
    ppermute x0 -> x15, waiting for transfers between devices: none -> 15.1 us  [send(): return lax.ppermute(value, 'row', [(r, target(r)) for r in range(size)])]
    ppermute x0 -> x15, starting transfers between devices: none -> 12.2 us  [send(): return lax.ppermute(value, 'row', [(r, target(r)) for r in range(size)])]
    all_to_all x1 -> x0, waiting for transfers between devices: 9.41 us -> none  [per_device(): lax.all_to_all(left_proj, 'row', split_axis=1, concat_axis=0, tiled=True)]
    all_to_all x1 -> x0, starting transfers between devices: 7.38 us -> none  [per_device(): lax.all_to_all(left_proj, 'row', split_axis=1, concat_axis=0, tiled=True)]
  transfers between devices with their start and end apart: 2 -> 15, of which waited for: 2 -> 4; matrix products, arithmetic and copies ran while one was open for 1% -> 2% of each run, Pallas kernels for 0% -> 20%
where the time goes in v1:
time: 52.7 us; the launch traced here: 52 us
  Pallas kernels  15.4 us (29%)
  waiting for transfers between devices  15.1 us (29%)
  starting transfers between devices  12.2 us (23%)
  local copies, waits for them, and re-layouts  9.29 us (18%)
    ppermute x15, waiting for transfers between devices, send(): return lax.ppermute(value, 'row', [(r, target(r)) for r in range(size)])  15.1 us
    pallas_call x4, Pallas kernels, per_device(): pl.pallas_call(functools.partial(pair_kernel, len(group), rows_here, samp...  13.8 us
    ppermute x15, starting transfers between devices, send(): return lax.ppermute(value, 'row', [(r, target(r)) for r in range(size)])  12.2 us
    unnamed x20, local copies, waits for them, and re-layouts  7.99 us
    pallas_call x1, Pallas kernels, per_device(): pl.pallas_call(functools.partial(project_kernel, rows_here), out_shape=[m...  1.52 us
    another operation x2, local copies, waits for them, and re-layouts, per_device(): jnp.tile(final_projector_coefficients.reshape(hidden, hidden * channels),...  1.3 us
  transfers between devices with their start and end apart: 15, of which 4 were waited for; matrix products, arithmetic and copies ran while one was open for 2% of the time, Pallas kernels for 20%

profile of v1, /device:TPU:0, one launch (start us, length us, event | category | flops | bytes accessed | tf_op | source)
XLA Modules:
  0.0 52.0 jit_solution(10913712163802132842)
XLA Ops:
  0.0 1.2 %copy-done.2 = bf16[8,256,256]{2,1,0:T(8,128)(2,1)S(1)} copy-done((bf16[8,256,256]{2,1,0:T(8,128)(2,1)S(1)}, bf16[8,256,256]{2,1,0:T(8,128)(2,1)}, u32[]{:S(2)}) %copy-start.2) | copy-done | bytes 1048600
  1.2 0.7 %copy-done.3 = bf16[256,32]{0,1:T(8,128)(2,1)S(1)} copy-done((bf16[256,32]{0,1:T(8,128)(2,1)S(1)}, bf16[256,32]{0,1:T(8,128)(2,1)}, u32[]{:S(2)}) %copy-start.3) | copy-done | bytes 16408
  2.0 0.7 %copy-done.4 = bf16[256,32]{0,1:T(8,128)(2,1)S(1)} copy-done((bf16[256,32]{0,1:T(8,128)(2,1)S(1)}, bf16[256,32]{0,1:T(8,128)(2,1)}, u32[]{:S(2)}) %copy-start.4) | copy-done | bytes 16408
  2.7 0.7 %copy-done.6 = f32[256]{0:T(256)S(1)} copy-done((f32[256]{0:T(256)S(1)}, f32[256]{0:T(256)}, u32[]{:S(2)}) %copy-start.6) | copy-done | bytes 1048
  3.4 0.7 %copy-done.7 = f32[256]{0:T(256)S(1)} copy-done((f32[256]{0:T(256)S(1)}, f32[256]{0:T(256)}, u32[]{:S(2)}) %copy-start.7) | copy-done | bytes 1048
  4.0 0.7 %copy-done.8 = f32[32]{0:T(128)S(1)} copy-done((f32[32]{0:T(128)S(1)}, f32[32]{0:T(128)}, u32[]{:S(2)}) %copy-start.8) | copy-done | bytes 152
  4.7 0.7 %copy-done.9 = f32[32]{0:T(128)S(1)} copy-done((f32[32]{0:T(128)S(1)}, f32[32]{0:T(128)}, u32[]{:S(2)}) %copy-start.9) | copy-done | bytes 152
  5.3 1.5 %shard_map.91 = (bf16[320,256]{1,0:T(8,128)(2,1)S(1)}, bf16[320,256]{1,0:T(8,128)(2,1)S(1)}, bf16[320,256]{1,0:T(8,128)(2,1)S(1)}, bf16[320,256]{1,0:T(8,128)(2,1)S(1)}) custom-call(bf16[8,256,256]{2,1,0:T(8,128)(2,1)S(1)} %copy-done.2, f32[1,256]{1,0:T(1,128)S(1)} %bitcast.18, f32[1,256]{1,0:T(1,128)S(1)} %bitcast.19, bf16[32,256]{1,0:T(8,128)(2,1)S(1)} %bitcast.12, ...), custom_call_target="tpu_custom_call" | custom-call | tf_op jit(solution)/shard_map/pallas_call | solution.py:157
  6.9 3.0 %collective-permute-start.12 = (bf16[320,256]{1,0:T(8,128)(2,1)S(1)}, bf16[320,256]{1,0:T(8,128)(2,1)S(1)}, u32[]{:S(2)}, u32[]{:S(2)}) collective-permute-start(bf16[320,256]{1,0:T(8,128)(2,1)S(1)} %get-tuple-element.12.refs_0_), channel_id=1, source_target_pairs={{0,2},{1,3},{2,0},{3,1},{4,6},{5,7},{6,4},{7,5},{8,10},{9,11},{10,... | collective-permute-start | bytes 491528 | tf_op jit(solution)/shard_map/ppermute | solution.py:175
  9.9 1.6 %collective-permute-start.8 = (bf16[320,256]{1,0:T(8,128)(2,1)S(1)}, bf16[320,256]{1,0:T(8,128)(2,1)S(1)}, u32[]{:S(2)}, u32[]{:S(2)}) collective-permute-start(bf16[320,256]{1,0:T(8,128)(2,1)S(1)} %get-tuple-element.11), channel_id=1, source_target_pairs={{0,4},{1,5},{2,6},{3,7},{4,8},{5,9},{6,10},{7,11},{8,12},{9,13},{1... | collective-permute-start | bytes 491528 | tf_op jit(solution)/shard_map/ppermute | solution.py:175
  11.5 2.6 %collective-permute-start.4 = (bf16[320,256]{1,0:T(8,128)(2,1)S(1)}, bf16[320,256]{1,0:T(8,128)(2,1)S(1)}, u32[]{:S(2)}, u32[]{:S(2)}) collective-permute-start(bf16[320,256]{1,0:T(8,128)(2,1)S(1)} %get-tuple-element.10), channel_id=1, source_target_pairs={{0,8},{1,9},{2,10},{3,11},{4,12},{5,13},{6,14},{7,15},{8,0},{9,1},... | collective-permute-start | bytes 491528 | tf_op jit(solution)/shard_map/ppermute | solution.py:175
  14.1 1.3 %collective-permute-start = (bf16[320,256]{1,0:T(8,128)(2,1)S(1)}, bf16[320,256]{1,0:T(8,128)(2,1)S(1)}, u32[]{:S(2)}, u32[]{:S(2)}) collective-permute-start(bf16[320,256]{1,0:T(8,128)(2,1)S(1)} %get-tuple-element.9), channel_id=1, source_target_pairs={{0,12},{1,13},{2,14},{3,15},{4,0},{5,1},{6,2},{7,3},{8,4},{9,5},{1... | collective-permute-start | bytes 491528 | tf_op jit(solution)/shard_map/ppermute | solution.py:175
  15.7 3.3 %collective-permute-done.8.refs_0_ = bf16[320,256]{1,0:T(8,128)(2,1)S(1)} collective-permute-done((bf16[320,256]{1,0:T(8,128)(2,1)S(1)}, bf16[320,256]{1,0:T(8,128)(2,1)S(1)}, u32[]{:S(2)}, u32[]{:S(2)}) %collective-permute-start.8) | collective-permute-done | bytes 163872 | tf_op jit(solution)/shard_map/ppermute | solution.py:175
  19.2 5.4 %collective-permute-done.4.refs_0_ = bf16[320,256]{1,0:T(8,128)(2,1)S(1)} collective-permute-done((bf16[320,256]{1,0:T(8,128)(2,1)S(1)}, bf16[320,256]{1,0:T(8,128)(2,1)S(1)}, u32[]{:S(2)}, u32[]{:S(2)}) %collective-permute-start.4) | collective-permute-done | bytes 163872 | tf_op jit(solution)/shard_map/ppermute | solution.py:175
  25.1 1.6 %collective-permute-start.1 = (bf16[320,256]{1,0:T(8,128)(2,1)S(1)}, bf16[320,256]{1,0:T(8,128)(2,1)S(1)}, u32[]{:S(2)}, u32[]{:S(2)}) collective-permute-start(bf16[320,256]{1,0:T(8,128)(2,1)S(1)} %collective-permute-done.refs_0_), channel_id=1, source_target_pairs={{0,2},{1,3},{2,0},{3,1},{4,6},{5,7},{6,4},{7,5},{8,10},{9,11},{10,... | collective-permute-start | bytes 491528 | tf_op jit(solution)/shard_map/ppermute | solution.py:175
  27.2 4.5 %collective-permute-done.5.refs_1_ = bf16[320,256]{1,0:T(8,128)(2,1)S(1)} collective-permute-done((bf16[320,256]{1,0:T(8,128)(2,1)S(1)}, bf16[320,256]{1,0:T(8,128)(2,1)S(1)}, u32[]{:S(2)}, u32[]{:S(2)}) %collective-permute-start.5) | collective-permute-done | bytes 163872 | tf_op jit(solution)/shard_map/ppermute | solution.py:175
  32.2 1.9 %collective-permute-done.1.refs_1_ = bf16[320,256]{1,0:T(8,128)(2,1)S(1)} collective-permute-done((bf16[320,256]{1,0:T(8,128)(2,1)S(1)}, bf16[320,256]{1,0:T(8,128)(2,1)S(1)}, u32[]{:S(2)}, u32[]{:S(2)}) %collective-permute-start.1) | collective-permute-done | bytes 163872 | tf_op jit(solution)/shard_map/ppermute | solution.py:175
  34.2 1.1 %tile.10 = bf16[32,4096]{1,0:T(8,128)(2,1)S(1)} reshape(bf16[1024,128]{1,0:T(8,128)(2,1)} %param.16) | data formatting | bytes 524288 | tf_op jit(solution)/shard_map/tile | solution.py:177
  35.5 2.4 %shard_map.92.refs_6_ = f32[256,2048]{1,0:T(8,128)S(1)} custom-call(bf16[320,256]{1,0:T(8,128)(2,1)S(1)} %get-tuple-element.12.refs_0_, bf16[320,256]{1,0:T(8,128)(2,1)S(1)} %collective-permute-done.12.refs_1_, bf16[320,256]{1,0:T(8,128)(2,1)S(1)} %collective-permute-done.13.refs_2_, bf16[320,256]{1,0:T(8,128)(2,1)S(1)} %collective-permute-done.14.refs_3_, ...), custom_call_target="tpu_custom_call" | custom-call | tf_op jit(solution)/shard_map/pallas_call | solution.py:190
  37.9 1.3 %copy-done = f32[256,2048]{1,0:T(8,128)} copy-done((f32[256,2048]{1,0:T(8,128)}, f32[256,2048]{1,0:T(8,128)S(1)}, u32[]{:S(2)}) %copy-start) | copy-done | bytes 2097176
  39.2 4.0 %shard_map.93.refs_6_ = f32[256,2048]{1,0:T(8,128)S(1)} custom-call(bf16[320,256]{1,0:T(8,128)(2,1)S(1)} %collective-permute-done.8.refs_0_, bf16[320,256]{1,0:T(8,128)(2,1)S(1)} %collective-permute-done.9.refs_1_, bf16[320,256]{1,0:T(8,128)(2,1)S(1)} %collective-permute-done.10.refs_2_, bf16[320,256]{1,0:T(8,128)(2,1)S(1)} %collective-permute-done.11.refs_3_, ...), custom_call_target="tpu_custom_call" | custom-call | tf_op jit(solution)/shard_map/pallas_call | solution.py:190
  43.3 1.3 %copy-done.1 = f32[256,2048]{1,0:T(8,128)} copy-done((f32[256,2048]{1,0:T(8,128)}, f32[256,2048]{1,0:T(8,128)S(1)}, u32[]{:S(2)}) %copy-start.1) | copy-done | bytes 2097176
  44.6 4.0 %shard_map.94.refs_6_ = f32[256,2048]{1,0:T(8,128)S(1)} custom-call(bf16[320,256]{1,0:T(8,128)(2,1)S(1)} %collective-permute-done.4.refs_0_, bf16[320,256]{1,0:T(8,128)(2,1)S(1)} %collective-permute-done.5.refs_1_, bf16[320,256]{1,0:T(8,128)(2,1)S(1)} %collective-permute-done.6.refs_2_, bf16[320,256]{1,0:T(8,128)(2,1)S(1)} %collective-permute-done.7.refs_3_, ...), custom_call_target="tpu_custom_call" | custom-call | tf_op jit(solution)/shard_map/pallas_call | solution.py:190
  48.6 3.4 %shard_map.95 = bf16[16,256,128]{2,1,0:T(8,128)(2,1)} custom-call(bf16[320,256]{1,0:T(8,128)(2,1)S(1)} %collective-permute-done.refs_0_, bf16[320,256]{1,0:T(8,128)(2,1)S(1)} %collective-permute-done.1.refs_1_, bf16[320,256]{1,0:T(8,128)(2,1)S(1)} %collective-permute-done.2.refs_2_, bf16[320,256]{1,0:T(8,128)(2,1)S(1)} %collective-permute-done.3.refs_3_, ...), custom_call_target="tpu_custom_call" | custom-call | tf_op jit(solution)/shard_map/pallas_call | solution.py:190
  (33 shorter events, 2.3 us)
Async XLA Ops:
  0.0 35.5 %copy-start.5 = (f32[128]{0:T(128)S(1)}, f32[128]{0:T(128)}, u32[]{:S(2)}) copy-start(f32[128]{0:T(128)} %param.17) | copy-start | bytes 1540
  0.0 1.2 %copy-start.2 = (bf16[8,256,256]{2,1,0:T(8,128)(2,1)S(1)}, bf16[8,256,256]{2,1,0:T(8,128)(2,1)}, u32[]{:S(2)}) copy-start(bf16[8,256,256]{2,1,0:T(8,128)(2,1)} %x_ref.1) | copy-start | bytes 3145732
  1.2 0.7 %copy-start.3 = (bf16[256,32]{0,1:T(8,128)(2,1)S(1)}, bf16[256,32]{0,1:T(8,128)(2,1)}, u32[]{:S(2)}) copy-start(bf16[256,32]{0,1:T(8,128)(2,1)} %param.12) | copy-start | bytes 49156
  2.0 0.7 %copy-start.4 = (bf16[256,32]{0,1:T(8,128)(2,1)S(1)}, bf16[256,32]{0,1:T(8,128)(2,1)}, u32[]{:S(2)}) copy-start(bf16[256,32]{0,1:T(8,128)(2,1)} %param.14) | copy-start | bytes 49156
  2.7 0.7 %copy-start.6 = (f32[256]{0:T(256)S(1)}, f32[256]{0:T(256)}, u32[]{:S(2)}) copy-start(f32[256]{0:T(256)} %param.10) | copy-start | bytes 3076
  3.4 0.7 %copy-start.7 = (f32[256]{0:T(256)S(1)}, f32[256]{0:T(256)}, u32[]{:S(2)}) copy-start(f32[256]{0:T(256)} %param.11) | copy-start | bytes 3076
  4.0 0.7 %copy-start.8 = (f32[32]{0:T(128)S(1)}, f32[32]{0:T(128)}, u32[]{:S(2)}) copy-start(f32[32]{0:T(128)} %param.13) | copy-start | bytes 388
  6.9 8.6 %collective-permute-start.12 = (bf16[320,256]{1,0:T(8,128)(2,1)S(1)}, bf16[320,256]{1,0:T(8,128)(2,1)S(1)}, u32[]{:S(2)}, u32[]{:S(2)}) collective-permute-start(bf16[320,256]{1,0:T(8,128)(2,1)S(1)} %get-tuple-element.12.refs_0_), channel_id=1, source_target_pairs={{0,2},{1,3},{2,0},{3,1},{4,6},{5,7},{6,4},{7,5},{8,10},{9,11},{10,... | collective-permute-start | bytes 491528 | tf_op jit(solution)/shard_map/ppermute | solution.py:175
  9.9 9.0 %collective-permute-start.8 = (bf16[320,256]{1,0:T(8,128)(2,1)S(1)}, bf16[320,256]{1,0:T(8,128)(2,1)S(1)}, u32[]{:S(2)}, u32[]{:S(2)}) collective-permute-start(bf16[320,256]{1,0:T(8,128)(2,1)S(1)} %get-tuple-element.11), channel_id=1, source_target_pairs={{0,4},{1,5},{2,6},{3,7},{4,8},{5,9},{6,10},{7,11},{8,12},{9,13},{1... | collective-permute-start | bytes 491528 | tf_op jit(solution)/shard_map/ppermute | solution.py:175
  11.5 13.1 %collective-permute-start.4 = (bf16[320,256]{1,0:T(8,128)(2,1)S(1)}, bf16[320,256]{1,0:T(8,128)(2,1)S(1)}, u32[]{:S(2)}, u32[]{:S(2)}) collective-permute-start(bf16[320,256]{1,0:T(8,128)(2,1)S(1)} %get-tuple-element.10), channel_id=1, source_target_pairs={{0,8},{1,9},{2,10},{3,11},{4,12},{5,13},{6,14},{7,15},{8,0},{9,1},... | collective-permute-start | bytes 491528 | tf_op jit(solution)/shard_map/ppermute | solution.py:175
  14.1 11.0 %collective-permute-start.13 = (bf16[320,256]{1,0:T(8,128)(2,1)S(1)}, bf16[320,256]{1,0:T(8,128)(2,1)S(1)}, u32[]{:S(2)}, u32[]{:S(2)}) collective-permute-start(bf16[320,256]{1,0:T(8,128)(2,1)S(1)} %get-tuple-element.12.refs_0_), channel_id=1, source_target_pairs={{0,1},{1,0},{2,3},{3,2},{4,5},{5,4},{6,7},{7,6},{8,9},{9,8},{10,11... | collective-permute-start | bytes 491528 | tf_op jit(solution)/shard_map/ppermute | solution.py:175
  14.1 11.0 %collective-permute-start = (bf16[320,256]{1,0:T(8,128)(2,1)S(1)}, bf16[320,256]{1,0:T(8,128)(2,1)S(1)}, u32[]{:S(2)}, u32[]{:S(2)}) collective-permute-start(bf16[320,256]{1,0:T(8,128)(2,1)S(1)} %get-tuple-element.9), channel_id=1, source_target_pairs={{0,12},{1,13},{2,14},{3,15},{4,0},{5,1},{6,2},{7,3},{8,4},{9,5},{1... | collective-permute-start | bytes 491528 | tf_op jit(solution)/shard_map/ppermute | solution.py:175
  15.4 11.3 %collective-permute-start.14 = (bf16[320,256]{1,0:T(8,128)(2,1)S(1)}, bf16[320,256]{1,0:T(8,128)(2,1)S(1)}, u32[]{:S(2)}, u32[]{:S(2)}) collective-permute-start(bf16[320,256]{1,0:T(8,128)(2,1)S(1)} %collective-permute-done.12.refs_1_), channel_id=1, source_target_pairs={{0,1},{1,0},{2,3},{3,2},{4,5},{5,4},{6,7},{7,6},{8,9},{9,8},{10,11... | collective-permute-start | bytes 491528 | tf_op jit(solution)/shard_map/ppermute | solution.py:175
  18.9 8.0 %collective-permute-start.9 = (bf16[320,256]{1,0:T(8,128)(2,1)S(1)}, bf16[320,256]{1,0:T(8,128)(2,1)S(1)}, u32[]{:S(2)}, u32[]{:S(2)}) collective-permute-start(bf16[320,256]{1,0:T(8,128)(2,1)S(1)} %collective-permute-done.8.refs_0_), channel_id=1, source_target_pairs={{0,2},{1,3},{2,0},{3,1},{4,6},{5,7},{6,4},{7,5},{8,10},{9,11},{10,... | collective-permute-start | bytes 491528 | tf_op jit(solution)/shard_map/ppermute | solution.py:175
  24.6 7.1 %collective-permute-start.5 = (bf16[320,256]{1,0:T(8,128)(2,1)S(1)}, bf16[320,256]{1,0:T(8,128)(2,1)S(1)}, u32[]{:S(2)}, u32[]{:S(2)}) collective-permute-start(bf16[320,256]{1,0:T(8,128)(2,1)S(1)} %collective-permute-done.4.refs_0_), channel_id=1, source_target_pairs={{0,2},{1,3},{2,0},{3,1},{4,6},{5,7},{6,4},{7,5},{8,10},{9,11},{10,... | collective-permute-start | bytes 491528 | tf_op jit(solution)/shard_map/ppermute | solution.py:175
  25.1 6.6 %collective-permute-start.10 = (bf16[320,256]{1,0:T(8,128)(2,1)S(1)}, bf16[320,256]{1,0:T(8,128)(2,1)S(1)}, u32[]{:S(2)}, u32[]{:S(2)}) collective-permute-start(bf16[320,256]{1,0:T(8,128)(2,1)S(1)} %collective-permute-done.8.refs_0_), channel_id=1, source_target_pairs={{0,1},{1,0},{2,3},{3,2},{4,5},{5,4},{6,7},{7,6},{8,9},{9,8},{10,11... | collective-permute-start | bytes 491528 | tf_op jit(solution)/shard_map/ppermute | solution.py:175
  25.1 9.0 %collective-permute-start.1 = (bf16[320,256]{1,0:T(8,128)(2,1)S(1)}, bf16[320,256]{1,0:T(8,128)(2,1)S(1)}, u32[]{:S(2)}, u32[]{:S(2)}) collective-permute-start(bf16[320,256]{1,0:T(8,128)(2,1)S(1)} %collective-permute-done.refs_0_), channel_id=1, source_target_pairs={{0,2},{1,3},{2,0},{3,1},{4,6},{5,7},{6,4},{7,5},{8,10},{9,11},{10,... | collective-permute-start | bytes 491528 | tf_op jit(solution)/shard_map/ppermute | solution.py:175
  26.7 17.9 %collective-permute-start.6 = (bf16[320,256]{1,0:T(8,128)(2,1)S(1)}, bf16[320,256]{1,0:T(8,128)(2,1)S(1)}, u32[]{:S(2)}, u32[]{:S(2)}) collective-permute-start(bf16[320,256]{1,0:T(8,128)(2,1)S(1)} %collective-permute-done.4.refs_0_), channel_id=1, source_target_pairs={{0,1},{1,0},{2,3},{3,2},{4,5},{5,4},{6,7},{7,6},{8,9},{9,8},{10,11... | collective-permute-start | bytes 491528 | tf_op jit(solution)/shard_map/ppermute | solution.py:175
  26.9 12.3 %collective-permute-start.11 = (bf16[320,256]{1,0:T(8,128)(2,1)S(1)}, bf16[320,256]{1,0:T(8,128)(2,1)S(1)}, u32[]{:S(2)}, u32[]{:S(2)}) collective-permute-start(bf16[320,256]{1,0:T(8,128)(2,1)S(1)} %collective-permute-done.9.refs_1_), channel_id=1, source_target_pairs={{0,1},{1,0},{2,3},{3,2},{4,5},{5,4},{6,7},{7,6},{8,9},{9,8},{10,11... | collective-permute-start | bytes 491528 | tf_op jit(solution)/shard_map/ppermute | solution.py:175
  31.7 12.9 %collective-permute-start.7 = (bf16[320,256]{1,0:T(8,128)(2,1)S(1)}, bf16[320,256]{1,0:T(8,128)(2,1)S(1)}, u32[]{:S(2)}, u32[]{:S(2)}) collective-permute-start(bf16[320,256]{1,0:T(8,128)(2,1)S(1)} %collective-permute-done.5.refs_1_), channel_id=1, source_target_pairs={{0,1},{1,0},{2,3},{3,2},{4,5},{5,4},{6,7},{7,6},{8,9},{9,8},{10,11... | collective-permute-start | bytes 491528 | tf_op jit(solution)/shard_map/ppermute | solution.py:175
  31.7 16.9 %collective-permute-start.2 = (bf16[320,256]{1,0:T(8,128)(2,1)S(1)}, bf16[320,256]{1,0:T(8,128)(2,1)S(1)}, u32[]{:S(2)}, u32[]{:S(2)}) collective-permute-start(bf16[320,256]{1,0:T(8,128)(2,1)S(1)} %collective-permute-done.refs_0_), channel_id=1, source_target_pairs={{0,1},{1,0},{2,3},{3,2},{4,5},{5,4},{6,7},{7,6},{8,9},{9,8},{10,11... | collective-permute-start | bytes 491528 | tf_op jit(solution)/shard_map/ppermute | solution.py:175
  34.2 14.5 %collective-permute-start.3 = (bf16[320,256]{1,0:T(8,128)(2,1)S(1)}, bf16[320,256]{1,0:T(8,128)(2,1)S(1)}, u32[]{:S(2)}, u32[]{:S(2)}) collective-permute-start(bf16[320,256]{1,0:T(8,128)(2,1)S(1)} %collective-permute-done.1.refs_1_), channel_id=1, source_target_pairs={{0,1},{1,0},{2,3},{3,2},{4,5},{5,4},{6,7},{7,6},{8,9},{9,8},{10,11... | collective-permute-start | bytes 491528 | tf_op jit(solution)/shard_map/ppermute | solution.py:175
  37.9 1.3 %copy-start = (f32[256,2048]{1,0:T(8,128)}, f32[256,2048]{1,0:T(8,128)S(1)}, u32[]{:S(2)}) copy-start(f32[256,2048]{1,0:T(8,128)S(1)} %shard_map.92.refs_6_) | copy-start | bytes 6291460
  43.2 1.3 %copy-start.1 = (f32[256,2048]{1,0:T(8,128)}, f32[256,2048]{1,0:T(8,128)S(1)}, u32[]{:S(2)}) copy-start(f32[256,2048]{1,0:T(8,128)S(1)} %shard_map.93.refs_6_) | copy-start | bytes 6291460
  (1 other events, 0.7 us)

commit v2 on v1

v2 whole, which is shorter than its diff:
```python
import functools

import jax
import jax.numpy as jnp
from jax import lax
from jax.experimental import pallas as pl
from jax.experimental.pallas import tpu as pltpu
from jax.sharding import PartitionSpec as P

MIB = 1024 * 1024


def repeat_rows(values, times):
    rows, cols = values.shape
    return jnp.broadcast_to(values[:, None, :], (rows, times, cols)).reshape(rows * times, cols)


def place_of(device, half):
    chip = device // 2
    return chip // 2 + (chip % 2) * (2 * half - 1 - 2 * (chip // 2))


def chip_at(place, half):
    return jnp.where(place < half, 2 * place, 2 * (2 * half - 1 - place) + 1)


def project_kernel(
    rows_here,
    x_hbm,
    gain_hbm,
    shift_hbm,
    first_hbm,
    first_offset_hbm,
    second_hbm,
    second_offset_hbm,
    keep_ref,
    give_ref,
    x_ref,
    gain_ref,
    shift_ref,
    first_ref,
    first_offset_ref,
    second_ref,
    second_offset_ref,
    left_ref,
    sems,
):
    samples, residues, _ = x_ref.shape
    hidden = first_ref.shape[0]
    width = samples * hidden
    small = [
        (first_hbm, first_ref),
        (second_hbm, second_ref),
        (gain_hbm, gain_ref),
        (shift_hbm, shift_ref),
        (first_offset_hbm, first_offset_ref),
        (second_offset_hbm, second_offset_ref),
    ]
    copies = [pltpu.make_async_copy(x_hbm.at[0], x_ref.at[0], sems.at[0])]
    copies += [
        pltpu.make_async_copy(src, dst, sems.at[samples + n]) for n, (src, dst) in enumerate(small)
    ]
    copies += [pltpu.make_async_copy(x_hbm.at[s], x_ref.at[s], sems.at[s]) for s in range(1, samples)]
    for copy in copies:
        copy.start()
    for copy in copies[1 : 1 + len(small)]:
        copy.wait()

    first = jnp.concatenate([first_ref[...].astype(jnp.float32)] * samples, axis=0)
    second = repeat_rows(second_ref[...].astype(jnp.float32), samples)
    row = lax.broadcasted_iota(jnp.int32, (width, 1), 0)
    spot = lax.broadcasted_iota(jnp.int32, (hidden, width), 1)
    channel = lax.broadcasted_iota(jnp.int32, (hidden, width), 0)

    def spread(offset_ref, owner):
        return jnp.dot(
            offset_ref[...],
            (owner == channel).astype(jnp.float32),
            precision=lax.Precision.HIGHEST,
            preferred_element_type=jnp.float32,
        )

    first_offset = spread(first_offset_ref, spot % hidden)
    second_offset = spread(second_offset_ref, spot // samples)
    left = jnp.zeros((residues, width), jnp.float32)
    right = jnp.zeros((residues, width), jnp.float32)
    dims = (((1,), (1,)), ((), ()))
    for s in range(samples):
        if s == 0:
            copies[0].wait()
        else:
            copies[len(small) + s].wait()
        values = x_ref[s].astype(jnp.float32)
        center = jnp.mean(values, axis=-1, keepdims=True)
        values = values - center
        variance = jnp.mean(jnp.square(values), axis=-1, keepdims=True)
        normed = (values * lax.rsqrt(variance + 1e-05) * gain_ref[...] + shift_ref[...]).astype(
            jnp.bfloat16
        )
        first_here = jnp.where(row // hidden == s, first, 0.0).astype(jnp.bfloat16)
        second_here = jnp.where(row % samples == s, second, 0.0).astype(jnp.bfloat16)
        left += lax.dot_general(normed, first_here, dims, preferred_element_type=jnp.float32)
        right += lax.dot_general(normed, second_here, dims, preferred_element_type=jnp.float32)
    left_ref[...] = (left + first_offset).astype(jnp.bfloat16)
    right = (right + second_offset).astype(jnp.bfloat16)
    keep_ref[:residues, :] = right
    give_ref[:residues, :] = right

    device = lax.axis_index("row")
    per_chip = 2 * rows_here
    half = residues // per_chip // 2
    way = 1 - 2 * (device % 2)
    place = place_of(device, half)
    for n in range(half):
        low = residues + n * per_chip
        for message, ahead in ((keep_ref, way * (half - n)), (give_ref, -way * (half - 1 - n))):
            chip = chip_at(lax.rem(place + ahead + 2 * half, 2 * half), half)
            start = pl.multiple_of(chip * per_chip, per_chip)
            message[low : low + per_chip, :] = left_ref[pl.ds(start, per_chip), :]


def pair_kernel(count, rows_here, samples, begins, ends, *refs):
    refs = list(refs)
    messages = [refs.pop(0) for _ in range(count)]
    if begins:
        final_ref, total_out, weight_ref, mixed_ref, wide_ref = refs
    elif ends:
        weight_ref, total_ref, offset_ref, out_hbm, mixed_ref, out_ref, sems = refs
    else:
        weight_ref, total_ref, total_out, mixed_ref = refs
    width, columns = weight_ref.shape
    channels = mixed_ref.shape[1] // rows_here
    hidden = columns // channels
    here = width // hidden
    residues = (total_out if begins else total_ref).shape[0]
    core = lax.rem(lax.axis_index("row"), 2)

    if begins:
        wide_ref[...] = final_ref[...].astype(jnp.float32)
        for e in range(hidden):
            rows = wide_ref[pl.ds(e, hidden, stride=hidden), :].astype(jnp.bfloat16)
            weight_ref[:, e * channels : (e + 1) * channels] = jnp.concatenate([rows] * here, axis=0)

    row = lax.broadcasted_iota(jnp.int32, (rows_here * here, width), 0)
    lane = lax.broadcasted_iota(jnp.int32, (rows_here * here, width), 1)
    mine = lane // hidden == row % here
    picked = []
    for message in messages:
        start = pl.multiple_of(message.shape[0] - (2 - core) * rows_here, rows_here)
        left = message[pl.ds(start, rows_here), :].astype(jnp.float32)
        picked.append(jnp.where(mine, repeat_rows(left, here), 0.0).astype(jnp.bfloat16))
    picked = jnp.concatenate(picked, axis=0)

    group = 8
    for chunk in range(hidden // group):
        mixed = jnp.dot(
            picked,
            weight_ref[:, chunk * group * channels : (chunk + 1) * group * channels],
            preferred_element_type=jnp.float32,
        )
        for n in range(count):
            for i in range(rows_here):
                top = (n * rows_here + i) * here
                piece = jnp.concatenate(
                    [mixed[top : top + here, e * channels : (e + 1) * channels] for e in range(group)],
                    axis=0,
                )
                low = n * width + chunk * group * here
                mixed_ref[low : low + group * here, i * channels : (i + 1) * channels] = piece.astype(
                    jnp.bfloat16
                )

    right = jnp.concatenate([message[:residues, :] for message in messages], axis=1)
    pair = 2
    copies = []
    for i in range(0, rows_here, pair):
        cols = slice(i * channels, (i + pair) * channels)
        value = jnp.dot(right, mixed_ref[:, cols], preferred_element_type=jnp.float32)
        if not begins:
            value = value + total_ref[:, cols]
        if ends:
            for k in range(pair):
                part = value[:, k * channels : (k + 1) * channels]
                out_ref[i + k] = (part * (1.0 / samples) + offset_ref[...]).astype(jnp.bfloat16)
            copies.append(
                pltpu.make_async_copy(
                    out_ref.at[pl.ds(i, pair)], out_hbm.at[pl.ds(i, pair)], sems.at[i // pair]
                )
            )
            copies[-1].start()
        else:
            total_out[:, cols] = value
    for copy in copies:
        copy.wait()


def per_device(
    size,
    alignment_embedding,
    rescaling_factor,
    recentering_offset,
    first_side_coefficients,
    first_side_offset,
    second_side_coefficients,
    second_side_offset,
    final_projector_coefficients,
    final_projector_offset,
):
    here, residues, features = alignment_embedding.shape
    hidden = first_side_coefficients.shape[1]
    channels = final_projector_coefficients.shape[1]
    width = here * hidden
    samples = here * size
    rows_here = residues // size
    per_chip = 2 * rows_here
    half = size // 4
    message = jax.ShapeDtypeStruct((residues + half * per_chip, width), jnp.bfloat16)

    vmem = pl.BlockSpec(memory_space=pltpu.VMEM)
    hbm = pl.BlockSpec(memory_space=pltpu.HBM)
    keep, give = pl.pallas_call(
        functools.partial(project_kernel, rows_here),
        out_shape=[message] * 2,
        in_specs=[hbm] * 7,
        out_specs=[vmem] * 2,
        scratch_shapes=[
            pltpu.VMEM((here, residues, features), jnp.bfloat16),
            pltpu.VMEM((1, features), jnp.float32),
            pltpu.VMEM((1, features), jnp.float32),
            pltpu.VMEM((hidden, features), jnp.bfloat16),
            pltpu.VMEM((1, hidden), jnp.float32),
            pltpu.VMEM((hidden, features), jnp.bfloat16),
            pltpu.VMEM((1, hidden), jnp.float32),
            pltpu.VMEM((residues, width), jnp.bfloat16),
            pltpu.SemaphoreType.DMA((here + 6,)),
        ],
        compiler_params=pltpu.CompilerParams(vmem_limit_bytes=32 * MIB),
        cost_estimate=pl.CostEstimate(
            flops=4 * here * residues * features * width,
            bytes_accessed=2 * here * residues * features,
            transcendentals=0,
        ),
    )(
        *[
            pltpu.with_memory_space_constraint(value, pltpu.HBM)
            for value in (
                alignment_embedding,
                rescaling_factor.reshape(1, features),
                recentering_offset.reshape(1, features),
                first_side_coefficients.T,
                first_side_offset.reshape(1, hidden),
                second_side_coefficients.T,
                second_side_offset.reshape(1, hidden),
            )
        ]
    )

    by_place = {(place_of(r, half), r % 2): r for r in range(size)}
    around = [
        (r, by_place[(place_of(r, half) + 1 - 2 * (r % 2)) % (2 * half), r % 2]) for r in range(size)
    ]
    across = [(r, r ^ 1) for r in range(size)]

    def pass_on(value):
        return lax.ppermute(value, "row", around)

    def swap(value):
        return lax.ppermute(value, "row", across)

    def accumulate(messages, total, weight, ends):
        begins = total is None
        flat = jax.ShapeDtypeStruct((residues, rows_here * channels), jnp.float32)
        spread = jax.ShapeDtypeStruct((width, hidden * channels), jnp.bfloat16)
        scratch = [pltpu.VMEM((len(messages) * width, rows_here * channels), jnp.bfloat16)]
        operands = list(messages)
        if begins:
            operands += [final_projector_coefficients]
            result, out_specs = [flat, spread], [vmem, vmem]
            scratch += [pltpu.VMEM(final_projector_coefficients.shape, jnp.float32)]
        elif ends:
            operands += [weight, total, final_projector_offset.reshape(1, channels)]
            result = jax.ShapeDtypeStruct((rows_here, residues, channels), jnp.bfloat16)
            out_specs = hbm
            scratch += [
                pltpu.VMEM((rows_here, residues, channels), jnp.bfloat16),
                pltpu.SemaphoreType.DMA((rows_here,)),
            ]
        else:
            operands += [weight, total]
            result, out_specs = flat, vmem
        work = 4 * len(messages) * residues * width * rows_here * channels
        return pl.pallas_call(
            functools.partial(pair_kernel, len(messages), rows_here, samples, begins, ends),
            out_shape=result,
            in_specs=[vmem] * len(operands),
            out_specs=out_specs,
            scratch_shapes=scratch,
            compiler_params=pltpu.CompilerParams(vmem_limit_bytes=32 * MIB),
            cost_estimate=pl.CostEstimate(flops=work, bytes_accessed=4 * MIB, transcendentals=0),
        )(*operands)

    given = swap(give)
    flying = [keep, given[: residues + (half - 1) * per_chip]]
    total, weight = accumulate([give, given], None, None, False)
    for step in range(1, half + 1):
        landed = [pass_on(value) for value in flying]
        messages = landed + [swap(value) for value in landed]
        total = accumulate(messages, total, weight, step == half)
        if step < half:
            flying = [value[: value.shape[0] - per_chip] for value in landed]
            if step == half - 1:
                flying = flying[:1]
    return total


def solution(mesh):
    return jax.shard_map(
        functools.partial(per_device, mesh.shape["row"]),
        mesh=mesh,
        in_specs=(P(("groups", "row"), None, None), P(), P(), P(), P(), P(), P(), P(), P()),
        out_specs=P(("groups", "row"), None, None),
        check_vma=False,
    )
```

time: 52.7 us -> 34.6 us (0.66); the launches traced: 52 us -> 34.5 us
  waiting for transfers between devices: 15.1 us -> 3.59 us
  local copies, waits for them, and re-layouts: 9.29 us -> 0.08 us
  starting transfers between devices: 12.2 us -> 15.6 us
    ppermute x15, waiting for transfers between devices: 15.1 us -> 3.59 us  [the longest x7 3.57 us: pass_on(): return lax.ppermute(value, 'row', around)]
    unnamed x20 -> x4, local copies, waits for them, and re-layouts: 7.99 us -> 0.01 us
    ppermute x15, starting transfers between devices: 12.2 us -> 15.6 us  [the longest x7 13.7 us: pass_on(): return lax.ppermute(value, 'row', around)]
    pallas_call x4 -> x5, Pallas kernels: 13.8 us -> 11.3 us  [accumulate(): pl.pallas_call(functools.partial(pair_kernel, len(messages), rows_here, s...]
    pallas_call x1, Pallas kernels: 1.52 us -> 3.62 us  [per_device(): pl.pallas_call(functools.partial(project_kernel, rows_here), out_shape=[m...]
    another operation x2 -> x0, local copies, waits for them, and re-layouts: 1.3 us -> none  [per_device(): jnp.tile(final_projector_coefficients.reshape(hidden, hidden * channels),...]
  transfers between devices with their start and end apart: 15 -> 15, of which waited for: 4 -> 3; matrix products, arithmetic and copies ran while one was open for 2% -> 0% of each run, Pallas kernels for 20% -> 26%
where the time goes in v2:
time: 34.6 us; the launch traced here: 34.5 us
  starting transfers between devices  15.6 us (45%)
  Pallas kernels  15 us (43%)
  waiting for transfers between devices  3.59 us (10%)
    ppermute x7, starting transfers between devices, pass_on(): return lax.ppermute(value, 'row', around)  13.7 us
    pallas_call x5, Pallas kernels, accumulate(): pl.pallas_call(functools.partial(pair_kernel, len(messages), rows_here, s...  11.3 us
    pallas_call x1, Pallas kernels, per_device(): pl.pallas_call(functools.partial(project_kernel, rows_here), out_shape=[m...  3.62 us
    ppermute x7, waiting for transfers between devices, pass_on(): return lax.ppermute(value, 'row', around)  3.57 us
    ppermute x8, starting transfers between devices, swap(): return lax.ppermute(value, 'row', across)  1.83 us
  transfers between devices with their start and end apart: 15, of which 3 were waited for; matrix products, arithmetic and copies ran while one was open for 0% of the time, Pallas kernels for 26%

profile of v2, /device:TPU:0, one launch (start us, length us, event | category | flops | bytes accessed | tf_op | source)
XLA Modules:
  0.0 34.5 jit_solution(2049784501879176657)
XLA Ops:
  0.0 3.6 %shard_map.91 = (bf16[384,256]{1,0:T(8,128)(2,1)S(1)}, bf16[384,256]{1,0:T(8,128)(2,1)S(1)}) custom-call(bf16[8,256,256]{2,1,0:T(8,128)(2,1)} %x_hbm.1, f32[1,256]{1,0:T(1,128)} %bitcast.10, f32[1,256]{1,0:T(1,128)} %bitcast.11, bf16[32,256]{1,0:T(8,128)(2,1)} %bitcast.8, f32[1,32]{1,0:T(1,128)} %bitcast.12, bf16[32,256]{1,0:T(8,128)(2,1)} %bitcast.9, ...), custom_call_target="tpu_custom_call" | custom-call | flops 536870912 | bytes 1048576 | tf_op jit(solution)/shard_map/pallas_call | solution.py:221
  3.6 0.5 %collective-permute-start.5 = (bf16[384,256]{1,0:T(8,128)(2,1)S(1)}, bf16[384,256]{1,0:T(8,128)(2,1)S(1)}, u32[]{:S(2)}, u32[]{:S(2)}) collective-permute-start(bf16[384,256]{1,0:T(8,128)(2,1)S(1)} %get-tuple-element.10.refs_0_), channel_id=1, source_target_pairs={{0,1},{1,0},{2,3},{3,2},{4,5},{5,4},{6,7},{7,6},{8,9},{9,8},{10,11... | collective-permute-start | bytes 589832 | tf_op jit(solution)/shard_map/ppermute | solution.py:268
  4.2 2.6 %collective-permute-start = (bf16[384,256]{1,0:T(8,128)(2,1)S(1)}, bf16[384,256]{1,0:T(8,128)(2,1)S(1)}, u32[]{:S(2)}, u32[]{:S(2)}) collective-permute-start(bf16[384,256]{1,0:T(8,128)(2,1)S(1)} %get-tuple-element.9), channel_id=1, source_target_pairs={{0,4},{1,3},{2,0},{3,7},{4,8},{5,1},{6,2},{7,11},{8,12},{9,5},{10,... | collective-permute-start | bytes 589832 | tf_op jit(solution)/shard_map/ppermute | solution.py:265
  6.8 1.6 %collective-permute-start.6 = (bf16[352,256]{1,0:T(8,128)(2,1)S(1)}, bf16[352,256]{1,0:T(8,128)(2,1)S(1)}, u32[]{:S(2)}, u32[]{:S(2)}) collective-permute-start(bf16[352,256]{1,0:T(8,128)(2,1)S(1)} %slice.27), channel_id=1, source_target_pairs={{0,4},{1,3},{2,0},{3,7},{4,8},{5,1},{6,2},{7,11},{8,12},{9,5},{10,... | collective-permute-start | bytes 540680 | tf_op jit(solution)/shard_map/ppermute | solution.py:265
  8.4 1.9 %collective-permute-done.refs_0_ = bf16[384,256]{1,0:T(8,128)(2,1)S(1)} collective-permute-done((bf16[384,256]{1,0:T(8,128)(2,1)S(1)}, bf16[384,256]{1,0:T(8,128)(2,1)S(1)}, u32[]{:S(2)}, u32[]{:S(2)}) %collective-permute-start) | collective-permute-done | bytes 196640 | tf_op jit(solution)/shard_map/ppermute | solution.py:265
  10.4 2.1 %collective-permute-start.1 = (bf16[352,256]{1,0:T(8,128)(2,1)S(1)}, bf16[352,256]{1,0:T(8,128)(2,1)S(1)}, u32[]{:S(2)}, u32[]{:S(2)}) collective-permute-start(bf16[352,256]{1,0:T(8,128)(2,1)S(1)} %slice.24), channel_id=1, source_target_pairs={{0,4},{1,3},{2,0},{3,7},{4,8},{5,1},{6,2},{7,11},{8,12},{9,5},{10,... | collective-permute-start | bytes 540680 | tf_op jit(solution)/shard_map/ppermute | solution.py:265
  12.5 0.0 collective-permute-start.13
  12.5 0.5 %collective-permute-start.14 = (bf16[352,256]{1,0:T(8,128)(2,1)S(1)}, bf16[352,256]{1,0:T(8,128)(2,1)S(1)}, u32[]{:S(2)}, u32[]{:S(2)}) collective-permute-start(bf16[352,256]{1,0:T(8,128)(2,1)S(1)} %collective-permute-done.6.refs_1_), channel_id=1, source_target_pairs={{0,1},{1,0},{2,3},{3,2},{4,5},{5,4},{6,7},{7,6},{8,9},{9,8},{10,11... | collective-permute-start | bytes 540680 | tf_op jit(solution)/shard_map/ppermute | solution.py:268
  13.1 1.6 %collective-permute-start.7 = (bf16[320,256]{1,0:T(8,128)(2,1)S(1)}, bf16[320,256]{1,0:T(8,128)(2,1)S(1)}, u32[]{:S(2)}, u32[]{:S(2)}) collective-permute-start(bf16[320,256]{1,0:T(8,128)(2,1)S(1)} %slice.28), channel_id=1, source_target_pairs={{0,4},{1,3},{2,0},{3,7},{4,8},{5,1},{6,2},{7,11},{8,12},{9,5},{10,... | collective-permute-start | bytes 491528 | tf_op jit(solution)/shard_map/ppermute | solution.py:265
  14.7 1.3 %collective-permute-done.1.refs_0_ = bf16[352,256]{1,0:T(8,128)(2,1)S(1)} collective-permute-done((bf16[352,256]{1,0:T(8,128)(2,1)S(1)}, bf16[352,256]{1,0:T(8,128)(2,1)S(1)}, u32[]{:S(2)}, u32[]{:S(2)}) %collective-permute-start.1) | collective-permute-done | bytes 180256 | tf_op jit(solution)/shard_map/ppermute | solution.py:265
  16.0 2.1 %collective-permute-start.2 = (bf16[320,256]{1,0:T(8,128)(2,1)S(1)}, bf16[320,256]{1,0:T(8,128)(2,1)S(1)}, u32[]{:S(2)}, u32[]{:S(2)}) collective-permute-start(bf16[320,256]{1,0:T(8,128)(2,1)S(1)} %slice.25), channel_id=1, source_target_pairs={{0,4},{1,3},{2,0},{3,7},{4,8},{5,1},{6,2},{7,11},{8,12},{9,5},{10,... | collective-permute-start | bytes 491528 | tf_op jit(solution)/shard_map/ppermute | solution.py:265
  18.1 1.9 %shard_map.92 = (f32[256,2048]{1,0:T(8,128)S(1)}, bf16[256,4096]{1,0:T(8,128)(2,1)S(1)}) custom-call(bf16[384,256]{1,0:T(8,128)(2,1)S(1)} %get-tuple-element.10.refs_0_, bf16[384,256]{1,0:T(8,128)(2,1)S(1)} %collective-permute-done.5.refs_1_, bf16[1024,128]{1,0:T(8,128)(2,1)S(1)} %copy-done.1), custom_call_target="tpu_custom_call" | custom-call | flops 1073741824 | bytes 4194304 | tf_op jit(solution)/shard_map/pallas_call | solution.py:292
  20.0 0.1 collective-permute-start.11
  20.1 1.6 %collective-permute-start.8 = (bf16[288,256]{1,0:T(8,128)(2,1)S(1)}, bf16[288,256]{1,0:T(8,128)(2,1)S(1)}, u32[]{:S(2)}, u32[]{:S(2)}) collective-permute-start(bf16[288,256]{1,0:T(8,128)(2,1)S(1)} %slice.29), channel_id=1, source_target_pairs={{0,4},{1,3},{2,0},{3,7},{4,8},{5,1},{6,2},{7,11},{8,12},{9,5},{10,... | collective-permute-start | bytes 442376 | tf_op jit(solution)/shard_map/ppermute | solution.py:265
  21.7 1.9 %collective-permute-start.3 = (bf16[288,256]{1,0:T(8,128)(2,1)S(1)}, bf16[288,256]{1,0:T(8,128)(2,1)S(1)}, u32[]{:S(2)}, u32[]{:S(2)}) collective-permute-start(bf16[288,256]{1,0:T(8,128)(2,1)S(1)} %slice.26), channel_id=1, source_target_pairs={{0,4},{1,3},{2,0},{3,7},{4,8},{5,1},{6,2},{7,11},{8,12},{9,5},{10,... | collective-permute-start | bytes 442376 | tf_op jit(solution)/shard_map/ppermute | solution.py:265
  23.7 0.5 %collective-permute-start.9 = (bf16[320,256]{1,0:T(8,128)(2,1)S(1)}, bf16[320,256]{1,0:T(8,128)(2,1)S(1)}, u32[]{:S(2)}, u32[]{:S(2)}) collective-permute-start(bf16[320,256]{1,0:T(8,128)(2,1)S(1)} %collective-permute-done.2.refs_0_), channel_id=1, source_target_pairs={{0,1},{1,0},{2,3},{3,2},{4,5},{5,4},{6,7},{7,6},{8,9},{9,8},{10,11... | collective-permute-start | bytes 491528 | tf_op jit(solution)/shard_map/ppermute | solution.py:268
  24.2 2.4 %shard_map.93.refs_5_ = f32[256,2048]{1,0:T(8,128)S(1)} custom-call(bf16[384,256]{1,0:T(8,128)(2,1)S(1)} %collective-permute-done.refs_0_, bf16[352,256]{1,0:T(8,128)(2,1)S(1)} %collective-permute-done.6.refs_1_, bf16[384,256]{1,0:T(8,128)(2,1)S(1)} %collective-permute-done.13.refs_2_, bf16[352,256]{1,0:T(8,128)(2,1)S(1)} %collective-permute-done.14.refs_3_, ...), custom_call_target="tpu_custom_call" | custom-call | flops 2147483648 | bytes 4194304 | tf_op jit(solution)/shard_map/pallas_call | solution.py:292
  26.6 0.1 collective-permute-start.10
  26.7 0.4 %collective-permute-done.3.refs_0_ = bf16[288,256]{1,0:T(8,128)(2,1)S(1)} collective-permute-done((bf16[288,256]{1,0:T(8,128)(2,1)S(1)}, bf16[288,256]{1,0:T(8,128)(2,1)S(1)}, u32[]{:S(2)}, u32[]{:S(2)}) %collective-permute-start.3) | collective-permute-done | bytes 147488 | tf_op jit(solution)/shard_map/ppermute | solution.py:265
  27.1 0.1 collective-permute-start.4
  27.2 2.4 %shard_map.94.refs_5_ = f32[256,2048]{1,0:T(8,128)S(1)} custom-call(bf16[352,256]{1,0:T(8,128)(2,1)S(1)} %collective-permute-done.1.refs_0_, bf16[320,256]{1,0:T(8,128)(2,1)S(1)} %collective-permute-done.7.refs_1_, bf16[352,256]{1,0:T(8,128)(2,1)S(1)} %collective-permute-done.11.refs_2_, bf16[320,256]{1,0:T(8,128)(2,1)S(1)} %collective-permute-done.12.refs_3_, ...), custom_call_target="tpu_custom_call" | custom-call | flops 2147483648 | bytes 4194304 | tf_op jit(solution)/shard_map/pallas_call | solution.py:292
  29.6 0.0 copy-start
  29.6 2.4 %shard_map.95.refs_3_ = f32[256,2048]{1,0:T(8,128)S(1)} custom-call(bf16[320,256]{1,0:T(8,128)(2,1)S(1)} %collective-permute-done.2.refs_0_, bf16[288,256]{1,0:T(8,128)(2,1)S(1)} %collective-permute-done.8.refs_1_, bf16[320,256]{1,0:T(8,128)(2,1)S(1)} %collective-permute-done.9.refs_2_, bf16[288,256]{1,0:T(8,128)(2,1)S(1)} %collective-permute-done.10.refs_3_, ...), custom_call_target="tpu_custom_call" | custom-call | flops 2147483648 | bytes 4194304 | tf_op jit(solution)/shard_map/pallas_call | solution.py:292
  32.1 2.2 %shard_map.96 = bf16[16,256,128]{2,1,0:T(8,128)(2,1)} custom-call(bf16[288,256]{1,0:T(8,128)(2,1)S(1)} %collective-permute-done.3.refs_0_, bf16[288,256]{1,0:T(8,128)(2,1)S(1)} %collective-permute-done.4.refs_1_, bf16[256,4096]{1,0:T(8,128)(2,1)S(1)} %get-tuple-element.11.refs_4_.refs_2_, f32[256,2048]{1,0:T(8,128)S(1)} %shard_map.95.refs_3_, ...), custom_call_target="tpu_custom_call" | custom-call | flops 1073741824 | bytes 4194304 | tf_op jit(solution)/shard_map/pallas_call | solution.py:292
  (22 shorter events, 0.1 us)
Async XLA Ops:
  0.0 18.1 %copy-start.1 = (bf16[1024,128]{1,0:T(8,128)(2,1)S(1)}, bf16[1024,128]{1,0:T(8,128)(2,1)}, u32[]{:S(2)}) copy-start(bf16[1024,128]{1,0:T(8,128)(2,1)} %refs_2_.1) | copy-start | bytes 786436
  3.6 3.2 %collective-permute-start.5 = (bf16[384,256]{1,0:T(8,128)(2,1)S(1)}, bf16[384,256]{1,0:T(8,128)(2,1)S(1)}, u32[]{:S(2)}, u32[]{:S(2)}) collective-permute-start(bf16[384,256]{1,0:T(8,128)(2,1)S(1)} %get-tuple-element.10.refs_0_), channel_id=1, source_target_pairs={{0,1},{1,0},{2,3},{3,2},{4,5},{5,4},{6,7},{7,6},{8,9},{9,8},{10,11... | collective-permute-start | bytes 589832 | tf_op jit(solution)/shard_map/ppermute | solution.py:268
  4.2 6.2 %collective-permute-start = (bf16[384,256]{1,0:T(8,128)(2,1)S(1)}, bf16[384,256]{1,0:T(8,128)(2,1)S(1)}, u32[]{:S(2)}, u32[]{:S(2)}) collective-permute-start(bf16[384,256]{1,0:T(8,128)(2,1)S(1)} %get-tuple-element.9), channel_id=1, source_target_pairs={{0,4},{1,3},{2,0},{3,7},{4,8},{5,1},{6,2},{7,11},{8,12},{9,5},{10,... | collective-permute-start | bytes 589832 | tf_op jit(solution)/shard_map/ppermute | solution.py:265
  6.8 5.7 %collective-permute-start.6 = (bf16[352,256]{1,0:T(8,128)(2,1)S(1)}, bf16[352,256]{1,0:T(8,128)(2,1)S(1)}, u32[]{:S(2)}, u32[]{:S(2)}) collective-permute-start(bf16[352,256]{1,0:T(8,128)(2,1)S(1)} %slice.27), channel_id=1, source_target_pairs={{0,4},{1,3},{2,0},{3,7},{4,8},{5,1},{6,2},{7,11},{8,12},{9,5},{10,... | collective-permute-start | bytes 540680 | tf_op jit(solution)/shard_map/ppermute | solution.py:265
  10.4 5.5 %collective-permute-start.1 = (bf16[352,256]{1,0:T(8,128)(2,1)S(1)}, bf16[352,256]{1,0:T(8,128)(2,1)S(1)}, u32[]{:S(2)}, u32[]{:S(2)}) collective-permute-start(bf16[352,256]{1,0:T(8,128)(2,1)S(1)} %slice.24), channel_id=1, source_target_pairs={{0,4},{1,3},{2,0},{3,7},{4,8},{5,1},{6,2},{7,11},{8,12},{9,5},{10,... | collective-permute-start | bytes 540680 | tf_op jit(solution)/shard_map/ppermute | solution.py:265
  12.5 11.1 %collective-permute-start.13 = (bf16[384,256]{1,0:T(8,128)(2,1)S(1)}, bf16[384,256]{1,0:T(8,128)(2,1)S(1)}, u32[]{:S(2)}, u32[]{:S(2)}) collective-permute-start(bf16[384,256]{1,0:T(8,128)(2,1)S(1)} %collective-permute-done.refs_0_), channel_id=1, source_target_pairs={{0,1},{1,0},{2,3},{3,2},{4,5},{5,4},{6,7},{7,6},{8,9},{9,8},{10,11... | collective-permute-start | bytes 589832 | tf_op jit(solution)/shard_map/ppermute | solution.py:268
  12.5 11.1 %collective-permute-start.14 = (bf16[352,256]{1,0:T(8,128)(2,1)S(1)}, bf16[352,256]{1,0:T(8,128)(2,1)S(1)}, u32[]{:S(2)}, u32[]{:S(2)}) collective-permute-start(bf16[352,256]{1,0:T(8,128)(2,1)S(1)} %collective-permute-done.6.refs_1_), channel_id=1, source_target_pairs={{0,1},{1,0},{2,3},{3,2},{4,5},{5,4},{6,7},{7,6},{8,9},{9,8},{10,11... | collective-permute-start | bytes 540680 | tf_op jit(solution)/shard_map/ppermute | solution.py:268
  13.1 7.0 %collective-permute-start.7 = (bf16[320,256]{1,0:T(8,128)(2,1)S(1)}, bf16[320,256]{1,0:T(8,128)(2,1)S(1)}, u32[]{:S(2)}, u32[]{:S(2)}) collective-permute-start(bf16[320,256]{1,0:T(8,128)(2,1)S(1)} %slice.28), channel_id=1, source_target_pairs={{0,4},{1,3},{2,0},{3,7},{4,8},{5,1},{6,2},{7,11},{8,12},{9,5},{10,... | collective-permute-start | bytes 491528 | tf_op jit(solution)/shard_map/ppermute | solution.py:265
  16.0 5.7 %collective-permute-start.2 = (bf16[320,256]{1,0:T(8,128)(2,1)S(1)}, bf16[320,256]{1,0:T(8,128)(2,1)S(1)}, u32[]{:S(2)}, u32[]{:S(2)}) collective-permute-start(bf16[320,256]{1,0:T(8,128)(2,1)S(1)} %slice.25), channel_id=1, source_target_pairs={{0,4},{1,3},{2,0},{3,7},{4,8},{5,1},{6,2},{7,11},{8,12},{9,5},{10,... | collective-permute-start | bytes 491528 | tf_op jit(solution)/shard_map/ppermute | solution.py:265
  20.0 7.2 %collective-permute-start.11 = (bf16[352,256]{1,0:T(8,128)(2,1)S(1)}, bf16[352,256]{1,0:T(8,128)(2,1)S(1)}, u32[]{:S(2)}, u32[]{:S(2)}) collective-permute-start(bf16[352,256]{1,0:T(8,128)(2,1)S(1)} %collective-permute-done.1.refs_0_), channel_id=1, source_target_pairs={{0,1},{1,0},{2,3},{3,2},{4,5},{5,4},{6,7},{7,6},{8,9},{9,8},{10,11... | collective-permute-start | bytes 540680 | tf_op jit(solution)/shard_map/ppermute | solution.py:268
  20.1 6.5 %collective-permute-start.8 = (bf16[288,256]{1,0:T(8,128)(2,1)S(1)}, bf16[288,256]{1,0:T(8,128)(2,1)S(1)}, u32[]{:S(2)}, u32[]{:S(2)}) collective-permute-start(bf16[288,256]{1,0:T(8,128)(2,1)S(1)} %slice.29), channel_id=1, source_target_pairs={{0,4},{1,3},{2,0},{3,7},{4,8},{5,1},{6,2},{7,11},{8,12},{9,5},{10,... | collective-permute-start | bytes 442376 | tf_op jit(solution)/shard_map/ppermute | solution.py:265
  21.7 5.4 %collective-permute-start.3 = (bf16[288,256]{1,0:T(8,128)(2,1)S(1)}, bf16[288,256]{1,0:T(8,128)(2,1)S(1)}, u32[]{:S(2)}, u32[]{:S(2)}) collective-permute-start(bf16[288,256]{1,0:T(8,128)(2,1)S(1)} %slice.26), channel_id=1, source_target_pairs={{0,4},{1,3},{2,0},{3,7},{4,8},{5,1},{6,2},{7,11},{8,12},{9,5},{10,... | collective-permute-start | bytes 442376 | tf_op jit(solution)/shard_map/ppermute | solution.py:265
  23.7 3.5 %collective-permute-start.12 = (bf16[320,256]{1,0:T(8,128)(2,1)S(1)}, bf16[320,256]{1,0:T(8,128)(2,1)S(1)}, u32[]{:S(2)}, u32[]{:S(2)}) collective-permute-start(bf16[320,256]{1,0:T(8,128)(2,1)S(1)} %collective-permute-done.7.refs_1_), channel_id=1, source_target_pairs={{0,1},{1,0},{2,3},{3,2},{4,5},{5,4},{6,7},{7,6},{8,9},{9,8},{10,11... | collective-permute-start | bytes 491528 | tf_op jit(solution)/shard_map/ppermute | solution.py:268
  23.7 6.0 %collective-permute-start.9 = (bf16[320,256]{1,0:T(8,128)(2,1)S(1)}, bf16[320,256]{1,0:T(8,128)(2,1)S(1)}, u32[]{:S(2)}, u32[]{:S(2)}) collective-permute-start(bf16[320,256]{1,0:T(8,128)(2,1)S(1)} %collective-permute-done.2.refs_0_), channel_id=1, source_target_pairs={{0,1},{1,0},{2,3},{3,2},{4,5},{5,4},{6,7},{7,6},{8,9},{9,8},{10,11... | collective-permute-start | bytes 491528 | tf_op jit(solution)/shard_map/ppermute | solution.py:268
  26.6 3.0 %collective-permute-start.10 = (bf16[288,256]{1,0:T(8,128)(2,1)S(1)}, bf16[288,256]{1,0:T(8,128)(2,1)S(1)}, u32[]{:S(2)}, u32[]{:S(2)}) collective-permute-start(bf16[288,256]{1,0:T(8,128)(2,1)S(1)} %collective-permute-done.8.refs_1_), channel_id=1, source_target_pairs={{0,1},{1,0},{2,3},{3,2},{4,5},{5,4},{6,7},{7,6},{8,9},{9,8},{10,11... | collective-permute-start | bytes 442376 | tf_op jit(solution)/shard_map/ppermute | solution.py:268
  27.1 5.0 %collective-permute-start.4 = (bf16[288,256]{1,0:T(8,128)(2,1)S(1)}, bf16[288,256]{1,0:T(8,128)(2,1)S(1)}, u32[]{:S(2)}, u32[]{:S(2)}) collective-permute-start(bf16[288,256]{1,0:T(8,128)(2,1)S(1)} %collective-permute-done.3.refs_0_), channel_id=1, source_target_pairs={{0,1},{1,0},{2,3},{3,2},{4,5},{5,4},{6,7},{7,6},{8,9},{9,8},{10,11... | collective-permute-start | bytes 442376 | tf_op jit(solution)/shard_map/ppermute | solution.py:268
  29.6 2.5 %copy-start = (f32[128]{0:T(128)S(1)}, f32[128]{0:T(128)}, u32[]{:S(2)}) copy-start(f32[128]{0:T(128)} %param.17) | copy-start | bytes 1540

commit v3 on v2

v3 whole, which is shorter than its diff:
```python
import functools
import math

import jax
import jax.numpy as jnp
from jax import lax
from jax.experimental import pallas as pl
from jax.experimental.pallas import tpu as pltpu
from jax.sharding import PartitionSpec as P

MIB = 1024 * 1024
LANES = 128


def repeat_rows(values, times):
    rows, cols = values.shape
    return jnp.broadcast_to(values[:, None, :], (rows, times, cols)).reshape(rows * times, cols)


def place_of(device, half):
    chip = device // 2
    return chip // 2 + (chip % 2) * (2 * half - 1 - 2 * (chip // 2))


def chip_at(place, half):
    return jnp.where(place < half, 2 * place, 2 * (2 * half - 1 - place) + 1)


def project_kernel(
    rows_here,
    x_hbm,
    gain_hbm,
    shift_hbm,
    first_hbm,
    first_offset_hbm,
    second_hbm,
    second_offset_hbm,
    keep_ref,
    give_ref,
    x_ref,
    gain_ref,
    shift_ref,
    first_ref,
    first_offset_ref,
    second_ref,
    second_offset_ref,
    packed_ref,
    left_ref,
    sems,
):
    samples, residues, features = x_ref.shape
    hidden = first_ref.shape[0]
    width = samples * hidden
    tile = keep_ref.shape[1]
    tiles = residues // tile
    fold = LANES // hidden
    groups = residues // fold
    small = [
        (first_hbm, first_ref),
        (second_hbm, second_ref),
        (gain_hbm, gain_ref),
        (shift_hbm, shift_ref),
        (first_offset_hbm, first_offset_ref),
        (second_offset_hbm, second_offset_ref),
    ]
    copies = [pltpu.make_async_copy(x_hbm.at[0], x_ref.at[0], sems.at[0])]
    copies += [
        pltpu.make_async_copy(src, dst, sems.at[samples + n]) for n, (src, dst) in enumerate(small)
    ]
    copies += [pltpu.make_async_copy(x_hbm.at[s], x_ref.at[s], sems.at[s]) for s in range(1, samples)]
    for copy in copies:
        copy.start()
    for copy in copies[1 : 1 + len(small)]:
        copy.wait()

    first = jnp.concatenate([first_ref[...]] * fold, axis=0)
    first_offset = jnp.concatenate([first_offset_ref[...]] * fold, axis=1)
    second = repeat_rows(second_ref[...].astype(jnp.float32), samples)
    row = lax.broadcasted_iota(jnp.int32, (width, 1), 0)
    spot = lax.broadcasted_iota(jnp.int32, (width, hidden), 0)
    channel = lax.broadcasted_iota(jnp.int32, (width, hidden), 1)
    second_offset = jnp.sum(
        jnp.where(spot // samples == channel, second_offset_ref[...], 0.0), axis=1, keepdims=True
    )
    residue = lax.broadcasted_iota(jnp.int32, (tile, LANES), 0)
    lane = lax.broadcasted_iota(jnp.int32, (tile, LANES), 1)
    own = residue % fold == lane // hidden
    group = lax.broadcasted_iota(jnp.int32, (tile // fold, tile), 0)
    member = lax.broadcasted_iota(jnp.int32, (tile // fold, tile), 1)
    gather = (member // fold == group).astype(jnp.bfloat16)

    dims = (((1,), (1,)), ((), ()))
    right = [jnp.zeros((width, tile), jnp.float32) for _ in range(tiles)]
    for s in range(samples):
        if s == 0:
            copies[0].wait()
        else:
            copies[len(small) + s].wait()
        values = x_ref[s].astype(jnp.float32)
        center = jnp.mean(values, axis=-1, keepdims=True)
        values = values - center
        variance = jnp.mean(jnp.square(values), axis=-1, keepdims=True)
        normed = (values * lax.rsqrt(variance + 1e-05) * gain_ref[...] + shift_ref[...]).astype(
            jnp.bfloat16
        )
        second_here = jnp.where(row % samples == s, second, 0.0).astype(jnp.bfloat16)
        for t in range(tiles):
            part = normed[t * tile : (t + 1) * tile]
            right[t] += lax.dot_general(second_here, part, dims, preferred_element_type=jnp.float32)
            left = lax.dot_general(part, first, dims, preferred_element_type=jnp.float32)
            left = jnp.where(own, left + first_offset, 0.0).astype(jnp.bfloat16)
            low = s * groups + t * (tile // fold)
            packed_ref[low : low + tile // fold, :] = jnp.dot(
                gather, left, preferred_element_type=jnp.float32
            )
    for t in range(tiles):
        value = (right[t] + second_offset).astype(jnp.bfloat16)
        keep_ref[t * width : (t + 1) * width, :] = value
        give_ref[t * width : (t + 1) * width, :] = value
    across = tile // LANES
    for low in range(0, groups, across):
        at = low // across * samples
        left_ref[at : at + samples, :] = jnp.concatenate(
            [packed_ref[pl.ds(low + n, samples, stride=groups), :] for n in range(across)], axis=1
        )

    device = lax.axis_index("row")
    per_chip = 2 * rows_here * hidden * samples // tile
    half = residues // rows_here // 4
    base = tiles * width
    way = 1 - 2 * (device % 2)
    place = place_of(device, half)
    for n in range(half):
        low = base + n * per_chip
        for message, ahead in ((keep_ref, way * (half - n)), (give_ref, -way * (half - 1 - n))):
            chip = chip_at(lax.rem(place + ahead + 2 * half, 2 * half), half)
            start = pl.multiple_of(chip * per_chip, per_chip)
            message[low : low + per_chip, :] = left_ref[pl.ds(start, per_chip), :].astype(jnp.bfloat16)


def weight_kernel(final_ref, out_ref, wide_ref):
    channels, columns = out_ref.shape
    hidden = math.isqrt(columns)
    wide_ref[...] = final_ref[...].astype(jnp.float32)
    step = LANES // hidden
    for e in range(0, hidden, step):
        rows = [wide_ref[pl.ds(e + n, hidden, stride=hidden), :] for n in range(step)]
        out_ref[:, e * hidden : (e + step) * hidden] = jnp.concatenate(rows, axis=0).T.astype(
            jnp.bfloat16
        )


def pair_kernel(count, gridded, rows_here, hidden, samples, *refs):
    refs = list(refs)
    rights = [refs.pop(0) for _ in range(count)]
    lefts = [refs.pop(0) for _ in range(count)] if gridded else rights
    weight_ref, offset_ref, out_hbm, left_ref, outer_ref, out_ref, sems = refs
    tile = rights[0].shape[1]
    here = samples // count
    span = rows_here * hidden
    deep = span * here // tile
    core = lax.rem(lax.axis_index("row"), 2)
    pieces = []
    for ref in lefts:
        start = pl.multiple_of(ref.shape[0] - (2 - core) * deep, deep)
        piece = ref[pl.ds(start, deep), :].astype(jnp.float32)
        pieces.append(
            jnp.concatenate([piece[n * here : (n + 1) * here] for n in range(span // tile)], axis=1)
        )
    left_ref[...] = jnp.concatenate(pieces, axis=0).T.astype(jnp.bfloat16)

    left = left_ref[...]
    for e in range(0, hidden, 2):
        both = [ref[e * here : (e + 2) * here, :].astype(jnp.float32) for ref in rights]
        for k in range(2):
            right = jnp.concatenate([x[k * here : (k + 1) * here] for x in both], axis=0)
            outer = jnp.dot(left, right.astype(jnp.bfloat16), preferred_element_type=jnp.float32)
            outer = outer.astype(jnp.bfloat16)
            for i in range(rows_here):
                outer_ref[i, (e + k) * hidden : (e + k + 1) * hidden, :] = outer[
                    i * hidden : (i + 1) * hidden
                ]

    first = pl.program_id(0) * tile if gridded else 0
    copies = []
    for i in range(rows_here):
        value = jnp.dot(weight_ref[...], outer_ref[i], preferred_element_type=jnp.float32)
        value = value.T * (1.0 / samples) + offset_ref[...]
        out_ref[i] = value.astype(jnp.bfloat16)
        copies.append(
            pltpu.make_async_copy(out_ref.at[i], out_hbm.at[i, pl.ds(first, tile)], sems.at[i])
        )
        copies[-1].start()
    for copy in copies:
        copy.wait()


def per_device(
    size,
    alignment_embedding,
    rescaling_factor,
    recentering_offset,
    first_side_coefficients,
    first_side_offset,
    second_side_coefficients,
    second_side_offset,
    final_projector_coefficients,
    final_projector_offset,
):
    here, residues, features = alignment_embedding.shape
    hidden = first_side_coefficients.shape[1]
    channels = final_projector_coefficients.shape[1]
    width = here * hidden
    samples = here * size
    rows_here = residues // size
    half = size // 4
    tile = 256
    tiles = residues // tile
    body = tiles * width
    per_chip = 2 * rows_here * width // tile
    message = jax.ShapeDtypeStruct((body + half * per_chip, tile), jnp.bfloat16)

    vmem = pl.BlockSpec(memory_space=pltpu.VMEM)
    hbm = pl.BlockSpec(memory_space=pltpu.HBM)
    keep, give = pl.pallas_call(
        functools.partial(project_kernel, rows_here),
        out_shape=[message] * 2,
        in_specs=[hbm] * 7,
        out_specs=[vmem] * 2,
        scratch_shapes=[
            pltpu.VMEM((here, residues, features), jnp.bfloat16),
            pltpu.VMEM((1, features), jnp.float32),
            pltpu.VMEM((1, features), jnp.float32),
            pltpu.VMEM((hidden, features), jnp.bfloat16),
            pltpu.VMEM((1, hidden), jnp.float32),
            pltpu.VMEM((hidden, features), jnp.bfloat16),
            pltpu.VMEM((1, hidden), jnp.float32),
            pltpu.VMEM((residues * width // LANES, LANES), jnp.float32),
            pltpu.VMEM((residues * width // tile, tile), jnp.float32),
            pltpu.SemaphoreType.DMA((here + 6,)),
        ],
        compiler_params=pltpu.CompilerParams(vmem_limit_bytes=32 * MIB),
        cost_estimate=pl.CostEstimate(
            flops=4 * here * residues * features * width,
            bytes_accessed=2 * here * residues * features,
            transcendentals=0,
        ),
    )(
        *[
            pltpu.with_memory_space_constraint(value, pltpu.HBM)
            for value in (
                alignment_embedding,
                rescaling_factor.reshape(1, features),
                recentering_offset.reshape(1, features),
                first_side_coefficients.T,
                first_side_offset.reshape(1, hidden),
                second_side_coefficients.T,
                second_side_offset.reshape(1, hidden),
            )
        ]
    )
    weight = pl.pallas_call(
        weight_kernel,
        out_shape=jax.ShapeDtypeStruct((channels, hidden * hidden), jnp.bfloat16),
        in_specs=[vmem],
        out_specs=vmem,
        scratch_shapes=[pltpu.VMEM((hidden * hidden, channels), jnp.float32)],
        cost_estimate=pl.CostEstimate(flops=2**28, bytes_accessed=2**20, transcendentals=0),
    )(final_projector_coefficients)

    by_place = {(place_of(r, half), r % 2): r for r in range(size)}
    around = [
        (r, by_place[(place_of(r, half) + 1 - 2 * (r % 2)) % (2 * half), r % 2]) for r in range(size)
    ]
    across = [(r, r ^ 1) for r in range(size)]

    def pass_on(value):
        return lax.ppermute(value, "row", around)

    def swap(value):
        return lax.ppermute(value, "row", across)

    given = swap(give)
    flying = [keep, given[: body + (half - 1) * per_chip]]
    messages = [give, given]
    for step in range(1, half + 1):
        landed = [pass_on(value) for value in flying]
        messages += landed + [swap(value) for value in landed]
        flying = [value[: value.shape[0] - per_chip] for value in landed]
        if step == half - 1:
            flying = flying[:1]

    count = len(messages)
    gridded = tiles > 1
    offset = final_projector_offset.reshape(1, channels)
    if gridded:
        operands = messages + messages
        specs = [pl.BlockSpec((width, tile), lambda t: (t, 0)) for _ in messages]
        specs += [
            pl.BlockSpec((per_chip, tile), lambda t, last=m.shape[0] // per_chip - 1: (last, 0))
            for m in messages
        ]
        specs += [
            pl.BlockSpec((channels, hidden * hidden), lambda t: (0, 0)),
            pl.BlockSpec((1, channels), lambda t: (0, 0)),
        ]
        grid = (tiles,)
    else:
        operands = messages
        specs = [vmem] * (count + 2)
        grid = ()
    return pl.pallas_call(
        functools.partial(pair_kernel, count, gridded, rows_here, hidden, samples),
        out_shape=jax.ShapeDtypeStruct((rows_here, residues, channels), jnp.bfloat16),
        grid=grid,
        in_specs=specs,
        out_specs=hbm,
        scratch_shapes=[
            pltpu.VMEM((rows_here * hidden, samples), jnp.bfloat16),
            pltpu.VMEM((rows_here, hidden * hidden, tile), jnp.bfloat16),
            pltpu.VMEM((rows_here, tile, channels), jnp.bfloat16),
            pltpu.SemaphoreType.DMA((rows_here,)),
        ],
        compiler_params=pltpu.CompilerParams(vmem_limit_bytes=40 * MIB),
    )(*operands, weight, offset)


def solution(mesh):
    return jax.shard_map(
        functools.partial(per_device, mesh.shape["row"]),
        mesh=mesh,
        in_specs=(P(("groups", "row"), None, None), P(), P(), P(), P(), P(), P(), P(), P()),
        out_specs=P(("groups", "row"), None, None),
        check_vma=False,
    )
```

time: 34.6 us -> 38.7 us (1.12)
  waiting for transfers between devices: 3.59 us -> 8.89 us
  Pallas kernels: 15 us -> 11.8 us
  local copies, waits for them, and re-layouts: 0.08 us -> 1.63 us
  starting transfers between devices: 15.6 us -> 16 us
    ppermute x7, waiting for transfers between devices: 3.57 us -> 8.87 us  [pass_on(): return lax.ppermute(value, 'row', around)]
    pallas_call x5 -> x2, Pallas kernels: 11.3 us -> 6.49 us  [the longest x1 4.43 us: per_device(): pl.pallas_call(functools.partial(pair_kernel, count, gridded, rows_here,...]
    pallas_call x1, Pallas kernels: 3.62 us -> 5.33 us  [per_device(): pl.pallas_call(functools.partial(project_kernel, rows_here), out_shape=[m...]
    unnamed x4, local copies, waits for them, and re-layouts: 0.01 us -> 1.56 us
    ppermute x7, starting transfers between devices: 13.7 us -> 14.9 us  [pass_on(): return lax.ppermute(value, 'row', around)]
    ppermute x8, starting transfers between devices: 1.83 us -> 1.1 us  [swap(): return lax.ppermute(value, 'row', across)]
  transfers between devices with their start and end apart: 15 -> 15, of which waited for: 3 -> 5; matrix products, arithmetic and copies ran while one was open for 0% -> 0% of each run, Pallas kernels for 26% -> 5%
where the time goes in v3:
time: 38.7 us; the launch traced here: 38.4 us
  starting transfers between devices  16 us (41%)
  Pallas kernels  11.8 us (30%)
  waiting for transfers between devices  8.89 us (23%)
  local copies, waits for them, and re-layouts  1.63 us (4%)
    ppermute x7, starting transfers between devices, pass_on(): return lax.ppermute(value, 'row', around)  14.9 us
    ppermute x7, waiting for transfers between devices, pass_on(): return lax.ppermute(value, 'row', around)  8.87 us
    pallas_call x1, Pallas kernels, per_device(): pl.pallas_call(functools.partial(project_kernel, rows_here), out_shape=[m...  5.33 us
    pallas_call x1, Pallas kernels, per_device(): pl.pallas_call(functools.partial(pair_kernel, count, gridded, rows_here,...  4.43 us
    pallas_call x1, Pallas kernels, per_device(): pl.pallas_call(weight_kernel, out_shape=jax.ShapeDtypeStruct((channels, h...  2.05 us
    unnamed x4, local copies, waits for them, and re-layouts  1.56 us
    ppermute x8, starting transfers between devices, swap(): return lax.ppermute(value, 'row', across)  1.1 us
  transfers between devices with their start and end apart: 15, of which 5 were waited for; matrix products, arithmetic and copies ran while one was open for 0% of the time, Pallas kernels for 5%

profile of v3, /device:TPU:0, one launch (start us, length us, event | category | flops | bytes accessed | tf_op | source)
XLA Modules:
  0.0 38.4 jit_solution(7974956746134128502)
XLA Ops:
  0.0 5.3 %shard_map.91 = (bf16[384,256]{1,0:T(8,128)(2,1)S(1)}, bf16[384,256]{1,0:T(8,128)(2,1)S(1)}) custom-call(bf16[8,256,256]{2,1,0:T(8,128)(2,1)} %x_hbm.1, f32[1,256]{1,0:T(1,128)} %bitcast.10, f32[1,256]{1,0:T(1,128)} %bitcast.11, bf16[32,256]{1,0:T(8,128)(2,1)} %bitcast.8, f32[1,32]{1,0:T(1,128)} %bitcast.12, bf16[32,256]{1,0:T(8,128)(2,1)} %bitcast.9, ...), custom_call_target="tpu_custom_call" | custom-call | flops 536870912 | bytes 1048576 | tf_op jit(solution)/shard_map/pallas_call | solution.py:225
  5.3 3.1 %collective-permute-start.1 = (bf16[384,256]{1,0:T(8,128)(2,1)S(1)}, bf16[384,256]{1,0:T(8,128)(2,1)S(1)}, u32[]{:S(2)}, u32[]{:S(2)}) collective-permute-start(bf16[384,256]{1,0:T(8,128)(2,1)S(1)} %get-tuple-element.8), channel_id=1, source_target_pairs={{0,4},{1,3},{2,0},{3,7},{4,8},{5,1},{6,2},{7,11},{8,12},{9,5},{10,... | collective-permute-start | bytes 589832 | tf_op jit(solution)/shard_map/ppermute | solution.py:278
  8.4 3.6 %collective-permute-done.1.refs_2_ = bf16[384,256]{1,0:T(8,128)(2,1)S(1)} collective-permute-done((bf16[384,256]{1,0:T(8,128)(2,1)S(1)}, bf16[384,256]{1,0:T(8,128)(2,1)S(1)}, u32[]{:S(2)}, u32[]{:S(2)}) %collective-permute-start.1) | collective-permute-done | bytes 196640 | tf_op jit(solution)/shard_map/ppermute | solution.py:278
  12.0 2.1 %collective-permute-start.5 = (bf16[352,256]{1,0:T(8,128)(2,1)S(1)}, bf16[352,256]{1,0:T(8,128)(2,1)S(1)}, u32[]{:S(2)}, u32[]{:S(2)}) collective-permute-start(bf16[352,256]{1,0:T(8,128)(2,1)S(1)} %slice.25), channel_id=1, source_target_pairs={{0,4},{1,3},{2,0},{3,7},{4,8},{5,1},{6,2},{7,11},{8,12},{9,5},{10,... | collective-permute-start | bytes 540680 | tf_op jit(solution)/shard_map/ppermute | solution.py:278
  14.1 0.0 collective-permute-done.refs_1_
  14.2 1.6 %collective-permute-start.2 = (bf16[352,256]{1,0:T(8,128)(2,1)S(1)}, bf16[352,256]{1,0:T(8,128)(2,1)S(1)}, u32[]{:S(2)}, u32[]{:S(2)}) collective-permute-start(bf16[352,256]{1,0:T(8,128)(2,1)S(1)} %slice.24), channel_id=1, source_target_pairs={{0,4},{1,3},{2,0},{3,7},{4,8},{5,1},{6,2},{7,11},{8,12},{9,5},{10,... | collective-permute-start | bytes 540680 | tf_op jit(solution)/shard_map/ppermute | solution.py:278
  15.8 1.8 %collective-permute-done.5.refs_6_ = bf16[352,256]{1,0:T(8,128)(2,1)S(1)} collective-permute-done((bf16[352,256]{1,0:T(8,128)(2,1)S(1)}, bf16[352,256]{1,0:T(8,128)(2,1)S(1)}, u32[]{:S(2)}, u32[]{:S(2)}) %collective-permute-start.5) | collective-permute-done | bytes 180256 | tf_op jit(solution)/shard_map/ppermute | solution.py:278
  17.6 2.1 %collective-permute-start.9 = (bf16[320,256]{1,0:T(8,128)(2,1)S(1)}, bf16[320,256]{1,0:T(8,128)(2,1)S(1)}, u32[]{:S(2)}, u32[]{:S(2)}) collective-permute-start(bf16[320,256]{1,0:T(8,128)(2,1)S(1)} %slice.27), channel_id=1, source_target_pairs={{0,4},{1,3},{2,0},{3,7},{4,8},{5,1},{6,2},{7,11},{8,12},{9,5},{10,... | collective-permute-start | bytes 491528 | tf_op jit(solution)/shard_map/ppermute | solution.py:278
  19.7 0.0 collective-permute-done.2.refs_3_
  19.7 1.9 %collective-permute-start.6 = (bf16[320,256]{1,0:T(8,128)(2,1)S(1)}, bf16[320,256]{1,0:T(8,128)(2,1)S(1)}, u32[]{:S(2)}, u32[]{:S(2)}) collective-permute-start(bf16[320,256]{1,0:T(8,128)(2,1)S(1)} %slice.26), channel_id=1, source_target_pairs={{0,4},{1,3},{2,0},{3,7},{4,8},{5,1},{6,2},{7,11},{8,12},{9,5},{10,... | collective-permute-start | bytes 491528 | tf_op jit(solution)/shard_map/ppermute | solution.py:278
  21.6 0.0 collective-permute-start.3
  21.6 0.5 %collective-permute-start.7 = (bf16[352,256]{1,0:T(8,128)(2,1)S(1)}, bf16[352,256]{1,0:T(8,128)(2,1)S(1)}, u32[]{:S(2)}, u32[]{:S(2)}) collective-permute-start(bf16[352,256]{1,0:T(8,128)(2,1)S(1)} %collective-permute-done.5.refs_6_), channel_id=1, source_target_pairs={{0,1},{1,0},{2,3},{3,2},{4,5},{5,4},{6,7},{7,6},{8,9},{9,8},{10,11... | collective-permute-start | bytes 540680 | tf_op jit(solution)/shard_map/ppermute | solution.py:281
  22.2 0.8 %collective-permute-done.9.refs_10_ = bf16[320,256]{1,0:T(8,128)(2,1)S(1)} collective-permute-done((bf16[320,256]{1,0:T(8,128)(2,1)S(1)}, bf16[320,256]{1,0:T(8,128)(2,1)S(1)}, u32[]{:S(2)}, u32[]{:S(2)}) %collective-permute-start.9) | collective-permute-done | bytes 163872 | tf_op jit(solution)/shard_map/ppermute | solution.py:278
  23.0 2.1 %collective-permute-start.13 = (bf16[288,256]{1,0:T(8,128)(2,1)S(1)}, bf16[288,256]{1,0:T(8,128)(2,1)S(1)}, u32[]{:S(2)}, u32[]{:S(2)}) collective-permute-start(bf16[288,256]{1,0:T(8,128)(2,1)S(1)} %slice.29), channel_id=1, source_target_pairs={{0,4},{1,3},{2,0},{3,7},{4,8},{5,1},{6,2},{7,11},{8,12},{9,5},{10,... | collective-permute-start | bytes 442376 | tf_op jit(solution)/shard_map/ppermute | solution.py:278
  25.1 0.0 collective-permute-done.6.refs_7_
  25.1 1.9 %collective-permute-start.10 = (bf16[288,256]{1,0:T(8,128)(2,1)S(1)}, bf16[288,256]{1,0:T(8,128)(2,1)S(1)}, u32[]{:S(2)}, u32[]{:S(2)}) collective-permute-start(bf16[288,256]{1,0:T(8,128)(2,1)S(1)} %slice.28), channel_id=1, source_target_pairs={{0,4},{1,3},{2,0},{3,7},{4,8},{5,1},{6,2},{7,11},{8,12},{9,5},{10,... | collective-permute-start | bytes 442376 | tf_op jit(solution)/shard_map/ppermute | solution.py:278
  27.0 0.5 %collective-permute-start.11 = (bf16[320,256]{1,0:T(8,128)(2,1)S(1)}, bf16[320,256]{1,0:T(8,128)(2,1)S(1)}, u32[]{:S(2)}, u32[]{:S(2)}) collective-permute-start(bf16[320,256]{1,0:T(8,128)(2,1)S(1)} %collective-permute-done.9.refs_10_), channel_id=1, source_target_pairs={{0,1},{1,0},{2,3},{3,2},{4,5},{5,4},{6,7},{7,6},{8,9},{9,8},{10,11... | collective-permute-start | bytes 491528 | tf_op jit(solution)/shard_map/ppermute | solution.py:281
  27.5 0.1 collective-permute-start.8
  27.6 0.6 %collective-permute-done.13.refs_14_ = bf16[288,256]{1,0:T(8,128)(2,1)S(1)} collective-permute-done((bf16[288,256]{1,0:T(8,128)(2,1)S(1)}, bf16[288,256]{1,0:T(8,128)(2,1)S(1)}, u32[]{:S(2)}, u32[]{:S(2)}) %collective-permute-start.13) | collective-permute-done | bytes 147488 | tf_op jit(solution)/shard_map/ppermute | solution.py:278
  28.2 2.1 %collective-permute-done.10.refs_11_ = bf16[288,256]{1,0:T(8,128)(2,1)S(1)} collective-permute-done((bf16[288,256]{1,0:T(8,128)(2,1)S(1)}, bf16[288,256]{1,0:T(8,128)(2,1)S(1)}, u32[]{:S(2)}, u32[]{:S(2)}) %collective-permute-start.10) | collective-permute-done | bytes 147488 | tf_op jit(solution)/shard_map/ppermute | solution.py:278
  30.3 2.1 %shard_map.92.refs_16_ = bf16[128,1024]{1,0:T(8,128)(2,1)} custom-call(bf16[1024,128]{1,0:T(8,128)(2,1)} %final_ref.1), custom_call_target="tpu_custom_call" | custom-call | flops 268435456 | bytes 1048576 | tf_op jit(solution)/shard_map/pallas_call | solution.py:262
  32.4 0.6 %copy-done.1 = f32[128]{0:T(128)S(1)} copy-done((f32[128]{0:T(128)S(1)}, f32[128]{0:T(128)}, u32[]{:S(2)}) %copy-start.1) | copy-done | bytes 536
  33.0 0.9 %copy-done = bf16[128,1024]{1,0:T(8,128)(2,1)S(1)} copy-done((bf16[128,1024]{1,0:T(8,128)(2,1)S(1)}, bf16[128,1024]{1,0:T(8,128)(2,1)}, u32[]{:S(2)}) %copy-start) | copy-done | bytes 262168
  34.0 4.4 %shard_map.93 = bf16[16,256,128]{2,1,0:T(8,128)(2,1)} custom-call(bf16[384,256]{1,0:T(8,128)(2,1)S(1)} %get-tuple-element.7.refs_0_, bf16[384,256]{1,0:T(8,128)(2,1)S(1)} %collective-permute-done.refs_1_, bf16[384,256]{1,0:T(8,128)(2,1)S(1)} %collective-permute-done.1.refs_2_, bf16[352,256]{1,0:T(8,128)(2,1)S(1)} %collective-permute-done.2.refs_3_, ...), custom_call_target="tpu_custom_call" | custom-call | tf_op jit(solution)/shard_map/pallas_call | solution.py:312
  (19 shorter events, 0.1 us)
Async XLA Ops:
  5.3 6.7 %collective-permute-start.1 = (bf16[384,256]{1,0:T(8,128)(2,1)S(1)}, bf16[384,256]{1,0:T(8,128)(2,1)S(1)}, u32[]{:S(2)}, u32[]{:S(2)}) collective-permute-start(bf16[384,256]{1,0:T(8,128)(2,1)S(1)} %get-tuple-element.8), channel_id=1, source_target_pairs={{0,4},{1,3},{2,0},{3,7},{4,8},{5,1},{6,2},{7,11},{8,12},{9,5},{10,... | collective-permute-start | bytes 589832 | tf_op jit(solution)/shard_map/ppermute | solution.py:278
  8.4 5.7 %collective-permute-start = (bf16[384,256]{1,0:T(8,128)(2,1)S(1)}, bf16[384,256]{1,0:T(8,128)(2,1)S(1)}, u32[]{:S(2)}, u32[]{:S(2)}) collective-permute-start(bf16[384,256]{1,0:T(8,128)(2,1)S(1)} %get-tuple-element.7.refs_0_), channel_id=1, source_target_pairs={{0,1},{1,0},{2,3},{3,2},{4,5},{5,4},{6,7},{7,6},{8,9},{9,8},{10,11... | collective-permute-start | bytes 589832 | tf_op jit(solution)/shard_map/ppermute | solution.py:281
  12.0 5.5 %collective-permute-start.5 = (bf16[352,256]{1,0:T(8,128)(2,1)S(1)}, bf16[352,256]{1,0:T(8,128)(2,1)S(1)}, u32[]{:S(2)}, u32[]{:S(2)}) collective-permute-start(bf16[352,256]{1,0:T(8,128)(2,1)S(1)} %slice.25), channel_id=1, source_target_pairs={{0,4},{1,3},{2,0},{3,7},{4,8},{5,1},{6,2},{7,11},{8,12},{9,5},{10,... | collective-permute-start | bytes 540680 | tf_op jit(solution)/shard_map/ppermute | solution.py:278
  14.2 5.5 %collective-permute-start.2 = (bf16[352,256]{1,0:T(8,128)(2,1)S(1)}, bf16[352,256]{1,0:T(8,128)(2,1)S(1)}, u32[]{:S(2)}, u32[]{:S(2)}) collective-permute-start(bf16[352,256]{1,0:T(8,128)(2,1)S(1)} %slice.24), channel_id=1, source_target_pairs={{0,4},{1,3},{2,0},{3,7},{4,8},{5,1},{6,2},{7,11},{8,12},{9,5},{10,... | collective-permute-start | bytes 540680 | tf_op jit(solution)/shard_map/ppermute | solution.py:278
  17.6 5.4 %collective-permute-start.9 = (bf16[320,256]{1,0:T(8,128)(2,1)S(1)}, bf16[320,256]{1,0:T(8,128)(2,1)S(1)}, u32[]{:S(2)}, u32[]{:S(2)}) collective-permute-start(bf16[320,256]{1,0:T(8,128)(2,1)S(1)} %slice.27), channel_id=1, source_target_pairs={{0,4},{1,3},{2,0},{3,7},{4,8},{5,1},{6,2},{7,11},{8,12},{9,5},{10,... | collective-permute-start | bytes 491528 | tf_op jit(solution)/shard_map/ppermute | solution.py:278
  19.7 5.4 %collective-permute-start.6 = (bf16[320,256]{1,0:T(8,128)(2,1)S(1)}, bf16[320,256]{1,0:T(8,128)(2,1)S(1)}, u32[]{:S(2)}, u32[]{:S(2)}) collective-permute-start(bf16[320,256]{1,0:T(8,128)(2,1)S(1)} %slice.26), channel_id=1, source_target_pairs={{0,4},{1,3},{2,0},{3,7},{4,8},{5,1},{6,2},{7,11},{8,12},{9,5},{10,... | collective-permute-start | bytes 491528 | tf_op jit(solution)/shard_map/ppermute | solution.py:278
  21.6 5.4 %collective-permute-start.3 = (bf16[384,256]{1,0:T(8,128)(2,1)S(1)}, bf16[384,256]{1,0:T(8,128)(2,1)S(1)}, u32[]{:S(2)}, u32[]{:S(2)}) collective-permute-start(bf16[384,256]{1,0:T(8,128)(2,1)S(1)} %collective-permute-done.1.refs_2_), channel_id=1, source_target_pairs={{0,1},{1,0},{2,3},{3,2},{4,5},{5,4},{6,7},{7,6},{8,9},{9,8},{10,11... | collective-permute-start | bytes 589832 | tf_op jit(solution)/shard_map/ppermute | solution.py:281
  21.6 5.9 %collective-permute-start.7 = (bf16[352,256]{1,0:T(8,128)(2,1)S(1)}, bf16[352,256]{1,0:T(8,128)(2,1)S(1)}, u32[]{:S(2)}, u32[]{:S(2)}) collective-permute-start(bf16[352,256]{1,0:T(8,128)(2,1)S(1)} %collective-permute-done.5.refs_6_), channel_id=1, source_target_pairs={{0,1},{1,0},{2,3},{3,2},{4,5},{5,4},{6,7},{7,6},{8,9},{9,8},{10,11... | collective-permute-start | bytes 540680 | tf_op jit(solution)/shard_map/ppermute | solution.py:281
  23.0 5.2 %collective-permute-start.13 = (bf16[288,256]{1,0:T(8,128)(2,1)S(1)}, bf16[288,256]{1,0:T(8,128)(2,1)S(1)}, u32[]{:S(2)}, u32[]{:S(2)}) collective-permute-start(bf16[288,256]{1,0:T(8,128)(2,1)S(1)} %slice.29), channel_id=1, source_target_pairs={{0,4},{1,3},{2,0},{3,7},{4,8},{5,1},{6,2},{7,11},{8,12},{9,5},{10,... | collective-permute-start | bytes 442376 | tf_op jit(solution)/shard_map/ppermute | solution.py:278
  25.1 5.2 %collective-permute-start.10 = (bf16[288,256]{1,0:T(8,128)(2,1)S(1)}, bf16[288,256]{1,0:T(8,128)(2,1)S(1)}, u32[]{:S(2)}, u32[]{:S(2)}) collective-permute-start(bf16[288,256]{1,0:T(8,128)(2,1)S(1)} %slice.28), channel_id=1, source_target_pairs={{0,4},{1,3},{2,0},{3,7},{4,8},{5,1},{6,2},{7,11},{8,12},{9,5},{10,... | collective-permute-start | bytes 442376 | tf_op jit(solution)/shard_map/ppermute | solution.py:278
  27.0 5.3 %collective-permute-start.4 = (bf16[352,256]{1,0:T(8,128)(2,1)S(1)}, bf16[352,256]{1,0:T(8,128)(2,1)S(1)}, u32[]{:S(2)}, u32[]{:S(2)}) collective-permute-start(bf16[352,256]{1,0:T(8,128)(2,1)S(1)} %collective-permute-done.2.refs_3_), channel_id=1, source_target_pairs={{0,1},{1,0},{2,3},{3,2},{4,5},{5,4},{6,7},{7,6},{8,9},{9,8},{10,11... | collective-permute-start | bytes 540680 | tf_op jit(solution)/shard_map/ppermute | solution.py:281
  27.0 5.3 %collective-permute-start.11 = (bf16[320,256]{1,0:T(8,128)(2,1)S(1)}, bf16[320,256]{1,0:T(8,128)(2,1)S(1)}, u32[]{:S(2)}, u32[]{:S(2)}) collective-permute-start(bf16[320,256]{1,0:T(8,128)(2,1)S(1)} %collective-permute-done.9.refs_10_), channel_id=1, source_target_pairs={{0,1},{1,0},{2,3},{3,2},{4,5},{5,4},{6,7},{7,6},{8,9},{9,8},{10,11... | collective-permute-start | bytes 491528 | tf_op jit(solution)/shard_map/ppermute | solution.py:281
  27.5 4.8 %collective-permute-start.8 = (bf16[320,256]{1,0:T(8,128)(2,1)S(1)}, bf16[320,256]{1,0:T(8,128)(2,1)S(1)}, u32[]{:S(2)}, u32[]{:S(2)}) collective-permute-start(bf16[320,256]{1,0:T(8,128)(2,1)S(1)} %collective-permute-done.6.refs_7_), channel_id=1, source_target_pairs={{0,1},{1,0},{2,3},{3,2},{4,5},{5,4},{6,7},{7,6},{8,9},{9,8},{10,11... | collective-permute-start | bytes 491528 | tf_op jit(solution)/shard_map/ppermute | solution.py:281
  28.2 4.2 %collective-permute-start.14 = (bf16[288,256]{1,0:T(8,128)(2,1)S(1)}, bf16[288,256]{1,0:T(8,128)(2,1)S(1)}, u32[]{:S(2)}, u32[]{:S(2)}) collective-permute-start(bf16[288,256]{1,0:T(8,128)(2,1)S(1)} %collective-permute-done.13.refs_14_), channel_id=1, source_target_pairs={{0,1},{1,0},{2,3},{3,2},{4,5},{5,4},{6,7},{7,6},{8,9},{9,8},{10,11... | collective-permute-start | bytes 442376 | tf_op jit(solution)/shard_map/ppermute | solution.py:281
  30.3 2.1 %collective-permute-start.12 = (bf16[288,256]{1,0:T(8,128)(2,1)S(1)}, bf16[288,256]{1,0:T(8,128)(2,1)S(1)}, u32[]{:S(2)}, u32[]{:S(2)}) collective-permute-start(bf16[288,256]{1,0:T(8,128)(2,1)S(1)} %collective-permute-done.10.refs_11_), channel_id=1, source_target_pairs={{0,1},{1,0},{2,3},{3,2},{4,5},{5,4},{6,7},{7,6},{8,9},{9,8},{10,11... | collective-permute-start | bytes 442376 | tf_op jit(solution)/shard_map/ppermute | solution.py:281
  32.4 0.7 %copy-start.1 = (f32[128]{0:T(128)S(1)}, f32[128]{0:T(128)}, u32[]{:S(2)}) copy-start(f32[128]{0:T(128)} %param.17) | copy-start | bytes 1540
  33.0 0.9 %copy-start = (bf16[128,1024]{1,0:T(8,128)(2,1)S(1)}, bf16[128,1024]{1,0:T(8,128)(2,1)}, u32[]{:S(2)}) copy-start(bf16[128,1024]{1,0:T(8,128)(2,1)} %shard_map.92.refs_16_) | copy-start | bytes 786436

commit v4 on v3

--- a/solution.py
+++ b/solution.py
@@ -10,6 +10,7 @@
 
 MIB = 1024 * 1024
 LANES = 128
+CHUNKS = 2
 
 
 def repeat_rows(values, times):
@@ -63,14 +64,18 @@
         (first_offset_hbm, first_offset_ref),
         (second_offset_hbm, second_offset_ref),
     ]
-    copies = [pltpu.make_async_copy(x_hbm.at[0], x_ref.at[0], sems.at[0])]
-    copies += [
-        pltpu.make_async_copy(src, dst, sems.at[samples + n]) for n, (src, dst) in enumerate(small)
+    some = samples // CHUNKS
+    large = []
+    for n in range(CHUNKS):
+        rows = pl.ds(n * some, some)
+        large.append(pltpu.make_async_copy(x_hbm.at[rows], x_ref.at[rows], sems.at[n]))
+        large[-1].start()
+    copies = [
+        pltpu.make_async_copy(src, dst, sems.at[CHUNKS + n]) for n, (src, dst) in enumerate(small)
     ]
-    copies += [pltpu.make_async_copy(x_hbm.at[s], x_ref.at[s], sems.at[s]) for s in range(1, samples)]
     for copy in copies:
         copy.start()
-    for copy in copies[1 : 1 + len(small)]:
+    for copy in copies:
         copy.wait()
 
     first = jnp.concatenate([first_ref[...]] * fold, axis=0)
@@ -92,10 +97,8 @@
     dims = (((1,), (1,)), ((), ()))
     right = [jnp.zeros((width, tile), jnp.float32) for _ in range(tiles)]
     for s in range(samples):
-        if s == 0:
-            copies[0].wait()
-        else:
-            copies[len(small) + s].wait()
+        if s % some == 0:
+            large[s // some].wait()
         values = x_ref[s].astype(jnp.float32)
         center = jnp.mean(values, axis=-1, keepdims=True)
         values = values - center
@@ -150,19 +153,25 @@
         )
 
 
-def pair_kernel(count, gridded, rows_here, hidden, samples, *refs):
+def pair_kernel(places, gridded, rows_here, hidden, samples, *refs):
     refs = list(refs)
-    rights = [refs.pop(0) for _ in range(count)]
-    lefts = [refs.pop(0) for _ in range(count)] if gridded else rights
-    weight_ref, offset_ref, out_hbm, left_ref, outer_ref, out_ref, sems = refs
-    tile = rights[0].shape[1]
+    count = len(places)
+    if gridded:
+        shards = [(refs.pop(0), 0, refs.pop(0), 0) for _ in places]
+    else:
+        messages = [refs.pop(0) for _ in range(1 + max(place[0] for place in places))]
+        shards = [(messages[n], right, messages[n], left) for n, right, left in places]
+    weight_ref, offset_hbm, out_hbm, left_ref, outer_ref, out_ref, offset_ref, sems = refs
+    offset_copy = pltpu.make_async_copy(offset_hbm, offset_ref, sems.at[rows_here])
+    offset_copy.start()
+    tile = shards[0][0].shape[1]
     here = samples // count
     span = rows_here * hidden
     deep = span * here // tile
     core = lax.rem(lax.axis_index("row"), 2)
     pieces = []
-    for ref in lefts:
-        start = pl.multiple_of(ref.shape[0] - (2 - core) * deep, deep)
+    for _, _, ref, base in shards:
+        start = pl.multiple_of(base + core * deep, deep)
         piece = ref[pl.ds(start, deep), :].astype(jnp.float32)
         pieces.append(
             jnp.concatenate([piece[n * here : (n + 1) * here] for n in range(span // tile)], axis=1)
@@ -171,7 +180,10 @@
 
     left = left_ref[...]
     for e in range(0, hidden, 2):
-        both = [ref[e * here : (e + 2) * here, :].astype(jnp.float32) for ref in rights]
+        both = [
+            ref[base + e * here : base + (e + 2) * here, :].astype(jnp.float32)
+            for ref, base, _, _ in shards
+        ]
         for k in range(2):
             right = jnp.concatenate([x[k * here : (k + 1) * here] for x in both], axis=0)
             outer = jnp.dot(left, right.astype(jnp.bfloat16), preferred_element_type=jnp.float32)
@@ -182,6 +194,7 @@
                 ]
 
     first = pl.program_id(0) * tile if gridded else 0
+    offset_copy.wait()
     copies = []
     for i in range(rows_here):
         value = jnp.dot(weight_ref[...], outer_ref[i], preferred_element_type=jnp.float32)
@@ -237,7 +250,7 @@
             pltpu.VMEM((1, hidden), jnp.float32),
             pltpu.VMEM((residues * width // LANES, LANES), jnp.float32),
             pltpu.VMEM((residues * width // tile, tile), jnp.float32),
-            pltpu.SemaphoreType.DMA((here + 6,)),
+            pltpu.SemaphoreType.DMA((CHUNKS + 6,)),
         ],
         compiler_params=pltpu.CompilerParams(vmem_limit_bytes=32 * MIB),
         cost_estimate=pl.CostEstimate(
@@ -265,52 +278,64 @@
         in_specs=[vmem],
         out_specs=vmem,
         scratch_shapes=[pltpu.VMEM((hidden * hidden, channels), jnp.float32)],
+        compiler_params=pltpu.CompilerParams(vmem_limit_bytes=16 * MIB),
         cost_estimate=pl.CostEstimate(flops=2**28, bytes_accessed=2**20, transcendentals=0),
     )(final_projector_coefficients)
 
     by_place = {(place_of(r, half), r % 2): r for r in range(size)}
-    around = [
-        (r, by_place[(place_of(r, half) + 1 - 2 * (r % 2)) % (2 * half), r % 2]) for r in range(size)
-    ]
-    across = [(r, r ^ 1) for r in range(size)]
-
-    def pass_on(value):
-        return lax.ppermute(value, "row", around)
+
+    def neighbours(way):
+        return [
+            (r, by_place[(place_of(r, half) + way * (1 - 2 * (r % 2))) % (2 * half), r % 2])
+            for r in range(size)
+        ]
 
     def swap(value):
-        return lax.ppermute(value, "row", across)
-
-    given = swap(give)
-    flying = [keep, given[: body + (half - 1) * per_chip]]
-    messages = [give, given]
+        return lax.ppermute(value, "row", [(r, r ^ 1) for r in range(size)])
+
+    messages, places = [], []
+
+    def take(pair):
+        for value in pair:
+            places.append((len(messages), 0, value.shape[0] - per_chip))
+            messages.append(value)
+
+    take([give, swap(give)])
+    flying = [keep, give[: body + (half - 1) * per_chip]]
+    swapped = []
     for step in range(1, half + 1):
-        landed = [pass_on(value) for value in flying]
-        messages += landed + [swap(value) for value in landed]
-        flying = [value[: value.shape[0] - per_chip] for value in landed]
+        landed = [lax.ppermute(x, "row", neighbours(way)) for x, way in zip(flying, (1, -1))]
+        if step == 1:
+            landed[0], weight = lax.optimization_barrier((landed[0], weight))
+        if step >= 3:
+            landed[0], swapped[step - 3] = lax.optimization_barrier((landed[0], swapped[step - 3]))
+        flying = [x[: x.shape[0] - per_chip] for x in landed]
         if step == half - 1:
             flying = flying[:1]
-
-    count = len(messages)
+        landed = lax.optimization_barrier(landed)
+        take(landed)
+        swapped.append([swap(x) for x in landed])
+    for pair in swapped:
+        take(pair)
+
     gridded = tiles > 1
-    offset = final_projector_offset.reshape(1, channels)
+    offset = pltpu.with_memory_space_constraint(final_projector_offset.reshape(1, channels), pltpu.HBM)
     if gridded:
-        operands = messages + messages
-        specs = [pl.BlockSpec((width, tile), lambda t: (t, 0)) for _ in messages]
-        specs += [
-            pl.BlockSpec((per_chip, tile), lambda t, last=m.shape[0] // per_chip - 1: (last, 0))
-            for m in messages
-        ]
-        specs += [
-            pl.BlockSpec((channels, hidden * hidden), lambda t: (0, 0)),
-            pl.BlockSpec((1, channels), lambda t: (0, 0)),
-        ]
+        operands, specs = [], []
+        for n, right, left in places:
+            operands += [messages[n]] * 2
+            specs += [
+                pl.BlockSpec((width, tile), lambda t, first=right // width: (first + t, 0)),
+                pl.BlockSpec((per_chip, tile), lambda t, at=left // per_chip: (at, 0)),
+            ]
+        specs += [pl.BlockSpec((channels, hidden * hidden), lambda t: (0, 0)), hbm]
         grid = (tiles,)
     else:
         operands = messages
-        specs = [vmem] * (count + 2)
+        specs = [vmem] * (len(messages) + 1) + [hbm]
         grid = ()
     return pl.pallas_call(
-        functools.partial(pair_kernel, count, gridded, rows_here, hidden, samples),
+        functools.partial(pair_kernel, places, gridded, rows_here, hidden, samples),
         out_shape=jax.ShapeDtypeStruct((rows_here, residues, channels), jnp.bfloat16),
         grid=grid,
         in_specs=specs,
@@ -319,7 +344,8 @@
             pltpu.VMEM((rows_here * hidden, samples), jnp.bfloat16),
             pltpu.VMEM((rows_here, hidden * hidden, tile), jnp.bfloat16),
             pltpu.VMEM((rows_here, tile, channels), jnp.bfloat16),
-            pltpu.SemaphoreType.DMA((rows_here,)),
+            pltpu.VMEM((1, channels), jnp.float32),
+            pltpu.SemaphoreType.DMA((rows_here + 1,)),
         ],
         compiler_params=pltpu.CompilerParams(vmem_limit_bytes=40 * MIB),
     )(*operands, weight, offset)

time: 38.7 us -> 38 us (0.982)
  waiting for transfers between devices: 8.89 us -> 18.4 us
  starting transfers between devices: 16 us -> 10.4 us
  Pallas kernels: 11.8 us -> 8.91 us
  local copies, waits for them, and re-layouts: 1.63 us -> 0.08 us
    ppermute x15, waiting for transfers between devices: 8.89 us -> 18.4 us  [the longest x7 17 us: per_device(): lax.ppermute(x, 'row', neighbours(way))]
    ppermute x15, starting transfers between devices: 16 us -> 10.4 us  [the longest x7 8.21 us: per_device(): lax.ppermute(x, 'row', neighbours(way))]
    pallas_call x1, Pallas kernels: 5.33 us -> 3.59 us  [per_device(): pl.pallas_call(functools.partial(project_kernel, rows_here), out_shape=[m...]
    pallas_call x1, Pallas kernels: 2.05 us -> 0.4 us  [per_device(): pl.pallas_call(weight_kernel, out_shape=jax.ShapeDtypeStruct((channels, h...]
    unnamed x4 -> x2, local copies, waits for them, and re-layouts: 1.56 us -> 0.01 us
    pallas_call x1, Pallas kernels: 4.43 us -> 4.92 us  [per_device(): pl.pallas_call(functools.partial(pair_kernel, places, gridded, rows_here,...]
  transfers between devices with their start and end apart: 15 -> 15, of which waited for: 5 -> 6; matrix products, arithmetic and copies ran while one was open for 0% -> 0% of each run, Pallas kernels for 5% -> 1%
where the time goes in v4:
time: 38 us; the launch traced here: 37.8 us
  waiting for transfers between devices  18.4 us (48%)
  starting transfers between devices  10.4 us (27%)
  Pallas kernels  8.91 us (23%)
    ppermute x7, waiting for transfers between devices, per_device(): lax.ppermute(x, 'row', neighbours(way))  17 us
    ppermute x7, starting transfers between devices, per_device(): lax.ppermute(x, 'row', neighbours(way))  8.21 us
    pallas_call x1, Pallas kernels, per_device(): pl.pallas_call(functools.partial(pair_kernel, places, gridded, rows_here,...  4.92 us
    pallas_call x1, Pallas kernels, per_device(): pl.pallas_call(functools.partial(project_kernel, rows_here), out_shape=[m...  3.59 us
    ppermute x8, starting transfers between devices, swap(): return lax.ppermute(value, 'row', [(r, r ^ 1) for r in range(size)])  2.16 us
    ppermute x8, waiting for transfers between devices, swap(): return lax.ppermute(value, 'row', [(r, r ^ 1) for r in range(size)])  1.37 us
  transfers between devices with their start and end apart: 15, of which 6 were waited for; matrix products, arithmetic and copies ran while one was open for 0% of the time, Pallas kernels for 1%

profile of v4, /device:TPU:0, one launch (start us, length us, event | category | flops | bytes accessed | tf_op | source)
XLA Modules:
  0.0 37.8 jit_solution(11025710642843158449)
XLA Ops:
  0.0 3.6 %shard_map.91 = (bf16[384,256]{1,0:T(8,128)(2,1)S(1)}, bf16[384,256]{1,0:T(8,128)(2,1)S(1)}) custom-call(bf16[8,256,256]{2,1,0:T(8,128)(2,1)} %x_hbm.1, f32[1,256]{1,0:T(1,128)} %bitcast.10, f32[1,256]{1,0:T(1,128)} %bitcast.11, bf16[32,256]{1,0:T(8,128)(2,1)} %bitcast.8, f32[1,32]{1,0:T(1,128)} %bitcast.12, bf16[32,256]{1,0:T(8,128)(2,1)} %bitcast.9, ...), custom_call_target="tpu_custom_call" | custom-call | flops 536870912 | bytes 1048576 | tf_op jit(solution)/shard_map/pallas_call | solution.py:238
  3.6 0.0 copy-start
  3.6 3.1 %collective-permute-start.1 = (bf16[384,256]{1,0:T(8,128)(2,1)S(1)}, bf16[384,256]{1,0:T(8,128)(2,1)S(1)}, u32[]{:S(2)}, u32[]{:S(2)}) collective-permute-start(bf16[384,256]{1,0:T(8,128)(2,1)S(1)} %get-tuple-element.22), channel_id=1, source_target_pairs={{0,4},{1,3},{2,0},{3,7},{4,8},{5,1},{6,2},{7,11},{8,12},{9,5},{10,... | collective-permute-start | bytes 589832 | tf_op jit(solution)/shard_map/ppermute | solution.py:307
  6.7 0.1 collective-permute-start.2
  6.8 0.4 %shard_map.92.refs_16_ = bf16[128,1024]{1,0:T(8,128)(2,1)S(1)} custom-call(bf16[1024,128]{1,0:T(8,128)(2,1)S(1)} %copy-done), custom_call_target="tpu_custom_call" | custom-call | flops 268435456 | bytes 1048576 | tf_op jit(solution)/shard_map/pallas_call | solution.py:275
  7.2 4.6 %collective-permute-done.1.refs_2_ = bf16[384,256]{1,0:T(8,128)(2,1)S(1)} collective-permute-done((bf16[384,256]{1,0:T(8,128)(2,1)S(1)}, bf16[384,256]{1,0:T(8,128)(2,1)S(1)}, u32[]{:S(2)}, u32[]{:S(2)}) %collective-permute-start.1) | collective-permute-done | bytes 196640 | tf_op jit(solution)/shard_map/ppermute | solution.py:307
  11.8 1.5 %collective-permute-start.3 = (bf16[352,256]{1,0:T(8,128)(2,1)S(1)}, bf16[352,256]{1,0:T(8,128)(2,1)S(1)}, u32[]{:S(2)}, u32[]{:S(2)}) collective-permute-start(bf16[352,256]{1,0:T(8,128)(2,1)S(1)} %slice.19), channel_id=1, source_target_pairs={{0,4},{1,3},{2,0},{3,7},{4,8},{5,1},{6,2},{7,11},{8,12},{9,5},{10,... | collective-permute-start | bytes 540680 | tf_op jit(solution)/shard_map/ppermute | solution.py:307
  13.3 0.1 collective-permute-start.6
  13.4 1.0 %collective-permute-start.4 = (bf16[320,256]{1,0:T(8,128)(2,1)S(1)}, bf16[320,256]{1,0:T(8,128)(2,1)S(1)}, u32[]{:S(2)}, u32[]{:S(2)}) collective-permute-start(bf16[320,256]{1,0:T(8,128)(2,1)S(1)} %slice.24), channel_id=1, source_target_pairs={{0,2},{1,5},{2,6},{3,1},{4,0},{5,9},{6,10},{7,3},{8,4},{9,13},{10,... | collective-permute-start | bytes 491528 | tf_op jit(solution)/shard_map/ppermute | solution.py:307
  14.4 0.9 %collective-permute-start.7 = (bf16[352,256]{1,0:T(8,128)(2,1)S(1)}, bf16[352,256]{1,0:T(8,128)(2,1)S(1)}, u32[]{:S(2)}, u32[]{:S(2)}) collective-permute-start(bf16[352,256]{1,0:T(8,128)(2,1)S(1)} %collective-permute-done.2.refs_3_), channel_id=1, source_target_pairs={{0,1},{1,0},{2,3},{3,2},{4,5},{5,4},{6,7},{7,6},{8,9},{9,8},{10,11... | collective-permute-start | bytes 540680 | tf_op jit(solution)/shard_map/ppermute | solution.py:294
  15.3 3.6 %collective-permute-done.3.refs_4_ = bf16[352,256]{1,0:T(8,128)(2,1)S(1)} collective-permute-done((bf16[352,256]{1,0:T(8,128)(2,1)S(1)}, bf16[352,256]{1,0:T(8,128)(2,1)S(1)}, u32[]{:S(2)}, u32[]{:S(2)}) %collective-permute-start.3) | collective-permute-done | bytes 180256 | tf_op jit(solution)/shard_map/ppermute | solution.py:307
  19.0 0.4 %collective-permute-start.5 = (bf16[320,256]{1,0:T(8,128)(2,1)S(1)}, bf16[320,256]{1,0:T(8,128)(2,1)S(1)}, u32[]{:S(2)}, u32[]{:S(2)}) collective-permute-start(bf16[320,256]{1,0:T(8,128)(2,1)S(1)} %slice.25), channel_id=1, source_target_pairs={{0,4},{1,3},{2,0},{3,7},{4,8},{5,1},{6,2},{7,11},{8,12},{9,5},{10,... | collective-permute-start | bytes 491528 | tf_op jit(solution)/shard_map/ppermute | solution.py:307
  19.4 0.1 collective-permute-done.4.refs_5_
  19.5 0.1 collective-permute-start.10
  19.6 0.5 %collective-permute-start.11 = (bf16[320,256]{1,0:T(8,128)(2,1)S(1)}, bf16[320,256]{1,0:T(8,128)(2,1)S(1)}, u32[]{:S(2)}, u32[]{:S(2)}) collective-permute-start(bf16[320,256]{1,0:T(8,128)(2,1)S(1)} %collective-permute-done.4.refs_5_), channel_id=1, source_target_pairs={{0,1},{1,0},{2,3},{3,2},{4,5},{5,4},{6,7},{7,6},{8,9},{9,8},{10,11... | collective-permute-start | bytes 491528 | tf_op jit(solution)/shard_map/ppermute | solution.py:294
  20.1 2.1 %collective-permute-start.8 = (bf16[288,256]{1,0:T(8,128)(2,1)S(1)}, bf16[288,256]{1,0:T(8,128)(2,1)S(1)}, u32[]{:S(2)}, u32[]{:S(2)}) collective-permute-start(bf16[288,256]{1,0:T(8,128)(2,1)S(1)} %slice.26), channel_id=1, source_target_pairs={{0,2},{1,5},{2,6},{3,1},{4,0},{5,9},{6,10},{7,3},{8,4},{9,13},{10,... | collective-permute-start | bytes 442376 | tf_op jit(solution)/shard_map/ppermute | solution.py:307
  22.1 4.2 %collective-permute-done.5.refs_6_ = bf16[320,256]{1,0:T(8,128)(2,1)S(1)} collective-permute-done((bf16[320,256]{1,0:T(8,128)(2,1)S(1)}, bf16[320,256]{1,0:T(8,128)(2,1)S(1)}, u32[]{:S(2)}, u32[]{:S(2)}) %collective-permute-start.5) | collective-permute-done | bytes 163872 | tf_op jit(solution)/shard_map/ppermute | solution.py:307
  26.4 0.1 collective-permute-start.9
  26.4 0.1 collective-permute-start
  26.5 0.5 %collective-permute-start.12 = (bf16[320,256]{1,0:T(8,128)(2,1)S(1)}, bf16[320,256]{1,0:T(8,128)(2,1)S(1)}, u32[]{:S(2)}, u32[]{:S(2)}) collective-permute-start(bf16[320,256]{1,0:T(8,128)(2,1)S(1)} %collective-permute-done.5.refs_6_), channel_id=1, source_target_pairs={{0,1},{1,0},{2,3},{3,2},{4,5},{5,4},{6,7},{7,6},{8,9},{9,8},{10,11... | collective-permute-start | bytes 491528 | tf_op jit(solution)/shard_map/ppermute | solution.py:294
  27.0 0.1 collective-permute-start.13
  27.1 4.5 %collective-permute-done.9.refs_8_ = bf16[288,256]{1,0:T(8,128)(2,1)S(1)} collective-permute-done((bf16[288,256]{1,0:T(8,128)(2,1)S(1)}, bf16[288,256]{1,0:T(8,128)(2,1)S(1)}, u32[]{:S(2)}, u32[]{:S(2)}) %collective-permute-start.9) | collective-permute-done | bytes 147488 | tf_op jit(solution)/shard_map/ppermute | solution.py:307
  31.6 1.3 %collective-permute-done.14.refs_15_ = bf16[288,256]{1,0:T(8,128)(2,1)S(1)} collective-permute-done((bf16[288,256]{1,0:T(8,128)(2,1)S(1)}, bf16[288,256]{1,0:T(8,128)(2,1)S(1)}, u32[]{:S(2)}, u32[]{:S(2)}) %collective-permute-start.14) | collective-permute-done | bytes 147488 | tf_op jit(solution)/shard_map/ppermute | solution.py:294
  32.9 4.9 %shard_map.93 = bf16[16,256,128]{2,1,0:T(8,128)(2,1)} custom-call(bf16[384,256]{1,0:T(8,128)(2,1)S(1)} %get-tuple-element.21.refs_0_, bf16[384,256]{1,0:T(8,128)(2,1)S(1)} %collective-permute-done.refs_1_, bf16[384,256]{1,0:T(8,128)(2,1)S(1)} %collective-permute-done.1.refs_2_, bf16[352,256]{1,0:T(8,128)(2,1)S(1)} %collective-permute-done.2.refs_3_, ...), custom_call_target="tpu_custom_call" | custom-call | tf_op jit(solution)/shard_map/pallas_call | solution.py:337
  (17 shorter events, 0.1 us)
Async XLA Ops:
  3.6 3.2 %copy-start = (bf16[1024,128]{1,0:T(8,128)(2,1)S(1)}, bf16[1024,128]{1,0:T(8,128)(2,1)}, u32[]{:S(2)}) copy-start(bf16[1024,128]{1,0:T(8,128)(2,1)} %final_ref.1) | copy-start | bytes 786436
  3.6 8.2 %collective-permute-start.1 = (bf16[384,256]{1,0:T(8,128)(2,1)S(1)}, bf16[384,256]{1,0:T(8,128)(2,1)S(1)}, u32[]{:S(2)}, u32[]{:S(2)}) collective-permute-start(bf16[384,256]{1,0:T(8,128)(2,1)S(1)} %get-tuple-element.22), channel_id=1, source_target_pairs={{0,4},{1,3},{2,0},{3,7},{4,8},{5,1},{6,2},{7,11},{8,12},{9,5},{10,... | collective-permute-start | bytes 589832 | tf_op jit(solution)/shard_map/ppermute | solution.py:307
  6.7 6.6 %collective-permute-start.2 = (bf16[352,256]{1,0:T(8,128)(2,1)S(1)}, bf16[352,256]{1,0:T(8,128)(2,1)S(1)}, u32[]{:S(2)}, u32[]{:S(2)}) collective-permute-start(bf16[352,256]{1,0:T(8,128)(2,1)S(1)} %slice.18), channel_id=1, source_target_pairs={{0,2},{1,5},{2,6},{3,1},{4,0},{5,9},{6,10},{7,3},{8,4},{9,13},{10,... | collective-permute-start | bytes 540680 | tf_op jit(solution)/shard_map/ppermute | solution.py:307
  11.8 7.2 %collective-permute-start.3 = (bf16[352,256]{1,0:T(8,128)(2,1)S(1)}, bf16[352,256]{1,0:T(8,128)(2,1)S(1)}, u32[]{:S(2)}, u32[]{:S(2)}) collective-permute-start(bf16[352,256]{1,0:T(8,128)(2,1)S(1)} %slice.19), channel_id=1, source_target_pairs={{0,4},{1,3},{2,0},{3,7},{4,8},{5,1},{6,2},{7,11},{8,12},{9,5},{10,... | collective-permute-start | bytes 540680 | tf_op jit(solution)/shard_map/ppermute | solution.py:307
  13.3 8.8 %collective-permute-start.6 = (bf16[384,256]{1,0:T(8,128)(2,1)S(1)}, bf16[384,256]{1,0:T(8,128)(2,1)S(1)}, u32[]{:S(2)}, u32[]{:S(2)}) collective-permute-start(bf16[384,256]{1,0:T(8,128)(2,1)S(1)} %collective-permute-done.1.refs_2_), channel_id=1, source_target_pairs={{0,1},{1,0},{2,3},{3,2},{4,5},{5,4},{6,7},{7,6},{8,9},{9,8},{10,11... | collective-permute-start | bytes 589832 | tf_op jit(solution)/shard_map/ppermute | solution.py:294
  13.4 6.1 %collective-permute-start.4 = (bf16[320,256]{1,0:T(8,128)(2,1)S(1)}, bf16[320,256]{1,0:T(8,128)(2,1)S(1)}, u32[]{:S(2)}, u32[]{:S(2)}) collective-permute-start(bf16[320,256]{1,0:T(8,128)(2,1)S(1)} %slice.24), channel_id=1, source_target_pairs={{0,2},{1,5},{2,6},{3,1},{4,0},{5,9},{6,10},{7,3},{8,4},{9,13},{10,... | collective-permute-start | bytes 491528 | tf_op jit(solution)/shard_map/ppermute | solution.py:307
  14.4 5.6 %collective-permute-start.7 = (bf16[352,256]{1,0:T(8,128)(2,1)S(1)}, bf16[352,256]{1,0:T(8,128)(2,1)S(1)}, u32[]{:S(2)}, u32[]{:S(2)}) collective-permute-start(bf16[352,256]{1,0:T(8,128)(2,1)S(1)} %collective-permute-done.2.refs_3_), channel_id=1, source_target_pairs={{0,1},{1,0},{2,3},{3,2},{4,5},{5,4},{6,7},{7,6},{8,9},{9,8},{10,11... | collective-permute-start | bytes 540680 | tf_op jit(solution)/shard_map/ppermute | solution.py:294
  19.0 7.4 %collective-permute-start.5 = (bf16[320,256]{1,0:T(8,128)(2,1)S(1)}, bf16[320,256]{1,0:T(8,128)(2,1)S(1)}, u32[]{:S(2)}, u32[]{:S(2)}) collective-permute-start(bf16[320,256]{1,0:T(8,128)(2,1)S(1)} %slice.25), channel_id=1, source_target_pairs={{0,4},{1,3},{2,0},{3,7},{4,8},{5,1},{6,2},{7,11},{8,12},{9,5},{10,... | collective-permute-start | bytes 491528 | tf_op jit(solution)/shard_map/ppermute | solution.py:307
  19.5 7.6 %collective-permute-start.10 = (bf16[352,256]{1,0:T(8,128)(2,1)S(1)}, bf16[352,256]{1,0:T(8,128)(2,1)S(1)}, u32[]{:S(2)}, u32[]{:S(2)}) collective-permute-start(bf16[352,256]{1,0:T(8,128)(2,1)S(1)} %collective-permute-done.3.refs_4_), channel_id=1, source_target_pairs={{0,1},{1,0},{2,3},{3,2},{4,5},{5,4},{6,7},{7,6},{8,9},{9,8},{10,11... | collective-permute-start | bytes 540680 | tf_op jit(solution)/shard_map/ppermute | solution.py:294
  19.6 7.4 %collective-permute-start.11 = (bf16[320,256]{1,0:T(8,128)(2,1)S(1)}, bf16[320,256]{1,0:T(8,128)(2,1)S(1)}, u32[]{:S(2)}, u32[]{:S(2)}) collective-permute-start(bf16[320,256]{1,0:T(8,128)(2,1)S(1)} %collective-permute-done.4.refs_5_), channel_id=1, source_target_pairs={{0,1},{1,0},{2,3},{3,2},{4,5},{5,4},{6,7},{7,6},{8,9},{9,8},{10,11... | collective-permute-start | bytes 491528 | tf_op jit(solution)/shard_map/ppermute | solution.py:294
  20.1 6.4 %collective-permute-start.8 = (bf16[288,256]{1,0:T(8,128)(2,1)S(1)}, bf16[288,256]{1,0:T(8,128)(2,1)S(1)}, u32[]{:S(2)}, u32[]{:S(2)}) collective-permute-start(bf16[288,256]{1,0:T(8,128)(2,1)S(1)} %slice.26), channel_id=1, source_target_pairs={{0,2},{1,5},{2,6},{3,1},{4,0},{5,9},{6,10},{7,3},{8,4},{9,13},{10,... | collective-permute-start | bytes 442376 | tf_op jit(solution)/shard_map/ppermute | solution.py:307
  26.4 5.2 %collective-permute-start.9 = (bf16[288,256]{1,0:T(8,128)(2,1)S(1)}, bf16[288,256]{1,0:T(8,128)(2,1)S(1)}, u32[]{:S(2)}, u32[]{:S(2)}) collective-permute-start(bf16[288,256]{1,0:T(8,128)(2,1)S(1)} %slice.23), channel_id=1, source_target_pairs={{0,4},{1,3},{2,0},{3,7},{4,8},{5,1},{6,2},{7,11},{8,12},{9,5},{10,... | collective-permute-start | bytes 442376 | tf_op jit(solution)/shard_map/ppermute | solution.py:307
  26.4 5.1 %collective-permute-start = (bf16[384,256]{1,0:T(8,128)(2,1)S(1)}, bf16[384,256]{1,0:T(8,128)(2,1)S(1)}, u32[]{:S(2)}, u32[]{:S(2)}) collective-permute-start(bf16[384,256]{1,0:T(8,128)(2,1)S(1)} %get-tuple-element.21.refs_0_), channel_id=1, source_target_pairs={{0,1},{1,0},{2,3},{3,2},{4,5},{5,4},{6,7},{7,6},{8,9},{9,8},{10,11... | collective-permute-start | bytes 589832 | tf_op jit(solution)/shard_map/ppermute | solution.py:294
  26.5 5.1 %collective-permute-start.12 = (bf16[320,256]{1,0:T(8,128)(2,1)S(1)}, bf16[320,256]{1,0:T(8,128)(2,1)S(1)}, u32[]{:S(2)}, u32[]{:S(2)}) collective-permute-start(bf16[320,256]{1,0:T(8,128)(2,1)S(1)} %collective-permute-done.5.refs_6_), channel_id=1, source_target_pairs={{0,1},{1,0},{2,3},{3,2},{4,5},{5,4},{6,7},{7,6},{8,9},{9,8},{10,11... | collective-permute-start | bytes 491528 | tf_op jit(solution)/shard_map/ppermute | solution.py:294
  27.0 4.6 %collective-permute-start.13 = (bf16[288,256]{1,0:T(8,128)(2,1)S(1)}, bf16[288,256]{1,0:T(8,128)(2,1)S(1)}, u32[]{:S(2)}, u32[]{:S(2)}) collective-permute-start(bf16[288,256]{1,0:T(8,128)(2,1)S(1)} %collective-permute-done.8.refs_7_), channel_id=1, source_target_pairs={{0,1},{1,0},{2,3},{3,2},{4,5},{5,4},{6,7},{7,6},{8,9},{9,8},{10,11... | collective-permute-start | bytes 442376 | tf_op jit(solution)/shard_map/ppermute | solution.py:294
  31.6 1.4 %collective-permute-start.14 = (bf16[288,256]{1,0:T(8,128)(2,1)S(1)}, bf16[288,256]{1,0:T(8,128)(2,1)S(1)}, u32[]{:S(2)}, u32[]{:S(2)}) collective-permute-start(bf16[288,256]{1,0:T(8,128)(2,1)S(1)} %collective-permute-done.9.refs_8_), channel_id=1, source_target_pairs={{0,1},{1,0},{2,3},{3,2},{4,5},{5,4},{6,7},{7,6},{8,9},{9,8},{10,11... | collective-permute-start | bytes 442376 | tf_op jit(solution)/shard_map/ppermute | solution.py:294

commit v5 on v4

--- a/solution.py
+++ b/solution.py
@@ -141,7 +141,8 @@
             message[low : low + per_chip, :] = left_ref[pl.ds(start, per_chip), :].astype(jnp.bfloat16)
 
 
-def weight_kernel(final_ref, out_ref, wide_ref):
+def weight_kernel(final_ref, offset_ref, out_ref, offset_out, wide_ref):
+    offset_out[...] = offset_ref[...]
     channels, columns = out_ref.shape
     hidden = math.isqrt(columns)
     wide_ref[...] = final_ref[...].astype(jnp.float32)
@@ -161,9 +162,7 @@
     else:
         messages = [refs.pop(0) for _ in range(1 + max(place[0] for place in places))]
         shards = [(messages[n], right, messages[n], left) for n, right, left in places]
-    weight_ref, offset_hbm, out_hbm, left_ref, outer_ref, out_ref, offset_ref, sems = refs
-    offset_copy = pltpu.make_async_copy(offset_hbm, offset_ref, sems.at[rows_here])
-    offset_copy.start()
+    weight_ref, offset_ref, out_hbm, left_ref, outer_ref, out_ref, sems = refs
     tile = shards[0][0].shape[1]
     here = samples // count
     span = rows_here * hidden
@@ -194,7 +193,6 @@
                 ]
 
     first = pl.program_id(0) * tile if gridded else 0
-    offset_copy.wait()
     copies = []
     for i in range(rows_here):
         value = jnp.dot(weight_ref[...], outer_ref[i], preferred_element_type=jnp.float32)
@@ -272,15 +270,18 @@
             )
         ]
     )
-    weight = pl.pallas_call(
+    weight, offset = pl.pallas_call(
         weight_kernel,
-        out_shape=jax.ShapeDtypeStruct((channels, hidden * hidden), jnp.bfloat16),
-        in_specs=[vmem],
-        out_specs=vmem,
+        out_shape=[
+            jax.ShapeDtypeStruct((channels, hidden * hidden), jnp.bfloat16),
+            jax.ShapeDtypeStruct((1, channels), jnp.float32),
+        ],
+        in_specs=[vmem, vmem],
+        out_specs=[vmem, vmem],
         scratch_shapes=[pltpu.VMEM((hidden * hidden, channels), jnp.float32)],
         compiler_params=pltpu.CompilerParams(vmem_limit_bytes=16 * MIB),
         cost_estimate=pl.CostEstimate(flops=2**28, bytes_accessed=2**20, transcendentals=0),
-    )(final_projector_coefficients)
+    )(final_projector_coefficients, final_projector_offset.reshape(1, channels))
 
     by_place = {(place_of(r, half), r % 2): r for r in range(size)}
 
@@ -300,15 +301,14 @@
             places.append((len(messages), 0, value.shape[0] - per_chip))
             messages.append(value)
 
-    take([give, swap(give)])
-    flying = [keep, give[: body + (half - 1) * per_chip]]
+    mine, theirs, weight, offset = lax.optimization_barrier((give, swap(give), weight, offset))
+    take([mine, theirs])
+    flying = [keep, mine[: body + (half - 1) * per_chip]]
     swapped = []
     for step in range(1, half + 1):
         landed = [lax.ppermute(x, "row", neighbours(way)) for x, way in zip(flying, (1, -1))]
-        if step == 1:
-            landed[0], weight = lax.optimization_barrier((landed[0], weight))
         if step >= 3:
-            landed[0], swapped[step - 3] = lax.optimization_barrier((landed[0], swapped[step - 3]))
+            landed[-1], swapped[step - 3] = lax.optimization_barrier((landed[-1], swapped[step - 3]))
         flying = [x[: x.shape[0] - per_chip] for x in landed]
         if step == half - 1:
             flying = flying[:1]
@@ -319,7 +319,6 @@
         take(pair)
 
     gridded = tiles > 1
-    offset = pltpu.with_memory_space_constraint(final_projector_offset.reshape(1, channels), pltpu.HBM)
     if gridded:
         operands, specs = [], []
         for n, right, left in places:
@@ -328,11 +327,14 @@
                 pl.BlockSpec((width, tile), lambda t, first=right // width: (first + t, 0)),
                 pl.BlockSpec((per_chip, tile), lambda t, at=left // per_chip: (at, 0)),
             ]
-        specs += [pl.BlockSpec((channels, hidden * hidden), lambda t: (0, 0)), hbm]
+        specs += [
+            pl.BlockSpec((channels, hidden * hidden), lambda t: (0, 0)),
+            pl.BlockSpec((1, channels), lambda t: (0, 0)),
+        ]
         grid = (tiles,)
     else:
         operands = messages
-        specs = [vmem] * (len(messages) + 1) + [hbm]
+        specs = [vmem] * (len(messages) + 2)
         grid = ()
     return pl.pallas_call(
         functools.partial(pair_kernel, places, gridded, rows_here, hidden, samples),
@@ -344,8 +346,7 @@
             pltpu.VMEM((rows_here * hidden, samples), jnp.bfloat16),
             pltpu.VMEM((rows_here, hidden * hidden, tile), jnp.bfloat16),
             pltpu.VMEM((rows_here, tile, channels), jnp.bfloat16),
-            pltpu.VMEM((1, channels), jnp.float32),
-            pltpu.SemaphoreType.DMA((rows_here + 1,)),
+            pltpu.SemaphoreType.DMA((rows_here,)),
         ],
         compiler_params=pltpu.CompilerParams(vmem_limit_bytes=40 * MIB),
     )(*operands, weight, offset)

time: 38 us -> 36.5 us (0.961)
  waiting for transfers between devices: 18.4 us -> 15.2 us
  starting transfers between devices: 10.4 us -> 12.5 us
  Pallas kernels: 8.91 us -> 8.46 us
    ppermute x7, waiting for transfers between devices: 17 us -> 13.8 us  [per_device(): lax.ppermute(x, 'row', neighbours(way))]
    ppermute x7, starting transfers between devices: 8.21 us -> 10.4 us  [per_device(): lax.ppermute(x, 'row', neighbours(way))]
    pallas_call x1, Pallas kernels: 4.92 us -> 4.43 us  [per_device(): pl.pallas_call(functools.partial(pair_kernel, places, gridded, rows_here,...]
where the time goes in v5:
time: 36.5 us; the launch traced here: 36.3 us
  waiting for transfers between devices  15.2 us (42%)
  starting transfers between devices  12.5 us (34%)
  Pallas kernels  8.46 us (23%)
    ppermute x7, waiting for transfers between devices, per_device(): lax.ppermute(x, 'row', neighbours(way))  13.8 us
    ppermute x7, starting transfers between devices, per_device(): lax.ppermute(x, 'row', neighbours(way))  10.4 us
    pallas_call x1, Pallas kernels, per_device(): pl.pallas_call(functools.partial(pair_kernel, places, gridded, rows_here,...  4.43 us
    pallas_call x1, Pallas kernels, per_device(): pl.pallas_call(functools.partial(project_kernel, rows_here), out_shape=[m...  3.63 us
    ppermute x8, starting transfers between devices, swap(): return lax.ppermute(value, 'row', [(r, r ^ 1) for r in range(size)])  2.11 us
    ppermute x8, waiting for transfers between devices, swap(): return lax.ppermute(value, 'row', [(r, r ^ 1) for r in range(size)])  1.36 us
  transfers between devices with their start and end apart: 15, of which 6 were waited for; matrix products, arithmetic and copies ran while one was open for 0% of the time, Pallas kernels for 1%

profile of v5, /device:TPU:0, one launch (start us, length us, event | category | flops | bytes accessed | tf_op | source)
XLA Modules:
  0.0 36.3 jit_solution(13635122658741536124)
XLA Ops:
  0.0 3.6 %shard_map.91 = (bf16[384,256]{1,0:T(8,128)(2,1)S(1)}, bf16[384,256]{1,0:T(8,128)(2,1)S(1)}) custom-call(bf16[8,256,256]{2,1,0:T(8,128)(2,1)} %x_hbm.1, f32[1,256]{1,0:T(1,128)} %bitcast.10, f32[1,256]{1,0:T(1,128)} %bitcast.11, bf16[32,256]{1,0:T(8,128)(2,1)} %bitcast.8, f32[1,32]{1,0:T(1,128)} %bitcast.12, bf16[32,256]{1,0:T(8,128)(2,1)} %bitcast.9, ...), custom_call_target="tpu_custom_call" | custom-call | flops 536870912 | bytes 1048576 | tf_op jit(solution)/shard_map/pallas_call | solution.py:236
  3.6 0.5 %collective-permute-start = (bf16[384,256]{1,0:T(8,128)(2,1)S(1)}, bf16[384,256]{1,0:T(8,128)(2,1)S(1)}, u32[]{:S(2)}, u32[]{:S(2)}) collective-permute-start(bf16[384,256]{1,0:T(8,128)(2,1)S(1)} %get-tuple-element.28.refs_0_), channel_id=1, source_target_pairs={{0,1},{1,0},{2,3},{3,2},{4,5},{5,4},{6,7},{7,6},{8,9},{9,8},{10,11... | collective-permute-start | bytes 589832 | tf_op jit(solution)/shard_map/ppermute | solution.py:295
  4.2 2.6 %collective-permute-start.1 = (bf16[384,256]{1,0:T(8,128)(2,1)S(1)}, bf16[384,256]{1,0:T(8,128)(2,1)S(1)}, u32[]{:S(2)}, u32[]{:S(2)}) collective-permute-start(bf16[384,256]{1,0:T(8,128)(2,1)S(1)} %get-tuple-element.30), channel_id=1, source_target_pairs={{0,4},{1,3},{2,0},{3,7},{4,8},{5,1},{6,2},{7,11},{8,12},{9,5},{10,... | collective-permute-start | bytes 589832 | tf_op jit(solution)/shard_map/ppermute | solution.py:309
  6.8 0.4 %shard_map.92 = (bf16[128,1024]{1,0:T(8,128)(2,1)S(1)}, f32[1,128]{1,0:T(1,128)S(1)}) custom-call(bf16[1024,128]{1,0:T(8,128)(2,1)S(1)} %copy-done, f32[1,128]{1,0:T(1,128)S(1)} %bitcast.7), custom_call_target="tpu_custom_call" | custom-call | flops 268435456 | bytes 1048576 | tf_op jit(solution)/shard_map/pallas_call | solution.py:273
  7.2 0.0 collective-permute-done.refs_1_
  7.3 0.9 %collective-permute-start.2 = (bf16[352,256]{1,0:T(8,128)(2,1)S(1)}, bf16[352,256]{1,0:T(8,128)(2,1)S(1)}, u32[]{:S(2)}, u32[]{:S(2)}) collective-permute-start(bf16[352,256]{1,0:T(8,128)(2,1)S(1)} %slice.18), channel_id=1, source_target_pairs={{0,2},{1,5},{2,6},{3,1},{4,0},{5,9},{6,10},{7,3},{8,4},{9,13},{10,... | collective-permute-start | bytes 540680 | tf_op jit(solution)/shard_map/ppermute | solution.py:309
  8.2 3.4 %collective-permute-done.1.refs_2_ = bf16[384,256]{1,0:T(8,128)(2,1)S(1)} collective-permute-done((bf16[384,256]{1,0:T(8,128)(2,1)S(1)}, bf16[384,256]{1,0:T(8,128)(2,1)S(1)}, u32[]{:S(2)}, u32[]{:S(2)}) %collective-permute-start.1) | collective-permute-done | bytes 196640 | tf_op jit(solution)/shard_map/ppermute | solution.py:309
  11.6 2.5 %collective-permute-start.3 = (bf16[352,256]{1,0:T(8,128)(2,1)S(1)}, bf16[352,256]{1,0:T(8,128)(2,1)S(1)}, u32[]{:S(2)}, u32[]{:S(2)}) collective-permute-start(bf16[352,256]{1,0:T(8,128)(2,1)S(1)} %slice.24), channel_id=1, source_target_pairs={{0,4},{1,3},{2,0},{3,7},{4,8},{5,1},{6,2},{7,11},{8,12},{9,5},{10,... | collective-permute-start | bytes 540680 | tf_op jit(solution)/shard_map/ppermute | solution.py:309
  14.1 0.0 collective-permute-done.2.refs_3_
  14.1 0.1 collective-permute-start.4
  14.2 4.6 %collective-permute-done.3.refs_4_ = bf16[352,256]{1,0:T(8,128)(2,1)S(1)} collective-permute-done((bf16[352,256]{1,0:T(8,128)(2,1)S(1)}, bf16[352,256]{1,0:T(8,128)(2,1)S(1)}, u32[]{:S(2)}, u32[]{:S(2)}) %collective-permute-start.3) | collective-permute-done | bytes 180256 | tf_op jit(solution)/shard_map/ppermute | solution.py:309
  18.8 2.1 %collective-permute-start.5 = (bf16[320,256]{1,0:T(8,128)(2,1)S(1)}, bf16[320,256]{1,0:T(8,128)(2,1)S(1)}, u32[]{:S(2)}, u32[]{:S(2)}) collective-permute-start(bf16[320,256]{1,0:T(8,128)(2,1)S(1)} %slice.26), channel_id=1, source_target_pairs={{0,4},{1,3},{2,0},{3,7},{4,8},{5,1},{6,2},{7,11},{8,12},{9,5},{10,... | collective-permute-start | bytes 491528 | tf_op jit(solution)/shard_map/ppermute | solution.py:309
  20.9 0.5 %collective-permute-start.7 = (bf16[384,256]{1,0:T(8,128)(2,1)S(1)}, bf16[384,256]{1,0:T(8,128)(2,1)S(1)}, u32[]{:S(2)}, u32[]{:S(2)}) collective-permute-start(bf16[384,256]{1,0:T(8,128)(2,1)S(1)} %collective-permute-done.1.refs_2_), channel_id=1, source_target_pairs={{0,1},{1,0},{2,3},{3,2},{4,5},{5,4},{6,7},{7,6},{8,9},{9,8},{10,11... | collective-permute-start | bytes 589832 | tf_op jit(solution)/shard_map/ppermute | solution.py:295
  21.4 0.0 collective-permute-done.4.refs_5_
  21.4 0.0 collective-permute-start.10
  21.4 0.1 collective-permute-start.6
  21.5 2.7 %collective-permute-done.5.refs_6_ = bf16[320,256]{1,0:T(8,128)(2,1)S(1)} collective-permute-done((bf16[320,256]{1,0:T(8,128)(2,1)S(1)}, bf16[320,256]{1,0:T(8,128)(2,1)S(1)}, u32[]{:S(2)}, u32[]{:S(2)}) %collective-permute-start.5) | collective-permute-done | bytes 163872 | tf_op jit(solution)/shard_map/ppermute | solution.py:309
  24.2 2.1 %collective-permute-start.9 = (bf16[288,256]{1,0:T(8,128)(2,1)S(1)}, bf16[288,256]{1,0:T(8,128)(2,1)S(1)}, u32[]{:S(2)}, u32[]{:S(2)}) collective-permute-start(bf16[288,256]{1,0:T(8,128)(2,1)S(1)} %slice.28), channel_id=1, source_target_pairs={{0,4},{1,3},{2,0},{3,7},{4,8},{5,1},{6,2},{7,11},{8,12},{9,5},{10,... | collective-permute-start | bytes 442376 | tf_op jit(solution)/shard_map/ppermute | solution.py:309
  26.3 0.3 collective-permute-done.6.refs_7_
  26.6 1.0 %collective-permute-start.12 = (bf16[320,256]{1,0:T(8,128)(2,1)S(1)}, bf16[320,256]{1,0:T(8,128)(2,1)S(1)}, u32[]{:S(2)}, u32[]{:S(2)}) collective-permute-start(bf16[320,256]{1,0:T(8,128)(2,1)S(1)} %collective-permute-done.5.refs_6_), channel_id=1, source_target_pairs={{0,1},{1,0},{2,3},{3,2},{4,5},{5,4},{6,7},{7,6},{8,9},{9,8},{10,11... | collective-permute-start | bytes 491528 | tf_op jit(solution)/shard_map/ppermute | solution.py:295
  27.6 0.1 collective-permute-start.13
  27.7 2.8 %collective-permute-done.9.refs_8_ = bf16[288,256]{1,0:T(8,128)(2,1)S(1)} collective-permute-done((bf16[288,256]{1,0:T(8,128)(2,1)S(1)}, bf16[288,256]{1,0:T(8,128)(2,1)S(1)}, u32[]{:S(2)}, u32[]{:S(2)}) %collective-permute-start.9) | collective-permute-done | bytes 147488 | tf_op jit(solution)/shard_map/ppermute | solution.py:309
  30.6 1.3 %collective-permute-done.14.refs_15_ = bf16[288,256]{1,0:T(8,128)(2,1)S(1)} collective-permute-done((bf16[288,256]{1,0:T(8,128)(2,1)S(1)}, bf16[288,256]{1,0:T(8,128)(2,1)S(1)}, u32[]{:S(2)}, u32[]{:S(2)}) %collective-permute-start.14) | collective-permute-done | bytes 147488 | tf_op jit(solution)/shard_map/ppermute | solution.py:295
  31.9 4.4 %shard_map.93 = bf16[16,256,128]{2,1,0:T(8,128)(2,1)} custom-call(bf16[384,256]{1,0:T(8,128)(2,1)S(1)} %get-tuple-element.28.refs_0_, bf16[384,256]{1,0:T(8,128)(2,1)S(1)} %collective-permute-done.refs_1_, bf16[384,256]{1,0:T(8,128)(2,1)S(1)} %collective-permute-done.1.refs_2_, bf16[352,256]{1,0:T(8,128)(2,1)S(1)} %collective-permute-done.2.refs_3_, ...), custom_call_target="tpu_custom_call" | custom-call | tf_op jit(solution)/shard_map/pallas_call | solution.py:339
  (19 shorter events, 0.1 us)
Async XLA Ops:
  0.0 6.8 %copy-start = (bf16[1024,128]{1,0:T(8,128)(2,1)S(1)}, bf16[1024,128]{1,0:T(8,128)(2,1)}, u32[]{:S(2)}) copy-start(bf16[1024,128]{1,0:T(8,128)(2,1)} %final_ref.1) | copy-start | bytes 786436
  3.6 3.6 %collective-permute-start = (bf16[384,256]{1,0:T(8,128)(2,1)S(1)}, bf16[384,256]{1,0:T(8,128)(2,1)S(1)}, u32[]{:S(2)}, u32[]{:S(2)}) collective-permute-start(bf16[384,256]{1,0:T(8,128)(2,1)S(1)} %get-tuple-element.28.refs_0_), channel_id=1, source_target_pairs={{0,1},{1,0},{2,3},{3,2},{4,5},{5,4},{6,7},{7,6},{8,9},{9,8},{10,11... | collective-permute-start | bytes 589832 | tf_op jit(solution)/shard_map/ppermute | solution.py:295
  4.2 2.7 %copy-start.1 = (f32[128]{0:T(128)S(1)}, f32[128]{0:T(128)}, u32[]{:S(2)}) copy-start(f32[128]{0:T(128)} %param.17) | copy-start | bytes 1540
  4.2 7.4 %collective-permute-start.1 = (bf16[384,256]{1,0:T(8,128)(2,1)S(1)}, bf16[384,256]{1,0:T(8,128)(2,1)S(1)}, u32[]{:S(2)}, u32[]{:S(2)}) collective-permute-start(bf16[384,256]{1,0:T(8,128)(2,1)S(1)} %get-tuple-element.30), channel_id=1, source_target_pairs={{0,4},{1,3},{2,0},{3,7},{4,8},{5,1},{6,2},{7,11},{8,12},{9,5},{10,... | collective-permute-start | bytes 589832 | tf_op jit(solution)/shard_map/ppermute | solution.py:309
  7.3 6.8 %collective-permute-start.2 = (bf16[352,256]{1,0:T(8,128)(2,1)S(1)}, bf16[352,256]{1,0:T(8,128)(2,1)S(1)}, u32[]{:S(2)}, u32[]{:S(2)}) collective-permute-start(bf16[352,256]{1,0:T(8,128)(2,1)S(1)} %slice.18), channel_id=1, source_target_pairs={{0,2},{1,5},{2,6},{3,1},{4,0},{5,9},{6,10},{7,3},{8,4},{9,13},{10,... | collective-permute-start | bytes 540680 | tf_op jit(solution)/shard_map/ppermute | solution.py:309
  11.6 7.2 %collective-permute-start.3 = (bf16[352,256]{1,0:T(8,128)(2,1)S(1)}, bf16[352,256]{1,0:T(8,128)(2,1)S(1)}, u32[]{:S(2)}, u32[]{:S(2)}) collective-permute-start(bf16[352,256]{1,0:T(8,128)(2,1)S(1)} %slice.24), channel_id=1, source_target_pairs={{0,4},{1,3},{2,0},{3,7},{4,8},{5,1},{6,2},{7,11},{8,12},{9,5},{10,... | collective-permute-start | bytes 540680 | tf_op jit(solution)/shard_map/ppermute | solution.py:309
  14.1 7.3 %collective-permute-start.4 = (bf16[320,256]{1,0:T(8,128)(2,1)S(1)}, bf16[320,256]{1,0:T(8,128)(2,1)S(1)}, u32[]{:S(2)}, u32[]{:S(2)}) collective-permute-start(bf16[320,256]{1,0:T(8,128)(2,1)S(1)} %slice.25), channel_id=1, source_target_pairs={{0,2},{1,5},{2,6},{3,1},{4,0},{5,9},{6,10},{7,3},{8,4},{9,13},{10,... | collective-permute-start | bytes 491528 | tf_op jit(solution)/shard_map/ppermute | solution.py:309
  18.8 5.4 %collective-permute-start.5 = (bf16[320,256]{1,0:T(8,128)(2,1)S(1)}, bf16[320,256]{1,0:T(8,128)(2,1)S(1)}, u32[]{:S(2)}, u32[]{:S(2)}) collective-permute-start(bf16[320,256]{1,0:T(8,128)(2,1)S(1)} %slice.26), channel_id=1, source_target_pairs={{0,4},{1,3},{2,0},{3,7},{4,8},{5,1},{6,2},{7,11},{8,12},{9,5},{10,... | collective-permute-start | bytes 491528 | tf_op jit(solution)/shard_map/ppermute | solution.py:309
  20.9 3.3 %collective-permute-start.8 = (bf16[352,256]{1,0:T(8,128)(2,1)S(1)}, bf16[352,256]{1,0:T(8,128)(2,1)S(1)}, u32[]{:S(2)}, u32[]{:S(2)}) collective-permute-start(bf16[352,256]{1,0:T(8,128)(2,1)S(1)} %collective-permute-done.2.refs_3_), channel_id=1, source_target_pairs={{0,1},{1,0},{2,3},{3,2},{4,5},{5,4},{6,7},{7,6},{8,9},{9,8},{10,11... | collective-permute-start | bytes 540680 | tf_op jit(solution)/shard_map/ppermute | solution.py:295
  20.9 5.4 %collective-permute-start.7 = (bf16[384,256]{1,0:T(8,128)(2,1)S(1)}, bf16[384,256]{1,0:T(8,128)(2,1)S(1)}, u32[]{:S(2)}, u32[]{:S(2)}) collective-permute-start(bf16[384,256]{1,0:T(8,128)(2,1)S(1)} %collective-permute-done.1.refs_2_), channel_id=1, source_target_pairs={{0,1},{1,0},{2,3},{3,2},{4,5},{5,4},{6,7},{7,6},{8,9},{9,8},{10,11... | collective-permute-start | bytes 589832 | tf_op jit(solution)/shard_map/ppermute | solution.py:295
  21.4 9.1 %collective-permute-start.10 = (bf16[352,256]{1,0:T(8,128)(2,1)S(1)}, bf16[352,256]{1,0:T(8,128)(2,1)S(1)}, u32[]{:S(2)}, u32[]{:S(2)}) collective-permute-start(bf16[352,256]{1,0:T(8,128)(2,1)S(1)} %collective-permute-done.3.refs_4_), channel_id=1, source_target_pairs={{0,1},{1,0},{2,3},{3,2},{4,5},{5,4},{6,7},{7,6},{8,9},{9,8},{10,11... | collective-permute-start | bytes 540680 | tf_op jit(solution)/shard_map/ppermute | solution.py:295
  21.4 5.2 %collective-permute-start.6 = (bf16[288,256]{1,0:T(8,128)(2,1)S(1)}, bf16[288,256]{1,0:T(8,128)(2,1)S(1)}, u32[]{:S(2)}, u32[]{:S(2)}) collective-permute-start(bf16[288,256]{1,0:T(8,128)(2,1)S(1)} %slice.27), channel_id=1, source_target_pairs={{0,2},{1,5},{2,6},{3,1},{4,0},{5,9},{6,10},{7,3},{8,4},{9,13},{10,... | collective-permute-start | bytes 442376 | tf_op jit(solution)/shard_map/ppermute | solution.py:309
  24.2 6.3 %collective-permute-start.11 = (bf16[320,256]{1,0:T(8,128)(2,1)S(1)}, bf16[320,256]{1,0:T(8,128)(2,1)S(1)}, u32[]{:S(2)}, u32[]{:S(2)}) collective-permute-start(bf16[320,256]{1,0:T(8,128)(2,1)S(1)} %collective-permute-done.4.refs_5_), channel_id=1, source_target_pairs={{0,1},{1,0},{2,3},{3,2},{4,5},{5,4},{6,7},{7,6},{8,9},{9,8},{10,11... | collective-permute-start | bytes 491528 | tf_op jit(solution)/shard_map/ppermute | solution.py:295
  24.2 6.3 %collective-permute-start.9 = (bf16[288,256]{1,0:T(8,128)(2,1)S(1)}, bf16[288,256]{1,0:T(8,128)(2,1)S(1)}, u32[]{:S(2)}, u32[]{:S(2)}) collective-permute-start(bf16[288,256]{1,0:T(8,128)(2,1)S(1)} %slice.28), channel_id=1, source_target_pairs={{0,4},{1,3},{2,0},{3,7},{4,8},{5,1},{6,2},{7,11},{8,12},{9,5},{10,... | collective-permute-start | bytes 442376 | tf_op jit(solution)/shard_map/ppermute | solution.py:309
  26.6 3.9 %collective-permute-start.12 = (bf16[320,256]{1,0:T(8,128)(2,1)S(1)}, bf16[320,256]{1,0:T(8,128)(2,1)S(1)}, u32[]{:S(2)}, u32[]{:S(2)}) collective-permute-start(bf16[320,256]{1,0:T(8,128)(2,1)S(1)} %collective-permute-done.5.refs_6_), channel_id=1, source_target_pairs={{0,1},{1,0},{2,3},{3,2},{4,5},{5,4},{6,7},{7,6},{8,9},{9,8},{10,11... | collective-permute-start | bytes 491528 | tf_op jit(solution)/shard_map/ppermute | solution.py:295
  27.6 2.9 %collective-permute-start.13 = (bf16[288,256]{1,0:T(8,128)(2,1)S(1)}, bf16[288,256]{1,0:T(8,128)(2,1)S(1)}, u32[]{:S(2)}, u32[]{:S(2)}) collective-permute-start(bf16[288,256]{1,0:T(8,128)(2,1)S(1)} %collective-permute-done.6.refs_7_), channel_id=1, source_target_pairs={{0,1},{1,0},{2,3},{3,2},{4,5},{5,4},{6,7},{7,6},{8,9},{9,8},{10,11... | collective-permute-start | bytes 442376 | tf_op jit(solution)/shard_map/ppermute | solution.py:295
  30.5 1.4 %collective-permute-start.14 = (bf16[288,256]{1,0:T(8,128)(2,1)S(1)}, bf16[288,256]{1,0:T(8,128)(2,1)S(1)}, u32[]{:S(2)}, u32[]{:S(2)}) collective-permute-start(bf16[288,256]{1,0:T(8,128)(2,1)S(1)} %collective-permute-done.9.refs_8_), channel_id=1, source_target_pairs={{0,1},{1,0},{2,3},{3,2},{4,5},{5,4},{6,7},{7,6},{8,9},{9,8},{10,11... | collective-permute-start | bytes 442376 | tf_op jit(solution)/shard_map/ppermute | solution.py:295

commit v6 on v5

--- a/solution.py
+++ b/solution.py
@@ -284,12 +284,9 @@
     )(final_projector_coefficients, final_projector_offset.reshape(1, channels))
 
     by_place = {(place_of(r, half), r % 2): r for r in range(size)}
-
-    def neighbours(way):
-        return [
-            (r, by_place[(place_of(r, half) + way * (1 - 2 * (r % 2))) % (2 * half), r % 2])
-            for r in range(size)
-        ]
+    around = [
+        (r, by_place[(place_of(r, half) + 1 - 2 * (r % 2)) % (2 * half), r % 2]) for r in range(size)
+    ]
 
     def swap(value):
         return lax.ppermute(value, "row", [(r, r ^ 1) for r in range(size)])
@@ -303,10 +300,10 @@
 
     mine, theirs, weight, offset = lax.optimization_barrier((give, swap(give), weight, offset))
     take([mine, theirs])
-    flying = [keep, mine[: body + (half - 1) * per_chip]]
+    flying = [keep, theirs[: body + (half - 1) * per_chip]]
     swapped = []
     for step in range(1, half + 1):
-        landed = [lax.ppermute(x, "row", neighbours(way)) for x, way in zip(flying, (1, -1))]
+        landed = [lax.ppermute(x, "row", around) for x in flying]
         if step >= 3:
             landed[-1], swapped[step - 3] = lax.optimization_barrier((landed[-1], swapped[step - 3]))
         flying = [x[: x.shape[0] - per_chip] for x in landed]

time: 36.5 us -> 32.5 us (0.89)
  waiting for transfers between devices: 15.2 us -> 8.24 us
  starting transfers between devices: 12.5 us -> 15.5 us
    ppermute x7, waiting for transfers between devices: 13.8 us -> 6.88 us  [per_device(): landed = [lax.ppermute(x, 'row', around) for x in flying]]
    ppermute x7, starting transfers between devices: 10.4 us -> 14 us  [per_device(): landed = [lax.ppermute(x, 'row', around) for x in flying]]
    ppermute x8, starting transfers between devices: 2.11 us -> 1.55 us  [swap(): return lax.ppermute(value, 'row', [(r, r ^ 1) for r in range(size)])]
  transfers between devices with their start and end apart: 15 -> 15, of which waited for: 6 -> 7; matrix products, arithmetic and copies ran while one was open for 0% -> 0% of each run, Pallas kernels for 1% -> 1%
where the time goes in v6:
time: 32.5 us; the launch traced here: 32.4 us
  starting transfers between devices  15.5 us (48%)
  Pallas kernels  8.46 us (26%)
  waiting for transfers between devices  8.24 us (25%)
    ppermute x7, starting transfers between devices, per_device(): landed = [lax.ppermute(x, 'row', around) for x in flying]  14 us
    ppermute x7, waiting for transfers between devices, per_device(): landed = [lax.ppermute(x, 'row', around) for x in flying]  6.88 us
    pallas_call x1, Pallas kernels, per_device(): pl.pallas_call(functools.partial(pair_kernel, places, gridded, rows_here,...  4.43 us
    pallas_call x1, Pallas kernels, per_device(): pl.pallas_call(functools.partial(project_kernel, rows_here), out_shape=[m...  3.63 us
    ppermute x8, starting transfers between devices, swap(): return lax.ppermute(value, 'row', [(r, r ^ 1) for r in range(size)])  1.55 us
    ppermute x8, waiting for transfers between devices, swap(): return lax.ppermute(value, 'row', [(r, r ^ 1) for r in range(size)])  1.36 us
  transfers between devices with their start and end apart: 15, of which 7 were waited for; matrix products, arithmetic and copies ran while one was open for 0% of the time, Pallas kernels for 1%

profile of v6, /device:TPU:0, one launch (start us, length us, event | category | flops | bytes accessed | tf_op | source)
XLA Modules:
  0.0 32.4 jit_solution(6171999589454833091)
XLA Ops:
  0.0 3.6 %shard_map.91 = (bf16[384,256]{1,0:T(8,128)(2,1)S(1)}, bf16[384,256]{1,0:T(8,128)(2,1)S(1)}) custom-call(bf16[8,256,256]{2,1,0:T(8,128)(2,1)} %x_hbm.1, f32[1,256]{1,0:T(1,128)} %bitcast.10, f32[1,256]{1,0:T(1,128)} %bitcast.11, bf16[32,256]{1,0:T(8,128)(2,1)} %bitcast.8, f32[1,32]{1,0:T(1,128)} %bitcast.12, bf16[32,256]{1,0:T(8,128)(2,1)} %bitcast.9, ...), custom_call_target="tpu_custom_call" | custom-call | flops 536870912 | bytes 1048576 | tf_op jit(solution)/shard_map/pallas_call | solution.py:236
  3.6 0.5 %collective-permute-start = (bf16[384,256]{1,0:T(8,128)(2,1)S(1)}, bf16[384,256]{1,0:T(8,128)(2,1)S(1)}, u32[]{:S(2)}, u32[]{:S(2)}) collective-permute-start(bf16[384,256]{1,0:T(8,128)(2,1)S(1)} %get-tuple-element.28.refs_0_), channel_id=1, source_target_pairs={{0,1},{1,0},{2,3},{3,2},{4,5},{5,4},{6,7},{7,6},{8,9},{9,8},{10,11... | collective-permute-start | bytes 589832 | tf_op jit(solution)/shard_map/ppermute | solution.py:292
  4.2 2.6 %collective-permute-start.1 = (bf16[384,256]{1,0:T(8,128)(2,1)S(1)}, bf16[384,256]{1,0:T(8,128)(2,1)S(1)}, u32[]{:S(2)}, u32[]{:S(2)}) collective-permute-start(bf16[384,256]{1,0:T(8,128)(2,1)S(1)} %get-tuple-element.30), channel_id=1, source_target_pairs={{0,4},{1,3},{2,0},{3,7},{4,8},{5,1},{6,2},{7,11},{8,12},{9,5},{10,... | collective-permute-start | bytes 589832 | tf_op jit(solution)/shard_map/ppermute | solution.py:306
  6.8 0.4 %shard_map.92 = (bf16[128,1024]{1,0:T(8,128)(2,1)S(1)}, f32[1,128]{1,0:T(1,128)S(1)}) custom-call(bf16[1024,128]{1,0:T(8,128)(2,1)S(1)} %copy-done, f32[1,128]{1,0:T(1,128)S(1)} %bitcast.7), custom_call_target="tpu_custom_call" | custom-call | flops 268435456 | bytes 1048576 | tf_op jit(solution)/shard_map/pallas_call | solution.py:273
  7.2 0.0 collective-permute-done.refs_1_
  7.3 1.6 %collective-permute-start.2 = (bf16[352,256]{1,0:T(8,128)(2,1)S(1)}, bf16[352,256]{1,0:T(8,128)(2,1)S(1)}, u32[]{:S(2)}, u32[]{:S(2)}) collective-permute-start(bf16[352,256]{1,0:T(8,128)(2,1)S(1)} %slice.18), channel_id=1, source_target_pairs={{0,4},{1,3},{2,0},{3,7},{4,8},{5,1},{6,2},{7,11},{8,12},{9,5},{10,... | collective-permute-start | bytes 540680 | tf_op jit(solution)/shard_map/ppermute | solution.py:306
  8.9 1.5 %collective-permute-done.1.refs_2_ = bf16[384,256]{1,0:T(8,128)(2,1)S(1)} collective-permute-done((bf16[384,256]{1,0:T(8,128)(2,1)S(1)}, bf16[384,256]{1,0:T(8,128)(2,1)S(1)}, u32[]{:S(2)}, u32[]{:S(2)}) %collective-permute-start.1) | collective-permute-done | bytes 196640 | tf_op jit(solution)/shard_map/ppermute | solution.py:306
  10.4 2.1 %collective-permute-start.3 = (bf16[352,256]{1,0:T(8,128)(2,1)S(1)}, bf16[352,256]{1,0:T(8,128)(2,1)S(1)}, u32[]{:S(2)}, u32[]{:S(2)}) collective-permute-start(bf16[352,256]{1,0:T(8,128)(2,1)S(1)} %slice.24), channel_id=1, source_target_pairs={{0,4},{1,3},{2,0},{3,7},{4,8},{5,1},{6,2},{7,11},{8,12},{9,5},{10,... | collective-permute-start | bytes 540680 | tf_op jit(solution)/shard_map/ppermute | solution.py:306
  12.5 0.3 collective-permute-done.2.refs_3_
  12.8 1.7 %collective-permute-start.4 = (bf16[320,256]{1,0:T(8,128)(2,1)S(1)}, bf16[320,256]{1,0:T(8,128)(2,1)S(1)}, u32[]{:S(2)}, u32[]{:S(2)}) collective-permute-start(bf16[320,256]{1,0:T(8,128)(2,1)S(1)} %slice.25), channel_id=1, source_target_pairs={{0,4},{1,3},{2,0},{3,7},{4,8},{5,1},{6,2},{7,11},{8,12},{9,5},{10,... | collective-permute-start | bytes 491528 | tf_op jit(solution)/shard_map/ppermute | solution.py:306
  14.5 1.5 %collective-permute-done.3.refs_4_ = bf16[352,256]{1,0:T(8,128)(2,1)S(1)} collective-permute-done((bf16[352,256]{1,0:T(8,128)(2,1)S(1)}, bf16[352,256]{1,0:T(8,128)(2,1)S(1)}, u32[]{:S(2)}, u32[]{:S(2)}) %collective-permute-start.3) | collective-permute-done | bytes 180256 | tf_op jit(solution)/shard_map/ppermute | solution.py:306
  16.0 2.1 %collective-permute-start.5 = (bf16[320,256]{1,0:T(8,128)(2,1)S(1)}, bf16[320,256]{1,0:T(8,128)(2,1)S(1)}, u32[]{:S(2)}, u32[]{:S(2)}) collective-permute-start(bf16[320,256]{1,0:T(8,128)(2,1)S(1)} %slice.26), channel_id=1, source_target_pairs={{0,4},{1,3},{2,0},{3,7},{4,8},{5,1},{6,2},{7,11},{8,12},{9,5},{10,... | collective-permute-start | bytes 491528 | tf_op jit(solution)/shard_map/ppermute | solution.py:306
  18.1 0.5 %collective-permute-start.7 = (bf16[384,256]{1,0:T(8,128)(2,1)S(1)}, bf16[384,256]{1,0:T(8,128)(2,1)S(1)}, u32[]{:S(2)}, u32[]{:S(2)}) collective-permute-start(bf16[384,256]{1,0:T(8,128)(2,1)S(1)} %collective-permute-done.1.refs_2_), channel_id=1, source_target_pairs={{0,1},{1,0},{2,3},{3,2},{4,5},{5,4},{6,7},{7,6},{8,9},{9,8},{10,11... | collective-permute-start | bytes 589832 | tf_op jit(solution)/shard_map/ppermute | solution.py:292
  18.6 0.0 collective-permute-done.4.refs_5_
  18.6 0.0 collective-permute-start.10
  18.6 1.6 %collective-permute-start.6 = (bf16[288,256]{1,0:T(8,128)(2,1)S(1)}, bf16[288,256]{1,0:T(8,128)(2,1)S(1)}, u32[]{:S(2)}, u32[]{:S(2)}) collective-permute-start(bf16[288,256]{1,0:T(8,128)(2,1)S(1)} %slice.27), channel_id=1, source_target_pairs={{0,4},{1,3},{2,0},{3,7},{4,8},{5,1},{6,2},{7,11},{8,12},{9,5},{10,... | collective-permute-start | bytes 442376 | tf_op jit(solution)/shard_map/ppermute | solution.py:306
  20.3 1.1 %collective-permute-done.5.refs_6_ = bf16[320,256]{1,0:T(8,128)(2,1)S(1)} collective-permute-done((bf16[320,256]{1,0:T(8,128)(2,1)S(1)}, bf16[320,256]{1,0:T(8,128)(2,1)S(1)}, u32[]{:S(2)}, u32[]{:S(2)}) %collective-permute-start.5) | collective-permute-done | bytes 163872 | tf_op jit(solution)/shard_map/ppermute | solution.py:306
  21.4 0.0 collective-permute-done.8.refs_10_
  21.4 2.1 %collective-permute-start.9 = (bf16[288,256]{1,0:T(8,128)(2,1)S(1)}, bf16[288,256]{1,0:T(8,128)(2,1)S(1)}, u32[]{:S(2)}, u32[]{:S(2)}) collective-permute-start(bf16[288,256]{1,0:T(8,128)(2,1)S(1)} %slice.28), channel_id=1, source_target_pairs={{0,4},{1,3},{2,0},{3,7},{4,8},{5,1},{6,2},{7,11},{8,12},{9,5},{10,... | collective-permute-start | bytes 442376 | tf_op jit(solution)/shard_map/ppermute | solution.py:306
  23.5 0.3 %collective-permute-done.6.refs_7_ = bf16[288,256]{1,0:T(8,128)(2,1)S(1)} collective-permute-done((bf16[288,256]{1,0:T(8,128)(2,1)S(1)}, bf16[288,256]{1,0:T(8,128)(2,1)S(1)}, u32[]{:S(2)}, u32[]{:S(2)}) %collective-permute-start.6) | collective-permute-done | bytes 147488 | tf_op jit(solution)/shard_map/ppermute | solution.py:306
  23.8 0.5 %collective-permute-start.13 = (bf16[288,256]{1,0:T(8,128)(2,1)S(1)}, bf16[288,256]{1,0:T(8,128)(2,1)S(1)}, u32[]{:S(2)}, u32[]{:S(2)}) collective-permute-start(bf16[288,256]{1,0:T(8,128)(2,1)S(1)} %collective-permute-done.6.refs_7_), channel_id=1, source_target_pairs={{0,1},{1,0},{2,3},{3,2},{4,5},{5,4},{6,7},{7,6},{8,9},{9,8},{10,11... | collective-permute-start | bytes 442376 | tf_op jit(solution)/shard_map/ppermute | solution.py:292
  24.3 2.2 %collective-permute-done.9.refs_8_ = bf16[288,256]{1,0:T(8,128)(2,1)S(1)} collective-permute-done((bf16[288,256]{1,0:T(8,128)(2,1)S(1)}, bf16[288,256]{1,0:T(8,128)(2,1)S(1)}, u32[]{:S(2)}, u32[]{:S(2)}) %collective-permute-start.9) | collective-permute-done | bytes 147488 | tf_op jit(solution)/shard_map/ppermute | solution.py:306
  26.6 1.3 %collective-permute-done.14.refs_15_ = bf16[288,256]{1,0:T(8,128)(2,1)S(1)} collective-permute-done((bf16[288,256]{1,0:T(8,128)(2,1)S(1)}, bf16[288,256]{1,0:T(8,128)(2,1)S(1)}, u32[]{:S(2)}, u32[]{:S(2)}) %collective-permute-start.14) | collective-permute-done | bytes 147488 | tf_op jit(solution)/shard_map/ppermute | solution.py:292
  28.0 4.4 %shard_map.93 = bf16[16,256,128]{2,1,0:T(8,128)(2,1)} custom-call(bf16[384,256]{1,0:T(8,128)(2,1)S(1)} %get-tuple-element.28.refs_0_, bf16[384,256]{1,0:T(8,128)(2,1)S(1)} %collective-permute-done.refs_1_, bf16[384,256]{1,0:T(8,128)(2,1)S(1)} %collective-permute-done.1.refs_2_, bf16[352,256]{1,0:T(8,128)(2,1)S(1)} %collective-permute-done.2.refs_3_, ...), custom_call_target="tpu_custom_call" | custom-call | tf_op jit(solution)/shard_map/pallas_call | solution.py:336
  (19 shorter events, 0.1 us)
Async XLA Ops:
  0.0 6.8 %copy-start = (bf16[1024,128]{1,0:T(8,128)(2,1)S(1)}, bf16[1024,128]{1,0:T(8,128)(2,1)}, u32[]{:S(2)}) copy-start(bf16[1024,128]{1,0:T(8,128)(2,1)} %final_ref.1) | copy-start | bytes 786436
  3.6 3.6 %collective-permute-start = (bf16[384,256]{1,0:T(8,128)(2,1)S(1)}, bf16[384,256]{1,0:T(8,128)(2,1)S(1)}, u32[]{:S(2)}, u32[]{:S(2)}) collective-permute-start(bf16[384,256]{1,0:T(8,128)(2,1)S(1)} %get-tuple-element.28.refs_0_), channel_id=1, source_target_pairs={{0,1},{1,0},{2,3},{3,2},{4,5},{5,4},{6,7},{7,6},{8,9},{9,8},{10,11... | collective-permute-start | bytes 589832 | tf_op jit(solution)/shard_map/ppermute | solution.py:292
  4.2 2.7 %copy-start.1 = (f32[128]{0:T(128)S(1)}, f32[128]{0:T(128)}, u32[]{:S(2)}) copy-start(f32[128]{0:T(128)} %param.17) | copy-start | bytes 1540
  4.2 6.2 %collective-permute-start.1 = (bf16[384,256]{1,0:T(8,128)(2,1)S(1)}, bf16[384,256]{1,0:T(8,128)(2,1)S(1)}, u32[]{:S(2)}, u32[]{:S(2)}) collective-permute-start(bf16[384,256]{1,0:T(8,128)(2,1)S(1)} %get-tuple-element.30), channel_id=1, source_target_pairs={{0,4},{1,3},{2,0},{3,7},{4,8},{5,1},{6,2},{7,11},{8,12},{9,5},{10,... | collective-permute-start | bytes 589832 | tf_op jit(solution)/shard_map/ppermute | solution.py:306
  7.3 5.5 %collective-permute-start.2 = (bf16[352,256]{1,0:T(8,128)(2,1)S(1)}, bf16[352,256]{1,0:T(8,128)(2,1)S(1)}, u32[]{:S(2)}, u32[]{:S(2)}) collective-permute-start(bf16[352,256]{1,0:T(8,128)(2,1)S(1)} %slice.18), channel_id=1, source_target_pairs={{0,4},{1,3},{2,0},{3,7},{4,8},{5,1},{6,2},{7,11},{8,12},{9,5},{10,... | collective-permute-start | bytes 540680 | tf_op jit(solution)/shard_map/ppermute | solution.py:306
  10.4 5.5 %collective-permute-start.3 = (bf16[352,256]{1,0:T(8,128)(2,1)S(1)}, bf16[352,256]{1,0:T(8,128)(2,1)S(1)}, u32[]{:S(2)}, u32[]{:S(2)}) collective-permute-start(bf16[352,256]{1,0:T(8,128)(2,1)S(1)} %slice.24), channel_id=1, source_target_pairs={{0,4},{1,3},{2,0},{3,7},{4,8},{5,1},{6,2},{7,11},{8,12},{9,5},{10,... | collective-permute-start | bytes 540680 | tf_op jit(solution)/shard_map/ppermute | solution.py:306
  12.8 5.8 %collective-permute-start.4 = (bf16[320,256]{1,0:T(8,128)(2,1)S(1)}, bf16[320,256]{1,0:T(8,128)(2,1)S(1)}, u32[]{:S(2)}, u32[]{:S(2)}) collective-permute-start(bf16[320,256]{1,0:T(8,128)(2,1)S(1)} %slice.25), channel_id=1, source_target_pairs={{0,4},{1,3},{2,0},{3,7},{4,8},{5,1},{6,2},{7,11},{8,12},{9,5},{10,... | collective-permute-start | bytes 491528 | tf_op jit(solution)/shard_map/ppermute | solution.py:306
  16.0 5.4 %collective-permute-start.5 = (bf16[320,256]{1,0:T(8,128)(2,1)S(1)}, bf16[320,256]{1,0:T(8,128)(2,1)S(1)}, u32[]{:S(2)}, u32[]{:S(2)}) collective-permute-start(bf16[320,256]{1,0:T(8,128)(2,1)S(1)} %slice.26), channel_id=1, source_target_pairs={{0,4},{1,3},{2,0},{3,7},{4,8},{5,1},{6,2},{7,11},{8,12},{9,5},{10,... | collective-permute-start | bytes 491528 | tf_op jit(solution)/shard_map/ppermute | solution.py:306
  18.1 3.3 %collective-permute-start.8 = (bf16[352,256]{1,0:T(8,128)(2,1)S(1)}, bf16[352,256]{1,0:T(8,128)(2,1)S(1)}, u32[]{:S(2)}, u32[]{:S(2)}) collective-permute-start(bf16[352,256]{1,0:T(8,128)(2,1)S(1)} %collective-permute-done.2.refs_3_), channel_id=1, source_target_pairs={{0,1},{1,0},{2,3},{3,2},{4,5},{5,4},{6,7},{7,6},{8,9},{9,8},{10,11... | collective-permute-start | bytes 540680 | tf_op jit(solution)/shard_map/ppermute | solution.py:292
  18.1 5.4 %collective-permute-start.7 = (bf16[384,256]{1,0:T(8,128)(2,1)S(1)}, bf16[384,256]{1,0:T(8,128)(2,1)S(1)}, u32[]{:S(2)}, u32[]{:S(2)}) collective-permute-start(bf16[384,256]{1,0:T(8,128)(2,1)S(1)} %collective-permute-done.1.refs_2_), channel_id=1, source_target_pairs={{0,1},{1,0},{2,3},{3,2},{4,5},{5,4},{6,7},{7,6},{8,9},{9,8},{10,11... | collective-permute-start | bytes 589832 | tf_op jit(solution)/shard_map/ppermute | solution.py:292
  18.6 8.0 %collective-permute-start.10 = (bf16[352,256]{1,0:T(8,128)(2,1)S(1)}, bf16[352,256]{1,0:T(8,128)(2,1)S(1)}, u32[]{:S(2)}, u32[]{:S(2)}) collective-permute-start(bf16[352,256]{1,0:T(8,128)(2,1)S(1)} %collective-permute-done.3.refs_4_), channel_id=1, source_target_pairs={{0,1},{1,0},{2,3},{3,2},{4,5},{5,4},{6,7},{7,6},{8,9},{9,8},{10,11... | collective-permute-start | bytes 540680 | tf_op jit(solution)/shard_map/ppermute | solution.py:292
  18.6 5.2 %collective-permute-start.6 = (bf16[288,256]{1,0:T(8,128)(2,1)S(1)}, bf16[288,256]{1,0:T(8,128)(2,1)S(1)}, u32[]{:S(2)}, u32[]{:S(2)}) collective-permute-start(bf16[288,256]{1,0:T(8,128)(2,1)S(1)} %slice.27), channel_id=1, source_target_pairs={{0,4},{1,3},{2,0},{3,7},{4,8},{5,1},{6,2},{7,11},{8,12},{9,5},{10,... | collective-permute-start | bytes 442376 | tf_op jit(solution)/shard_map/ppermute | solution.py:306
  21.3 5.2 %collective-permute-start.11 = (bf16[320,256]{1,0:T(8,128)(2,1)S(1)}, bf16[320,256]{1,0:T(8,128)(2,1)S(1)}, u32[]{:S(2)}, u32[]{:S(2)}) collective-permute-start(bf16[320,256]{1,0:T(8,128)(2,1)S(1)} %collective-permute-done.4.refs_5_), channel_id=1, source_target_pairs={{0,1},{1,0},{2,3},{3,2},{4,5},{5,4},{6,7},{7,6},{8,9},{9,8},{10,11... | collective-permute-start | bytes 491528 | tf_op jit(solution)/shard_map/ppermute | solution.py:292
  21.4 5.2 %collective-permute-start.9 = (bf16[288,256]{1,0:T(8,128)(2,1)S(1)}, bf16[288,256]{1,0:T(8,128)(2,1)S(1)}, u32[]{:S(2)}, u32[]{:S(2)}) collective-permute-start(bf16[288,256]{1,0:T(8,128)(2,1)S(1)} %slice.28), channel_id=1, source_target_pairs={{0,4},{1,3},{2,0},{3,7},{4,8},{5,1},{6,2},{7,11},{8,12},{9,5},{10,... | collective-permute-start | bytes 442376 | tf_op jit(solution)/shard_map/ppermute | solution.py:306
  23.8 2.8 %collective-permute-start.12 = (bf16[320,256]{1,0:T(8,128)(2,1)S(1)}, bf16[320,256]{1,0:T(8,128)(2,1)S(1)}, u32[]{:S(2)}, u32[]{:S(2)}) collective-permute-start(bf16[320,256]{1,0:T(8,128)(2,1)S(1)} %collective-permute-done.5.refs_6_), channel_id=1, source_target_pairs={{0,1},{1,0},{2,3},{3,2},{4,5},{5,4},{6,7},{7,6},{8,9},{9,8},{10,11... | collective-permute-start | bytes 491528 | tf_op jit(solution)/shard_map/ppermute | solution.py:292
  23.8 2.8 %collective-permute-start.13 = (bf16[288,256]{1,0:T(8,128)(2,1)S(1)}, bf16[288,256]{1,0:T(8,128)(2,1)S(1)}, u32[]{:S(2)}, u32[]{:S(2)}) collective-permute-start(bf16[288,256]{1,0:T(8,128)(2,1)S(1)} %collective-permute-done.6.refs_7_), channel_id=1, source_target_pairs={{0,1},{1,0},{2,3},{3,2},{4,5},{5,4},{6,7},{7,6},{8,9},{9,8},{10,11... | collective-permute-start | bytes 442376 | tf_op jit(solution)/shard_map/ppermute | solution.py:292
  26.6 1.4 %collective-permute-start.14 = (bf16[288,256]{1,0:T(8,128)(2,1)S(1)}, bf16[288,256]{1,0:T(8,128)(2,1)S(1)}, u32[]{:S(2)}, u32[]{:S(2)}) collective-permute-start(bf16[288,256]{1,0:T(8,128)(2,1)S(1)} %collective-permute-done.9.refs_8_), channel_id=1, source_target_pairs={{0,1},{1,0},{2,3},{3,2},{4,5},{5,4},{6,7},{7,6},{8,9},{9,8},{10,11... | collective-permute-start | bytes 442376 | tf_op jit(solution)/shard_map/ppermute | solution.py:292

commit v7 on v6

--- a/solution.py
+++ b/solution.py
@@ -287,6 +287,7 @@
     around = [
         (r, by_place[(place_of(r, half) + 1 - 2 * (r % 2)) % (2 * half), r % 2]) for r in range(size)
     ]
+    turns = [[(r, t) for r, t in around if place_of(r, half) % 2 == n] for n in range(2)]
 
     def swap(value):
         return lax.ppermute(value, "row", [(r, r ^ 1) for r in range(size)])
@@ -300,16 +301,19 @@
 
     mine, theirs, weight, offset = lax.optimization_barrier((give, swap(give), weight, offset))
     take([mine, theirs])
-    flying = [keep, theirs[: body + (half - 1) * per_chip]]
+    flying = [[keep] * 2, [theirs[: body + (half - 1) * per_chip]] * 2]
     swapped = []
     for step in range(1, half + 1):
-        landed = [lax.ppermute(x, "row", around) for x in flying]
+        flown = [
+            [lax.ppermute(x, "row", turns[(n + step + 1) % 2]) for n, x in enumerate(pair)]
+            for pair in flying
+        ]
         if step >= 3:
-            landed[-1], swapped[step - 3] = lax.optimization_barrier((landed[-1], swapped[step - 3]))
-        flying = [x[: x.shape[0] - per_chip] for x in landed]
+            flown[-1], swapped[step - 3] = lax.optimization_barrier((flown[-1], swapped[step - 3]))
+        flying = [[x[: x.shape[0] - per_chip] for x in pair] for pair in flown]
         if step == half - 1:
             flying = flying[:1]
-        landed = lax.optimization_barrier(landed)
+        landed = lax.optimization_barrier([first + second for first, second in flown])
         take(landed)
         swapped.append([swap(x) for x in landed])
     for pair in swapped:

time: 32.5 us -> 55.5 us (1.71)
  starting transfers between devices: 15.5 us -> 38.7 us
  waiting for transfers between devices: 8.24 us -> 7.11 us
    ppermute x7 -> x14, starting transfers between devices: 14 us -> 35.4 us  [per_device(): lax.ppermute(x, 'row', turns[(n + step + 1) % 2])]
    ppermute x8, starting transfers between devices: 1.55 us -> 3.24 us  [swap(): return lax.ppermute(value, 'row', [(r, r ^ 1) for r in range(size)])]
    ppermute x7 -> x14, waiting for transfers between devices: 6.88 us -> 5.85 us  [per_device(): lax.ppermute(x, 'row', turns[(n + step + 1) % 2])]
  transfers between devices with their start and end apart: 15 -> 22, of which waited for: 7 -> 6; matrix products, arithmetic and copies ran while one was open for 0% -> 1% of each run, Pallas kernels for 1% -> 1%
where the time goes in v7:
time: 55.5 us; the launch traced here: 55.1 us
  starting transfers between devices  38.7 us (70%)
  Pallas kernels  8.49 us (15%)
  waiting for transfers between devices  7.11 us (13%)
    ppermute x14, starting transfers between devices, per_device(): lax.ppermute(x, 'row', turns[(n + step + 1) % 2])  35.4 us
    ppermute x14, waiting for transfers between devices, per_device(): lax.ppermute(x, 'row', turns[(n + step + 1) % 2])  5.85 us
    pallas_call x1, Pallas kernels, per_device(): pl.pallas_call(functools.partial(pair_kernel, places, gridded, rows_here,...  4.43 us
    pallas_call x1, Pallas kernels, per_device(): pl.pallas_call(functools.partial(project_kernel, rows_here), out_shape=[m...  3.65 us
    ppermute x8, starting transfers between devices, swap(): return lax.ppermute(value, 'row', [(r, r ^ 1) for r in range(size)])  3.24 us
    ppermute x8, waiting for transfers between devices, swap(): return lax.ppermute(value, 'row', [(r, r ^ 1) for r in range(size)])  1.27 us
  transfers between devices with their start and end apart: 22, of which 6 were waited for; matrix products, arithmetic and copies ran while one was open for 1% of the time, Pallas kernels for 1%

profile of v7, /device:TPU:0, one launch (start us, length us, event | category | flops | bytes accessed | tf_op | source)
XLA Modules:
  0.0 55.1 jit_solution(8043035817998055266)
XLA Ops:
  0.0 3.7 %shard_map.91 = (bf16[384,256]{1,0:T(8,128)(2,1)S(1)}, bf16[384,256]{1,0:T(8,128)(2,1)S(1)}) custom-call(bf16[8,256,256]{2,1,0:T(8,128)(2,1)} %x_hbm.1, f32[1,256]{1,0:T(1,128)} %bitcast.10, f32[1,256]{1,0:T(1,128)} %bitcast.11, bf16[32,256]{1,0:T(8,128)(2,1)} %bitcast.8, f32[1,32]{1,0:T(1,128)} %bitcast.12, bf16[32,256]{1,0:T(8,128)(2,1)} %bitcast.9, ...), custom_call_target="tpu_custom_call" | custom-call | flops 536870912 | bytes 1048576 | tf_op jit(solution)/shard_map/pallas_call | solution.py:236
  3.7 0.5 collective-permute-start
  4.2 1.4 %collective-permute-start.2 = (bf16[384,256]{1,0:T(8,128)(2,1)S(1)}, bf16[384,256]{1,0:T(8,128)(2,1)S(1)}, u32[]{:S(2)}, u32[]{:S(2)}) collective-permute-start(bf16[384,256]{1,0:T(8,128)(2,1)S(1)} %get-tuple-element.32), channel_id=1, source_target_pairs={{2,0},{3,7},{4,8},{5,1},{10,6},{11,15},{12,14},{13,9},{18,16},{19,... | collective-permute-start | bytes 589832 | tf_op jit(solution)/shard_map/ppermute | solution.py:308
  5.6 6.6 %collective-permute-start.1 = (bf16[384,256]{1,0:T(8,128)(2,1)S(1)}, bf16[384,256]{1,0:T(8,128)(2,1)S(1)}, u32[]{:S(2)}, u32[]{:S(2)}) collective-permute-start(bf16[384,256]{1,0:T(8,128)(2,1)S(1)} %get-tuple-element.32), channel_id=1, source_target_pairs={{0,4},{1,3},{6,2},{7,11},{8,12},{9,5},{14,10},{15,13},{16,20},{17,... | collective-permute-start | bytes 589832 | tf_op jit(solution)/shard_map/ppermute | solution.py:308
  12.7 1.3 %collective-permute-start.4 = (bf16[352,256]{1,0:T(8,128)(2,1)S(1)}, bf16[352,256]{1,0:T(8,128)(2,1)S(1)}, u32[]{:S(2)}, u32[]{:S(2)}) collective-permute-start(bf16[352,256]{1,0:T(8,128)(2,1)S(1)} %slice.33), channel_id=1, source_target_pairs={{2,0},{3,7},{4,8},{5,1},{10,6},{11,15},{12,14},{13,9},{18,16},{19,... | collective-permute-start | bytes 540680 | tf_op jit(solution)/shard_map/ppermute | solution.py:308
  14.0 5.6 %collective-permute-start.3 = (bf16[352,256]{1,0:T(8,128)(2,1)S(1)}, bf16[352,256]{1,0:T(8,128)(2,1)S(1)}, u32[]{:S(2)}, u32[]{:S(2)}) collective-permute-start(bf16[352,256]{1,0:T(8,128)(2,1)S(1)} %slice.33), channel_id=1, source_target_pairs={{0,4},{1,3},{6,2},{7,11},{8,12},{9,5},{14,10},{15,13},{16,20},{17,... | collective-permute-start | bytes 540680 | tf_op jit(solution)/shard_map/ppermute | solution.py:308
  19.6 1.3 %collective-permute-start.6 = (bf16[352,256]{1,0:T(8,128)(2,1)S(1)}, bf16[352,256]{1,0:T(8,128)(2,1)S(1)}, u32[]{:S(2)}, u32[]{:S(2)}) collective-permute-start(bf16[352,256]{1,0:T(8,128)(2,1)S(1)} %slice.45), channel_id=1, source_target_pairs={{0,4},{1,3},{6,2},{7,11},{8,12},{9,5},{14,10},{15,13},{16,20},{17,... | collective-permute-start | bytes 540680 | tf_op jit(solution)/shard_map/ppermute | solution.py:308
  21.0 1.3 %collective-permute-start.5 = (bf16[352,256]{1,0:T(8,128)(2,1)S(1)}, bf16[352,256]{1,0:T(8,128)(2,1)S(1)}, u32[]{:S(2)}, u32[]{:S(2)}) collective-permute-start(bf16[352,256]{1,0:T(8,128)(2,1)S(1)} %slice.44), channel_id=1, source_target_pairs={{2,0},{3,7},{4,8},{5,1},{10,6},{11,15},{12,14},{13,9},{18,16},{19,... | collective-permute-start | bytes 540680 | tf_op jit(solution)/shard_map/ppermute | solution.py:308
  22.3 3.4 %collective-permute-start.8 = (bf16[320,256]{1,0:T(8,128)(2,1)S(1)}, bf16[320,256]{1,0:T(8,128)(2,1)S(1)}, u32[]{:S(2)}, u32[]{:S(2)}) collective-permute-start(bf16[320,256]{1,0:T(8,128)(2,1)S(1)} %slice.47), channel_id=1, source_target_pairs={{0,4},{1,3},{6,2},{7,11},{8,12},{9,5},{14,10},{15,13},{16,20},{17,... | collective-permute-start | bytes 491528 | tf_op jit(solution)/shard_map/ppermute | solution.py:308
  25.8 1.3 %collective-permute-start.7 = (bf16[320,256]{1,0:T(8,128)(2,1)S(1)}, bf16[320,256]{1,0:T(8,128)(2,1)S(1)}, u32[]{:S(2)}, u32[]{:S(2)}) collective-permute-start(bf16[320,256]{1,0:T(8,128)(2,1)S(1)} %slice.46), channel_id=1, source_target_pairs={{2,0},{3,7},{4,8},{5,1},{10,6},{11,15},{12,14},{13,9},{18,16},{19,... | collective-permute-start | bytes 491528 | tf_op jit(solution)/shard_map/ppermute | solution.py:308
  27.3 0.5 collective-permute-start.14
  27.8 0.6 %collective-permute-done.5 = bf16[352,256]{1,0:T(8,128)(2,1)S(1)} collective-permute-done((bf16[352,256]{1,0:T(8,128)(2,1)S(1)}, bf16[352,256]{1,0:T(8,128)(2,1)S(1)}, u32[]{:S(2)}, u32[]{:S(2)}) %collective-permute-start.5) | collective-permute-done | bytes 180256 | tf_op jit(solution)/shard_map/ppermute | solution.py:308
  28.4 1.3 %collective-permute-start.10 = (bf16[320,256]{1,0:T(8,128)(2,1)S(1)}, bf16[320,256]{1,0:T(8,128)(2,1)S(1)}, u32[]{:S(2)}, u32[]{:S(2)}) collective-permute-start(bf16[320,256]{1,0:T(8,128)(2,1)S(1)} %slice.49), channel_id=1, source_target_pairs={{2,0},{3,7},{4,8},{5,1},{10,6},{11,15},{12,14},{13,9},{18,16},{19,... | collective-permute-start | bytes 491528 | tf_op jit(solution)/shard_map/ppermute | solution.py:308
  29.7 3.6 %collective-permute-start.9 = (bf16[320,256]{1,0:T(8,128)(2,1)S(1)}, bf16[320,256]{1,0:T(8,128)(2,1)S(1)}, u32[]{:S(2)}, u32[]{:S(2)}) collective-permute-start(bf16[320,256]{1,0:T(8,128)(2,1)S(1)} %slice.48), channel_id=1, source_target_pairs={{0,4},{1,3},{6,2},{7,11},{8,12},{9,5},{14,10},{15,13},{16,20},{17,... | collective-permute-start | bytes 491528 | tf_op jit(solution)/shard_map/ppermute | solution.py:308
  33.3 1.3 %collective-permute-start.12 = (bf16[288,256]{1,0:T(8,128)(2,1)S(1)}, bf16[288,256]{1,0:T(8,128)(2,1)S(1)}, u32[]{:S(2)}, u32[]{:S(2)}) collective-permute-start(bf16[288,256]{1,0:T(8,128)(2,1)S(1)} %slice.51), channel_id=1, source_target_pairs={{2,0},{3,7},{4,8},{5,1},{10,6},{11,15},{12,14},{13,9},{18,16},{19,... | collective-permute-start | bytes 442376 | tf_op jit(solution)/shard_map/ppermute | solution.py:308
  34.8 0.8 %collective-permute-done.10 = bf16[320,256]{1,0:T(8,128)(2,1)S(1)} collective-permute-done((bf16[320,256]{1,0:T(8,128)(2,1)S(1)}, bf16[320,256]{1,0:T(8,128)(2,1)S(1)}, u32[]{:S(2)}, u32[]{:S(2)}) %collective-permute-start.10) | collective-permute-done | bytes 163872 | tf_op jit(solution)/shard_map/ppermute | solution.py:308
  36.1 4.4 %collective-permute-start.11 = (bf16[288,256]{1,0:T(8,128)(2,1)S(1)}, bf16[288,256]{1,0:T(8,128)(2,1)S(1)}, u32[]{:S(2)}, u32[]{:S(2)}) collective-permute-start(bf16[288,256]{1,0:T(8,128)(2,1)S(1)} %slice.50), channel_id=1, source_target_pairs={{0,4},{1,3},{6,2},{7,11},{8,12},{9,5},{14,10},{15,13},{16,20},{17,... | collective-permute-start | bytes 442376 | tf_op jit(solution)/shard_map/ppermute | solution.py:308
  40.8 1.3 %collective-permute-start.16 = (bf16[288,256]{1,0:T(8,128)(2,1)S(1)}, bf16[288,256]{1,0:T(8,128)(2,1)S(1)}, u32[]{:S(2)}, u32[]{:S(2)}) collective-permute-start(bf16[288,256]{1,0:T(8,128)(2,1)S(1)} %slice.53), channel_id=1, source_target_pairs={{0,4},{1,3},{6,2},{7,11},{8,12},{9,5},{14,10},{15,13},{16,20},{17,... | collective-permute-start | bytes 442376 | tf_op jit(solution)/shard_map/ppermute | solution.py:308
  42.1 1.3 %collective-permute-start.15 = (bf16[288,256]{1,0:T(8,128)(2,1)S(1)}, bf16[288,256]{1,0:T(8,128)(2,1)S(1)}, u32[]{:S(2)}, u32[]{:S(2)}) collective-permute-start(bf16[288,256]{1,0:T(8,128)(2,1)S(1)} %slice.52), channel_id=1, source_target_pairs={{2,0},{3,7},{4,8},{5,1},{10,6},{11,15},{12,14},{13,9},{18,16},{19,... | collective-permute-start | bytes 442376 | tf_op jit(solution)/shard_map/ppermute | solution.py:308
  43.5 1.0 %collective-permute-start.19 = (bf16[320,256]{1,0:T(8,128)(2,1)S(1)}, bf16[320,256]{1,0:T(8,128)(2,1)S(1)}, u32[]{:S(2)}, u32[]{:S(2)}) collective-permute-start(bf16[320,256]{1,0:T(8,128)(2,1)S(1)} %add.25.refs_6_), channel_id=1, source_target_pairs={{0,1},{1,0},{2,3},{3,2},{4,5},{5,4},{6,7},{7,6},{8,9},{9,8},{10,11... | collective-permute-start | bytes 491528 | tf_op jit(solution)/shard_map/ppermute | solution.py:293
  44.7 0.4 collective-permute-start.20
  45.2 4.0 %collective-permute-done.15 = bf16[288,256]{1,0:T(8,128)(2,1)S(1)} collective-permute-done((bf16[288,256]{1,0:T(8,128)(2,1)S(1)}, bf16[288,256]{1,0:T(8,128)(2,1)S(1)}, u32[]{:S(2)}, u32[]{:S(2)}) %collective-permute-start.15) | collective-permute-done | bytes 147488 | tf_op jit(solution)/shard_map/ppermute | solution.py:308
  49.4 1.2 %collective-permute-done.21.refs_15_ = bf16[288,256]{1,0:T(8,128)(2,1)S(1)} collective-permute-done((bf16[288,256]{1,0:T(8,128)(2,1)S(1)}, bf16[288,256]{1,0:T(8,128)(2,1)S(1)}, u32[]{:S(2)}, u32[]{:S(2)}) %collective-permute-start.21) | collective-permute-done | bytes 147488 | tf_op jit(solution)/shard_map/ppermute | solution.py:293
  50.6 4.4 %shard_map.93 = bf16[16,256,128]{2,1,0:T(8,128)(2,1)} custom-call(bf16[384,256]{1,0:T(8,128)(2,1)S(1)} %get-tuple-element.30.refs_0_, bf16[384,256]{1,0:T(8,128)(2,1)S(1)} %collective-permute-done.refs_1_, bf16[384,256]{1,0:T(8,128)(2,1)S(1)} %add.21.refs_2_, bf16[352,256]{1,0:T(8,128)(2,1)S(1)} %add.22.refs_3_, bf16[352,256]{1,0:T(8,128)(2,1)S(1)} %add.23.refs_4_, ...), custom_call_target="tpu_custom_call" | custom-call | tf_op jit(solution)/shard_map/pallas_call | solution.py:340
  (45 shorter events, 2.1 us)
Async XLA Ops:
  0.0 12.2 %copy-start = (bf16[1024,128]{1,0:T(8,128)(2,1)S(1)}, bf16[1024,128]{1,0:T(8,128)(2,1)}, u32[]{:S(2)}) copy-start(bf16[1024,128]{1,0:T(8,128)(2,1)} %final_ref.1) | copy-start | bytes 786436
  3.7 9.0 %collective-permute-start = (bf16[384,256]{1,0:T(8,128)(2,1)S(1)}, bf16[384,256]{1,0:T(8,128)(2,1)S(1)}, u32[]{:S(2)}, u32[]{:S(2)}) collective-permute-start(bf16[384,256]{1,0:T(8,128)(2,1)S(1)} %get-tuple-element.30.refs_0_), channel_id=1, source_target_pairs={{0,1},{1,0},{2,3},{3,2},{4,5},{5,4},{6,7},{7,6},{8,9},{9,8},{10,11... | collective-permute-start | bytes 589832 | tf_op jit(solution)/shard_map/ppermute | solution.py:293
  4.2 8.0 %copy-start.1 = (f32[128]{0:T(128)S(1)}, f32[128]{0:T(128)}, u32[]{:S(2)}) copy-start(f32[128]{0:T(128)} %param.17) | copy-start | bytes 1540
  4.2 15.4 %collective-permute-start.2 = (bf16[384,256]{1,0:T(8,128)(2,1)S(1)}, bf16[384,256]{1,0:T(8,128)(2,1)S(1)}, u32[]{:S(2)}, u32[]{:S(2)}) collective-permute-start(bf16[384,256]{1,0:T(8,128)(2,1)S(1)} %get-tuple-element.32), channel_id=1, source_target_pairs={{2,0},{3,7},{4,8},{5,1},{10,6},{11,15},{12,14},{13,9},{18,16},{19,... | collective-permute-start | bytes 589832 | tf_op jit(solution)/shard_map/ppermute | solution.py:308
  5.6 15.3 %collective-permute-start.1 = (bf16[384,256]{1,0:T(8,128)(2,1)S(1)}, bf16[384,256]{1,0:T(8,128)(2,1)S(1)}, u32[]{:S(2)}, u32[]{:S(2)}) collective-permute-start(bf16[384,256]{1,0:T(8,128)(2,1)S(1)} %get-tuple-element.32), channel_id=1, source_target_pairs={{0,4},{1,3},{6,2},{7,11},{8,12},{9,5},{14,10},{15,13},{16,20},{17,... | collective-permute-start | bytes 589832 | tf_op jit(solution)/shard_map/ppermute | solution.py:308
  12.7 9.6 %collective-permute-start.4 = (bf16[352,256]{1,0:T(8,128)(2,1)S(1)}, bf16[352,256]{1,0:T(8,128)(2,1)S(1)}, u32[]{:S(2)}, u32[]{:S(2)}) collective-permute-start(bf16[352,256]{1,0:T(8,128)(2,1)S(1)} %slice.33), channel_id=1, source_target_pairs={{2,0},{3,7},{4,8},{5,1},{10,6},{11,15},{12,14},{13,9},{18,16},{19,... | collective-permute-start | bytes 540680 | tf_op jit(solution)/shard_map/ppermute | solution.py:308
  14.0 11.8 %collective-permute-start.3 = (bf16[352,256]{1,0:T(8,128)(2,1)S(1)}, bf16[352,256]{1,0:T(8,128)(2,1)S(1)}, u32[]{:S(2)}, u32[]{:S(2)}) collective-permute-start(bf16[352,256]{1,0:T(8,128)(2,1)S(1)} %slice.33), channel_id=1, source_target_pairs={{0,4},{1,3},{6,2},{7,11},{8,12},{9,5},{14,10},{15,13},{16,20},{17,... | collective-permute-start | bytes 540680 | tf_op jit(solution)/shard_map/ppermute | solution.py:308
  19.6 7.6 %collective-permute-start.6 = (bf16[352,256]{1,0:T(8,128)(2,1)S(1)}, bf16[352,256]{1,0:T(8,128)(2,1)S(1)}, u32[]{:S(2)}, u32[]{:S(2)}) collective-permute-start(bf16[352,256]{1,0:T(8,128)(2,1)S(1)} %slice.45), channel_id=1, source_target_pairs={{0,4},{1,3},{6,2},{7,11},{8,12},{9,5},{14,10},{15,13},{16,20},{17,... | collective-permute-start | bytes 540680 | tf_op jit(solution)/shard_map/ppermute | solution.py:308
  21.0 7.4 %collective-permute-start.5 = (bf16[352,256]{1,0:T(8,128)(2,1)S(1)}, bf16[352,256]{1,0:T(8,128)(2,1)S(1)}, u32[]{:S(2)}, u32[]{:S(2)}) collective-permute-start(bf16[352,256]{1,0:T(8,128)(2,1)S(1)} %slice.44), channel_id=1, source_target_pairs={{2,0},{3,7},{4,8},{5,1},{10,6},{11,15},{12,14},{13,9},{18,16},{19,... | collective-permute-start | bytes 540680 | tf_op jit(solution)/shard_map/ppermute | solution.py:308
  22.3 7.4 %collective-permute-start.8 = (bf16[320,256]{1,0:T(8,128)(2,1)S(1)}, bf16[320,256]{1,0:T(8,128)(2,1)S(1)}, u32[]{:S(2)}, u32[]{:S(2)}) collective-permute-start(bf16[320,256]{1,0:T(8,128)(2,1)S(1)} %slice.47), channel_id=1, source_target_pairs={{0,4},{1,3},{6,2},{7,11},{8,12},{9,5},{14,10},{15,13},{16,20},{17,... | collective-permute-start | bytes 491528 | tf_op jit(solution)/shard_map/ppermute | solution.py:308
  25.8 7.6 %collective-permute-start.7 = (bf16[320,256]{1,0:T(8,128)(2,1)S(1)}, bf16[320,256]{1,0:T(8,128)(2,1)S(1)}, u32[]{:S(2)}, u32[]{:S(2)}) collective-permute-start(bf16[320,256]{1,0:T(8,128)(2,1)S(1)} %slice.46), channel_id=1, source_target_pairs={{2,0},{3,7},{4,8},{5,1},{10,6},{11,15},{12,14},{13,9},{18,16},{19,... | collective-permute-start | bytes 491528 | tf_op jit(solution)/shard_map/ppermute | solution.py:308
  27.2 13.6 %collective-permute-start.13 = (bf16[384,256]{1,0:T(8,128)(2,1)S(1)}, bf16[384,256]{1,0:T(8,128)(2,1)S(1)}, u32[]{:S(2)}, u32[]{:S(2)}) collective-permute-start(bf16[384,256]{1,0:T(8,128)(2,1)S(1)} %add.21.refs_2_), channel_id=1, source_target_pairs={{0,1},{1,0},{2,3},{3,2},{4,5},{5,4},{6,7},{7,6},{8,9},{9,8},{10,11... | collective-permute-start | bytes 589832 | tf_op jit(solution)/shard_map/ppermute | solution.py:293
  27.3 13.2 %collective-permute-start.14 = (bf16[352,256]{1,0:T(8,128)(2,1)S(1)}, bf16[352,256]{1,0:T(8,128)(2,1)S(1)}, u32[]{:S(2)}, u32[]{:S(2)}) collective-permute-start(bf16[352,256]{1,0:T(8,128)(2,1)S(1)} %add.22.refs_3_), channel_id=1, source_target_pairs={{0,1},{1,0},{2,3},{3,2},{4,5},{5,4},{6,7},{7,6},{8,9},{9,8},{10,11... | collective-permute-start | bytes 540680 | tf_op jit(solution)/shard_map/ppermute | solution.py:293
  28.4 7.2 %collective-permute-start.10 = (bf16[320,256]{1,0:T(8,128)(2,1)S(1)}, bf16[320,256]{1,0:T(8,128)(2,1)S(1)}, u32[]{:S(2)}, u32[]{:S(2)}) collective-permute-start(bf16[320,256]{1,0:T(8,128)(2,1)S(1)} %slice.49), channel_id=1, source_target_pairs={{2,0},{3,7},{4,8},{5,1},{10,6},{11,15},{12,14},{13,9},{18,16},{19,... | collective-permute-start | bytes 491528 | tf_op jit(solution)/shard_map/ppermute | solution.py:308
  29.7 6.5 %collective-permute-start.9 = (bf16[320,256]{1,0:T(8,128)(2,1)S(1)}, bf16[320,256]{1,0:T(8,128)(2,1)S(1)}, u32[]{:S(2)}, u32[]{:S(2)}) collective-permute-start(bf16[320,256]{1,0:T(8,128)(2,1)S(1)} %slice.48), channel_id=1, source_target_pairs={{0,4},{1,3},{6,2},{7,11},{8,12},{9,5},{14,10},{15,13},{16,20},{17,... | collective-permute-start | bytes 491528 | tf_op jit(solution)/shard_map/ppermute | solution.py:308
  33.3 8.8 %collective-permute-start.12 = (bf16[288,256]{1,0:T(8,128)(2,1)S(1)}, bf16[288,256]{1,0:T(8,128)(2,1)S(1)}, u32[]{:S(2)}, u32[]{:S(2)}) collective-permute-start(bf16[288,256]{1,0:T(8,128)(2,1)S(1)} %slice.51), channel_id=1, source_target_pairs={{2,0},{3,7},{4,8},{5,1},{10,6},{11,15},{12,14},{13,9},{18,16},{19,... | collective-permute-start | bytes 442376 | tf_op jit(solution)/shard_map/ppermute | solution.py:308
  35.6 13.6 %collective-permute-start.17 = (bf16[352,256]{1,0:T(8,128)(2,1)S(1)}, bf16[352,256]{1,0:T(8,128)(2,1)S(1)}, u32[]{:S(2)}, u32[]{:S(2)}) collective-permute-start(bf16[352,256]{1,0:T(8,128)(2,1)S(1)} %add.23.refs_4_), channel_id=1, source_target_pairs={{0,1},{1,0},{2,3},{3,2},{4,5},{5,4},{6,7},{7,6},{8,9},{9,8},{10,11... | collective-permute-start | bytes 540680 | tf_op jit(solution)/shard_map/ppermute | solution.py:293
  36.1 7.3 %collective-permute-start.11 = (bf16[288,256]{1,0:T(8,128)(2,1)S(1)}, bf16[288,256]{1,0:T(8,128)(2,1)S(1)}, u32[]{:S(2)}, u32[]{:S(2)}) collective-permute-start(bf16[288,256]{1,0:T(8,128)(2,1)S(1)} %slice.50), channel_id=1, source_target_pairs={{0,4},{1,3},{6,2},{7,11},{8,12},{9,5},{14,10},{15,13},{16,20},{17,... | collective-permute-start | bytes 442376 | tf_op jit(solution)/shard_map/ppermute | solution.py:308
  40.5 8.6 %collective-permute-start.18 = (bf16[320,256]{1,0:T(8,128)(2,1)S(1)}, bf16[320,256]{1,0:T(8,128)(2,1)S(1)}, u32[]{:S(2)}, u32[]{:S(2)}) collective-permute-start(bf16[320,256]{1,0:T(8,128)(2,1)S(1)} %add.24.refs_5_), channel_id=1, source_target_pairs={{0,1},{1,0},{2,3},{3,2},{4,5},{5,4},{6,7},{7,6},{8,9},{9,8},{10,11... | collective-permute-start | bytes 491528 | tf_op jit(solution)/shard_map/ppermute | solution.py:293
  40.8 4.0 %collective-permute-start.16 = (bf16[288,256]{1,0:T(8,128)(2,1)S(1)}, bf16[288,256]{1,0:T(8,128)(2,1)S(1)}, u32[]{:S(2)}, u32[]{:S(2)}) collective-permute-start(bf16[288,256]{1,0:T(8,128)(2,1)S(1)} %slice.53), channel_id=1, source_target_pairs={{0,4},{1,3},{6,2},{7,11},{8,12},{9,5},{14,10},{15,13},{16,20},{17,... | collective-permute-start | bytes 442376 | tf_op jit(solution)/shard_map/ppermute | solution.py:308
  42.1 7.0 %collective-permute-start.15 = (bf16[288,256]{1,0:T(8,128)(2,1)S(1)}, bf16[288,256]{1,0:T(8,128)(2,1)S(1)}, u32[]{:S(2)}, u32[]{:S(2)}) collective-permute-start(bf16[288,256]{1,0:T(8,128)(2,1)S(1)} %slice.52), channel_id=1, source_target_pairs={{2,0},{3,7},{4,8},{5,1},{10,6},{11,15},{12,14},{13,9},{18,16},{19,... | collective-permute-start | bytes 442376 | tf_op jit(solution)/shard_map/ppermute | solution.py:308
  43.5 5.9 %collective-permute-start.19 = (bf16[320,256]{1,0:T(8,128)(2,1)S(1)}, bf16[320,256]{1,0:T(8,128)(2,1)S(1)}, u32[]{:S(2)}, u32[]{:S(2)}) collective-permute-start(bf16[320,256]{1,0:T(8,128)(2,1)S(1)} %add.25.refs_6_), channel_id=1, source_target_pairs={{0,1},{1,0},{2,3},{3,2},{4,5},{5,4},{6,7},{7,6},{8,9},{9,8},{10,11... | collective-permute-start | bytes 491528 | tf_op jit(solution)/shard_map/ppermute | solution.py:293
  44.7 4.7 %collective-permute-start.20 = (bf16[288,256]{1,0:T(8,128)(2,1)S(1)}, bf16[288,256]{1,0:T(8,128)(2,1)S(1)}, u32[]{:S(2)}, u32[]{:S(2)}) collective-permute-start(bf16[288,256]{1,0:T(8,128)(2,1)S(1)} %add.26.refs_7_), channel_id=1, source_target_pairs={{0,1},{1,0},{2,3},{3,2},{4,5},{5,4},{6,7},{7,6},{8,9},{9,8},{10,11... | collective-permute-start | bytes 442376 | tf_op jit(solution)/shard_map/ppermute | solution.py:293
  49.2 1.4 %collective-permute-start.21 = (bf16[288,256]{1,0:T(8,128)(2,1)S(1)}, bf16[288,256]{1,0:T(8,128)(2,1)S(1)}, u32[]{:S(2)}, u32[]{:S(2)}) collective-permute-start(bf16[288,256]{1,0:T(8,128)(2,1)S(1)} %add.27.refs_8_), channel_id=1, source_target_pairs={{0,1},{1,0},{2,3},{3,2},{4,5},{5,4},{6,7},{7,6},{8,9},{9,8},{10,11... | collective-permute-start | bytes 442376 | tf_op jit(solution)/shard_map/ppermute | solution.py:293

commit v8 on v6

--- a/solution.py
+++ b/solution.py
@@ -284,9 +284,13 @@
     )(final_projector_coefficients, final_projector_offset.reshape(1, channels))
 
     by_place = {(place_of(r, half), r % 2): r for r in range(size)}
-    around = [
-        (r, by_place[(place_of(r, half) + 1 - 2 * (r % 2)) % (2 * half), r % 2]) for r in range(size)
-    ]
+
+    def hop(value, way, cross):
+        pairs = []
+        for r in range(size):
+            place = place_of(r, half) + way * (1 - 2 * (r % 2))
+            pairs.append((r, by_place[place % (2 * half), (r + cross) % 2]))
+        return lax.ppermute(value, "row", pairs)
 
     def swap(value):
         return lax.ppermute(value, "row", [(r, r ^ 1) for r in range(size)])
@@ -298,20 +302,22 @@
             places.append((len(messages), 0, value.shape[0] - per_chip))
             messages.append(value)
 
-    mine, theirs, weight, offset = lax.optimization_barrier((give, swap(give), weight, offset))
-    take([mine, theirs])
-    flying = [keep, theirs[: body + (half - 1) * per_chip]]
-    swapped = []
+    landed = [hop(keep, 1, 0), hop(give[: body + (half - 1) * per_chip], -1, 1)]
+    take([give])
+    swapped = [[swap(give)]]
     for step in range(1, half + 1):
-        landed = [lax.ppermute(x, "row", around) for x in flying]
-        if step >= 3:
-            landed[-1], swapped[step - 3] = lax.optimization_barrier((landed[-1], swapped[step - 3]))
+        if step == 1:
+            landed[0], weight, offset = lax.optimization_barrier((landed[0], weight, offset))
+        if step >= 2:
+            landed[-1], swapped[step - 2] = lax.optimization_barrier((landed[-1], swapped[step - 2]))
         flying = [x[: x.shape[0] - per_chip] for x in landed]
-        if step == half - 1:
-            flying = flying[:1]
         landed = lax.optimization_barrier(landed)
         take(landed)
         swapped.append([swap(x) for x in landed])
+        if step == half - 1:
+            flying = flying[:1]
+        if step < half:
+            landed = [hop(x, 1, 0) for x in flying]
     for pair in swapped:
         take(pair)
 

time: 32.5 us -> 34.3 us (1.055)
  waiting for transfers between devices: 8.24 us -> 12.3 us
  starting transfers between devices: 15.5 us -> 13.3 us
    ppermute x7, waiting for transfers between devices: 6.88 us -> 10.9 us  [hop(): return lax.ppermute(value, 'row', pairs)]
    ppermute x7, starting transfers between devices: 14 us -> 12 us  [hop(): return lax.ppermute(value, 'row', pairs)]
  transfers between devices with their start and end apart: 15 -> 15, of which waited for: 7 -> 6; matrix products, arithmetic and copies ran while one was open for 0% -> 0% of each run, Pallas kernels for 1% -> 1%
where the time goes in v8:
time: 34.3 us; the launch traced here: 34.2 us
  starting transfers between devices  13.3 us (39%)
  waiting for transfers between devices  12.3 us (36%)
  Pallas kernels  8.42 us (25%)
    ppermute x7, starting transfers between devices, hop(): return lax.ppermute(value, 'row', pairs)  12 us
    ppermute x7, waiting for transfers between devices, hop(): return lax.ppermute(value, 'row', pairs)  10.9 us
    pallas_call x1, Pallas kernels, per_device(): pl.pallas_call(functools.partial(pair_kernel, places, gridded, rows_here,...  4.43 us
    pallas_call x1, Pallas kernels, per_device(): pl.pallas_call(functools.partial(project_kernel, rows_here), out_shape=[m...  3.59 us
    ppermute x8, waiting for transfers between devices, swap(): return lax.ppermute(value, 'row', [(r, r ^ 1) for r in range(size)])  1.38 us
    ppermute x8, starting transfers between devices, swap(): return lax.ppermute(value, 'row', [(r, r ^ 1) for r in range(size)])  1.35 us
  transfers between devices with their start and end apart: 15, of which 6 were waited for; matrix products, arithmetic and copies ran while one was open for 0% of the time, Pallas kernels for 1%

profile of v8, /device:TPU:0, one launch (start us, length us, event | category | flops | bytes accessed | tf_op | source)
XLA Modules:
  0.0 34.2 jit_solution(7500298331543533253)
XLA Ops:
  0.0 3.6 %shard_map.91 = (bf16[384,256]{1,0:T(8,128)(2,1)S(1)}, bf16[384,256]{1,0:T(8,128)(2,1)S(1)}) custom-call(bf16[8,256,256]{2,1,0:T(8,128)(2,1)} %x_hbm.1, f32[1,256]{1,0:T(1,128)} %bitcast.10, f32[1,256]{1,0:T(1,128)} %bitcast.11, bf16[32,256]{1,0:T(8,128)(2,1)} %bitcast.8, f32[1,32]{1,0:T(1,128)} %bitcast.12, bf16[32,256]{1,0:T(8,128)(2,1)} %bitcast.9, ...), custom_call_target="tpu_custom_call" | custom-call | flops 536870912 | bytes 1048576 | tf_op jit(solution)/shard_map/pallas_call | solution.py:236
  3.6 0.0 copy-start
  3.6 3.1 %collective-permute-start = (bf16[384,256]{1,0:T(8,128)(2,1)S(1)}, bf16[384,256]{1,0:T(8,128)(2,1)S(1)}, u32[]{:S(2)}, u32[]{:S(2)}) collective-permute-start(bf16[384,256]{1,0:T(8,128)(2,1)S(1)} %get-tuple-element.27), channel_id=1, source_target_pairs={{0,4},{1,3},{2,0},{3,7},{4,8},{5,1},{6,2},{7,11},{8,12},{9,5},{10,... | collective-permute-start | bytes 589832 | tf_op jit(solution)/shard_map/ppermute | solution.py:293
  6.7 0.0 copy-start.1
  6.7 0.7 %collective-permute-start.1 = (bf16[352,256]{1,0:T(8,128)(2,1)S(1)}, bf16[352,256]{1,0:T(8,128)(2,1)S(1)}, u32[]{:S(2)}, u32[]{:S(2)}) collective-permute-start(bf16[352,256]{1,0:T(8,128)(2,1)S(1)} %slice.18), channel_id=1, source_target_pairs={{0,3},{1,4},{2,7},{3,0},{4,1},{5,8},{6,11},{7,2},{8,5},{9,12},{10,... | collective-permute-start | bytes 540680 | tf_op jit(solution)/shard_map/ppermute | solution.py:293
  7.5 0.4 %shard_map.92 = (bf16[128,1024]{1,0:T(8,128)(2,1)S(1)}, f32[1,128]{1,0:T(1,128)S(1)}) custom-call(bf16[1024,128]{1,0:T(8,128)(2,1)S(1)} %copy-done, f32[1,128]{1,0:T(1,128)S(1)} %bitcast.7), custom_call_target="tpu_custom_call" | custom-call | flops 268435456 | bytes 1048576 | tf_op jit(solution)/shard_map/pallas_call | solution.py:273
  7.9 3.0 %collective-permute-done.refs_1_ = bf16[384,256]{1,0:T(8,128)(2,1)S(1)} collective-permute-done((bf16[384,256]{1,0:T(8,128)(2,1)S(1)}, bf16[384,256]{1,0:T(8,128)(2,1)S(1)}, u32[]{:S(2)}, u32[]{:S(2)}) %collective-permute-start) | collective-permute-done | bytes 196640 | tf_op jit(solution)/shard_map/ppermute | solution.py:293
  10.9 2.5 %collective-permute-start.2 = (bf16[352,256]{1,0:T(8,128)(2,1)S(1)}, bf16[352,256]{1,0:T(8,128)(2,1)S(1)}, u32[]{:S(2)}, u32[]{:S(2)}) collective-permute-start(bf16[352,256]{1,0:T(8,128)(2,1)S(1)} %slice.19), channel_id=1, source_target_pairs={{0,4},{1,3},{2,0},{3,7},{4,8},{5,1},{6,2},{7,11},{8,12},{9,5},{10,... | collective-permute-start | bytes 540680 | tf_op jit(solution)/shard_map/ppermute | solution.py:293
  13.4 0.0 collective-permute-start.4
  13.5 1.6 %collective-permute-start.3 = (bf16[320,256]{1,0:T(8,128)(2,1)S(1)}, bf16[320,256]{1,0:T(8,128)(2,1)S(1)}, u32[]{:S(2)}, u32[]{:S(2)}) collective-permute-start(bf16[320,256]{1,0:T(8,128)(2,1)S(1)} %slice.24), channel_id=1, source_target_pairs={{0,4},{1,3},{2,0},{3,7},{4,8},{5,1},{6,2},{7,11},{8,12},{9,5},{10,... | collective-permute-start | bytes 491528 | tf_op jit(solution)/shard_map/ppermute | solution.py:293
  15.1 2.7 %collective-permute-done.2.refs_3_ = bf16[352,256]{1,0:T(8,128)(2,1)S(1)} collective-permute-done((bf16[352,256]{1,0:T(8,128)(2,1)S(1)}, bf16[352,256]{1,0:T(8,128)(2,1)S(1)}, u32[]{:S(2)}, u32[]{:S(2)}) %collective-permute-start.2) | collective-permute-done | bytes 180256 | tf_op jit(solution)/shard_map/ppermute | solution.py:293
  17.8 1.2 %collective-permute-start.5 = (bf16[320,256]{1,0:T(8,128)(2,1)S(1)}, bf16[320,256]{1,0:T(8,128)(2,1)S(1)}, u32[]{:S(2)}, u32[]{:S(2)}) collective-permute-start(bf16[320,256]{1,0:T(8,128)(2,1)S(1)} %slice.25), channel_id=1, source_target_pairs={{0,4},{1,3},{2,0},{3,7},{4,8},{5,1},{6,2},{7,11},{8,12},{9,5},{10,... | collective-permute-start | bytes 491528 | tf_op jit(solution)/shard_map/ppermute | solution.py:293
  19.0 0.5 %collective-permute-start.7 = (bf16[384,256]{1,0:T(8,128)(2,1)S(1)}, bf16[384,256]{1,0:T(8,128)(2,1)S(1)}, u32[]{:S(2)}, u32[]{:S(2)}) collective-permute-start(bf16[384,256]{1,0:T(8,128)(2,1)S(1)} %collective-permute-done.refs_1_), channel_id=1, source_target_pairs={{0,1},{1,0},{2,3},{3,2},{4,5},{5,4},{6,7},{7,6},{8,9},{9,8},{10,11... | collective-permute-start | bytes 589832 | tf_op jit(solution)/shard_map/ppermute | solution.py:296
  19.5 0.0 collective-permute-done.3.refs_4_
  19.5 0.1 collective-permute-start.10
  19.6 1.6 %collective-permute-start.6 = (bf16[288,256]{1,0:T(8,128)(2,1)S(1)}, bf16[288,256]{1,0:T(8,128)(2,1)S(1)}, u32[]{:S(2)}, u32[]{:S(2)}) collective-permute-start(bf16[288,256]{1,0:T(8,128)(2,1)S(1)} %slice.22), channel_id=1, source_target_pairs={{0,4},{1,3},{2,0},{3,7},{4,8},{5,1},{6,2},{7,11},{8,12},{9,5},{10,... | collective-permute-start | bytes 442376 | tf_op jit(solution)/shard_map/ppermute | solution.py:293
  21.2 1.9 %collective-permute-done.5.refs_5_ = bf16[320,256]{1,0:T(8,128)(2,1)S(1)} collective-permute-done((bf16[320,256]{1,0:T(8,128)(2,1)S(1)}, bf16[320,256]{1,0:T(8,128)(2,1)S(1)}, u32[]{:S(2)}, u32[]{:S(2)}) %collective-permute-start.5) | collective-permute-done | bytes 163872 | tf_op jit(solution)/shard_map/ppermute | solution.py:293
  23.2 1.2 %collective-permute-start.9 = (bf16[288,256]{1,0:T(8,128)(2,1)S(1)}, bf16[288,256]{1,0:T(8,128)(2,1)S(1)}, u32[]{:S(2)}, u32[]{:S(2)}) collective-permute-start(bf16[288,256]{1,0:T(8,128)(2,1)S(1)} %slice.26), channel_id=1, source_target_pairs={{0,4},{1,3},{2,0},{3,7},{4,8},{5,1},{6,2},{7,11},{8,12},{9,5},{10,... | collective-permute-start | bytes 442376 | tf_op jit(solution)/shard_map/ppermute | solution.py:293
  24.4 0.4 %collective-permute-done.6.refs_6_ = bf16[288,256]{1,0:T(8,128)(2,1)S(1)} collective-permute-done((bf16[288,256]{1,0:T(8,128)(2,1)S(1)}, bf16[288,256]{1,0:T(8,128)(2,1)S(1)}, u32[]{:S(2)}, u32[]{:S(2)}) %collective-permute-start.6) | collective-permute-done | bytes 147488 | tf_op jit(solution)/shard_map/ppermute | solution.py:293
  24.8 0.7 %collective-permute-start.12 = (bf16[320,256]{1,0:T(8,128)(2,1)S(1)}, bf16[320,256]{1,0:T(8,128)(2,1)S(1)}, u32[]{:S(2)}, u32[]{:S(2)}) collective-permute-start(bf16[320,256]{1,0:T(8,128)(2,1)S(1)} %collective-permute-done.5.refs_5_), channel_id=1, source_target_pairs={{0,1},{1,0},{2,3},{3,2},{4,5},{5,4},{6,7},{7,6},{8,9},{9,8},{10,11... | collective-permute-start | bytes 491528 | tf_op jit(solution)/shard_map/ppermute | solution.py:296
  25.5 0.1 collective-permute-start.13
  25.6 2.8 %collective-permute-done.9.refs_7_ = bf16[288,256]{1,0:T(8,128)(2,1)S(1)} collective-permute-done((bf16[288,256]{1,0:T(8,128)(2,1)S(1)}, bf16[288,256]{1,0:T(8,128)(2,1)S(1)}, u32[]{:S(2)}, u32[]{:S(2)}) %collective-permute-start.9) | collective-permute-done | bytes 147488 | tf_op jit(solution)/shard_map/ppermute | solution.py:293
  28.4 1.4 %collective-permute-done.14.refs_15_ = bf16[288,256]{1,0:T(8,128)(2,1)S(1)} collective-permute-done((bf16[288,256]{1,0:T(8,128)(2,1)S(1)}, bf16[288,256]{1,0:T(8,128)(2,1)S(1)}, u32[]{:S(2)}, u32[]{:S(2)}) %collective-permute-start.14) | collective-permute-done | bytes 147488 | tf_op jit(solution)/shard_map/ppermute | solution.py:296
  29.8 4.4 %shard_map.93 = bf16[16,256,128]{2,1,0:T(8,128)(2,1)} custom-call(bf16[384,256]{1,0:T(8,128)(2,1)S(1)} %get-tuple-element.26.refs_0_, bf16[384,256]{1,0:T(8,128)(2,1)S(1)} %collective-permute-done.refs_1_, bf16[352,256]{1,0:T(8,128)(2,1)S(1)} %collective-permute-done.1.refs_2_, bf16[352,256]{1,0:T(8,128)(2,1)S(1)} %collective-permute-done.2.refs_3_, ...), custom_call_target="tpu_custom_call" | custom-call | tf_op jit(solution)/shard_map/pallas_call | solution.py:342
  (19 shorter events, 0.1 us)
Async XLA Ops:
  3.6 3.9 %copy-start = (bf16[1024,128]{1,0:T(8,128)(2,1)S(1)}, bf16[1024,128]{1,0:T(8,128)(2,1)}, u32[]{:S(2)}) copy-start(bf16[1024,128]{1,0:T(8,128)(2,1)} %final_ref.1) | copy-start | bytes 786436
  3.6 7.3 %collective-permute-start = (bf16[384,256]{1,0:T(8,128)(2,1)S(1)}, bf16[384,256]{1,0:T(8,128)(2,1)S(1)}, u32[]{:S(2)}, u32[]{:S(2)}) collective-permute-start(bf16[384,256]{1,0:T(8,128)(2,1)S(1)} %get-tuple-element.27), channel_id=1, source_target_pairs={{0,4},{1,3},{2,0},{3,7},{4,8},{5,1},{6,2},{7,11},{8,12},{9,5},{10,... | collective-permute-start | bytes 589832 | tf_op jit(solution)/shard_map/ppermute | solution.py:293
  6.7 0.8 %copy-start.1 = (f32[128]{0:T(128)S(1)}, f32[128]{0:T(128)}, u32[]{:S(2)}) copy-start(f32[128]{0:T(128)} %param.17) | copy-start | bytes 1540
  6.7 6.7 %collective-permute-start.1 = (bf16[352,256]{1,0:T(8,128)(2,1)S(1)}, bf16[352,256]{1,0:T(8,128)(2,1)S(1)}, u32[]{:S(2)}, u32[]{:S(2)}) collective-permute-start(bf16[352,256]{1,0:T(8,128)(2,1)S(1)} %slice.18), channel_id=1, source_target_pairs={{0,3},{1,4},{2,7},{3,0},{4,1},{5,8},{6,11},{7,2},{8,5},{9,12},{10,... | collective-permute-start | bytes 540680 | tf_op jit(solution)/shard_map/ppermute | solution.py:293
  10.9 6.9 %collective-permute-start.2 = (bf16[352,256]{1,0:T(8,128)(2,1)S(1)}, bf16[352,256]{1,0:T(8,128)(2,1)S(1)}, u32[]{:S(2)}, u32[]{:S(2)}) collective-permute-start(bf16[352,256]{1,0:T(8,128)(2,1)S(1)} %slice.19), channel_id=1, source_target_pairs={{0,4},{1,3},{2,0},{3,7},{4,8},{5,1},{6,2},{7,11},{8,12},{9,5},{10,... | collective-permute-start | bytes 540680 | tf_op jit(solution)/shard_map/ppermute | solution.py:293
  13.4 6.1 %collective-permute-start.4 = (bf16[384,256]{1,0:T(8,128)(2,1)S(1)}, bf16[384,256]{1,0:T(8,128)(2,1)S(1)}, u32[]{:S(2)}, u32[]{:S(2)}) collective-permute-start(bf16[384,256]{1,0:T(8,128)(2,1)S(1)} %get-tuple-element.26.refs_0_), channel_id=1, source_target_pairs={{0,1},{1,0},{2,3},{3,2},{4,5},{5,4},{6,7},{7,6},{8,9},{9,8},{10,11... | collective-permute-start | bytes 589832 | tf_op jit(solution)/shard_map/ppermute | solution.py:296
  13.5 6.1 %collective-permute-start.3 = (bf16[320,256]{1,0:T(8,128)(2,1)S(1)}, bf16[320,256]{1,0:T(8,128)(2,1)S(1)}, u32[]{:S(2)}, u32[]{:S(2)}) collective-permute-start(bf16[320,256]{1,0:T(8,128)(2,1)S(1)} %slice.24), channel_id=1, source_target_pairs={{0,4},{1,3},{2,0},{3,7},{4,8},{5,1},{6,2},{7,11},{8,12},{9,5},{10,... | collective-permute-start | bytes 491528 | tf_op jit(solution)/shard_map/ppermute | solution.py:293
  17.8 5.4 %collective-permute-start.5 = (bf16[320,256]{1,0:T(8,128)(2,1)S(1)}, bf16[320,256]{1,0:T(8,128)(2,1)S(1)}, u32[]{:S(2)}, u32[]{:S(2)}) collective-permute-start(bf16[320,256]{1,0:T(8,128)(2,1)S(1)} %slice.25), channel_id=1, source_target_pairs={{0,4},{1,3},{2,0},{3,7},{4,8},{5,1},{6,2},{7,11},{8,12},{9,5},{10,... | collective-permute-start | bytes 491528 | tf_op jit(solution)/shard_map/ppermute | solution.py:293
  19.0 4.2 %collective-permute-start.8 = (bf16[352,256]{1,0:T(8,128)(2,1)S(1)}, bf16[352,256]{1,0:T(8,128)(2,1)S(1)}, u32[]{:S(2)}, u32[]{:S(2)}) collective-permute-start(bf16[352,256]{1,0:T(8,128)(2,1)S(1)} %collective-permute-done.1.refs_2_), channel_id=1, source_target_pairs={{0,1},{1,0},{2,3},{3,2},{4,5},{5,4},{6,7},{7,6},{8,9},{9,8},{10,11... | collective-permute-start | bytes 540680 | tf_op jit(solution)/shard_map/ppermute | solution.py:296
  19.0 5.4 %collective-permute-start.7 = (bf16[384,256]{1,0:T(8,128)(2,1)S(1)}, bf16[384,256]{1,0:T(8,128)(2,1)S(1)}, u32[]{:S(2)}, u32[]{:S(2)}) collective-permute-start(bf16[384,256]{1,0:T(8,128)(2,1)S(1)} %collective-permute-done.refs_1_), channel_id=1, source_target_pairs={{0,1},{1,0},{2,3},{3,2},{4,5},{5,4},{6,7},{7,6},{8,9},{9,8},{10,11... | collective-permute-start | bytes 589832 | tf_op jit(solution)/shard_map/ppermute | solution.py:296
  19.5 6.0 %collective-permute-start.10 = (bf16[352,256]{1,0:T(8,128)(2,1)S(1)}, bf16[352,256]{1,0:T(8,128)(2,1)S(1)}, u32[]{:S(2)}, u32[]{:S(2)}) collective-permute-start(bf16[352,256]{1,0:T(8,128)(2,1)S(1)} %collective-permute-done.2.refs_3_), channel_id=1, source_target_pairs={{0,1},{1,0},{2,3},{3,2},{4,5},{5,4},{6,7},{7,6},{8,9},{9,8},{10,11... | collective-permute-start | bytes 540680 | tf_op jit(solution)/shard_map/ppermute | solution.py:296
  19.6 5.2 %collective-permute-start.6 = (bf16[288,256]{1,0:T(8,128)(2,1)S(1)}, bf16[288,256]{1,0:T(8,128)(2,1)S(1)}, u32[]{:S(2)}, u32[]{:S(2)}) collective-permute-start(bf16[288,256]{1,0:T(8,128)(2,1)S(1)} %slice.22), channel_id=1, source_target_pairs={{0,4},{1,3},{2,0},{3,7},{4,8},{5,1},{6,2},{7,11},{8,12},{9,5},{10,... | collective-permute-start | bytes 442376 | tf_op jit(solution)/shard_map/ppermute | solution.py:293
  23.2 2.4 %collective-permute-start.11 = (bf16[320,256]{1,0:T(8,128)(2,1)S(1)}, bf16[320,256]{1,0:T(8,128)(2,1)S(1)}, u32[]{:S(2)}, u32[]{:S(2)}) collective-permute-start(bf16[320,256]{1,0:T(8,128)(2,1)S(1)} %collective-permute-done.3.refs_4_), channel_id=1, source_target_pairs={{0,1},{1,0},{2,3},{3,2},{4,5},{5,4},{6,7},{7,6},{8,9},{9,8},{10,11... | collective-permute-start | bytes 491528 | tf_op jit(solution)/shard_map/ppermute | solution.py:296
  23.2 5.2 %collective-permute-start.9 = (bf16[288,256]{1,0:T(8,128)(2,1)S(1)}, bf16[288,256]{1,0:T(8,128)(2,1)S(1)}, u32[]{:S(2)}, u32[]{:S(2)}) collective-permute-start(bf16[288,256]{1,0:T(8,128)(2,1)S(1)} %slice.26), channel_id=1, source_target_pairs={{0,4},{1,3},{2,0},{3,7},{4,8},{5,1},{6,2},{7,11},{8,12},{9,5},{10,... | collective-permute-start | bytes 442376 | tf_op jit(solution)/shard_map/ppermute | solution.py:293
  24.8 3.6 %collective-permute-start.12 = (bf16[320,256]{1,0:T(8,128)(2,1)S(1)}, bf16[320,256]{1,0:T(8,128)(2,1)S(1)}, u32[]{:S(2)}, u32[]{:S(2)}) collective-permute-start(bf16[320,256]{1,0:T(8,128)(2,1)S(1)} %collective-permute-done.5.refs_5_), channel_id=1, source_target_pairs={{0,1},{1,0},{2,3},{3,2},{4,5},{5,4},{6,7},{7,6},{8,9},{9,8},{10,11... | collective-permute-start | bytes 491528 | tf_op jit(solution)/shard_map/ppermute | solution.py:296
  25.5 2.9 %collective-permute-start.13 = (bf16[288,256]{1,0:T(8,128)(2,1)S(1)}, bf16[288,256]{1,0:T(8,128)(2,1)S(1)}, u32[]{:S(2)}, u32[]{:S(2)}) collective-permute-start(bf16[288,256]{1,0:T(8,128)(2,1)S(1)} %collective-permute-done.6.refs_6_), channel_id=1, source_target_pairs={{0,1},{1,0},{2,3},{3,2},{4,5},{5,4},{6,7},{7,6},{8,9},{9,8},{10,11... | collective-permute-start | bytes 442376 | tf_op jit(solution)/shard_map/ppermute | solution.py:296
  28.4 1.4 %collective-permute-start.14 = (bf16[288,256]{1,0:T(8,128)(2,1)S(1)}, bf16[288,256]{1,0:T(8,128)(2,1)S(1)}, u32[]{:S(2)}, u32[]{:S(2)}) collective-permute-start(bf16[288,256]{1,0:T(8,128)(2,1)S(1)} %collective-permute-done.9.refs_7_), channel_id=1, source_target_pairs={{0,1},{1,0},{2,3},{3,2},{4,5},{5,4},{6,7},{7,6},{8,9},{9,8},{10,11... | collective-permute-start | bytes 442376 | tf_op jit(solution)/shard_map/ppermute | solution.py:296

commit v9 on v5

--- a/solution.py
+++ b/solution.py
@@ -11,6 +11,7 @@
 MIB = 1024 * 1024
 LANES = 128
 CHUNKS = 2
+BLOCK = 64
 
 
 def repeat_rows(values, times):
@@ -99,13 +100,15 @@
     for s in range(samples):
         if s % some == 0:
             large[s // some].wait()
-        values = x_ref[s].astype(jnp.float32)
-        center = jnp.mean(values, axis=-1, keepdims=True)
-        values = values - center
-        variance = jnp.mean(jnp.square(values), axis=-1, keepdims=True)
-        normed = (values * lax.rsqrt(variance + 1e-05) * gain_ref[...] + shift_ref[...]).astype(
-            jnp.bfloat16
-        )
+        normed = []
+        for low in range(0, residues, BLOCK):
+            values = x_ref[s, low : low + BLOCK, :].astype(jnp.float32)
+            center = jnp.mean(values, axis=-1, keepdims=True)
+            values = values - center
+            variance = jnp.mean(jnp.square(values), axis=-1, keepdims=True)
+            values = values * lax.rsqrt(variance + 1e-05) * gain_ref[...] + shift_ref[...]
+            normed.append(values.astype(jnp.bfloat16))
+        normed = jnp.concatenate(normed, axis=0)
         second_here = jnp.where(row % samples == s, second, 0.0).astype(jnp.bfloat16)
         for t in range(tiles):
             part = normed[t * tile : (t + 1) * tile]
@@ -133,12 +136,21 @@
     base = tiles * width
     way = 1 - 2 * (device % 2)
     place = place_of(device, half)
-    for n in range(half):
+    spots = [(keep_ref, base + n * per_chip, half - n) for n in range(half)]
+    spots += [(give_ref, base + n * per_chip, n + 1 - half) for n in range(half)]
+    for message, low, ahead in spots:
+        chip = chip_at(lax.rem(place + way * ahead + 2 * half, 2 * half), half)
+        start = pl.multiple_of(chip * per_chip, per_chip)
+        message[low : low + per_chip, :] = left_ref[pl.ds(start, per_chip), :].astype(jnp.bfloat16)
+
+
+def join_kernel(base, per_chip, mine_ref, theirs_ref, next_ref):
+    next_ref[:base, :] = theirs_ref[:base, :]
+    for n in range((next_ref.shape[0] - base) // (2 * per_chip)):
         low = base + n * per_chip
-        for message, ahead in ((keep_ref, way * (half - n)), (give_ref, -way * (half - 1 - n))):
-            chip = chip_at(lax.rem(place + ahead + 2 * half, 2 * half), half)
-            start = pl.multiple_of(chip * per_chip, per_chip)
-            message[low : low + per_chip, :] = left_ref[pl.ds(start, per_chip), :].astype(jnp.bfloat16)
+        at = low + n * per_chip
+        next_ref[at : at + per_chip, :] = mine_ref[low + per_chip : low + 2 * per_chip, :]
+        next_ref[at + per_chip : at + 2 * per_chip, :] = theirs_ref[low : low + per_chip, :]
 
 
 def weight_kernel(final_ref, offset_ref, out_ref, offset_out, wide_ref):
@@ -160,8 +172,8 @@
     if gridded:
         shards = [(refs.pop(0), 0, refs.pop(0), 0) for _ in places]
     else:
-        messages = [refs.pop(0) for _ in range(1 + max(place[0] for place in places))]
-        shards = [(messages[n], right, messages[n], left) for n, right, left in places]
+        messages = [refs.pop(0) for _ in places]
+        shards = [(messages[n], right, messages[m], left) for n, right, m, left in places]
     weight_ref, offset_ref, out_hbm, left_ref, outer_ref, out_ref, sems = refs
     tile = shards[0][0].shape[1]
     here = samples // count
@@ -229,13 +241,15 @@
     tiles = residues // tile
     body = tiles * width
     per_chip = 2 * rows_here * width // tile
-    message = jax.ShapeDtypeStruct((body + half * per_chip, tile), jnp.bfloat16)
+
+    def rows(count):
+        return jax.ShapeDtypeStruct((count, tile), jnp.bfloat16)
 
     vmem = pl.BlockSpec(memory_space=pltpu.VMEM)
     hbm = pl.BlockSpec(memory_space=pltpu.HBM)
     keep, give = pl.pallas_call(
         functools.partial(project_kernel, rows_here),
-        out_shape=[message] * 2,
+        out_shape=[rows(body + half * per_chip)] * 2,
         in_specs=[hbm] * 7,
         out_specs=[vmem] * 2,
         scratch_shapes=[
@@ -270,59 +284,71 @@
             )
         ]
     )
+    by_place = {(place_of(r, half), r % 2): r for r in range(size)}
+    around = [
+        (r, by_place[(place_of(r, half) + 1 - 2 * (r % 2)) % (2 * half), r % 2]) for r in range(size)
+    ]
+
+    def swap(value):
+        return lax.ppermute(value, "row", [(r, r ^ 1) for r in range(size)])
+
     weight, offset = pl.pallas_call(
         weight_kernel,
         out_shape=[
             jax.ShapeDtypeStruct((channels, hidden * hidden), jnp.bfloat16),
             jax.ShapeDtypeStruct((1, channels), jnp.float32),
         ],
-        in_specs=[vmem, vmem],
-        out_specs=[vmem, vmem],
+        in_specs=[vmem] * 2,
+        out_specs=[vmem] * 2,
         scratch_shapes=[pltpu.VMEM((hidden * hidden, channels), jnp.float32)],
         compiler_params=pltpu.CompilerParams(vmem_limit_bytes=16 * MIB),
         cost_estimate=pl.CostEstimate(flops=2**28, bytes_accessed=2**20, transcendentals=0),
     )(final_projector_coefficients, final_projector_offset.reshape(1, channels))
-
-    by_place = {(place_of(r, half), r % 2): r for r in range(size)}
-
-    def neighbours(way):
-        return [
-            (r, by_place[(place_of(r, half) + way * (1 - 2 * (r % 2))) % (2 * half), r % 2])
-            for r in range(size)
-        ]
-
-    def swap(value):
-        return lax.ppermute(value, "row", [(r, r ^ 1) for r in range(size)])
-
-    messages, places = [], []
-
-    def take(pair):
-        for value in pair:
-            places.append((len(messages), 0, value.shape[0] - per_chip))
-            messages.append(value)
-
-    mine, theirs, weight, offset = lax.optimization_barrier((give, swap(give), weight, offset))
-    take([mine, theirs])
-    flying = [keep, mine[: body + (half - 1) * per_chip]]
-    swapped = []
+    theirs, weight, offset = lax.optimization_barrier((swap(give), weight, offset))
+    messages = [give, theirs]
+    places = [(n, 0, n, body + (half - 1) * per_chip) for n in range(2)]
+
+    def take(*lefts):
+        places.extend((len(messages) + n, 0, len(messages) + m, low) for n, (m, low) in enumerate(lefts))
+
+    flying = [keep, theirs[: body + (half - 1) * per_chip]]
+    swapped, lefts = [], []
     for step in range(1, half + 1):
-        landed = [lax.ppermute(x, "row", neighbours(way)) for x, way in zip(flying, (1, -1))]
+        landed = [lax.ppermute(x, "row", around) for x in flying]
         if step >= 3:
             landed[-1], swapped[step - 3] = lax.optimization_barrier((landed[-1], swapped[step - 3]))
-        flying = [x[: x.shape[0] - per_chip] for x in landed]
-        if step == half - 1:
-            flying = flying[:1]
+        low = [x.shape[0] - per_chip for x in landed]
+        if step == 1:
+            lefts.append([(0, low[0]), (1, low[1])])
+        elif step < half:
+            lefts.append([(1, low[1] - per_chip), (1, low[1])])
+        else:
+            lefts.append([(0, low[0])])
+        flying = [landed[0][: body + per_chip]]
+        if step == 1:
+            flying += pl.pallas_call(
+                functools.partial(join_kernel, body, per_chip),
+                out_shape=[rows(body + 2 * (half - 2) * per_chip)],
+                in_specs=[vmem] * 2,
+                out_specs=[vmem],
+                compiler_params=pltpu.CompilerParams(vmem_limit_bytes=16 * MIB),
+                cost_estimate=pl.CostEstimate(flops=0, bytes_accessed=2**19, transcendentals=0),
+            )(*landed)
+        elif step < half - 1:
+            flying.append(landed[1][: landed[1].shape[0] - 2 * per_chip])
         landed = lax.optimization_barrier(landed)
-        take(landed)
+        take(*lefts[-1])
+        messages += landed
         swapped.append([swap(x) for x in landed])
-    for pair in swapped:
-        take(pair)
+    for pair, left in zip(swapped, lefts):
+        take(*left)
+        messages += pair
 
     gridded = tiles > 1
     if gridded:
         operands, specs = [], []
-        for n, right, left in places:
-            operands += [messages[n]] * 2
+        for n, right, m, left in places:
+            operands += [messages[n], messages[m]]
             specs += [
                 pl.BlockSpec((width, tile), lambda t, first=right // width: (first + t, 0)),
                 pl.BlockSpec((per_chip, tile), lambda t, at=left // per_chip: (at, 0)),

time: 36.5 us -> 31.9 us (0.87)
  waiting for transfers between devices: 15.2 us -> 8.17 us
  starting transfers between devices: 12.5 us -> 14.9 us
    ppermute x7, waiting for transfers between devices: 13.8 us -> 6.81 us  [per_device(): landed = [lax.ppermute(x, 'row', around) for x in flying]]
    ppermute x7, starting transfers between devices: 10.4 us -> 13.9 us  [per_device(): landed = [lax.ppermute(x, 'row', around) for x in flying]]
    ppermute x8, starting transfers between devices: 2.11 us -> 1.04 us  [swap(): return lax.ppermute(value, 'row', [(r, r ^ 1) for r in range(size)])]
    pallas_call x1 -> x2, Pallas kernels: 3.63 us -> 3.68 us  [the longest x1 3.67 us: per_device(): pl.pallas_call(functools.partial(project_kernel, rows_here), out_shape=[r...]
  transfers between devices with their start and end apart: 15 -> 15, of which waited for: 6 -> 8; matrix products, arithmetic and copies ran while one was open for 0% -> 0% of each run, Pallas kernels for 1% -> 1%
where the time goes in v9:
time: 31.9 us; the launch traced here: 31.7 us
  starting transfers between devices  14.9 us (47%)
  Pallas kernels  8.52 us (27%)
  waiting for transfers between devices  8.17 us (26%)
    ppermute x7, starting transfers between devices, per_device(): landed = [lax.ppermute(x, 'row', around) for x in flying]  13.9 us
    ppermute x7, waiting for transfers between devices, per_device(): landed = [lax.ppermute(x, 'row', around) for x in flying]  6.81 us
    pallas_call x1, Pallas kernels, per_device(): pl.pallas_call(functools.partial(pair_kernel, places, gridded, rows_here,...  4.43 us
    pallas_call x1, Pallas kernels, per_device(): pl.pallas_call(functools.partial(project_kernel, rows_here), out_shape=[r...  3.67 us
    ppermute x8, waiting for transfers between devices, swap(): return lax.ppermute(value, 'row', [(r, r ^ 1) for r in range(size)])  1.36 us
    ppermute x8, starting transfers between devices, swap(): return lax.ppermute(value, 'row', [(r, r ^ 1) for r in range(size)])  1.04 us
  transfers between devices with their start and end apart: 15, of which 8 were waited for; matrix products, arithmetic and copies ran while one was open for 0% of the time, Pallas kernels for 1%

profile of v9, /device:TPU:0, one launch (start us, length us, event | category | flops | bytes accessed | tf_op | source)
XLA Modules:
  0.0 31.7 jit_solution(16221224328058524423)
XLA Ops:
  0.0 3.7 %shard_map.91 = (bf16[384,256]{1,0:T(8,128)(2,1)S(1)}, bf16[384,256]{1,0:T(8,128)(2,1)S(1)}) custom-call(bf16[8,256,256]{2,1,0:T(8,128)(2,1)} %x_hbm.1, f32[1,256]{1,0:T(1,128)} %bitcast.10, f32[1,256]{1,0:T(1,128)} %bitcast.11, bf16[32,256]{1,0:T(8,128)(2,1)} %bitcast.8, f32[1,32]{1,0:T(1,128)} %bitcast.12, bf16[32,256]{1,0:T(8,128)(2,1)} %bitcast.9, ...), custom_call_target="tpu_custom_call" | custom-call | flops 536870912 | bytes 1048576 | tf_op jit(solution)/shard_map/pallas_call | solution.py:250
  3.7 0.5 %collective-permute-start = (bf16[384,256]{1,0:T(8,128)(2,1)S(1)}, bf16[384,256]{1,0:T(8,128)(2,1)S(1)}, u32[]{:S(2)}, u32[]{:S(2)}) collective-permute-start(bf16[384,256]{1,0:T(8,128)(2,1)S(1)} %get-tuple-element.24.refs_0_), channel_id=1, source_target_pairs={{0,1},{1,0},{2,3},{3,2},{4,5},{5,4},{6,7},{7,6},{8,9},{9,8},{10,11... | collective-permute-start | bytes 589832 | tf_op jit(solution)/shard_map/ppermute | solution.py:293
  4.2 2.6 %collective-permute-start.1 = (bf16[384,256]{1,0:T(8,128)(2,1)S(1)}, bf16[384,256]{1,0:T(8,128)(2,1)S(1)}, u32[]{:S(2)}, u32[]{:S(2)}) collective-permute-start(bf16[384,256]{1,0:T(8,128)(2,1)S(1)} %get-tuple-element.28), channel_id=1, source_target_pairs={{0,4},{1,3},{2,0},{3,7},{4,8},{5,1},{6,2},{7,11},{8,12},{9,5},{10,... | collective-permute-start | bytes 589832 | tf_op jit(solution)/shard_map/ppermute | solution.py:317
  6.9 0.4 %shard_map.92 = (bf16[128,1024]{1,0:T(8,128)(2,1)S(1)}, f32[1,128]{1,0:T(1,128)S(1)}) custom-call(bf16[1024,128]{1,0:T(8,128)(2,1)S(1)} %copy-done, f32[1,128]{1,0:T(1,128)S(1)} %bitcast.7), custom_call_target="tpu_custom_call" | custom-call | flops 268435456 | bytes 1048576 | tf_op jit(solution)/shard_map/pallas_call | solution.py:295
  7.3 0.0 collective-permute-done.refs_1_
  7.3 1.6 %collective-permute-start.2 = (bf16[352,256]{1,0:T(8,128)(2,1)S(1)}, bf16[352,256]{1,0:T(8,128)(2,1)S(1)}, u32[]{:S(2)}, u32[]{:S(2)}) collective-permute-start(bf16[352,256]{1,0:T(8,128)(2,1)S(1)} %slice.9), channel_id=1, source_target_pairs={{0,4},{1,3},{2,0},{3,7},{4,8},{5,1},{6,2},{7,11},{8,12},{9,5},{10,... | collective-permute-start | bytes 540680 | tf_op jit(solution)/shard_map/ppermute | solution.py:317
  8.9 1.5 %collective-permute-done.1.mine_ref.refs_2_ = bf16[384,256]{1,0:T(8,128)(2,1)S(1)} collective-permute-done((bf16[384,256]{1,0:T(8,128)(2,1)S(1)}, bf16[384,256]{1,0:T(8,128)(2,1)S(1)}, u32[]{:S(2)}, u32[]{:S(2)}) %collective-permute-start.1) | collective-permute-done | bytes 196640 | tf_op jit(solution)/shard_map/ppermute | solution.py:317
  10.5 2.1 %collective-permute-start.3 = (bf16[288,256]{1,0:T(8,128)(2,1)S(1)}, bf16[288,256]{1,0:T(8,128)(2,1)S(1)}, u32[]{:S(2)}, u32[]{:S(2)}) collective-permute-start(bf16[288,256]{1,0:T(8,128)(2,1)S(1)} %slice.12), channel_id=1, source_target_pairs={{0,4},{1,3},{2,0},{3,7},{4,8},{5,1},{6,2},{7,11},{8,12},{9,5},{10,... | collective-permute-start | bytes 442376 | tf_op jit(solution)/shard_map/ppermute | solution.py:317
  12.6 0.3 collective-permute-done.2.theirs_ref.refs_3_
  12.9 1.7 %collective-permute-start.4 = (bf16[384,256]{1,0:T(8,128)(2,1)S(1)}, bf16[384,256]{1,0:T(8,128)(2,1)S(1)}, u32[]{:S(2)}, u32[]{:S(2)}) collective-permute-start(bf16[384,256]{1,0:T(8,128)(2,1)S(1)} %shard_map.93), channel_id=1, source_target_pairs={{0,4},{1,3},{2,0},{3,7},{4,8},{5,1},{6,2},{7,11},{8,12},{9,5},{10,... | collective-permute-start | bytes 589832 | tf_op jit(solution)/shard_map/ppermute | solution.py:317
  14.5 0.0 collective-permute-start.8
  14.5 1.1 %collective-permute-done.3.refs_4_ = bf16[288,256]{1,0:T(8,128)(2,1)S(1)} collective-permute-done((bf16[288,256]{1,0:T(8,128)(2,1)S(1)}, bf16[288,256]{1,0:T(8,128)(2,1)S(1)}, u32[]{:S(2)}, u32[]{:S(2)}) %collective-permute-start.3) | collective-permute-done | bytes 147488 | tf_op jit(solution)/shard_map/ppermute | solution.py:317
  15.6 2.1 %collective-permute-start.5 = (bf16[288,256]{1,0:T(8,128)(2,1)S(1)}, bf16[288,256]{1,0:T(8,128)(2,1)S(1)}, u32[]{:S(2)}, u32[]{:S(2)}) collective-permute-start(bf16[288,256]{1,0:T(8,128)(2,1)S(1)} %collective-permute-done.3.refs_4_), channel_id=1, source_target_pairs={{0,4},{1,3},{2,0},{3,7},{4,8},{5,1},{6,2},{7,11},{8,12},{9,5},{10,... | collective-permute-start | bytes 442376 | tf_op jit(solution)/shard_map/ppermute | solution.py:317
  17.7 0.0 collective-permute-start.7
  17.7 0.8 %collective-permute-done.4.refs_5_ = bf16[384,256]{1,0:T(8,128)(2,1)S(1)} collective-permute-done((bf16[384,256]{1,0:T(8,128)(2,1)S(1)}, bf16[384,256]{1,0:T(8,128)(2,1)S(1)}, u32[]{:S(2)}, u32[]{:S(2)}) %collective-permute-start.4) | collective-permute-done | bytes 196640 | tf_op jit(solution)/shard_map/ppermute | solution.py:317
  18.6 1.7 %collective-permute-start.6 = (bf16[320,256]{1,0:T(8,128)(2,1)S(1)}, bf16[320,256]{1,0:T(8,128)(2,1)S(1)}, u32[]{:S(2)}, u32[]{:S(2)}) collective-permute-start(bf16[320,256]{1,0:T(8,128)(2,1)S(1)} %slice.13), channel_id=1, source_target_pairs={{0,4},{1,3},{2,0},{3,7},{4,8},{5,1},{6,2},{7,11},{8,12},{9,5},{10,... | collective-permute-start | bytes 491528 | tf_op jit(solution)/shard_map/ppermute | solution.py:317
  20.3 0.5 %collective-permute-done.5.refs_6_ = bf16[288,256]{1,0:T(8,128)(2,1)S(1)} collective-permute-done((bf16[288,256]{1,0:T(8,128)(2,1)S(1)}, bf16[288,256]{1,0:T(8,128)(2,1)S(1)}, u32[]{:S(2)}, u32[]{:S(2)}) %collective-permute-start.5) | collective-permute-done | bytes 147488 | tf_op jit(solution)/shard_map/ppermute | solution.py:317
  20.8 2.1 %collective-permute-start.9 = (bf16[288,256]{1,0:T(8,128)(2,1)S(1)}, bf16[288,256]{1,0:T(8,128)(2,1)S(1)}, u32[]{:S(2)}, u32[]{:S(2)}) collective-permute-start(bf16[288,256]{1,0:T(8,128)(2,1)S(1)} %collective-permute-done.5.refs_6_), channel_id=1, source_target_pairs={{0,4},{1,3},{2,0},{3,7},{4,8},{5,1},{6,2},{7,11},{8,12},{9,5},{10,... | collective-permute-start | bytes 442376 | tf_op jit(solution)/shard_map/ppermute | solution.py:317
  22.9 0.0 collective-permute-done.8.refs_10_
  22.9 1.1 %collective-permute-done.6.refs_7_ = bf16[320,256]{1,0:T(8,128)(2,1)S(1)} collective-permute-done((bf16[320,256]{1,0:T(8,128)(2,1)S(1)}, bf16[320,256]{1,0:T(8,128)(2,1)S(1)}, u32[]{:S(2)}, u32[]{:S(2)}) %collective-permute-start.6) | collective-permute-done | bytes 163872 | tf_op jit(solution)/shard_map/ppermute | solution.py:317
  24.0 0.5 %collective-permute-start.12 = (bf16[288,256]{1,0:T(8,128)(2,1)S(1)}, bf16[288,256]{1,0:T(8,128)(2,1)S(1)}, u32[]{:S(2)}, u32[]{:S(2)}) collective-permute-start(bf16[288,256]{1,0:T(8,128)(2,1)S(1)} %collective-permute-done.5.refs_6_), channel_id=1, source_target_pairs={{0,1},{1,0},{2,3},{3,2},{4,5},{5,4},{6,7},{7,6},{8,9},{9,8},{10,11... | collective-permute-start | bytes 442376 | tf_op jit(solution)/shard_map/ppermute | solution.py:293
  24.5 1.5 %collective-permute-done.9.refs_8_ = bf16[288,256]{1,0:T(8,128)(2,1)S(1)} collective-permute-done((bf16[288,256]{1,0:T(8,128)(2,1)S(1)}, bf16[288,256]{1,0:T(8,128)(2,1)S(1)}, u32[]{:S(2)}, u32[]{:S(2)}) %collective-permute-start.9) | collective-permute-done | bytes 147488 | tf_op jit(solution)/shard_map/ppermute | solution.py:317
  26.0 1.3 %collective-permute-done.14.refs_15_ = bf16[288,256]{1,0:T(8,128)(2,1)S(1)} collective-permute-done((bf16[288,256]{1,0:T(8,128)(2,1)S(1)}, bf16[288,256]{1,0:T(8,128)(2,1)S(1)}, u32[]{:S(2)}, u32[]{:S(2)}) %collective-permute-start.14) | collective-permute-done | bytes 147488 | tf_op jit(solution)/shard_map/ppermute | solution.py:293
  27.3 4.4 %shard_map.94 = bf16[16,256,128]{2,1,0:T(8,128)(2,1)} custom-call(bf16[384,256]{1,0:T(8,128)(2,1)S(1)} %get-tuple-element.24.refs_0_, bf16[384,256]{1,0:T(8,128)(2,1)S(1)} %collective-permute-done.refs_1_, bf16[384,256]{1,0:T(8,128)(2,1)S(1)} %collective-permute-done.1.mine_ref.refs_2_, bf16[352,256]{1,0:T(8,128)(2,1)S(1)} %collective-permute-done.2.theirs_ref.refs_3_, ...), custom_call_target="tpu_custom_call" | custom-call | tf_op jit(solution)/shard_map/pallas_call | solution.py:365
  (17 shorter events, 0.1 us)
Async XLA Ops:
  0.0 6.8 %copy-start = (bf16[1024,128]{1,0:T(8,128)(2,1)S(1)}, bf16[1024,128]{1,0:T(8,128)(2,1)}, u32[]{:S(2)}) copy-start(bf16[1024,128]{1,0:T(8,128)(2,1)} %final_ref.1) | copy-start | bytes 786436
  3.7 3.6 %collective-permute-start = (bf16[384,256]{1,0:T(8,128)(2,1)S(1)}, bf16[384,256]{1,0:T(8,128)(2,1)S(1)}, u32[]{:S(2)}, u32[]{:S(2)}) collective-permute-start(bf16[384,256]{1,0:T(8,128)(2,1)S(1)} %get-tuple-element.24.refs_0_), channel_id=1, source_target_pairs={{0,1},{1,0},{2,3},{3,2},{4,5},{5,4},{6,7},{7,6},{8,9},{9,8},{10,11... | collective-permute-start | bytes 589832 | tf_op jit(solution)/shard_map/ppermute | solution.py:293
  4.2 2.7 %copy-start.1 = (f32[128]{0:T(128)S(1)}, f32[128]{0:T(128)}, u32[]{:S(2)}) copy-start(f32[128]{0:T(128)} %param.17) | copy-start | bytes 1540
  4.2 6.2 %collective-permute-start.1 = (bf16[384,256]{1,0:T(8,128)(2,1)S(1)}, bf16[384,256]{1,0:T(8,128)(2,1)S(1)}, u32[]{:S(2)}, u32[]{:S(2)}) collective-permute-start(bf16[384,256]{1,0:T(8,128)(2,1)S(1)} %get-tuple-element.28), channel_id=1, source_target_pairs={{0,4},{1,3},{2,0},{3,7},{4,8},{5,1},{6,2},{7,11},{8,12},{9,5},{10,... | collective-permute-start | bytes 589832 | tf_op jit(solution)/shard_map/ppermute | solution.py:317
  7.3 5.5 %collective-permute-start.2 = (bf16[352,256]{1,0:T(8,128)(2,1)S(1)}, bf16[352,256]{1,0:T(8,128)(2,1)S(1)}, u32[]{:S(2)}, u32[]{:S(2)}) collective-permute-start(bf16[352,256]{1,0:T(8,128)(2,1)S(1)} %slice.9), channel_id=1, source_target_pairs={{0,4},{1,3},{2,0},{3,7},{4,8},{5,1},{6,2},{7,11},{8,12},{9,5},{10,... | collective-permute-start | bytes 540680 | tf_op jit(solution)/shard_map/ppermute | solution.py:317
  10.5 5.2 %collective-permute-start.3 = (bf16[288,256]{1,0:T(8,128)(2,1)S(1)}, bf16[288,256]{1,0:T(8,128)(2,1)S(1)}, u32[]{:S(2)}, u32[]{:S(2)}) collective-permute-start(bf16[288,256]{1,0:T(8,128)(2,1)S(1)} %slice.12), channel_id=1, source_target_pairs={{0,4},{1,3},{2,0},{3,7},{4,8},{5,1},{6,2},{7,11},{8,12},{9,5},{10,... | collective-permute-start | bytes 442376 | tf_op jit(solution)/shard_map/ppermute | solution.py:317
  12.9 5.7 %collective-permute-start.4 = (bf16[384,256]{1,0:T(8,128)(2,1)S(1)}, bf16[384,256]{1,0:T(8,128)(2,1)S(1)}, u32[]{:S(2)}, u32[]{:S(2)}) collective-permute-start(bf16[384,256]{1,0:T(8,128)(2,1)S(1)} %shard_map.93), channel_id=1, source_target_pairs={{0,4},{1,3},{2,0},{3,7},{4,8},{5,1},{6,2},{7,11},{8,12},{9,5},{10,... | collective-permute-start | bytes 589832 | tf_op jit(solution)/shard_map/ppermute | solution.py:317
  14.5 8.4 %collective-permute-start.8 = (bf16[352,256]{1,0:T(8,128)(2,1)S(1)}, bf16[352,256]{1,0:T(8,128)(2,1)S(1)}, u32[]{:S(2)}, u32[]{:S(2)}) collective-permute-start(bf16[352,256]{1,0:T(8,128)(2,1)S(1)} %collective-permute-done.2.theirs_ref.refs_3_), channel_id=1, source_target_pairs={{0,1},{1,0},{2,3},{3,2},{4,5},{5,4},{6,7},{7,6},{8,9},{9,8},{10,11... | collective-permute-start | bytes 540680 | tf_op jit(solution)/shard_map/ppermute | solution.py:293
  15.6 5.1 %collective-permute-start.5 = (bf16[288,256]{1,0:T(8,128)(2,1)S(1)}, bf16[288,256]{1,0:T(8,128)(2,1)S(1)}, u32[]{:S(2)}, u32[]{:S(2)}) collective-permute-start(bf16[288,256]{1,0:T(8,128)(2,1)S(1)} %collective-permute-done.3.refs_4_), channel_id=1, source_target_pairs={{0,4},{1,3},{2,0},{3,7},{4,8},{5,1},{6,2},{7,11},{8,12},{9,5},{10,... | collective-permute-start | bytes 442376 | tf_op jit(solution)/shard_map/ppermute | solution.py:317
  17.7 5.2 %collective-permute-start.7 = (bf16[384,256]{1,0:T(8,128)(2,1)S(1)}, bf16[384,256]{1,0:T(8,128)(2,1)S(1)}, u32[]{:S(2)}, u32[]{:S(2)}) collective-permute-start(bf16[384,256]{1,0:T(8,128)(2,1)S(1)} %collective-permute-done.1.mine_ref.refs_2_), channel_id=1, source_target_pairs={{0,1},{1,0},{2,3},{3,2},{4,5},{5,4},{6,7},{7,6},{8,9},{9,8},{10,11... | collective-permute-start | bytes 589832 | tf_op jit(solution)/shard_map/ppermute | solution.py:293
  18.6 7.4 %collective-permute-start.11 = (bf16[384,256]{1,0:T(8,128)(2,1)S(1)}, bf16[384,256]{1,0:T(8,128)(2,1)S(1)}, u32[]{:S(2)}, u32[]{:S(2)}) collective-permute-start(bf16[384,256]{1,0:T(8,128)(2,1)S(1)} %collective-permute-done.4.refs_5_), channel_id=1, source_target_pairs={{0,1},{1,0},{2,3},{3,2},{4,5},{5,4},{6,7},{7,6},{8,9},{9,8},{10,11... | collective-permute-start | bytes 589832 | tf_op jit(solution)/shard_map/ppermute | solution.py:293
  18.6 5.4 %collective-permute-start.6 = (bf16[320,256]{1,0:T(8,128)(2,1)S(1)}, bf16[320,256]{1,0:T(8,128)(2,1)S(1)}, u32[]{:S(2)}, u32[]{:S(2)}) collective-permute-start(bf16[320,256]{1,0:T(8,128)(2,1)S(1)} %slice.13), channel_id=1, source_target_pairs={{0,4},{1,3},{2,0},{3,7},{4,8},{5,1},{6,2},{7,11},{8,12},{9,5},{10,... | collective-permute-start | bytes 491528 | tf_op jit(solution)/shard_map/ppermute | solution.py:317
  20.8 5.1 %collective-permute-start.9 = (bf16[288,256]{1,0:T(8,128)(2,1)S(1)}, bf16[288,256]{1,0:T(8,128)(2,1)S(1)}, u32[]{:S(2)}, u32[]{:S(2)}) collective-permute-start(bf16[288,256]{1,0:T(8,128)(2,1)S(1)} %collective-permute-done.5.refs_6_), channel_id=1, source_target_pairs={{0,4},{1,3},{2,0},{3,7},{4,8},{5,1},{6,2},{7,11},{8,12},{9,5},{10,... | collective-permute-start | bytes 442376 | tf_op jit(solution)/shard_map/ppermute | solution.py:317
  22.9 3.1 %collective-permute-start.10 = (bf16[288,256]{1,0:T(8,128)(2,1)S(1)}, bf16[288,256]{1,0:T(8,128)(2,1)S(1)}, u32[]{:S(2)}, u32[]{:S(2)}) collective-permute-start(bf16[288,256]{1,0:T(8,128)(2,1)S(1)} %collective-permute-done.3.refs_4_), channel_id=1, source_target_pairs={{0,1},{1,0},{2,3},{3,2},{4,5},{5,4},{6,7},{7,6},{8,9},{9,8},{10,11... | collective-permute-start | bytes 442376 | tf_op jit(solution)/shard_map/ppermute | solution.py:293
  24.0 2.0 %collective-permute-start.13 = (bf16[320,256]{1,0:T(8,128)(2,1)S(1)}, bf16[320,256]{1,0:T(8,128)(2,1)S(1)}, u32[]{:S(2)}, u32[]{:S(2)}) collective-permute-start(bf16[320,256]{1,0:T(8,128)(2,1)S(1)} %collective-permute-done.6.refs_7_), channel_id=1, source_target_pairs={{0,1},{1,0},{2,3},{3,2},{4,5},{5,4},{6,7},{7,6},{8,9},{9,8},{10,11... | collective-permute-start | bytes 491528 | tf_op jit(solution)/shard_map/ppermute | solution.py:293
  24.0 2.0 %collective-permute-start.12 = (bf16[288,256]{1,0:T(8,128)(2,1)S(1)}, bf16[288,256]{1,0:T(8,128)(2,1)S(1)}, u32[]{:S(2)}, u32[]{:S(2)}) collective-permute-start(bf16[288,256]{1,0:T(8,128)(2,1)S(1)} %collective-permute-done.5.refs_6_), channel_id=1, source_target_pairs={{0,1},{1,0},{2,3},{3,2},{4,5},{5,4},{6,7},{7,6},{8,9},{9,8},{10,11... | collective-permute-start | bytes 442376 | tf_op jit(solution)/shard_map/ppermute | solution.py:293
  25.9 1.4 %collective-permute-start.14 = (bf16[288,256]{1,0:T(8,128)(2,1)S(1)}, bf16[288,256]{1,0:T(8,128)(2,1)S(1)}, u32[]{:S(2)}, u32[]{:S(2)}) collective-permute-start(bf16[288,256]{1,0:T(8,128)(2,1)S(1)} %collective-permute-done.9.refs_8_), channel_id=1, source_target_pairs={{0,1},{1,0},{2,3},{3,2},{4,5},{5,4},{6,7},{7,6},{8,9},{9,8},{10,11... | collective-permute-start | bytes 442376 | tf_op jit(solution)/shard_map/ppermute | solution.py:293

commit v10 on v9

--- a/solution.py
+++ b/solution.py
@@ -66,23 +66,24 @@
         (second_offset_hbm, second_offset_ref),
     ]
     some = samples // CHUNKS
+    copies = [
+        pltpu.make_async_copy(src, dst, sems.at[CHUNKS + n]) for n, (src, dst) in enumerate(small)
+    ]
+    for copy in copies:
+        copy.start()
     large = []
     for n in range(CHUNKS):
         rows = pl.ds(n * some, some)
         large.append(pltpu.make_async_copy(x_hbm.at[rows], x_ref.at[rows], sems.at[n]))
         large[-1].start()
-    copies = [
-        pltpu.make_async_copy(src, dst, sems.at[CHUNKS + n]) for n, (src, dst) in enumerate(small)
-    ]
-    for copy in copies:
-        copy.start()
     for copy in copies:
         copy.wait()
 
-    first = jnp.concatenate([first_ref[...]] * fold, axis=0)
+    first = jnp.concatenate([first_ref[...].astype(jnp.float32)] * fold, axis=0).T
+    first = first.astype(jnp.bfloat16)
     first_offset = jnp.concatenate([first_offset_ref[...]] * fold, axis=1)
-    second = repeat_rows(second_ref[...].astype(jnp.float32), samples)
-    row = lax.broadcasted_iota(jnp.int32, (width, 1), 0)
+    second = repeat_rows(second_ref[...].astype(jnp.float32), samples).T
+    column = lax.broadcasted_iota(jnp.int32, (1, width), 1)
     spot = lax.broadcasted_iota(jnp.int32, (width, hidden), 0)
     channel = lax.broadcasted_iota(jnp.int32, (width, hidden), 1)
     second_offset = jnp.sum(
@@ -95,8 +96,7 @@
     member = lax.broadcasted_iota(jnp.int32, (tile // fold, tile), 1)
     gather = (member // fold == group).astype(jnp.bfloat16)
 
-    dims = (((1,), (1,)), ((), ()))
-    right = [jnp.zeros((width, tile), jnp.float32) for _ in range(tiles)]
+    right = [jnp.zeros((tile, width), jnp.float32) for _ in range(tiles)]
     for s in range(samples):
         if s % some == 0:
             large[s // some].wait()
@@ -109,18 +109,18 @@
             values = values * lax.rsqrt(variance + 1e-05) * gain_ref[...] + shift_ref[...]
             normed.append(values.astype(jnp.bfloat16))
         normed = jnp.concatenate(normed, axis=0)
-        second_here = jnp.where(row % samples == s, second, 0.0).astype(jnp.bfloat16)
+        second_here = jnp.where(column % samples == s, second, 0.0).astype(jnp.bfloat16)
         for t in range(tiles):
             part = normed[t * tile : (t + 1) * tile]
-            right[t] += lax.dot_general(second_here, part, dims, preferred_element_type=jnp.float32)
-            left = lax.dot_general(part, first, dims, preferred_element_type=jnp.float32)
+            right[t] += jnp.dot(part, second_here, preferred_element_type=jnp.float32)
+            left = jnp.dot(part, first, preferred_element_type=jnp.float32)
             left = jnp.where(own, left + first_offset, 0.0).astype(jnp.bfloat16)
             low = s * groups + t * (tile // fold)
             packed_ref[low : low + tile // fold, :] = jnp.dot(
                 gather, left, preferred_element_type=jnp.float32
             )
     for t in range(tiles):
-        value = (right[t] + second_offset).astype(jnp.bfloat16)
+        value = (right[t].T + second_offset).astype(jnp.bfloat16)
         keep_ref[t * width : (t + 1) * width, :] = value
         give_ref[t * width : (t + 1) * width, :] = value
     across = tile // LANES

time: 31.9 us -> 31.7 us (level)
  no operation moved by 1% of the time
where the time goes in v10:
time: 31.7 us; the launch traced here: 31.5 us
  starting transfers between devices  14.9 us (47%)
  Pallas kernels  8.31 us (26%)
  waiting for transfers between devices  8.17 us (26%)
    ppermute x7, starting transfers between devices, per_device(): landed = [lax.ppermute(x, 'row', around) for x in flying]  13.9 us
    ppermute x7, waiting for transfers between devices, per_device(): landed = [lax.ppermute(x, 'row', around) for x in flying]  6.81 us
    pallas_call x1, Pallas kernels, per_device(): pl.pallas_call(functools.partial(pair_kernel, places, gridded, rows_here,...  4.43 us
    pallas_call x1, Pallas kernels, per_device(): pl.pallas_call(functools.partial(project_kernel, rows_here), out_shape=[r...  3.47 us
    ppermute x8, waiting for transfers between devices, swap(): return lax.ppermute(value, 'row', [(r, r ^ 1) for r in range(size)])  1.36 us
    ppermute x8, starting transfers between devices, swap(): return lax.ppermute(value, 'row', [(r, r ^ 1) for r in range(size)])  1.04 us
  transfers between devices with their start and end apart: 15, of which 8 were waited for; matrix products, arithmetic and copies ran while one was open for 0% of the time, Pallas kernels for 1%

profile of v10, /device:TPU:0, one launch (start us, length us, event | category | flops | bytes accessed | tf_op | source)
XLA Modules:
  0.0 31.5 jit_solution(11633498150778409686)
XLA Ops:
  0.0 3.5 %shard_map.91 = (bf16[384,256]{1,0:T(8,128)(2,1)S(1)}, bf16[384,256]{1,0:T(8,128)(2,1)S(1)}) custom-call(bf16[8,256,256]{2,1,0:T(8,128)(2,1)} %x_hbm.1, f32[1,256]{1,0:T(1,128)} %bitcast.10, f32[1,256]{1,0:T(1,128)} %bitcast.11, bf16[32,256]{1,0:T(8,128)(2,1)} %bitcast.8, f32[1,32]{1,0:T(1,128)} %bitcast.12, bf16[32,256]{1,0:T(8,128)(2,1)} %bitcast.9, ...), custom_call_target="tpu_custom_call" | custom-call | flops 536870912 | bytes 1048576 | tf_op jit(solution)/shard_map/pallas_call | solution.py:250
  3.5 0.5 %collective-permute-start = (bf16[384,256]{1,0:T(8,128)(2,1)S(1)}, bf16[384,256]{1,0:T(8,128)(2,1)S(1)}, u32[]{:S(2)}, u32[]{:S(2)}) collective-permute-start(bf16[384,256]{1,0:T(8,128)(2,1)S(1)} %get-tuple-element.24.refs_0_), channel_id=1, source_target_pairs={{0,1},{1,0},{2,3},{3,2},{4,5},{5,4},{6,7},{7,6},{8,9},{9,8},{10,11... | collective-permute-start | bytes 589832 | tf_op jit(solution)/shard_map/ppermute | solution.py:293
  4.0 2.6 %collective-permute-start.1 = (bf16[384,256]{1,0:T(8,128)(2,1)S(1)}, bf16[384,256]{1,0:T(8,128)(2,1)S(1)}, u32[]{:S(2)}, u32[]{:S(2)}) collective-permute-start(bf16[384,256]{1,0:T(8,128)(2,1)S(1)} %get-tuple-element.28), channel_id=1, source_target_pairs={{0,4},{1,3},{2,0},{3,7},{4,8},{5,1},{6,2},{7,11},{8,12},{9,5},{10,... | collective-permute-start | bytes 589832 | tf_op jit(solution)/shard_map/ppermute | solution.py:317
  6.6 0.4 %shard_map.92 = (bf16[128,1024]{1,0:T(8,128)(2,1)S(1)}, f32[1,128]{1,0:T(1,128)S(1)}) custom-call(bf16[1024,128]{1,0:T(8,128)(2,1)S(1)} %copy-done, f32[1,128]{1,0:T(1,128)S(1)} %bitcast.7), custom_call_target="tpu_custom_call" | custom-call | flops 268435456 | bytes 1048576 | tf_op jit(solution)/shard_map/pallas_call | solution.py:295
  7.1 0.0 collective-permute-done.refs_1_
  7.1 1.6 %collective-permute-start.2 = (bf16[352,256]{1,0:T(8,128)(2,1)S(1)}, bf16[352,256]{1,0:T(8,128)(2,1)S(1)}, u32[]{:S(2)}, u32[]{:S(2)}) collective-permute-start(bf16[352,256]{1,0:T(8,128)(2,1)S(1)} %slice.9), channel_id=1, source_target_pairs={{0,4},{1,3},{2,0},{3,7},{4,8},{5,1},{6,2},{7,11},{8,12},{9,5},{10,... | collective-permute-start | bytes 540680 | tf_op jit(solution)/shard_map/ppermute | solution.py:317
  8.7 1.5 %collective-permute-done.1.mine_ref.refs_2_ = bf16[384,256]{1,0:T(8,128)(2,1)S(1)} collective-permute-done((bf16[384,256]{1,0:T(8,128)(2,1)S(1)}, bf16[384,256]{1,0:T(8,128)(2,1)S(1)}, u32[]{:S(2)}, u32[]{:S(2)}) %collective-permute-start.1) | collective-permute-done | bytes 196640 | tf_op jit(solution)/shard_map/ppermute | solution.py:317
  10.2 2.1 %collective-permute-start.3 = (bf16[288,256]{1,0:T(8,128)(2,1)S(1)}, bf16[288,256]{1,0:T(8,128)(2,1)S(1)}, u32[]{:S(2)}, u32[]{:S(2)}) collective-permute-start(bf16[288,256]{1,0:T(8,128)(2,1)S(1)} %slice.12), channel_id=1, source_target_pairs={{0,4},{1,3},{2,0},{3,7},{4,8},{5,1},{6,2},{7,11},{8,12},{9,5},{10,... | collective-permute-start | bytes 442376 | tf_op jit(solution)/shard_map/ppermute | solution.py:317
  12.4 0.3 collective-permute-done.2.theirs_ref.refs_3_
  12.7 1.7 %collective-permute-start.4 = (bf16[384,256]{1,0:T(8,128)(2,1)S(1)}, bf16[384,256]{1,0:T(8,128)(2,1)S(1)}, u32[]{:S(2)}, u32[]{:S(2)}) collective-permute-start(bf16[384,256]{1,0:T(8,128)(2,1)S(1)} %shard_map.93), channel_id=1, source_target_pairs={{0,4},{1,3},{2,0},{3,7},{4,8},{5,1},{6,2},{7,11},{8,12},{9,5},{10,... | collective-permute-start | bytes 589832 | tf_op jit(solution)/shard_map/ppermute | solution.py:317
  14.3 1.1 %collective-permute-done.3.refs_4_ = bf16[288,256]{1,0:T(8,128)(2,1)S(1)} collective-permute-done((bf16[288,256]{1,0:T(8,128)(2,1)S(1)}, bf16[288,256]{1,0:T(8,128)(2,1)S(1)}, u32[]{:S(2)}, u32[]{:S(2)}) %collective-permute-start.3) | collective-permute-done | bytes 147488 | tf_op jit(solution)/shard_map/ppermute | solution.py:317
  15.4 2.1 %collective-permute-start.5 = (bf16[288,256]{1,0:T(8,128)(2,1)S(1)}, bf16[288,256]{1,0:T(8,128)(2,1)S(1)}, u32[]{:S(2)}, u32[]{:S(2)}) collective-permute-start(bf16[288,256]{1,0:T(8,128)(2,1)S(1)} %collective-permute-done.3.refs_4_), channel_id=1, source_target_pairs={{0,4},{1,3},{2,0},{3,7},{4,8},{5,1},{6,2},{7,11},{8,12},{9,5},{10,... | collective-permute-start | bytes 442376 | tf_op jit(solution)/shard_map/ppermute | solution.py:317
  17.5 0.0 collective-permute-start.7
  17.5 0.8 %collective-permute-done.4.refs_5_ = bf16[384,256]{1,0:T(8,128)(2,1)S(1)} collective-permute-done((bf16[384,256]{1,0:T(8,128)(2,1)S(1)}, bf16[384,256]{1,0:T(8,128)(2,1)S(1)}, u32[]{:S(2)}, u32[]{:S(2)}) %collective-permute-start.4) | collective-permute-done | bytes 196640 | tf_op jit(solution)/shard_map/ppermute | solution.py:317
  18.4 1.7 %collective-permute-start.6 = (bf16[320,256]{1,0:T(8,128)(2,1)S(1)}, bf16[320,256]{1,0:T(8,128)(2,1)S(1)}, u32[]{:S(2)}, u32[]{:S(2)}) collective-permute-start(bf16[320,256]{1,0:T(8,128)(2,1)S(1)} %slice.13), channel_id=1, source_target_pairs={{0,4},{1,3},{2,0},{3,7},{4,8},{5,1},{6,2},{7,11},{8,12},{9,5},{10,... | collective-permute-start | bytes 491528 | tf_op jit(solution)/shard_map/ppermute | solution.py:317
  20.1 0.5 %collective-permute-done.5.refs_6_ = bf16[288,256]{1,0:T(8,128)(2,1)S(1)} collective-permute-done((bf16[288,256]{1,0:T(8,128)(2,1)S(1)}, bf16[288,256]{1,0:T(8,128)(2,1)S(1)}, u32[]{:S(2)}, u32[]{:S(2)}) %collective-permute-start.5) | collective-permute-done | bytes 147488 | tf_op jit(solution)/shard_map/ppermute | solution.py:317
  20.6 2.1 %collective-permute-start.9 = (bf16[288,256]{1,0:T(8,128)(2,1)S(1)}, bf16[288,256]{1,0:T(8,128)(2,1)S(1)}, u32[]{:S(2)}, u32[]{:S(2)}) collective-permute-start(bf16[288,256]{1,0:T(8,128)(2,1)S(1)} %collective-permute-done.5.refs_6_), channel_id=1, source_target_pairs={{0,4},{1,3},{2,0},{3,7},{4,8},{5,1},{6,2},{7,11},{8,12},{9,5},{10,... | collective-permute-start | bytes 442376 | tf_op jit(solution)/shard_map/ppermute | solution.py:317
  22.7 0.0 collective-permute-done.8.refs_10_
  22.7 0.0 collective-permute-start.10
  22.7 1.1 %collective-permute-done.6.refs_7_ = bf16[320,256]{1,0:T(8,128)(2,1)S(1)} collective-permute-done((bf16[320,256]{1,0:T(8,128)(2,1)S(1)}, bf16[320,256]{1,0:T(8,128)(2,1)S(1)}, u32[]{:S(2)}, u32[]{:S(2)}) %collective-permute-start.6) | collective-permute-done | bytes 163872 | tf_op jit(solution)/shard_map/ppermute | solution.py:317
  23.8 0.5 %collective-permute-start.12 = (bf16[288,256]{1,0:T(8,128)(2,1)S(1)}, bf16[288,256]{1,0:T(8,128)(2,1)S(1)}, u32[]{:S(2)}, u32[]{:S(2)}) collective-permute-start(bf16[288,256]{1,0:T(8,128)(2,1)S(1)} %collective-permute-done.5.refs_6_), channel_id=1, source_target_pairs={{0,1},{1,0},{2,3},{3,2},{4,5},{5,4},{6,7},{7,6},{8,9},{9,8},{10,11... | collective-permute-start | bytes 442376 | tf_op jit(solution)/shard_map/ppermute | solution.py:293
  24.3 1.5 %collective-permute-done.9.refs_8_ = bf16[288,256]{1,0:T(8,128)(2,1)S(1)} collective-permute-done((bf16[288,256]{1,0:T(8,128)(2,1)S(1)}, bf16[288,256]{1,0:T(8,128)(2,1)S(1)}, u32[]{:S(2)}, u32[]{:S(2)}) %collective-permute-start.9) | collective-permute-done | bytes 147488 | tf_op jit(solution)/shard_map/ppermute | solution.py:317
  25.8 1.3 %collective-permute-done.14.refs_15_ = bf16[288,256]{1,0:T(8,128)(2,1)S(1)} collective-permute-done((bf16[288,256]{1,0:T(8,128)(2,1)S(1)}, bf16[288,256]{1,0:T(8,128)(2,1)S(1)}, u32[]{:S(2)}, u32[]{:S(2)}) %collective-permute-start.14) | collective-permute-done | bytes 147488 | tf_op jit(solution)/shard_map/ppermute | solution.py:293
  27.1 4.4 %shard_map.94 = bf16[16,256,128]{2,1,0:T(8,128)(2,1)} custom-call(bf16[384,256]{1,0:T(8,128)(2,1)S(1)} %get-tuple-element.24.refs_0_, bf16[384,256]{1,0:T(8,128)(2,1)S(1)} %collective-permute-done.refs_1_, bf16[384,256]{1,0:T(8,128)(2,1)S(1)} %collective-permute-done.1.mine_ref.refs_2_, bf16[352,256]{1,0:T(8,128)(2,1)S(1)} %collective-permute-done.2.theirs_ref.refs_3_, ...), custom_call_target="tpu_custom_call" | custom-call | tf_op jit(solution)/shard_map/pallas_call | solution.py:365
  (17 shorter events, 0.1 us)
Async XLA Ops:
  0.0 6.6 %copy-start = (bf16[1024,128]{1,0:T(8,128)(2,1)S(1)}, bf16[1024,128]{1,0:T(8,128)(2,1)}, u32[]{:S(2)}) copy-start(bf16[1024,128]{1,0:T(8,128)(2,1)} %final_ref.1) | copy-start | bytes 786436
  3.5 3.6 %collective-permute-start = (bf16[384,256]{1,0:T(8,128)(2,1)S(1)}, bf16[384,256]{1,0:T(8,128)(2,1)S(1)}, u32[]{:S(2)}, u32[]{:S(2)}) collective-permute-start(bf16[384,256]{1,0:T(8,128)(2,1)S(1)} %get-tuple-element.24.refs_0_), channel_id=1, source_target_pairs={{0,1},{1,0},{2,3},{3,2},{4,5},{5,4},{6,7},{7,6},{8,9},{9,8},{10,11... | collective-permute-start | bytes 589832 | tf_op jit(solution)/shard_map/ppermute | solution.py:293
  4.0 2.7 %copy-start.1 = (f32[128]{0:T(128)S(1)}, f32[128]{0:T(128)}, u32[]{:S(2)}) copy-start(f32[128]{0:T(128)} %param.17) | copy-start | bytes 1540
  4.0 6.2 %collective-permute-start.1 = (bf16[384,256]{1,0:T(8,128)(2,1)S(1)}, bf16[384,256]{1,0:T(8,128)(2,1)S(1)}, u32[]{:S(2)}, u32[]{:S(2)}) collective-permute-start(bf16[384,256]{1,0:T(8,128)(2,1)S(1)} %get-tuple-element.28), channel_id=1, source_target_pairs={{0,4},{1,3},{2,0},{3,7},{4,8},{5,1},{6,2},{7,11},{8,12},{9,5},{10,... | collective-permute-start | bytes 589832 | tf_op jit(solution)/shard_map/ppermute | solution.py:317
  7.1 5.5 %collective-permute-start.2 = (bf16[352,256]{1,0:T(8,128)(2,1)S(1)}, bf16[352,256]{1,0:T(8,128)(2,1)S(1)}, u32[]{:S(2)}, u32[]{:S(2)}) collective-permute-start(bf16[352,256]{1,0:T(8,128)(2,1)S(1)} %slice.9), channel_id=1, source_target_pairs={{0,4},{1,3},{2,0},{3,7},{4,8},{5,1},{6,2},{7,11},{8,12},{9,5},{10,... | collective-permute-start | bytes 540680 | tf_op jit(solution)/shard_map/ppermute | solution.py:317
  10.2 5.2 %collective-permute-start.3 = (bf16[288,256]{1,0:T(8,128)(2,1)S(1)}, bf16[288,256]{1,0:T(8,128)(2,1)S(1)}, u32[]{:S(2)}, u32[]{:S(2)}) collective-permute-start(bf16[288,256]{1,0:T(8,128)(2,1)S(1)} %slice.12), channel_id=1, source_target_pairs={{0,4},{1,3},{2,0},{3,7},{4,8},{5,1},{6,2},{7,11},{8,12},{9,5},{10,... | collective-permute-start | bytes 442376 | tf_op jit(solution)/shard_map/ppermute | solution.py:317
  12.7 5.7 %collective-permute-start.4 = (bf16[384,256]{1,0:T(8,128)(2,1)S(1)}, bf16[384,256]{1,0:T(8,128)(2,1)S(1)}, u32[]{:S(2)}, u32[]{:S(2)}) collective-permute-start(bf16[384,256]{1,0:T(8,128)(2,1)S(1)} %shard_map.93), channel_id=1, source_target_pairs={{0,4},{1,3},{2,0},{3,7},{4,8},{5,1},{6,2},{7,11},{8,12},{9,5},{10,... | collective-permute-start | bytes 589832 | tf_op jit(solution)/shard_map/ppermute | solution.py:317
  14.3 8.4 %collective-permute-start.8 = (bf16[352,256]{1,0:T(8,128)(2,1)S(1)}, bf16[352,256]{1,0:T(8,128)(2,1)S(1)}, u32[]{:S(2)}, u32[]{:S(2)}) collective-permute-start(bf16[352,256]{1,0:T(8,128)(2,1)S(1)} %collective-permute-done.2.theirs_ref.refs_3_), channel_id=1, source_target_pairs={{0,1},{1,0},{2,3},{3,2},{4,5},{5,4},{6,7},{7,6},{8,9},{9,8},{10,11... | collective-permute-start | bytes 540680 | tf_op jit(solution)/shard_map/ppermute | solution.py:293
  15.4 5.1 %collective-permute-start.5 = (bf16[288,256]{1,0:T(8,128)(2,1)S(1)}, bf16[288,256]{1,0:T(8,128)(2,1)S(1)}, u32[]{:S(2)}, u32[]{:S(2)}) collective-permute-start(bf16[288,256]{1,0:T(8,128)(2,1)S(1)} %collective-permute-done.3.refs_4_), channel_id=1, source_target_pairs={{0,4},{1,3},{2,0},{3,7},{4,8},{5,1},{6,2},{7,11},{8,12},{9,5},{10,... | collective-permute-start | bytes 442376 | tf_op jit(solution)/shard_map/ppermute | solution.py:317
  17.5 5.2 %collective-permute-start.7 = (bf16[384,256]{1,0:T(8,128)(2,1)S(1)}, bf16[384,256]{1,0:T(8,128)(2,1)S(1)}, u32[]{:S(2)}, u32[]{:S(2)}) collective-permute-start(bf16[384,256]{1,0:T(8,128)(2,1)S(1)} %collective-permute-done.1.mine_ref.refs_2_), channel_id=1, source_target_pairs={{0,1},{1,0},{2,3},{3,2},{4,5},{5,4},{6,7},{7,6},{8,9},{9,8},{10,11... | collective-permute-start | bytes 589832 | tf_op jit(solution)/shard_map/ppermute | solution.py:293
  18.4 7.4 %collective-permute-start.11 = (bf16[384,256]{1,0:T(8,128)(2,1)S(1)}, bf16[384,256]{1,0:T(8,128)(2,1)S(1)}, u32[]{:S(2)}, u32[]{:S(2)}) collective-permute-start(bf16[384,256]{1,0:T(8,128)(2,1)S(1)} %collective-permute-done.4.refs_5_), channel_id=1, source_target_pairs={{0,1},{1,0},{2,3},{3,2},{4,5},{5,4},{6,7},{7,6},{8,9},{9,8},{10,11... | collective-permute-start | bytes 589832 | tf_op jit(solution)/shard_map/ppermute | solution.py:293
  18.4 5.4 %collective-permute-start.6 = (bf16[320,256]{1,0:T(8,128)(2,1)S(1)}, bf16[320,256]{1,0:T(8,128)(2,1)S(1)}, u32[]{:S(2)}, u32[]{:S(2)}) collective-permute-start(bf16[320,256]{1,0:T(8,128)(2,1)S(1)} %slice.13), channel_id=1, source_target_pairs={{0,4},{1,3},{2,0},{3,7},{4,8},{5,1},{6,2},{7,11},{8,12},{9,5},{10,... | collective-permute-start | bytes 491528 | tf_op jit(solution)/shard_map/ppermute | solution.py:317
  20.6 5.1 %collective-permute-start.9 = (bf16[288,256]{1,0:T(8,128)(2,1)S(1)}, bf16[288,256]{1,0:T(8,128)(2,1)S(1)}, u32[]{:S(2)}, u32[]{:S(2)}) collective-permute-start(bf16[288,256]{1,0:T(8,128)(2,1)S(1)} %collective-permute-done.5.refs_6_), channel_id=1, source_target_pairs={{0,4},{1,3},{2,0},{3,7},{4,8},{5,1},{6,2},{7,11},{8,12},{9,5},{10,... | collective-permute-start | bytes 442376 | tf_op jit(solution)/shard_map/ppermute | solution.py:317
  22.7 3.1 %collective-permute-start.10 = (bf16[288,256]{1,0:T(8,128)(2,1)S(1)}, bf16[288,256]{1,0:T(8,128)(2,1)S(1)}, u32[]{:S(2)}, u32[]{:S(2)}) collective-permute-start(bf16[288,256]{1,0:T(8,128)(2,1)S(1)} %collective-permute-done.3.refs_4_), channel_id=1, source_target_pairs={{0,1},{1,0},{2,3},{3,2},{4,5},{5,4},{6,7},{7,6},{8,9},{9,8},{10,11... | collective-permute-start | bytes 442376 | tf_op jit(solution)/shard_map/ppermute | solution.py:293
  23.8 2.0 %collective-permute-start.13 = (bf16[320,256]{1,0:T(8,128)(2,1)S(1)}, bf16[320,256]{1,0:T(8,128)(2,1)S(1)}, u32[]{:S(2)}, u32[]{:S(2)}) collective-permute-start(bf16[320,256]{1,0:T(8,128)(2,1)S(1)} %collective-permute-done.6.refs_7_), channel_id=1, source_target_pairs={{0,1},{1,0},{2,3},{3,2},{4,5},{5,4},{6,7},{7,6},{8,9},{9,8},{10,11... | collective-permute-start | bytes 491528 | tf_op jit(solution)/shard_map/ppermute | solution.py:293
  23.8 2.0 %collective-permute-start.12 = (bf16[288,256]{1,0:T(8,128)(2,1)S(1)}, bf16[288,256]{1,0:T(8,128)(2,1)S(1)}, u32[]{:S(2)}, u32[]{:S(2)}) collective-permute-start(bf16[288,256]{1,0:T(8,128)(2,1)S(1)} %collective-permute-done.5.refs_6_), channel_id=1, source_target_pairs={{0,1},{1,0},{2,3},{3,2},{4,5},{5,4},{6,7},{7,6},{8,9},{9,8},{10,11... | collective-permute-start | bytes 442376 | tf_op jit(solution)/shard_map/ppermute | solution.py:293
  25.7 1.4 %collective-permute-start.14 = (bf16[288,256]{1,0:T(8,128)(2,1)S(1)}, bf16[288,256]{1,0:T(8,128)(2,1)S(1)}, u32[]{:S(2)}, u32[]{:S(2)}) collective-permute-start(bf16[288,256]{1,0:T(8,128)(2,1)S(1)} %collective-permute-done.9.refs_8_), channel_id=1, source_target_pairs={{0,1},{1,0},{2,3},{3,2},{4,5},{5,4},{6,7},{7,6},{8,9},{9,8},{10,11... | collective-permute-start | bytes 442376 | tf_op jit(solution)/shard_map/ppermute | solution.py:293

commit v11 on v10

--- a/solution.py
+++ b/solution.py
@@ -97,28 +97,39 @@
     gather = (member // fold == group).astype(jnp.bfloat16)
 
     right = [jnp.zeros((tile, width), jnp.float32) for _ in range(tiles)]
-    for s in range(samples):
-        if s % some == 0:
-            large[s // some].wait()
-        normed = []
-        for low in range(0, residues, BLOCK):
-            values = x_ref[s, low : low + BLOCK, :].astype(jnp.float32)
-            center = jnp.mean(values, axis=-1, keepdims=True)
-            values = values - center
-            variance = jnp.mean(jnp.square(values), axis=-1, keepdims=True)
-            values = values * lax.rsqrt(variance + 1e-05) * gain_ref[...] + shift_ref[...]
-            normed.append(values.astype(jnp.bfloat16))
-        normed = jnp.concatenate(normed, axis=0)
-        second_here = jnp.where(column % samples == s, second, 0.0).astype(jnp.bfloat16)
+    for chunk in range(CHUNKS):
+        large[chunk].wait()
+        normed, placed = [], []
+        for s in range(chunk * some, (chunk + 1) * some):
+            pieces = []
+            for low in range(0, residues, BLOCK):
+                values = x_ref[s, low : low + BLOCK, :].astype(jnp.float32)
+                center = jnp.mean(values, axis=-1, keepdims=True)
+                values = values - center
+                variance = jnp.mean(jnp.square(values), axis=-1, keepdims=True)
+                values = values * lax.rsqrt(variance + 1e-05) * gain_ref[...] + shift_ref[...]
+                pieces.append(values.astype(jnp.bfloat16))
+            normed.append(jnp.concatenate(pieces, axis=0))
+            placed.append(jnp.where(column % samples == s, second, 0.0).astype(jnp.bfloat16))
+        placed = jnp.concatenate(placed, axis=0)
         for t in range(tiles):
-            part = normed[t * tile : (t + 1) * tile]
-            right[t] += jnp.dot(part, second_here, preferred_element_type=jnp.float32)
-            left = jnp.dot(part, first, preferred_element_type=jnp.float32)
-            left = jnp.where(own, left + first_offset, 0.0).astype(jnp.bfloat16)
-            low = s * groups + t * (tile // fold)
-            packed_ref[low : low + tile // fold, :] = jnp.dot(
-                gather, left, preferred_element_type=jnp.float32
+            parts = [x[t * tile : (t + 1) * tile] for x in normed]
+            right[t] += jnp.dot(
+                jnp.concatenate(parts, axis=1), placed, preferred_element_type=jnp.float32
             )
+            left = jnp.dot(
+                jnp.concatenate(parts, axis=0), first, preferred_element_type=jnp.float32
+            )
+            lefts = [
+                jnp.where(own, left[n * tile : (n + 1) * tile] + first_offset, 0.0).astype(jnp.bfloat16)
+                for n in range(some)
+            ]
+            packed = jnp.dot(
+                gather, jnp.concatenate(lefts, axis=1), preferred_element_type=jnp.float32
+            )
+            for n in range(some):
+                low = (chunk * some + n) * groups + t * (tile // fold)
+                packed_ref[low : low + tile // fold, :] = packed[:, n * LANES : (n + 1) * LANES]
     for t in range(tiles):
         value = (right[t].T + second_offset).astype(jnp.bfloat16)
         keep_ref[t * width : (t + 1) * width, :] = value
@@ -195,25 +206,36 @@
             ref[base + e * here : base + (e + 2) * here, :].astype(jnp.float32)
             for ref, base, _, _ in shards
         ]
+        right = [
+            jnp.concatenate([x[k * here : (k + 1) * here] for x in both], axis=0).astype(jnp.bfloat16)
+            for k in range(2)
+        ]
+        outer = jnp.dot(left, jnp.concatenate(right, axis=1), preferred_element_type=jnp.float32)
+        outer = outer.astype(jnp.bfloat16)
         for k in range(2):
-            right = jnp.concatenate([x[k * here : (k + 1) * here] for x in both], axis=0)
-            outer = jnp.dot(left, right.astype(jnp.bfloat16), preferred_element_type=jnp.float32)
-            outer = outer.astype(jnp.bfloat16)
+            low = (e + k) * hidden
             for i in range(rows_here):
-                outer_ref[i, (e + k) * hidden : (e + k + 1) * hidden, :] = outer[
-                    i * hidden : (i + 1) * hidden
+                outer_ref[low : low + hidden, i * tile : (i + 1) * tile] = outer[
+                    i * hidden : (i + 1) * hidden, k * tile : (k + 1) * tile
                 ]
 
     first = pl.program_id(0) * tile if gridded else 0
     copies = []
-    for i in range(rows_here):
-        value = jnp.dot(weight_ref[...], outer_ref[i], preferred_element_type=jnp.float32)
-        value = value.T * (1.0 / samples) + offset_ref[...]
-        out_ref[i] = value.astype(jnp.bfloat16)
-        copies.append(
-            pltpu.make_async_copy(out_ref.at[i], out_hbm.at[i, pl.ds(first, tile)], sems.at[i])
+    some = 4
+    for group in range(0, rows_here, some):
+        values = jnp.dot(
+            weight_ref[...],
+            outer_ref[:, group * tile : (group + some) * tile],
+            preferred_element_type=jnp.float32,
         )
-        copies[-1].start()
+        for n in range(some):
+            i = group + n
+            value = values[:, n * tile : (n + 1) * tile].T * (1.0 / samples) + offset_ref[...]
+            out_ref[i] = value.astype(jnp.bfloat16)
+            copies.append(
+                pltpu.make_async_copy(out_ref.at[i], out_hbm.at[i, pl.ds(first, tile)], sems.at[i])
+            )
+            copies[-1].start()
     for copy in copies:
         copy.wait()
 
@@ -370,7 +392,7 @@
         out_specs=hbm,
         scratch_shapes=[
             pltpu.VMEM((rows_here * hidden, samples), jnp.bfloat16),
-            pltpu.VMEM((rows_here, hidden * hidden, tile), jnp.bfloat16),
+            pltpu.VMEM((hidden * hidden, rows_here * tile), jnp.bfloat16),
             pltpu.VMEM((rows_here, tile, channels), jnp.bfloat16),
             pltpu.SemaphoreType.DMA((rows_here,)),
         ],

time: 31.7 us -> 31.8 us (level)
  no operation moved by 1% of the time
where the time goes in v11:
time: 31.8 us; the launch traced here: 31.6 us
  starting transfers between devices  14.9 us (47%)
  Pallas kernels  8.38 us (26%)
  waiting for transfers between devices  8.17 us (26%)
    ppermute x7, starting transfers between devices, per_device(): landed = [lax.ppermute(x, 'row', around) for x in flying]  13.9 us
    ppermute x7, waiting for transfers between devices, per_device(): landed = [lax.ppermute(x, 'row', around) for x in flying]  6.81 us
    pallas_call x1, Pallas kernels, per_device(): pl.pallas_call(functools.partial(pair_kernel, places, gridded, rows_here,...  4.43 us
    pallas_call x1, Pallas kernels, per_device(): pl.pallas_call(functools.partial(project_kernel, rows_here), out_shape=[r...  3.54 us
    ppermute x8, waiting for transfers between devices, swap(): return lax.ppermute(value, 'row', [(r, r ^ 1) for r in range(size)])  1.36 us
    ppermute x8, starting transfers between devices, swap(): return lax.ppermute(value, 'row', [(r, r ^ 1) for r in range(size)])  1.04 us
  transfers between devices with their start and end apart: 15, of which 8 were waited for; matrix products, arithmetic and copies ran while one was open for 0% of the time, Pallas kernels for 1%

profile of v11, /device:TPU:0, one launch (start us, length us, event | category | flops | bytes accessed | tf_op | source)
XLA Modules:
  0.0 31.6 jit_solution(5785001894176456488)
XLA Ops:
  0.0 3.5 %shard_map.91 = (bf16[384,256]{1,0:T(8,128)(2,1)S(1)}, bf16[384,256]{1,0:T(8,128)(2,1)S(1)}) custom-call(bf16[8,256,256]{2,1,0:T(8,128)(2,1)} %x_hbm.1, f32[1,256]{1,0:T(1,128)} %bitcast.10, f32[1,256]{1,0:T(1,128)} %bitcast.11, bf16[32,256]{1,0:T(8,128)(2,1)} %bitcast.8, f32[1,32]{1,0:T(1,128)} %bitcast.12, bf16[32,256]{1,0:T(8,128)(2,1)} %bitcast.9, ...), custom_call_target="tpu_custom_call" | custom-call | flops 536870912 | bytes 1048576 | tf_op jit(solution)/shard_map/pallas_call | solution.py:272
  3.5 0.5 %collective-permute-start = (bf16[384,256]{1,0:T(8,128)(2,1)S(1)}, bf16[384,256]{1,0:T(8,128)(2,1)S(1)}, u32[]{:S(2)}, u32[]{:S(2)}) collective-permute-start(bf16[384,256]{1,0:T(8,128)(2,1)S(1)} %get-tuple-element.24.refs_0_), channel_id=1, source_target_pairs={{0,1},{1,0},{2,3},{3,2},{4,5},{5,4},{6,7},{7,6},{8,9},{9,8},{10,11... | collective-permute-start | bytes 589832 | tf_op jit(solution)/shard_map/ppermute | solution.py:315
  4.1 2.6 %collective-permute-start.1 = (bf16[384,256]{1,0:T(8,128)(2,1)S(1)}, bf16[384,256]{1,0:T(8,128)(2,1)S(1)}, u32[]{:S(2)}, u32[]{:S(2)}) collective-permute-start(bf16[384,256]{1,0:T(8,128)(2,1)S(1)} %get-tuple-element.28), channel_id=1, source_target_pairs={{0,4},{1,3},{2,0},{3,7},{4,8},{5,1},{6,2},{7,11},{8,12},{9,5},{10,... | collective-permute-start | bytes 589832 | tf_op jit(solution)/shard_map/ppermute | solution.py:339
  6.7 0.4 %shard_map.92 = (bf16[128,1024]{1,0:T(8,128)(2,1)S(1)}, f32[1,128]{1,0:T(1,128)S(1)}) custom-call(bf16[1024,128]{1,0:T(8,128)(2,1)S(1)} %copy-done, f32[1,128]{1,0:T(1,128)S(1)} %bitcast.7), custom_call_target="tpu_custom_call" | custom-call | flops 268435456 | bytes 1048576 | tf_op jit(solution)/shard_map/pallas_call | solution.py:317
  7.2 1.6 %collective-permute-start.2 = (bf16[352,256]{1,0:T(8,128)(2,1)S(1)}, bf16[352,256]{1,0:T(8,128)(2,1)S(1)}, u32[]{:S(2)}, u32[]{:S(2)}) collective-permute-start(bf16[352,256]{1,0:T(8,128)(2,1)S(1)} %slice.9), channel_id=1, source_target_pairs={{0,4},{1,3},{2,0},{3,7},{4,8},{5,1},{6,2},{7,11},{8,12},{9,5},{10,... | collective-permute-start | bytes 540680 | tf_op jit(solution)/shard_map/ppermute | solution.py:339
  8.8 1.5 %collective-permute-done.1.mine_ref.refs_2_ = bf16[384,256]{1,0:T(8,128)(2,1)S(1)} collective-permute-done((bf16[384,256]{1,0:T(8,128)(2,1)S(1)}, bf16[384,256]{1,0:T(8,128)(2,1)S(1)}, u32[]{:S(2)}, u32[]{:S(2)}) %collective-permute-start.1) | collective-permute-done | bytes 196640 | tf_op jit(solution)/shard_map/ppermute | solution.py:339
  10.3 2.1 %collective-permute-start.3 = (bf16[288,256]{1,0:T(8,128)(2,1)S(1)}, bf16[288,256]{1,0:T(8,128)(2,1)S(1)}, u32[]{:S(2)}, u32[]{:S(2)}) collective-permute-start(bf16[288,256]{1,0:T(8,128)(2,1)S(1)} %slice.12), channel_id=1, source_target_pairs={{0,4},{1,3},{2,0},{3,7},{4,8},{5,1},{6,2},{7,11},{8,12},{9,5},{10,... | collective-permute-start | bytes 442376 | tf_op jit(solution)/shard_map/ppermute | solution.py:339
  12.5 0.3 collective-permute-done.2.theirs_ref.refs_3_
  12.7 1.7 %collective-permute-start.4 = (bf16[384,256]{1,0:T(8,128)(2,1)S(1)}, bf16[384,256]{1,0:T(8,128)(2,1)S(1)}, u32[]{:S(2)}, u32[]{:S(2)}) collective-permute-start(bf16[384,256]{1,0:T(8,128)(2,1)S(1)} %shard_map.93), channel_id=1, source_target_pairs={{0,4},{1,3},{2,0},{3,7},{4,8},{5,1},{6,2},{7,11},{8,12},{9,5},{10,... | collective-permute-start | bytes 589832 | tf_op jit(solution)/shard_map/ppermute | solution.py:339
  14.4 0.0 collective-permute-start.8
  14.4 1.1 %collective-permute-done.3.refs_4_ = bf16[288,256]{1,0:T(8,128)(2,1)S(1)} collective-permute-done((bf16[288,256]{1,0:T(8,128)(2,1)S(1)}, bf16[288,256]{1,0:T(8,128)(2,1)S(1)}, u32[]{:S(2)}, u32[]{:S(2)}) %collective-permute-start.3) | collective-permute-done | bytes 147488 | tf_op jit(solution)/shard_map/ppermute | solution.py:339
  15.5 2.1 %collective-permute-start.5 = (bf16[288,256]{1,0:T(8,128)(2,1)S(1)}, bf16[288,256]{1,0:T(8,128)(2,1)S(1)}, u32[]{:S(2)}, u32[]{:S(2)}) collective-permute-start(bf16[288,256]{1,0:T(8,128)(2,1)S(1)} %collective-permute-done.3.refs_4_), channel_id=1, source_target_pairs={{0,4},{1,3},{2,0},{3,7},{4,8},{5,1},{6,2},{7,11},{8,12},{9,5},{10,... | collective-permute-start | bytes 442376 | tf_op jit(solution)/shard_map/ppermute | solution.py:339
  17.6 0.8 %collective-permute-done.4.refs_5_ = bf16[384,256]{1,0:T(8,128)(2,1)S(1)} collective-permute-done((bf16[384,256]{1,0:T(8,128)(2,1)S(1)}, bf16[384,256]{1,0:T(8,128)(2,1)S(1)}, u32[]{:S(2)}, u32[]{:S(2)}) %collective-permute-start.4) | collective-permute-done | bytes 196640 | tf_op jit(solution)/shard_map/ppermute | solution.py:339
  18.4 0.0 collective-permute-start.11
  18.5 1.7 %collective-permute-start.6 = (bf16[320,256]{1,0:T(8,128)(2,1)S(1)}, bf16[320,256]{1,0:T(8,128)(2,1)S(1)}, u32[]{:S(2)}, u32[]{:S(2)}) collective-permute-start(bf16[320,256]{1,0:T(8,128)(2,1)S(1)} %slice.13), channel_id=1, source_target_pairs={{0,4},{1,3},{2,0},{3,7},{4,8},{5,1},{6,2},{7,11},{8,12},{9,5},{10,... | collective-permute-start | bytes 491528 | tf_op jit(solution)/shard_map/ppermute | solution.py:339
  20.1 0.5 %collective-permute-done.5.refs_6_ = bf16[288,256]{1,0:T(8,128)(2,1)S(1)} collective-permute-done((bf16[288,256]{1,0:T(8,128)(2,1)S(1)}, bf16[288,256]{1,0:T(8,128)(2,1)S(1)}, u32[]{:S(2)}, u32[]{:S(2)}) %collective-permute-start.5) | collective-permute-done | bytes 147488 | tf_op jit(solution)/shard_map/ppermute | solution.py:339
  20.7 2.1 %collective-permute-start.9 = (bf16[288,256]{1,0:T(8,128)(2,1)S(1)}, bf16[288,256]{1,0:T(8,128)(2,1)S(1)}, u32[]{:S(2)}, u32[]{:S(2)}) collective-permute-start(bf16[288,256]{1,0:T(8,128)(2,1)S(1)} %collective-permute-done.5.refs_6_), channel_id=1, source_target_pairs={{0,4},{1,3},{2,0},{3,7},{4,8},{5,1},{6,2},{7,11},{8,12},{9,5},{10,... | collective-permute-start | bytes 442376 | tf_op jit(solution)/shard_map/ppermute | solution.py:339
  22.7 0.0 collective-permute-done.8.refs_10_
  22.8 1.1 %collective-permute-done.6.refs_7_ = bf16[320,256]{1,0:T(8,128)(2,1)S(1)} collective-permute-done((bf16[320,256]{1,0:T(8,128)(2,1)S(1)}, bf16[320,256]{1,0:T(8,128)(2,1)S(1)}, u32[]{:S(2)}, u32[]{:S(2)}) %collective-permute-start.6) | collective-permute-done | bytes 163872 | tf_op jit(solution)/shard_map/ppermute | solution.py:339
  23.8 0.5 %collective-permute-start.12 = (bf16[288,256]{1,0:T(8,128)(2,1)S(1)}, bf16[288,256]{1,0:T(8,128)(2,1)S(1)}, u32[]{:S(2)}, u32[]{:S(2)}) collective-permute-start(bf16[288,256]{1,0:T(8,128)(2,1)S(1)} %collective-permute-done.5.refs_6_), channel_id=1, source_target_pairs={{0,1},{1,0},{2,3},{3,2},{4,5},{5,4},{6,7},{7,6},{8,9},{9,8},{10,11... | collective-permute-start | bytes 442376 | tf_op jit(solution)/shard_map/ppermute | solution.py:315
  24.3 1.5 %collective-permute-done.9.refs_8_ = bf16[288,256]{1,0:T(8,128)(2,1)S(1)} collective-permute-done((bf16[288,256]{1,0:T(8,128)(2,1)S(1)}, bf16[288,256]{1,0:T(8,128)(2,1)S(1)}, u32[]{:S(2)}, u32[]{:S(2)}) %collective-permute-start.9) | collective-permute-done | bytes 147488 | tf_op jit(solution)/shard_map/ppermute | solution.py:339
  25.8 0.0 collective-permute-done.10.refs_11_
  25.8 1.3 %collective-permute-done.14.refs_15_ = bf16[288,256]{1,0:T(8,128)(2,1)S(1)} collective-permute-done((bf16[288,256]{1,0:T(8,128)(2,1)S(1)}, bf16[288,256]{1,0:T(8,128)(2,1)S(1)}, u32[]{:S(2)}, u32[]{:S(2)}) %collective-permute-start.14) | collective-permute-done | bytes 147488 | tf_op jit(solution)/shard_map/ppermute | solution.py:315
  27.2 4.4 %shard_map.94 = bf16[16,256,128]{2,1,0:T(8,128)(2,1)} custom-call(bf16[384,256]{1,0:T(8,128)(2,1)S(1)} %get-tuple-element.24.refs_0_, bf16[384,256]{1,0:T(8,128)(2,1)S(1)} %collective-permute-done.refs_1_, bf16[384,256]{1,0:T(8,128)(2,1)S(1)} %collective-permute-done.1.mine_ref.refs_2_, bf16[352,256]{1,0:T(8,128)(2,1)S(1)} %collective-permute-done.2.theirs_ref.refs_3_, ...), custom_call_target="tpu_custom_call" | custom-call | tf_op jit(solution)/shard_map/pallas_call | solution.py:387
  (17 shorter events, 0.1 us)
Async XLA Ops:
  0.0 6.7 %copy-start = (bf16[1024,128]{1,0:T(8,128)(2,1)S(1)}, bf16[1024,128]{1,0:T(8,128)(2,1)}, u32[]{:S(2)}) copy-start(bf16[1024,128]{1,0:T(8,128)(2,1)} %final_ref.1) | copy-start | bytes 786436
  3.5 3.6 %collective-permute-start = (bf16[384,256]{1,0:T(8,128)(2,1)S(1)}, bf16[384,256]{1,0:T(8,128)(2,1)S(1)}, u32[]{:S(2)}, u32[]{:S(2)}) collective-permute-start(bf16[384,256]{1,0:T(8,128)(2,1)S(1)} %get-tuple-element.24.refs_0_), channel_id=1, source_target_pairs={{0,1},{1,0},{2,3},{3,2},{4,5},{5,4},{6,7},{7,6},{8,9},{9,8},{10,11... | collective-permute-start | bytes 589832 | tf_op jit(solution)/shard_map/ppermute | solution.py:315
  4.1 2.7 %copy-start.1 = (f32[128]{0:T(128)S(1)}, f32[128]{0:T(128)}, u32[]{:S(2)}) copy-start(f32[128]{0:T(128)} %param.17) | copy-start | bytes 1540
  4.1 6.2 %collective-permute-start.1 = (bf16[384,256]{1,0:T(8,128)(2,1)S(1)}, bf16[384,256]{1,0:T(8,128)(2,1)S(1)}, u32[]{:S(2)}, u32[]{:S(2)}) collective-permute-start(bf16[384,256]{1,0:T(8,128)(2,1)S(1)} %get-tuple-element.28), channel_id=1, source_target_pairs={{0,4},{1,3},{2,0},{3,7},{4,8},{5,1},{6,2},{7,11},{8,12},{9,5},{10,... | collective-permute-start | bytes 589832 | tf_op jit(solution)/shard_map/ppermute | solution.py:339
  7.2 5.5 %collective-permute-start.2 = (bf16[352,256]{1,0:T(8,128)(2,1)S(1)}, bf16[352,256]{1,0:T(8,128)(2,1)S(1)}, u32[]{:S(2)}, u32[]{:S(2)}) collective-permute-start(bf16[352,256]{1,0:T(8,128)(2,1)S(1)} %slice.9), channel_id=1, source_target_pairs={{0,4},{1,3},{2,0},{3,7},{4,8},{5,1},{6,2},{7,11},{8,12},{9,5},{10,... | collective-permute-start | bytes 540680 | tf_op jit(solution)/shard_map/ppermute | solution.py:339
  10.3 5.2 %collective-permute-start.3 = (bf16[288,256]{1,0:T(8,128)(2,1)S(1)}, bf16[288,256]{1,0:T(8,128)(2,1)S(1)}, u32[]{:S(2)}, u32[]{:S(2)}) collective-permute-start(bf16[288,256]{1,0:T(8,128)(2,1)S(1)} %slice.12), channel_id=1, source_target_pairs={{0,4},{1,3},{2,0},{3,7},{4,8},{5,1},{6,2},{7,11},{8,12},{9,5},{10,... | collective-permute-start | bytes 442376 | tf_op jit(solution)/shard_map/ppermute | solution.py:339
  12.7 5.7 %collective-permute-start.4 = (bf16[384,256]{1,0:T(8,128)(2,1)S(1)}, bf16[384,256]{1,0:T(8,128)(2,1)S(1)}, u32[]{:S(2)}, u32[]{:S(2)}) collective-permute-start(bf16[384,256]{1,0:T(8,128)(2,1)S(1)} %shard_map.93), channel_id=1, source_target_pairs={{0,4},{1,3},{2,0},{3,7},{4,8},{5,1},{6,2},{7,11},{8,12},{9,5},{10,... | collective-permute-start | bytes 589832 | tf_op jit(solution)/shard_map/ppermute | solution.py:339
  14.4 8.4 %collective-permute-start.8 = (bf16[352,256]{1,0:T(8,128)(2,1)S(1)}, bf16[352,256]{1,0:T(8,128)(2,1)S(1)}, u32[]{:S(2)}, u32[]{:S(2)}) collective-permute-start(bf16[352,256]{1,0:T(8,128)(2,1)S(1)} %collective-permute-done.2.theirs_ref.refs_3_), channel_id=1, source_target_pairs={{0,1},{1,0},{2,3},{3,2},{4,5},{5,4},{6,7},{7,6},{8,9},{9,8},{10,11... | collective-permute-start | bytes 540680 | tf_op jit(solution)/shard_map/ppermute | solution.py:315
  15.5 5.1 %collective-permute-start.5 = (bf16[288,256]{1,0:T(8,128)(2,1)S(1)}, bf16[288,256]{1,0:T(8,128)(2,1)S(1)}, u32[]{:S(2)}, u32[]{:S(2)}) collective-permute-start(bf16[288,256]{1,0:T(8,128)(2,1)S(1)} %collective-permute-done.3.refs_4_), channel_id=1, source_target_pairs={{0,4},{1,3},{2,0},{3,7},{4,8},{5,1},{6,2},{7,11},{8,12},{9,5},{10,... | collective-permute-start | bytes 442376 | tf_op jit(solution)/shard_map/ppermute | solution.py:339
  17.6 5.2 %collective-permute-start.7 = (bf16[384,256]{1,0:T(8,128)(2,1)S(1)}, bf16[384,256]{1,0:T(8,128)(2,1)S(1)}, u32[]{:S(2)}, u32[]{:S(2)}) collective-permute-start(bf16[384,256]{1,0:T(8,128)(2,1)S(1)} %collective-permute-done.1.mine_ref.refs_2_), channel_id=1, source_target_pairs={{0,1},{1,0},{2,3},{3,2},{4,5},{5,4},{6,7},{7,6},{8,9},{9,8},{10,11... | collective-permute-start | bytes 589832 | tf_op jit(solution)/shard_map/ppermute | solution.py:315
  18.4 7.4 %collective-permute-start.11 = (bf16[384,256]{1,0:T(8,128)(2,1)S(1)}, bf16[384,256]{1,0:T(8,128)(2,1)S(1)}, u32[]{:S(2)}, u32[]{:S(2)}) collective-permute-start(bf16[384,256]{1,0:T(8,128)(2,1)S(1)} %collective-permute-done.4.refs_5_), channel_id=1, source_target_pairs={{0,1},{1,0},{2,3},{3,2},{4,5},{5,4},{6,7},{7,6},{8,9},{9,8},{10,11... | collective-permute-start | bytes 589832 | tf_op jit(solution)/shard_map/ppermute | solution.py:315
  18.5 5.4 %collective-permute-start.6 = (bf16[320,256]{1,0:T(8,128)(2,1)S(1)}, bf16[320,256]{1,0:T(8,128)(2,1)S(1)}, u32[]{:S(2)}, u32[]{:S(2)}) collective-permute-start(bf16[320,256]{1,0:T(8,128)(2,1)S(1)} %slice.13), channel_id=1, source_target_pairs={{0,4},{1,3},{2,0},{3,7},{4,8},{5,1},{6,2},{7,11},{8,12},{9,5},{10,... | collective-permute-start | bytes 491528 | tf_op jit(solution)/shard_map/ppermute | solution.py:339
  20.7 5.1 %collective-permute-start.9 = (bf16[288,256]{1,0:T(8,128)(2,1)S(1)}, bf16[288,256]{1,0:T(8,128)(2,1)S(1)}, u32[]{:S(2)}, u32[]{:S(2)}) collective-permute-start(bf16[288,256]{1,0:T(8,128)(2,1)S(1)} %collective-permute-done.5.refs_6_), channel_id=1, source_target_pairs={{0,4},{1,3},{2,0},{3,7},{4,8},{5,1},{6,2},{7,11},{8,12},{9,5},{10,... | collective-permute-start | bytes 442376 | tf_op jit(solution)/shard_map/ppermute | solution.py:339
  22.7 3.1 %collective-permute-start.10 = (bf16[288,256]{1,0:T(8,128)(2,1)S(1)}, bf16[288,256]{1,0:T(8,128)(2,1)S(1)}, u32[]{:S(2)}, u32[]{:S(2)}) collective-permute-start(bf16[288,256]{1,0:T(8,128)(2,1)S(1)} %collective-permute-done.3.refs_4_), channel_id=1, source_target_pairs={{0,1},{1,0},{2,3},{3,2},{4,5},{5,4},{6,7},{7,6},{8,9},{9,8},{10,11... | collective-permute-start | bytes 442376 | tf_op jit(solution)/shard_map/ppermute | solution.py:315
  23.8 2.0 %collective-permute-start.13 = (bf16[320,256]{1,0:T(8,128)(2,1)S(1)}, bf16[320,256]{1,0:T(8,128)(2,1)S(1)}, u32[]{:S(2)}, u32[]{:S(2)}) collective-permute-start(bf16[320,256]{1,0:T(8,128)(2,1)S(1)} %collective-permute-done.6.refs_7_), channel_id=1, source_target_pairs={{0,1},{1,0},{2,3},{3,2},{4,5},{5,4},{6,7},{7,6},{8,9},{9,8},{10,11... | collective-permute-start | bytes 491528 | tf_op jit(solution)/shard_map/ppermute | solution.py:315
  23.8 2.0 %collective-permute-start.12 = (bf16[288,256]{1,0:T(8,128)(2,1)S(1)}, bf16[288,256]{1,0:T(8,128)(2,1)S(1)}, u32[]{:S(2)}, u32[]{:S(2)}) collective-permute-start(bf16[288,256]{1,0:T(8,128)(2,1)S(1)} %collective-permute-done.5.refs_6_), channel_id=1, source_target_pairs={{0,1},{1,0},{2,3},{3,2},{4,5},{5,4},{6,7},{7,6},{8,9},{9,8},{10,11... | collective-permute-start | bytes 442376 | tf_op jit(solution)/shard_map/ppermute | solution.py:315
  25.8 1.4 %collective-permute-start.14 = (bf16[288,256]{1,0:T(8,128)(2,1)S(1)}, bf16[288,256]{1,0:T(8,128)(2,1)S(1)}, u32[]{:S(2)}, u32[]{:S(2)}) collective-permute-start(bf16[288,256]{1,0:T(8,128)(2,1)S(1)} %collective-permute-done.9.refs_8_), channel_id=1, source_target_pairs={{0,1},{1,0},{2,3},{3,2},{4,5},{5,4},{6,7},{7,6},{8,9},{9,8},{10,11... | collective-permute-start | bytes 442376 | tf_op jit(solution)/shard_map/ppermute | solution.py:315

commit v12 on v10

--- a/solution.py
+++ b/solution.py
@@ -47,7 +47,6 @@
     second_ref,
     second_offset_ref,
     packed_ref,
-    left_ref,
     sems,
 ):
     samples, residues, features = x_ref.shape
@@ -56,7 +55,6 @@
     tile = keep_ref.shape[1]
     tiles = residues // tile
     fold = LANES // hidden
-    groups = residues // fold
     small = [
         (first_hbm, first_ref),
         (second_hbm, second_ref),
@@ -112,24 +110,17 @@
         second_here = jnp.where(column % samples == s, second, 0.0).astype(jnp.bfloat16)
         for t in range(tiles):
             part = normed[t * tile : (t + 1) * tile]
+            left = jnp.dot(part, first, preferred_element_type=jnp.float32)
             right[t] += jnp.dot(part, second_here, preferred_element_type=jnp.float32)
-            left = jnp.dot(part, first, preferred_element_type=jnp.float32)
             left = jnp.where(own, left + first_offset, 0.0).astype(jnp.bfloat16)
-            low = s * groups + t * (tile // fold)
-            packed_ref[low : low + tile // fold, :] = jnp.dot(
+            low = t * (tile // fold) * samples + s
+            packed_ref[pl.ds(low, tile // fold, stride=samples), :] = jnp.dot(
                 gather, left, preferred_element_type=jnp.float32
             )
     for t in range(tiles):
         value = (right[t].T + second_offset).astype(jnp.bfloat16)
         keep_ref[t * width : (t + 1) * width, :] = value
         give_ref[t * width : (t + 1) * width, :] = value
-    across = tile // LANES
-    for low in range(0, groups, across):
-        at = low // across * samples
-        left_ref[at : at + samples, :] = jnp.concatenate(
-            [packed_ref[pl.ds(low + n, samples, stride=groups), :] for n in range(across)], axis=1
-        )
-
     device = lax.axis_index("row")
     per_chip = 2 * rows_here * hidden * samples // tile
     half = residues // rows_here // 4
@@ -140,8 +131,12 @@
     spots += [(give_ref, base + n * per_chip, n + 1 - half) for n in range(half)]
     for message, low, ahead in spots:
         chip = chip_at(lax.rem(place + way * ahead + 2 * half, 2 * half), half)
-        start = pl.multiple_of(chip * per_chip, per_chip)
-        message[low : low + per_chip, :] = left_ref[pl.ds(start, per_chip), :].astype(jnp.bfloat16)
+        across = tile // LANES
+        start = pl.multiple_of(chip * per_chip * across, per_chip * across)
+        block = packed_ref[pl.ds(start, per_chip * across), :]
+        block = [block[n : n + samples] for n in range(0, per_chip * across, samples)]
+        block = [jnp.concatenate(block[n : n + across], axis=1) for n in range(0, len(block), across)]
+        message[low : low + per_chip, :] = jnp.concatenate(block, axis=0).astype(jnp.bfloat16)
 
 
 def join_kernel(base, per_chip, mine_ref, theirs_ref, next_ref):
@@ -261,7 +256,6 @@
             pltpu.VMEM((hidden, features), jnp.bfloat16),
             pltpu.VMEM((1, hidden), jnp.float32),
             pltpu.VMEM((residues * width // LANES, LANES), jnp.float32),
-            pltpu.VMEM((residues * width // tile, tile), jnp.float32),
             pltpu.SemaphoreType.DMA((CHUNKS + 6,)),
         ],
         compiler_params=pltpu.CompilerParams(vmem_limit_bytes=32 * MIB),

time: 31.7 us -> 31.6 us (level)
  no operation moved by 1% of the time
where the time goes in v12:
time: 31.6 us; the launch traced here: 31.5 us
  starting transfers between devices  14.9 us (47%)
  Pallas kernels  8.24 us (26%)
  waiting for transfers between devices  8.18 us (26%)
    ppermute x7, starting transfers between devices, per_device(): landed = [lax.ppermute(x, 'row', around) for x in flying]  13.9 us
    ppermute x7, waiting for transfers between devices, per_device(): landed = [lax.ppermute(x, 'row', around) for x in flying]  6.82 us
    pallas_call x1, Pallas kernels, per_device(): pl.pallas_call(functools.partial(pair_kernel, places, gridded, rows_here,...  4.43 us
    pallas_call x1, Pallas kernels, per_device(): pl.pallas_call(functools.partial(project_kernel, rows_here), out_shape=[r...  3.4 us
    ppermute x8, waiting for transfers between devices, swap(): return lax.ppermute(value, 'row', [(r, r ^ 1) for r in range(size)])  1.36 us
    ppermute x8, starting transfers between devices, swap(): return lax.ppermute(value, 'row', [(r, r ^ 1) for r in range(size)])  1.04 us
  transfers between devices with their start and end apart: 15, of which 8 were waited for; matrix products, arithmetic and copies ran while one was open for 0% of the time, Pallas kernels for 1%

profile of v12, /device:TPU:0, one launch (start us, length us, event | category | flops | bytes accessed | tf_op | source)
XLA Modules:
  0.0 31.5 jit_solution(6643053986996586424)
XLA Ops:
  0.0 3.4 %shard_map.91 = (bf16[384,256]{1,0:T(8,128)(2,1)S(1)}, bf16[384,256]{1,0:T(8,128)(2,1)S(1)}) custom-call(bf16[8,256,256]{2,1,0:T(8,128)(2,1)} %x_hbm.1, f32[1,256]{1,0:T(1,128)} %bitcast.10, f32[1,256]{1,0:T(1,128)} %bitcast.11, bf16[32,256]{1,0:T(8,128)(2,1)} %bitcast.8, f32[1,32]{1,0:T(1,128)} %bitcast.12, bf16[32,256]{1,0:T(8,128)(2,1)} %bitcast.9, ...), custom_call_target="tpu_custom_call" | custom-call | flops 536870912 | bytes 1048576 | tf_op jit(solution)/shard_map/pallas_call | solution.py:245
  3.4 0.5 %collective-permute-start = (bf16[384,256]{1,0:T(8,128)(2,1)S(1)}, bf16[384,256]{1,0:T(8,128)(2,1)S(1)}, u32[]{:S(2)}, u32[]{:S(2)}) collective-permute-start(bf16[384,256]{1,0:T(8,128)(2,1)S(1)} %get-tuple-element.24.refs_0_), channel_id=1, source_target_pairs={{0,1},{1,0},{2,3},{3,2},{4,5},{5,4},{6,7},{7,6},{8,9},{9,8},{10,11... | collective-permute-start | bytes 589832 | tf_op jit(solution)/shard_map/ppermute | solution.py:287
  3.9 2.6 %collective-permute-start.1 = (bf16[384,256]{1,0:T(8,128)(2,1)S(1)}, bf16[384,256]{1,0:T(8,128)(2,1)S(1)}, u32[]{:S(2)}, u32[]{:S(2)}) collective-permute-start(bf16[384,256]{1,0:T(8,128)(2,1)S(1)} %get-tuple-element.28), channel_id=1, source_target_pairs={{0,4},{1,3},{2,0},{3,7},{4,8},{5,1},{6,2},{7,11},{8,12},{9,5},{10,... | collective-permute-start | bytes 589832 | tf_op jit(solution)/shard_map/ppermute | solution.py:311
  6.6 0.4 %shard_map.92 = (bf16[128,1024]{1,0:T(8,128)(2,1)S(1)}, f32[1,128]{1,0:T(1,128)S(1)}) custom-call(bf16[1024,128]{1,0:T(8,128)(2,1)S(1)} %copy-done, f32[1,128]{1,0:T(1,128)S(1)} %bitcast.7), custom_call_target="tpu_custom_call" | custom-call | flops 268435456 | bytes 1048576 | tf_op jit(solution)/shard_map/pallas_call | solution.py:289
  7.0 1.6 %collective-permute-start.2 = (bf16[352,256]{1,0:T(8,128)(2,1)S(1)}, bf16[352,256]{1,0:T(8,128)(2,1)S(1)}, u32[]{:S(2)}, u32[]{:S(2)}) collective-permute-start(bf16[352,256]{1,0:T(8,128)(2,1)S(1)} %slice.9), channel_id=1, source_target_pairs={{0,4},{1,3},{2,0},{3,7},{4,8},{5,1},{6,2},{7,11},{8,12},{9,5},{10,... | collective-permute-start | bytes 540680 | tf_op jit(solution)/shard_map/ppermute | solution.py:311
  8.6 1.5 %collective-permute-done.1.mine_ref.refs_2_ = bf16[384,256]{1,0:T(8,128)(2,1)S(1)} collective-permute-done((bf16[384,256]{1,0:T(8,128)(2,1)S(1)}, bf16[384,256]{1,0:T(8,128)(2,1)S(1)}, u32[]{:S(2)}, u32[]{:S(2)}) %collective-permute-start.1) | collective-permute-done | bytes 196640 | tf_op jit(solution)/shard_map/ppermute | solution.py:311
  10.2 2.1 %collective-permute-start.3 = (bf16[288,256]{1,0:T(8,128)(2,1)S(1)}, bf16[288,256]{1,0:T(8,128)(2,1)S(1)}, u32[]{:S(2)}, u32[]{:S(2)}) collective-permute-start(bf16[288,256]{1,0:T(8,128)(2,1)S(1)} %slice.12), channel_id=1, source_target_pairs={{0,4},{1,3},{2,0},{3,7},{4,8},{5,1},{6,2},{7,11},{8,12},{9,5},{10,... | collective-permute-start | bytes 442376 | tf_op jit(solution)/shard_map/ppermute | solution.py:311
  12.3 0.3 collective-permute-done.2.theirs_ref.refs_3_
  12.6 1.7 %collective-permute-start.4 = (bf16[384,256]{1,0:T(8,128)(2,1)S(1)}, bf16[384,256]{1,0:T(8,128)(2,1)S(1)}, u32[]{:S(2)}, u32[]{:S(2)}) collective-permute-start(bf16[384,256]{1,0:T(8,128)(2,1)S(1)} %shard_map.93), channel_id=1, source_target_pairs={{0,4},{1,3},{2,0},{3,7},{4,8},{5,1},{6,2},{7,11},{8,12},{9,5},{10,... | collective-permute-start | bytes 589832 | tf_op jit(solution)/shard_map/ppermute | solution.py:311
  14.2 0.0 collective-permute-start.8
  14.2 1.1 %collective-permute-done.3.refs_4_ = bf16[288,256]{1,0:T(8,128)(2,1)S(1)} collective-permute-done((bf16[288,256]{1,0:T(8,128)(2,1)S(1)}, bf16[288,256]{1,0:T(8,128)(2,1)S(1)}, u32[]{:S(2)}, u32[]{:S(2)}) %collective-permute-start.3) | collective-permute-done | bytes 147488 | tf_op jit(solution)/shard_map/ppermute | solution.py:311
  15.4 2.1 %collective-permute-start.5 = (bf16[288,256]{1,0:T(8,128)(2,1)S(1)}, bf16[288,256]{1,0:T(8,128)(2,1)S(1)}, u32[]{:S(2)}, u32[]{:S(2)}) collective-permute-start(bf16[288,256]{1,0:T(8,128)(2,1)S(1)} %collective-permute-done.3.refs_4_), channel_id=1, source_target_pairs={{0,4},{1,3},{2,0},{3,7},{4,8},{5,1},{6,2},{7,11},{8,12},{9,5},{10,... | collective-permute-start | bytes 442376 | tf_op jit(solution)/shard_map/ppermute | solution.py:311
  17.5 0.8 %collective-permute-done.4.refs_5_ = bf16[384,256]{1,0:T(8,128)(2,1)S(1)} collective-permute-done((bf16[384,256]{1,0:T(8,128)(2,1)S(1)}, bf16[384,256]{1,0:T(8,128)(2,1)S(1)}, u32[]{:S(2)}, u32[]{:S(2)}) %collective-permute-start.4) | collective-permute-done | bytes 196640 | tf_op jit(solution)/shard_map/ppermute | solution.py:311
  18.3 0.0 collective-permute-start.11
  18.3 1.7 %collective-permute-start.6 = (bf16[320,256]{1,0:T(8,128)(2,1)S(1)}, bf16[320,256]{1,0:T(8,128)(2,1)S(1)}, u32[]{:S(2)}, u32[]{:S(2)}) collective-permute-start(bf16[320,256]{1,0:T(8,128)(2,1)S(1)} %slice.13), channel_id=1, source_target_pairs={{0,4},{1,3},{2,0},{3,7},{4,8},{5,1},{6,2},{7,11},{8,12},{9,5},{10,... | collective-permute-start | bytes 491528 | tf_op jit(solution)/shard_map/ppermute | solution.py:311
  20.0 0.5 %collective-permute-done.5.refs_6_ = bf16[288,256]{1,0:T(8,128)(2,1)S(1)} collective-permute-done((bf16[288,256]{1,0:T(8,128)(2,1)S(1)}, bf16[288,256]{1,0:T(8,128)(2,1)S(1)}, u32[]{:S(2)}, u32[]{:S(2)}) %collective-permute-start.5) | collective-permute-done | bytes 147488 | tf_op jit(solution)/shard_map/ppermute | solution.py:311
  20.5 2.1 %collective-permute-start.9 = (bf16[288,256]{1,0:T(8,128)(2,1)S(1)}, bf16[288,256]{1,0:T(8,128)(2,1)S(1)}, u32[]{:S(2)}, u32[]{:S(2)}) collective-permute-start(bf16[288,256]{1,0:T(8,128)(2,1)S(1)} %collective-permute-done.5.refs_6_), channel_id=1, source_target_pairs={{0,4},{1,3},{2,0},{3,7},{4,8},{5,1},{6,2},{7,11},{8,12},{9,5},{10,... | collective-permute-start | bytes 442376 | tf_op jit(solution)/shard_map/ppermute | solution.py:311
  22.6 1.1 %collective-permute-done.6.refs_7_ = bf16[320,256]{1,0:T(8,128)(2,1)S(1)} collective-permute-done((bf16[320,256]{1,0:T(8,128)(2,1)S(1)}, bf16[320,256]{1,0:T(8,128)(2,1)S(1)}, u32[]{:S(2)}, u32[]{:S(2)}) %collective-permute-start.6) | collective-permute-done | bytes 163872 | tf_op jit(solution)/shard_map/ppermute | solution.py:311
  23.7 0.5 %collective-permute-start.12 = (bf16[288,256]{1,0:T(8,128)(2,1)S(1)}, bf16[288,256]{1,0:T(8,128)(2,1)S(1)}, u32[]{:S(2)}, u32[]{:S(2)}) collective-permute-start(bf16[288,256]{1,0:T(8,128)(2,1)S(1)} %collective-permute-done.5.refs_6_), channel_id=1, source_target_pairs={{0,1},{1,0},{2,3},{3,2},{4,5},{5,4},{6,7},{7,6},{8,9},{9,8},{10,11... | collective-permute-start | bytes 442376 | tf_op jit(solution)/shard_map/ppermute | solution.py:287
  24.2 1.5 %collective-permute-done.9.refs_8_ = bf16[288,256]{1,0:T(8,128)(2,1)S(1)} collective-permute-done((bf16[288,256]{1,0:T(8,128)(2,1)S(1)}, bf16[288,256]{1,0:T(8,128)(2,1)S(1)}, u32[]{:S(2)}, u32[]{:S(2)}) %collective-permute-start.9) | collective-permute-done | bytes 147488 | tf_op jit(solution)/shard_map/ppermute | solution.py:311
  25.7 0.0 collective-permute-start.14
  25.7 0.0 collective-permute-done.12.refs_13_
  25.7 1.3 %collective-permute-done.14.refs_15_ = bf16[288,256]{1,0:T(8,128)(2,1)S(1)} collective-permute-done((bf16[288,256]{1,0:T(8,128)(2,1)S(1)}, bf16[288,256]{1,0:T(8,128)(2,1)S(1)}, u32[]{:S(2)}, u32[]{:S(2)}) %collective-permute-start.14) | collective-permute-done | bytes 147488 | tf_op jit(solution)/shard_map/ppermute | solution.py:287
  27.0 4.4 %shard_map.94 = bf16[16,256,128]{2,1,0:T(8,128)(2,1)} custom-call(bf16[384,256]{1,0:T(8,128)(2,1)S(1)} %get-tuple-element.24.refs_0_, bf16[384,256]{1,0:T(8,128)(2,1)S(1)} %collective-permute-done.refs_1_, bf16[384,256]{1,0:T(8,128)(2,1)S(1)} %collective-permute-done.1.mine_ref.refs_2_, bf16[352,256]{1,0:T(8,128)(2,1)S(1)} %collective-permute-done.2.theirs_ref.refs_3_, ...), custom_call_target="tpu_custom_call" | custom-call | tf_op jit(solution)/shard_map/pallas_call | solution.py:359
  (17 shorter events, 0.1 us)
Async XLA Ops:
  0.0 6.6 %copy-start = (bf16[1024,128]{1,0:T(8,128)(2,1)S(1)}, bf16[1024,128]{1,0:T(8,128)(2,1)}, u32[]{:S(2)}) copy-start(bf16[1024,128]{1,0:T(8,128)(2,1)} %final_ref.1) | copy-start | bytes 786436
  3.4 3.6 %collective-permute-start = (bf16[384,256]{1,0:T(8,128)(2,1)S(1)}, bf16[384,256]{1,0:T(8,128)(2,1)S(1)}, u32[]{:S(2)}, u32[]{:S(2)}) collective-permute-start(bf16[384,256]{1,0:T(8,128)(2,1)S(1)} %get-tuple-element.24.refs_0_), channel_id=1, source_target_pairs={{0,1},{1,0},{2,3},{3,2},{4,5},{5,4},{6,7},{7,6},{8,9},{9,8},{10,11... | collective-permute-start | bytes 589832 | tf_op jit(solution)/shard_map/ppermute | solution.py:287
  3.9 2.7 %copy-start.1 = (f32[128]{0:T(128)S(1)}, f32[128]{0:T(128)}, u32[]{:S(2)}) copy-start(f32[128]{0:T(128)} %param.17) | copy-start | bytes 1540
  3.9 6.2 %collective-permute-start.1 = (bf16[384,256]{1,0:T(8,128)(2,1)S(1)}, bf16[384,256]{1,0:T(8,128)(2,1)S(1)}, u32[]{:S(2)}, u32[]{:S(2)}) collective-permute-start(bf16[384,256]{1,0:T(8,128)(2,1)S(1)} %get-tuple-element.28), channel_id=1, source_target_pairs={{0,4},{1,3},{2,0},{3,7},{4,8},{5,1},{6,2},{7,11},{8,12},{9,5},{10,... | collective-permute-start | bytes 589832 | tf_op jit(solution)/shard_map/ppermute | solution.py:311
  7.0 5.5 %collective-permute-start.2 = (bf16[352,256]{1,0:T(8,128)(2,1)S(1)}, bf16[352,256]{1,0:T(8,128)(2,1)S(1)}, u32[]{:S(2)}, u32[]{:S(2)}) collective-permute-start(bf16[352,256]{1,0:T(8,128)(2,1)S(1)} %slice.9), channel_id=1, source_target_pairs={{0,4},{1,3},{2,0},{3,7},{4,8},{5,1},{6,2},{7,11},{8,12},{9,5},{10,... | collective-permute-start | bytes 540680 | tf_op jit(solution)/shard_map/ppermute | solution.py:311
  10.2 5.2 %collective-permute-start.3 = (bf16[288,256]{1,0:T(8,128)(2,1)S(1)}, bf16[288,256]{1,0:T(8,128)(2,1)S(1)}, u32[]{:S(2)}, u32[]{:S(2)}) collective-permute-start(bf16[288,256]{1,0:T(8,128)(2,1)S(1)} %slice.12), channel_id=1, source_target_pairs={{0,4},{1,3},{2,0},{3,7},{4,8},{5,1},{6,2},{7,11},{8,12},{9,5},{10,... | collective-permute-start | bytes 442376 | tf_op jit(solution)/shard_map/ppermute | solution.py:311
  12.6 5.7 %collective-permute-start.4 = (bf16[384,256]{1,0:T(8,128)(2,1)S(1)}, bf16[384,256]{1,0:T(8,128)(2,1)S(1)}, u32[]{:S(2)}, u32[]{:S(2)}) collective-permute-start(bf16[384,256]{1,0:T(8,128)(2,1)S(1)} %shard_map.93), channel_id=1, source_target_pairs={{0,4},{1,3},{2,0},{3,7},{4,8},{5,1},{6,2},{7,11},{8,12},{9,5},{10,... | collective-permute-start | bytes 589832 | tf_op jit(solution)/shard_map/ppermute | solution.py:311
  14.2 8.4 %collective-permute-start.8 = (bf16[352,256]{1,0:T(8,128)(2,1)S(1)}, bf16[352,256]{1,0:T(8,128)(2,1)S(1)}, u32[]{:S(2)}, u32[]{:S(2)}) collective-permute-start(bf16[352,256]{1,0:T(8,128)(2,1)S(1)} %collective-permute-done.2.theirs_ref.refs_3_), channel_id=1, source_target_pairs={{0,1},{1,0},{2,3},{3,2},{4,5},{5,4},{6,7},{7,6},{8,9},{9,8},{10,11... | collective-permute-start | bytes 540680 | tf_op jit(solution)/shard_map/ppermute | solution.py:287
  15.4 5.1 %collective-permute-start.5 = (bf16[288,256]{1,0:T(8,128)(2,1)S(1)}, bf16[288,256]{1,0:T(8,128)(2,1)S(1)}, u32[]{:S(2)}, u32[]{:S(2)}) collective-permute-start(bf16[288,256]{1,0:T(8,128)(2,1)S(1)} %collective-permute-done.3.refs_4_), channel_id=1, source_target_pairs={{0,4},{1,3},{2,0},{3,7},{4,8},{5,1},{6,2},{7,11},{8,12},{9,5},{10,... | collective-permute-start | bytes 442376 | tf_op jit(solution)/shard_map/ppermute | solution.py:311
  17.5 5.2 %collective-permute-start.7 = (bf16[384,256]{1,0:T(8,128)(2,1)S(1)}, bf16[384,256]{1,0:T(8,128)(2,1)S(1)}, u32[]{:S(2)}, u32[]{:S(2)}) collective-permute-start(bf16[384,256]{1,0:T(8,128)(2,1)S(1)} %collective-permute-done.1.mine_ref.refs_2_), channel_id=1, source_target_pairs={{0,1},{1,0},{2,3},{3,2},{4,5},{5,4},{6,7},{7,6},{8,9},{9,8},{10,11... | collective-permute-start | bytes 589832 | tf_op jit(solution)/shard_map/ppermute | solution.py:287
  18.3 7.4 %collective-permute-start.11 = (bf16[384,256]{1,0:T(8,128)(2,1)S(1)}, bf16[384,256]{1,0:T(8,128)(2,1)S(1)}, u32[]{:S(2)}, u32[]{:S(2)}) collective-permute-start(bf16[384,256]{1,0:T(8,128)(2,1)S(1)} %collective-permute-done.4.refs_5_), channel_id=1, source_target_pairs={{0,1},{1,0},{2,3},{3,2},{4,5},{5,4},{6,7},{7,6},{8,9},{9,8},{10,11... | collective-permute-start | bytes 589832 | tf_op jit(solution)/shard_map/ppermute | solution.py:287
  18.3 5.4 %collective-permute-start.6 = (bf16[320,256]{1,0:T(8,128)(2,1)S(1)}, bf16[320,256]{1,0:T(8,128)(2,1)S(1)}, u32[]{:S(2)}, u32[]{:S(2)}) collective-permute-start(bf16[320,256]{1,0:T(8,128)(2,1)S(1)} %slice.13), channel_id=1, source_target_pairs={{0,4},{1,3},{2,0},{3,7},{4,8},{5,1},{6,2},{7,11},{8,12},{9,5},{10,... | collective-permute-start | bytes 491528 | tf_op jit(solution)/shard_map/ppermute | solution.py:311
  20.5 5.1 %collective-permute-start.9 = (bf16[288,256]{1,0:T(8,128)(2,1)S(1)}, bf16[288,256]{1,0:T(8,128)(2,1)S(1)}, u32[]{:S(2)}, u32[]{:S(2)}) collective-permute-start(bf16[288,256]{1,0:T(8,128)(2,1)S(1)} %collective-permute-done.5.refs_6_), channel_id=1, source_target_pairs={{0,4},{1,3},{2,0},{3,7},{4,8},{5,1},{6,2},{7,11},{8,12},{9,5},{10,... | collective-permute-start | bytes 442376 | tf_op jit(solution)/shard_map/ppermute | solution.py:311
  22.6 3.1 %collective-permute-start.10 = (bf16[288,256]{1,0:T(8,128)(2,1)S(1)}, bf16[288,256]{1,0:T(8,128)(2,1)S(1)}, u32[]{:S(2)}, u32[]{:S(2)}) collective-permute-start(bf16[288,256]{1,0:T(8,128)(2,1)S(1)} %collective-permute-done.3.refs_4_), channel_id=1, source_target_pairs={{0,1},{1,0},{2,3},{3,2},{4,5},{5,4},{6,7},{7,6},{8,9},{9,8},{10,11... | collective-permute-start | bytes 442376 | tf_op jit(solution)/shard_map/ppermute | solution.py:287
  23.7 2.0 %collective-permute-start.13 = (bf16[320,256]{1,0:T(8,128)(2,1)S(1)}, bf16[320,256]{1,0:T(8,128)(2,1)S(1)}, u32[]{:S(2)}, u32[]{:S(2)}) collective-permute-start(bf16[320,256]{1,0:T(8,128)(2,1)S(1)} %collective-permute-done.6.refs_7_), channel_id=1, source_target_pairs={{0,1},{1,0},{2,3},{3,2},{4,5},{5,4},{6,7},{7,6},{8,9},{9,8},{10,11... | collective-permute-start | bytes 491528 | tf_op jit(solution)/shard_map/ppermute | solution.py:287
  23.7 2.0 %collective-permute-start.12 = (bf16[288,256]{1,0:T(8,128)(2,1)S(1)}, bf16[288,256]{1,0:T(8,128)(2,1)S(1)}, u32[]{:S(2)}, u32[]{:S(2)}) collective-permute-start(bf16[288,256]{1,0:T(8,128)(2,1)S(1)} %collective-permute-done.5.refs_6_), channel_id=1, source_target_pairs={{0,1},{1,0},{2,3},{3,2},{4,5},{5,4},{6,7},{7,6},{8,9},{9,8},{10,11... | collective-permute-start | bytes 442376 | tf_op jit(solution)/shard_map/ppermute | solution.py:287
  25.7 1.4 %collective-permute-start.14 = (bf16[288,256]{1,0:T(8,128)(2,1)S(1)}, bf16[288,256]{1,0:T(8,128)(2,1)S(1)}, u32[]{:S(2)}, u32[]{:S(2)}) collective-permute-start(bf16[288,256]{1,0:T(8,128)(2,1)S(1)} %collective-permute-done.9.refs_8_), channel_id=1, source_target_pairs={{0,1},{1,0},{2,3},{3,2},{4,5},{5,4},{6,7},{7,6},{8,9},{9,8},{10,11... | collective-permute-start | bytes 442376 | tf_op jit(solution)/shard_map/ppermute | solution.py:287

commit v13 on v12

--- a/solution.py
+++ b/solution.py
@@ -10,7 +10,7 @@
 
 MIB = 1024 * 1024
 LANES = 128
-CHUNKS = 2
+CHUNKS = 1
 BLOCK = 64
 
 

time: 31.6 us -> 31.4 us (level)
  no operation moved by 1% of the time
where the time goes in v13:
time: 31.4 us; the launch traced here: 31.3 us
  starting transfers between devices  14.9 us (47%)
  waiting for transfers between devices  8.19 us (26%)
  Pallas kernels  8.07 us (26%)
    ppermute x7, starting transfers between devices, per_device(): landed = [lax.ppermute(x, 'row', around) for x in flying]  13.9 us
    ppermute x7, waiting for transfers between devices, per_device(): landed = [lax.ppermute(x, 'row', around) for x in flying]  6.82 us
    pallas_call x1, Pallas kernels, per_device(): pl.pallas_call(functools.partial(pair_kernel, places, gridded, rows_here,...  4.43 us
    pallas_call x1, Pallas kernels, per_device(): pl.pallas_call(functools.partial(project_kernel, rows_here), out_shape=[r...  3.22 us
    ppermute x8, waiting for transfers between devices, swap(): return lax.ppermute(value, 'row', [(r, r ^ 1) for r in range(size)])  1.36 us
    ppermute x8, starting transfers between devices, swap(): return lax.ppermute(value, 'row', [(r, r ^ 1) for r in range(size)])  1.04 us
  transfers between devices with their start and end apart: 15, of which 8 were waited for; matrix products, arithmetic and copies ran while one was open for 0% of the time, Pallas kernels for 1%

profile of v13, /device:TPU:0, one launch (start us, length us, event | category | flops | bytes accessed | tf_op | source)
XLA Modules:
  0.0 31.3 jit_solution(345300767546850033)
XLA Ops:
  0.0 3.2 %shard_map.91 = (bf16[384,256]{1,0:T(8,128)(2,1)S(1)}, bf16[384,256]{1,0:T(8,128)(2,1)S(1)}) custom-call(bf16[8,256,256]{2,1,0:T(8,128)(2,1)} %x_hbm.1, f32[1,256]{1,0:T(1,128)} %bitcast.10, f32[1,256]{1,0:T(1,128)} %bitcast.11, bf16[32,256]{1,0:T(8,128)(2,1)} %bitcast.8, f32[1,32]{1,0:T(1,128)} %bitcast.12, bf16[32,256]{1,0:T(8,128)(2,1)} %bitcast.9, ...), custom_call_target="tpu_custom_call" | custom-call | flops 536870912 | bytes 1048576 | tf_op jit(solution)/shard_map/pallas_call | solution.py:245
  3.2 0.5 %collective-permute-start = (bf16[384,256]{1,0:T(8,128)(2,1)S(1)}, bf16[384,256]{1,0:T(8,128)(2,1)S(1)}, u32[]{:S(2)}, u32[]{:S(2)}) collective-permute-start(bf16[384,256]{1,0:T(8,128)(2,1)S(1)} %get-tuple-element.24.refs_0_), channel_id=1, source_target_pairs={{0,1},{1,0},{2,3},{3,2},{4,5},{5,4},{6,7},{7,6},{8,9},{9,8},{10,11... | collective-permute-start | bytes 589832 | tf_op jit(solution)/shard_map/ppermute | solution.py:287
  3.8 2.6 %collective-permute-start.1 = (bf16[384,256]{1,0:T(8,128)(2,1)S(1)}, bf16[384,256]{1,0:T(8,128)(2,1)S(1)}, u32[]{:S(2)}, u32[]{:S(2)}) collective-permute-start(bf16[384,256]{1,0:T(8,128)(2,1)S(1)} %get-tuple-element.28), channel_id=1, source_target_pairs={{0,4},{1,3},{2,0},{3,7},{4,8},{5,1},{6,2},{7,11},{8,12},{9,5},{10,... | collective-permute-start | bytes 589832 | tf_op jit(solution)/shard_map/ppermute | solution.py:311
  6.4 0.4 %shard_map.92 = (bf16[128,1024]{1,0:T(8,128)(2,1)S(1)}, f32[1,128]{1,0:T(1,128)S(1)}) custom-call(bf16[1024,128]{1,0:T(8,128)(2,1)S(1)} %copy-done, f32[1,128]{1,0:T(1,128)S(1)} %bitcast.7), custom_call_target="tpu_custom_call" | custom-call | flops 268435456 | bytes 1048576 | tf_op jit(solution)/shard_map/pallas_call | solution.py:289
  6.8 1.6 %collective-permute-start.2 = (bf16[352,256]{1,0:T(8,128)(2,1)S(1)}, bf16[352,256]{1,0:T(8,128)(2,1)S(1)}, u32[]{:S(2)}, u32[]{:S(2)}) collective-permute-start(bf16[352,256]{1,0:T(8,128)(2,1)S(1)} %slice.9), channel_id=1, source_target_pairs={{0,4},{1,3},{2,0},{3,7},{4,8},{5,1},{6,2},{7,11},{8,12},{9,5},{10,... | collective-permute-start | bytes 540680 | tf_op jit(solution)/shard_map/ppermute | solution.py:311
  8.5 1.5 %collective-permute-done.1.mine_ref.refs_2_ = bf16[384,256]{1,0:T(8,128)(2,1)S(1)} collective-permute-done((bf16[384,256]{1,0:T(8,128)(2,1)S(1)}, bf16[384,256]{1,0:T(8,128)(2,1)S(1)}, u32[]{:S(2)}, u32[]{:S(2)}) %collective-permute-start.1) | collective-permute-done | bytes 196640 | tf_op jit(solution)/shard_map/ppermute | solution.py:311
  10.0 2.1 %collective-permute-start.3 = (bf16[288,256]{1,0:T(8,128)(2,1)S(1)}, bf16[288,256]{1,0:T(8,128)(2,1)S(1)}, u32[]{:S(2)}, u32[]{:S(2)}) collective-permute-start(bf16[288,256]{1,0:T(8,128)(2,1)S(1)} %slice.12), channel_id=1, source_target_pairs={{0,4},{1,3},{2,0},{3,7},{4,8},{5,1},{6,2},{7,11},{8,12},{9,5},{10,... | collective-permute-start | bytes 442376 | tf_op jit(solution)/shard_map/ppermute | solution.py:311
  12.1 0.3 collective-permute-done.2.theirs_ref.refs_3_
  12.4 1.7 %collective-permute-start.4 = (bf16[384,256]{1,0:T(8,128)(2,1)S(1)}, bf16[384,256]{1,0:T(8,128)(2,1)S(1)}, u32[]{:S(2)}, u32[]{:S(2)}) collective-permute-start(bf16[384,256]{1,0:T(8,128)(2,1)S(1)} %shard_map.93), channel_id=1, source_target_pairs={{0,4},{1,3},{2,0},{3,7},{4,8},{5,1},{6,2},{7,11},{8,12},{9,5},{10,... | collective-permute-start | bytes 589832 | tf_op jit(solution)/shard_map/ppermute | solution.py:311
  14.1 0.0 collective-permute-start.8
  14.1 1.1 %collective-permute-done.3.refs_4_ = bf16[288,256]{1,0:T(8,128)(2,1)S(1)} collective-permute-done((bf16[288,256]{1,0:T(8,128)(2,1)S(1)}, bf16[288,256]{1,0:T(8,128)(2,1)S(1)}, u32[]{:S(2)}, u32[]{:S(2)}) %collective-permute-start.3) | collective-permute-done | bytes 147488 | tf_op jit(solution)/shard_map/ppermute | solution.py:311
  15.2 2.1 %collective-permute-start.5 = (bf16[288,256]{1,0:T(8,128)(2,1)S(1)}, bf16[288,256]{1,0:T(8,128)(2,1)S(1)}, u32[]{:S(2)}, u32[]{:S(2)}) collective-permute-start(bf16[288,256]{1,0:T(8,128)(2,1)S(1)} %collective-permute-done.3.refs_4_), channel_id=1, source_target_pairs={{0,4},{1,3},{2,0},{3,7},{4,8},{5,1},{6,2},{7,11},{8,12},{9,5},{10,... | collective-permute-start | bytes 442376 | tf_op jit(solution)/shard_map/ppermute | solution.py:311
  17.3 0.8 %collective-permute-done.4.refs_5_ = bf16[384,256]{1,0:T(8,128)(2,1)S(1)} collective-permute-done((bf16[384,256]{1,0:T(8,128)(2,1)S(1)}, bf16[384,256]{1,0:T(8,128)(2,1)S(1)}, u32[]{:S(2)}, u32[]{:S(2)}) %collective-permute-start.4) | collective-permute-done | bytes 196640 | tf_op jit(solution)/shard_map/ppermute | solution.py:311
  18.1 0.0 collective-permute-start.11
  18.1 1.7 %collective-permute-start.6 = (bf16[320,256]{1,0:T(8,128)(2,1)S(1)}, bf16[320,256]{1,0:T(8,128)(2,1)S(1)}, u32[]{:S(2)}, u32[]{:S(2)}) collective-permute-start(bf16[320,256]{1,0:T(8,128)(2,1)S(1)} %slice.13), channel_id=1, source_target_pairs={{0,4},{1,3},{2,0},{3,7},{4,8},{5,1},{6,2},{7,11},{8,12},{9,5},{10,... | collective-permute-start | bytes 491528 | tf_op jit(solution)/shard_map/ppermute | solution.py:311
  19.8 0.5 %collective-permute-done.5.refs_6_ = bf16[288,256]{1,0:T(8,128)(2,1)S(1)} collective-permute-done((bf16[288,256]{1,0:T(8,128)(2,1)S(1)}, bf16[288,256]{1,0:T(8,128)(2,1)S(1)}, u32[]{:S(2)}, u32[]{:S(2)}) %collective-permute-start.5) | collective-permute-done | bytes 147488 | tf_op jit(solution)/shard_map/ppermute | solution.py:311
  20.3 2.1 %collective-permute-start.9 = (bf16[288,256]{1,0:T(8,128)(2,1)S(1)}, bf16[288,256]{1,0:T(8,128)(2,1)S(1)}, u32[]{:S(2)}, u32[]{:S(2)}) collective-permute-start(bf16[288,256]{1,0:T(8,128)(2,1)S(1)} %collective-permute-done.5.refs_6_), channel_id=1, source_target_pairs={{0,4},{1,3},{2,0},{3,7},{4,8},{5,1},{6,2},{7,11},{8,12},{9,5},{10,... | collective-permute-start | bytes 442376 | tf_op jit(solution)/shard_map/ppermute | solution.py:311
  22.4 0.0 collective-permute-done.8.refs_10_
  22.4 0.0 collective-permute-start.10
  22.4 1.1 %collective-permute-done.6.refs_7_ = bf16[320,256]{1,0:T(8,128)(2,1)S(1)} collective-permute-done((bf16[320,256]{1,0:T(8,128)(2,1)S(1)}, bf16[320,256]{1,0:T(8,128)(2,1)S(1)}, u32[]{:S(2)}, u32[]{:S(2)}) %collective-permute-start.6) | collective-permute-done | bytes 163872 | tf_op jit(solution)/shard_map/ppermute | solution.py:311
  23.5 0.5 %collective-permute-start.12 = (bf16[288,256]{1,0:T(8,128)(2,1)S(1)}, bf16[288,256]{1,0:T(8,128)(2,1)S(1)}, u32[]{:S(2)}, u32[]{:S(2)}) collective-permute-start(bf16[288,256]{1,0:T(8,128)(2,1)S(1)} %collective-permute-done.5.refs_6_), channel_id=1, source_target_pairs={{0,1},{1,0},{2,3},{3,2},{4,5},{5,4},{6,7},{7,6},{8,9},{9,8},{10,11... | collective-permute-start | bytes 442376 | tf_op jit(solution)/shard_map/ppermute | solution.py:287
  24.0 1.5 %collective-permute-done.9.refs_8_ = bf16[288,256]{1,0:T(8,128)(2,1)S(1)} collective-permute-done((bf16[288,256]{1,0:T(8,128)(2,1)S(1)}, bf16[288,256]{1,0:T(8,128)(2,1)S(1)}, u32[]{:S(2)}, u32[]{:S(2)}) %collective-permute-start.9) | collective-permute-done | bytes 147488 | tf_op jit(solution)/shard_map/ppermute | solution.py:311
  25.5 1.3 %collective-permute-done.14.refs_15_ = bf16[288,256]{1,0:T(8,128)(2,1)S(1)} collective-permute-done((bf16[288,256]{1,0:T(8,128)(2,1)S(1)}, bf16[288,256]{1,0:T(8,128)(2,1)S(1)}, u32[]{:S(2)}, u32[]{:S(2)}) %collective-permute-start.14) | collective-permute-done | bytes 147488 | tf_op jit(solution)/shard_map/ppermute | solution.py:287
  26.9 4.4 %shard_map.94 = bf16[16,256,128]{2,1,0:T(8,128)(2,1)} custom-call(bf16[384,256]{1,0:T(8,128)(2,1)S(1)} %get-tuple-element.24.refs_0_, bf16[384,256]{1,0:T(8,128)(2,1)S(1)} %collective-permute-done.refs_1_, bf16[384,256]{1,0:T(8,128)(2,1)S(1)} %collective-permute-done.1.mine_ref.refs_2_, bf16[352,256]{1,0:T(8,128)(2,1)S(1)} %collective-permute-done.2.theirs_ref.refs_3_, ...), custom_call_target="tpu_custom_call" | custom-call | tf_op jit(solution)/shard_map/pallas_call | solution.py:359
  (17 shorter events, 0.1 us)
Async XLA Ops:
  0.0 6.4 %copy-start = (bf16[1024,128]{1,0:T(8,128)(2,1)S(1)}, bf16[1024,128]{1,0:T(8,128)(2,1)}, u32[]{:S(2)}) copy-start(bf16[1024,128]{1,0:T(8,128)(2,1)} %final_ref.1) | copy-start | bytes 786436
  3.2 3.6 %collective-permute-start = (bf16[384,256]{1,0:T(8,128)(2,1)S(1)}, bf16[384,256]{1,0:T(8,128)(2,1)S(1)}, u32[]{:S(2)}, u32[]{:S(2)}) collective-permute-start(bf16[384,256]{1,0:T(8,128)(2,1)S(1)} %get-tuple-element.24.refs_0_), channel_id=1, source_target_pairs={{0,1},{1,0},{2,3},{3,2},{4,5},{5,4},{6,7},{7,6},{8,9},{9,8},{10,11... | collective-permute-start | bytes 589832 | tf_op jit(solution)/shard_map/ppermute | solution.py:287
  3.8 2.7 %copy-start.1 = (f32[128]{0:T(128)S(1)}, f32[128]{0:T(128)}, u32[]{:S(2)}) copy-start(f32[128]{0:T(128)} %param.17) | copy-start | bytes 1540
  3.8 6.2 %collective-permute-start.1 = (bf16[384,256]{1,0:T(8,128)(2,1)S(1)}, bf16[384,256]{1,0:T(8,128)(2,1)S(1)}, u32[]{:S(2)}, u32[]{:S(2)}) collective-permute-start(bf16[384,256]{1,0:T(8,128)(2,1)S(1)} %get-tuple-element.28), channel_id=1, source_target_pairs={{0,4},{1,3},{2,0},{3,7},{4,8},{5,1},{6,2},{7,11},{8,12},{9,5},{10,... | collective-permute-start | bytes 589832 | tf_op jit(solution)/shard_map/ppermute | solution.py:311
  6.8 5.5 %collective-permute-start.2 = (bf16[352,256]{1,0:T(8,128)(2,1)S(1)}, bf16[352,256]{1,0:T(8,128)(2,1)S(1)}, u32[]{:S(2)}, u32[]{:S(2)}) collective-permute-start(bf16[352,256]{1,0:T(8,128)(2,1)S(1)} %slice.9), channel_id=1, source_target_pairs={{0,4},{1,3},{2,0},{3,7},{4,8},{5,1},{6,2},{7,11},{8,12},{9,5},{10,... | collective-permute-start | bytes 540680 | tf_op jit(solution)/shard_map/ppermute | solution.py:311
  10.0 5.2 %collective-permute-start.3 = (bf16[288,256]{1,0:T(8,128)(2,1)S(1)}, bf16[288,256]{1,0:T(8,128)(2,1)S(1)}, u32[]{:S(2)}, u32[]{:S(2)}) collective-permute-start(bf16[288,256]{1,0:T(8,128)(2,1)S(1)} %slice.12), channel_id=1, source_target_pairs={{0,4},{1,3},{2,0},{3,7},{4,8},{5,1},{6,2},{7,11},{8,12},{9,5},{10,... | collective-permute-start | bytes 442376 | tf_op jit(solution)/shard_map/ppermute | solution.py:311
  12.4 5.7 %collective-permute-start.4 = (bf16[384,256]{1,0:T(8,128)(2,1)S(1)}, bf16[384,256]{1,0:T(8,128)(2,1)S(1)}, u32[]{:S(2)}, u32[]{:S(2)}) collective-permute-start(bf16[384,256]{1,0:T(8,128)(2,1)S(1)} %shard_map.93), channel_id=1, source_target_pairs={{0,4},{1,3},{2,0},{3,7},{4,8},{5,1},{6,2},{7,11},{8,12},{9,5},{10,... | collective-permute-start | bytes 589832 | tf_op jit(solution)/shard_map/ppermute | solution.py:311
  14.1 8.4 %collective-permute-start.8 = (bf16[352,256]{1,0:T(8,128)(2,1)S(1)}, bf16[352,256]{1,0:T(8,128)(2,1)S(1)}, u32[]{:S(2)}, u32[]{:S(2)}) collective-permute-start(bf16[352,256]{1,0:T(8,128)(2,1)S(1)} %collective-permute-done.2.theirs_ref.refs_3_), channel_id=1, source_target_pairs={{0,1},{1,0},{2,3},{3,2},{4,5},{5,4},{6,7},{7,6},{8,9},{9,8},{10,11... | collective-permute-start | bytes 540680 | tf_op jit(solution)/shard_map/ppermute | solution.py:287
  15.2 5.1 %collective-permute-start.5 = (bf16[288,256]{1,0:T(8,128)(2,1)S(1)}, bf16[288,256]{1,0:T(8,128)(2,1)S(1)}, u32[]{:S(2)}, u32[]{:S(2)}) collective-permute-start(bf16[288,256]{1,0:T(8,128)(2,1)S(1)} %collective-permute-done.3.refs_4_), channel_id=1, source_target_pairs={{0,4},{1,3},{2,0},{3,7},{4,8},{5,1},{6,2},{7,11},{8,12},{9,5},{10,... | collective-permute-start | bytes 442376 | tf_op jit(solution)/shard_map/ppermute | solution.py:311
  17.3 5.2 %collective-permute-start.7 = (bf16[384,256]{1,0:T(8,128)(2,1)S(1)}, bf16[384,256]{1,0:T(8,128)(2,1)S(1)}, u32[]{:S(2)}, u32[]{:S(2)}) collective-permute-start(bf16[384,256]{1,0:T(8,128)(2,1)S(1)} %collective-permute-done.1.mine_ref.refs_2_), channel_id=1, source_target_pairs={{0,1},{1,0},{2,3},{3,2},{4,5},{5,4},{6,7},{7,6},{8,9},{9,8},{10,11... | collective-permute-start | bytes 589832 | tf_op jit(solution)/shard_map/ppermute | solution.py:287
  18.1 7.4 %collective-permute-start.11 = (bf16[384,256]{1,0:T(8,128)(2,1)S(1)}, bf16[384,256]{1,0:T(8,128)(2,1)S(1)}, u32[]{:S(2)}, u32[]{:S(2)}) collective-permute-start(bf16[384,256]{1,0:T(8,128)(2,1)S(1)} %collective-permute-done.4.refs_5_), channel_id=1, source_target_pairs={{0,1},{1,0},{2,3},{3,2},{4,5},{5,4},{6,7},{7,6},{8,9},{9,8},{10,11... | collective-permute-start | bytes 589832 | tf_op jit(solution)/shard_map/ppermute | solution.py:287
  18.1 5.4 %collective-permute-start.6 = (bf16[320,256]{1,0:T(8,128)(2,1)S(1)}, bf16[320,256]{1,0:T(8,128)(2,1)S(1)}, u32[]{:S(2)}, u32[]{:S(2)}) collective-permute-start(bf16[320,256]{1,0:T(8,128)(2,1)S(1)} %slice.13), channel_id=1, source_target_pairs={{0,4},{1,3},{2,0},{3,7},{4,8},{5,1},{6,2},{7,11},{8,12},{9,5},{10,... | collective-permute-start | bytes 491528 | tf_op jit(solution)/shard_map/ppermute | solution.py:311
  20.3 5.1 %collective-permute-start.9 = (bf16[288,256]{1,0:T(8,128)(2,1)S(1)}, bf16[288,256]{1,0:T(8,128)(2,1)S(1)}, u32[]{:S(2)}, u32[]{:S(2)}) collective-permute-start(bf16[288,256]{1,0:T(8,128)(2,1)S(1)} %collective-permute-done.5.refs_6_), channel_id=1, source_target_pairs={{0,4},{1,3},{2,0},{3,7},{4,8},{5,1},{6,2},{7,11},{8,12},{9,5},{10,... | collective-permute-start | bytes 442376 | tf_op jit(solution)/shard_map/ppermute | solution.py:311
  22.4 3.1 %collective-permute-start.10 = (bf16[288,256]{1,0:T(8,128)(2,1)S(1)}, bf16[288,256]{1,0:T(8,128)(2,1)S(1)}, u32[]{:S(2)}, u32[]{:S(2)}) collective-permute-start(bf16[288,256]{1,0:T(8,128)(2,1)S(1)} %collective-permute-done.3.refs_4_), channel_id=1, source_target_pairs={{0,1},{1,0},{2,3},{3,2},{4,5},{5,4},{6,7},{7,6},{8,9},{9,8},{10,11... | collective-permute-start | bytes 442376 | tf_op jit(solution)/shard_map/ppermute | solution.py:287
  23.5 2.0 %collective-permute-start.13 = (bf16[320,256]{1,0:T(8,128)(2,1)S(1)}, bf16[320,256]{1,0:T(8,128)(2,1)S(1)}, u32[]{:S(2)}, u32[]{:S(2)}) collective-permute-start(bf16[320,256]{1,0:T(8,128)(2,1)S(1)} %collective-permute-done.6.refs_7_), channel_id=1, source_target_pairs={{0,1},{1,0},{2,3},{3,2},{4,5},{5,4},{6,7},{7,6},{8,9},{9,8},{10,11... | collective-permute-start | bytes 491528 | tf_op jit(solution)/shard_map/ppermute | solution.py:287
  23.5 2.0 %collective-permute-start.12 = (bf16[288,256]{1,0:T(8,128)(2,1)S(1)}, bf16[288,256]{1,0:T(8,128)(2,1)S(1)}, u32[]{:S(2)}, u32[]{:S(2)}) collective-permute-start(bf16[288,256]{1,0:T(8,128)(2,1)S(1)} %collective-permute-done.5.refs_6_), channel_id=1, source_target_pairs={{0,1},{1,0},{2,3},{3,2},{4,5},{5,4},{6,7},{7,6},{8,9},{9,8},{10,11... | collective-permute-start | bytes 442376 | tf_op jit(solution)/shard_map/ppermute | solution.py:287
  25.5 1.4 %collective-permute-start.14 = (bf16[288,256]{1,0:T(8,128)(2,1)S(1)}, bf16[288,256]{1,0:T(8,128)(2,1)S(1)}, u32[]{:S(2)}, u32[]{:S(2)}) collective-permute-start(bf16[288,256]{1,0:T(8,128)(2,1)S(1)} %collective-permute-done.9.refs_8_), channel_id=1, source_target_pairs={{0,1},{1,0},{2,3},{3,2},{4,5},{5,4},{6,7},{7,6},{8,9},{9,8},{10,11... | collective-permute-start | bytes 442376 | tf_op jit(solution)/shard_map/ppermute | solution.py:287

commit v14 on v13

--- a/solution.py
+++ b/solution.py
@@ -10,7 +10,6 @@
 
 MIB = 1024 * 1024
 LANES = 128
-CHUNKS = 1
 BLOCK = 64
 
 
@@ -63,17 +62,14 @@
         (first_offset_hbm, first_offset_ref),
         (second_offset_hbm, second_offset_ref),
     ]
-    some = samples // CHUNKS
     copies = [
-        pltpu.make_async_copy(src, dst, sems.at[CHUNKS + n]) for n, (src, dst) in enumerate(small)
+        pltpu.make_async_copy(src, dst, sems.at[samples + n]) for n, (src, dst) in enumerate(small)
     ]
     for copy in copies:
         copy.start()
-    large = []
-    for n in range(CHUNKS):
-        rows = pl.ds(n * some, some)
-        large.append(pltpu.make_async_copy(x_hbm.at[rows], x_ref.at[rows], sems.at[n]))
-        large[-1].start()
+    large = [pltpu.make_async_copy(x_hbm.at[s], x_ref.at[s], sems.at[s]) for s in range(samples)]
+    for copy in large:
+        copy.start()
     for copy in copies:
         copy.wait()
 
@@ -95,9 +91,9 @@
     gather = (member // fold == group).astype(jnp.bfloat16)
 
     right = [jnp.zeros((tile, width), jnp.float32) for _ in range(tiles)]
+    for copy in large:
+        copy.wait()
     for s in range(samples):
-        if s % some == 0:
-            large[s // some].wait()
         normed = []
         for low in range(0, residues, BLOCK):
             values = x_ref[s, low : low + BLOCK, :].astype(jnp.float32)
@@ -256,7 +252,7 @@
             pltpu.VMEM((hidden, features), jnp.bfloat16),
             pltpu.VMEM((1, hidden), jnp.float32),
             pltpu.VMEM((residues * width // LANES, LANES), jnp.float32),
-            pltpu.SemaphoreType.DMA((CHUNKS + 6,)),
+            pltpu.SemaphoreType.DMA((here + 6,)),
         ],
         compiler_params=pltpu.CompilerParams(vmem_limit_bytes=32 * MIB),
         cost_estimate=pl.CostEstimate(

time: 31.4 us -> 31.6 us (level)
  no operation moved by 1% of the time
where the time goes in v14:
time: 31.6 us; the launch traced here: 31.4 us
  starting transfers between devices  14.9 us (47%)
  waiting for transfers between devices  8.19 us (26%)
  Pallas kernels  8.18 us (26%)
    ppermute x7, starting transfers between devices, per_device(): landed = [lax.ppermute(x, 'row', around) for x in flying]  13.9 us
    ppermute x7, waiting for transfers between devices, per_device(): landed = [lax.ppermute(x, 'row', around) for x in flying]  6.83 us
    pallas_call x1, Pallas kernels, per_device(): pl.pallas_call(functools.partial(pair_kernel, places, gridded, rows_here,...  4.43 us
    pallas_call x1, Pallas kernels, per_device(): pl.pallas_call(functools.partial(project_kernel, rows_here), out_shape=[r...  3.33 us
    ppermute x8, waiting for transfers between devices, swap(): return lax.ppermute(value, 'row', [(r, r ^ 1) for r in range(size)])  1.36 us
    ppermute x8, starting transfers between devices, swap(): return lax.ppermute(value, 'row', [(r, r ^ 1) for r in range(size)])  1.04 us
  transfers between devices with their start and end apart: 15, of which 8 were waited for; matrix products, arithmetic and copies ran while one was open for 0% of the time, Pallas kernels for 1%

profile of v14, /device:TPU:0, one launch (start us, length us, event | category | flops | bytes accessed | tf_op | source)
XLA Modules:
  0.0 31.4 jit_solution(2260356589629443572)
XLA Ops:
  0.0 3.3 %shard_map.91 = (bf16[384,256]{1,0:T(8,128)(2,1)S(1)}, bf16[384,256]{1,0:T(8,128)(2,1)S(1)}) custom-call(bf16[8,256,256]{2,1,0:T(8,128)(2,1)} %x_hbm.1, f32[1,256]{1,0:T(1,128)} %bitcast.10, f32[1,256]{1,0:T(1,128)} %bitcast.11, bf16[32,256]{1,0:T(8,128)(2,1)} %bitcast.8, f32[1,32]{1,0:T(1,128)} %bitcast.12, bf16[32,256]{1,0:T(8,128)(2,1)} %bitcast.9, ...), custom_call_target="tpu_custom_call" | custom-call | flops 536870912 | bytes 1048576 | tf_op jit(solution)/shard_map/pallas_call | solution.py:241
  3.3 0.5 %collective-permute-start = (bf16[384,256]{1,0:T(8,128)(2,1)S(1)}, bf16[384,256]{1,0:T(8,128)(2,1)S(1)}, u32[]{:S(2)}, u32[]{:S(2)}) collective-permute-start(bf16[384,256]{1,0:T(8,128)(2,1)S(1)} %get-tuple-element.24.refs_0_), channel_id=1, source_target_pairs={{0,1},{1,0},{2,3},{3,2},{4,5},{5,4},{6,7},{7,6},{8,9},{9,8},{10,11... | collective-permute-start | bytes 589832 | tf_op jit(solution)/shard_map/ppermute | solution.py:283
  3.9 2.6 %collective-permute-start.1 = (bf16[384,256]{1,0:T(8,128)(2,1)S(1)}, bf16[384,256]{1,0:T(8,128)(2,1)S(1)}, u32[]{:S(2)}, u32[]{:S(2)}) collective-permute-start(bf16[384,256]{1,0:T(8,128)(2,1)S(1)} %get-tuple-element.28), channel_id=1, source_target_pairs={{0,4},{1,3},{2,0},{3,7},{4,8},{5,1},{6,2},{7,11},{8,12},{9,5},{10,... | collective-permute-start | bytes 589832 | tf_op jit(solution)/shard_map/ppermute | solution.py:307
  6.5 0.4 %shard_map.92 = (bf16[128,1024]{1,0:T(8,128)(2,1)S(1)}, f32[1,128]{1,0:T(1,128)S(1)}) custom-call(bf16[1024,128]{1,0:T(8,128)(2,1)S(1)} %copy-done, f32[1,128]{1,0:T(1,128)S(1)} %bitcast.7), custom_call_target="tpu_custom_call" | custom-call | flops 268435456 | bytes 1048576 | tf_op jit(solution)/shard_map/pallas_call | solution.py:285
  6.9 0.0 collective-permute-done.refs_1_
  7.0 1.6 %collective-permute-start.2 = (bf16[352,256]{1,0:T(8,128)(2,1)S(1)}, bf16[352,256]{1,0:T(8,128)(2,1)S(1)}, u32[]{:S(2)}, u32[]{:S(2)}) collective-permute-start(bf16[352,256]{1,0:T(8,128)(2,1)S(1)} %slice.9), channel_id=1, source_target_pairs={{0,4},{1,3},{2,0},{3,7},{4,8},{5,1},{6,2},{7,11},{8,12},{9,5},{10,... | collective-permute-start | bytes 540680 | tf_op jit(solution)/shard_map/ppermute | solution.py:307
  8.6 1.5 %collective-permute-done.1.mine_ref.refs_2_ = bf16[384,256]{1,0:T(8,128)(2,1)S(1)} collective-permute-done((bf16[384,256]{1,0:T(8,128)(2,1)S(1)}, bf16[384,256]{1,0:T(8,128)(2,1)S(1)}, u32[]{:S(2)}, u32[]{:S(2)}) %collective-permute-start.1) | collective-permute-done | bytes 196640 | tf_op jit(solution)/shard_map/ppermute | solution.py:307
  10.1 2.1 %collective-permute-start.3 = (bf16[288,256]{1,0:T(8,128)(2,1)S(1)}, bf16[288,256]{1,0:T(8,128)(2,1)S(1)}, u32[]{:S(2)}, u32[]{:S(2)}) collective-permute-start(bf16[288,256]{1,0:T(8,128)(2,1)S(1)} %slice.12), channel_id=1, source_target_pairs={{0,4},{1,3},{2,0},{3,7},{4,8},{5,1},{6,2},{7,11},{8,12},{9,5},{10,... | collective-permute-start | bytes 442376 | tf_op jit(solution)/shard_map/ppermute | solution.py:307
  12.2 0.3 collective-permute-done.2.theirs_ref.refs_3_
  12.5 1.7 %collective-permute-start.4 = (bf16[384,256]{1,0:T(8,128)(2,1)S(1)}, bf16[384,256]{1,0:T(8,128)(2,1)S(1)}, u32[]{:S(2)}, u32[]{:S(2)}) collective-permute-start(bf16[384,256]{1,0:T(8,128)(2,1)S(1)} %shard_map.93), channel_id=1, source_target_pairs={{0,4},{1,3},{2,0},{3,7},{4,8},{5,1},{6,2},{7,11},{8,12},{9,5},{10,... | collective-permute-start | bytes 589832 | tf_op jit(solution)/shard_map/ppermute | solution.py:307
  14.2 1.1 %collective-permute-done.3.refs_4_ = bf16[288,256]{1,0:T(8,128)(2,1)S(1)} collective-permute-done((bf16[288,256]{1,0:T(8,128)(2,1)S(1)}, bf16[288,256]{1,0:T(8,128)(2,1)S(1)}, u32[]{:S(2)}, u32[]{:S(2)}) %collective-permute-start.3) | collective-permute-done | bytes 147488 | tf_op jit(solution)/shard_map/ppermute | solution.py:307
  15.3 2.1 %collective-permute-start.5 = (bf16[288,256]{1,0:T(8,128)(2,1)S(1)}, bf16[288,256]{1,0:T(8,128)(2,1)S(1)}, u32[]{:S(2)}, u32[]{:S(2)}) collective-permute-start(bf16[288,256]{1,0:T(8,128)(2,1)S(1)} %collective-permute-done.3.refs_4_), channel_id=1, source_target_pairs={{0,4},{1,3},{2,0},{3,7},{4,8},{5,1},{6,2},{7,11},{8,12},{9,5},{10,... | collective-permute-start | bytes 442376 | tf_op jit(solution)/shard_map/ppermute | solution.py:307
  17.4 0.0 collective-permute-start.7
  17.4 0.8 %collective-permute-done.4.refs_5_ = bf16[384,256]{1,0:T(8,128)(2,1)S(1)} collective-permute-done((bf16[384,256]{1,0:T(8,128)(2,1)S(1)}, bf16[384,256]{1,0:T(8,128)(2,1)S(1)}, u32[]{:S(2)}, u32[]{:S(2)}) %collective-permute-start.4) | collective-permute-done | bytes 196640 | tf_op jit(solution)/shard_map/ppermute | solution.py:307
  18.3 1.7 %collective-permute-start.6 = (bf16[320,256]{1,0:T(8,128)(2,1)S(1)}, bf16[320,256]{1,0:T(8,128)(2,1)S(1)}, u32[]{:S(2)}, u32[]{:S(2)}) collective-permute-start(bf16[320,256]{1,0:T(8,128)(2,1)S(1)} %slice.13), channel_id=1, source_target_pairs={{0,4},{1,3},{2,0},{3,7},{4,8},{5,1},{6,2},{7,11},{8,12},{9,5},{10,... | collective-permute-start | bytes 491528 | tf_op jit(solution)/shard_map/ppermute | solution.py:307
  19.9 0.5 %collective-permute-done.5.refs_6_ = bf16[288,256]{1,0:T(8,128)(2,1)S(1)} collective-permute-done((bf16[288,256]{1,0:T(8,128)(2,1)S(1)}, bf16[288,256]{1,0:T(8,128)(2,1)S(1)}, u32[]{:S(2)}, u32[]{:S(2)}) %collective-permute-start.5) | collective-permute-done | bytes 147488 | tf_op jit(solution)/shard_map/ppermute | solution.py:307
  20.5 2.1 %collective-permute-start.9 = (bf16[288,256]{1,0:T(8,128)(2,1)S(1)}, bf16[288,256]{1,0:T(8,128)(2,1)S(1)}, u32[]{:S(2)}, u32[]{:S(2)}) collective-permute-start(bf16[288,256]{1,0:T(8,128)(2,1)S(1)} %collective-permute-done.5.refs_6_), channel_id=1, source_target_pairs={{0,4},{1,3},{2,0},{3,7},{4,8},{5,1},{6,2},{7,11},{8,12},{9,5},{10,... | collective-permute-start | bytes 442376 | tf_op jit(solution)/shard_map/ppermute | solution.py:307
  22.5 0.0 collective-permute-done.8.refs_10_
  22.5 0.0 collective-permute-start.10
  22.5 1.1 %collective-permute-done.6.refs_7_ = bf16[320,256]{1,0:T(8,128)(2,1)S(1)} collective-permute-done((bf16[320,256]{1,0:T(8,128)(2,1)S(1)}, bf16[320,256]{1,0:T(8,128)(2,1)S(1)}, u32[]{:S(2)}, u32[]{:S(2)}) %collective-permute-start.6) | collective-permute-done | bytes 163872 | tf_op jit(solution)/shard_map/ppermute | solution.py:307
  23.6 0.5 %collective-permute-start.12 = (bf16[288,256]{1,0:T(8,128)(2,1)S(1)}, bf16[288,256]{1,0:T(8,128)(2,1)S(1)}, u32[]{:S(2)}, u32[]{:S(2)}) collective-permute-start(bf16[288,256]{1,0:T(8,128)(2,1)S(1)} %collective-permute-done.5.refs_6_), channel_id=1, source_target_pairs={{0,1},{1,0},{2,3},{3,2},{4,5},{5,4},{6,7},{7,6},{8,9},{9,8},{10,11... | collective-permute-start | bytes 442376 | tf_op jit(solution)/shard_map/ppermute | solution.py:283
  24.1 1.5 %collective-permute-done.9.refs_8_ = bf16[288,256]{1,0:T(8,128)(2,1)S(1)} collective-permute-done((bf16[288,256]{1,0:T(8,128)(2,1)S(1)}, bf16[288,256]{1,0:T(8,128)(2,1)S(1)}, u32[]{:S(2)}, u32[]{:S(2)}) %collective-permute-start.9) | collective-permute-done | bytes 147488 | tf_op jit(solution)/shard_map/ppermute | solution.py:307
  25.6 1.3 %collective-permute-done.14.refs_15_ = bf16[288,256]{1,0:T(8,128)(2,1)S(1)} collective-permute-done((bf16[288,256]{1,0:T(8,128)(2,1)S(1)}, bf16[288,256]{1,0:T(8,128)(2,1)S(1)}, u32[]{:S(2)}, u32[]{:S(2)}) %collective-permute-start.14) | collective-permute-done | bytes 147488 | tf_op jit(solution)/shard_map/ppermute | solution.py:283
  27.0 4.4 %shard_map.94 = bf16[16,256,128]{2,1,0:T(8,128)(2,1)} custom-call(bf16[384,256]{1,0:T(8,128)(2,1)S(1)} %get-tuple-element.24.refs_0_, bf16[384,256]{1,0:T(8,128)(2,1)S(1)} %collective-permute-done.refs_1_, bf16[384,256]{1,0:T(8,128)(2,1)S(1)} %collective-permute-done.1.mine_ref.refs_2_, bf16[352,256]{1,0:T(8,128)(2,1)S(1)} %collective-permute-done.2.theirs_ref.refs_3_, ...), custom_call_target="tpu_custom_call" | custom-call | tf_op jit(solution)/shard_map/pallas_call | solution.py:355
  (17 shorter events, 0.1 us)
Async XLA Ops:
  0.0 6.5 %copy-start = (bf16[1024,128]{1,0:T(8,128)(2,1)S(1)}, bf16[1024,128]{1,0:T(8,128)(2,1)}, u32[]{:S(2)}) copy-start(bf16[1024,128]{1,0:T(8,128)(2,1)} %final_ref.1) | copy-start | bytes 786436
  3.3 3.6 %collective-permute-start = (bf16[384,256]{1,0:T(8,128)(2,1)S(1)}, bf16[384,256]{1,0:T(8,128)(2,1)S(1)}, u32[]{:S(2)}, u32[]{:S(2)}) collective-permute-start(bf16[384,256]{1,0:T(8,128)(2,1)S(1)} %get-tuple-element.24.refs_0_), channel_id=1, source_target_pairs={{0,1},{1,0},{2,3},{3,2},{4,5},{5,4},{6,7},{7,6},{8,9},{9,8},{10,11... | collective-permute-start | bytes 589832 | tf_op jit(solution)/shard_map/ppermute | solution.py:283
  3.9 2.7 %copy-start.1 = (f32[128]{0:T(128)S(1)}, f32[128]{0:T(128)}, u32[]{:S(2)}) copy-start(f32[128]{0:T(128)} %param.17) | copy-start | bytes 1540
  3.9 6.2 %collective-permute-start.1 = (bf16[384,256]{1,0:T(8,128)(2,1)S(1)}, bf16[384,256]{1,0:T(8,128)(2,1)S(1)}, u32[]{:S(2)}, u32[]{:S(2)}) collective-permute-start(bf16[384,256]{1,0:T(8,128)(2,1)S(1)} %get-tuple-element.28), channel_id=1, source_target_pairs={{0,4},{1,3},{2,0},{3,7},{4,8},{5,1},{6,2},{7,11},{8,12},{9,5},{10,... | collective-permute-start | bytes 589832 | tf_op jit(solution)/shard_map/ppermute | solution.py:307
  7.0 5.5 %collective-permute-start.2 = (bf16[352,256]{1,0:T(8,128)(2,1)S(1)}, bf16[352,256]{1,0:T(8,128)(2,1)S(1)}, u32[]{:S(2)}, u32[]{:S(2)}) collective-permute-start(bf16[352,256]{1,0:T(8,128)(2,1)S(1)} %slice.9), channel_id=1, source_target_pairs={{0,4},{1,3},{2,0},{3,7},{4,8},{5,1},{6,2},{7,11},{8,12},{9,5},{10,... | collective-permute-start | bytes 540680 | tf_op jit(solution)/shard_map/ppermute | solution.py:307
  10.1 5.2 %collective-permute-start.3 = (bf16[288,256]{1,0:T(8,128)(2,1)S(1)}, bf16[288,256]{1,0:T(8,128)(2,1)S(1)}, u32[]{:S(2)}, u32[]{:S(2)}) collective-permute-start(bf16[288,256]{1,0:T(8,128)(2,1)S(1)} %slice.12), channel_id=1, source_target_pairs={{0,4},{1,3},{2,0},{3,7},{4,8},{5,1},{6,2},{7,11},{8,12},{9,5},{10,... | collective-permute-start | bytes 442376 | tf_op jit(solution)/shard_map/ppermute | solution.py:307
  12.5 5.7 %collective-permute-start.4 = (bf16[384,256]{1,0:T(8,128)(2,1)S(1)}, bf16[384,256]{1,0:T(8,128)(2,1)S(1)}, u32[]{:S(2)}, u32[]{:S(2)}) collective-permute-start(bf16[384,256]{1,0:T(8,128)(2,1)S(1)} %shard_map.93), channel_id=1, source_target_pairs={{0,4},{1,3},{2,0},{3,7},{4,8},{5,1},{6,2},{7,11},{8,12},{9,5},{10,... | collective-permute-start | bytes 589832 | tf_op jit(solution)/shard_map/ppermute | solution.py:307
  14.2 8.4 %collective-permute-start.8 = (bf16[352,256]{1,0:T(8,128)(2,1)S(1)}, bf16[352,256]{1,0:T(8,128)(2,1)S(1)}, u32[]{:S(2)}, u32[]{:S(2)}) collective-permute-start(bf16[352,256]{1,0:T(8,128)(2,1)S(1)} %collective-permute-done.2.theirs_ref.refs_3_), channel_id=1, source_target_pairs={{0,1},{1,0},{2,3},{3,2},{4,5},{5,4},{6,7},{7,6},{8,9},{9,8},{10,11... | collective-permute-start | bytes 540680 | tf_op jit(solution)/shard_map/ppermute | solution.py:283
  15.3 5.1 %collective-permute-start.5 = (bf16[288,256]{1,0:T(8,128)(2,1)S(1)}, bf16[288,256]{1,0:T(8,128)(2,1)S(1)}, u32[]{:S(2)}, u32[]{:S(2)}) collective-permute-start(bf16[288,256]{1,0:T(8,128)(2,1)S(1)} %collective-permute-done.3.refs_4_), channel_id=1, source_target_pairs={{0,4},{1,3},{2,0},{3,7},{4,8},{5,1},{6,2},{7,11},{8,12},{9,5},{10,... | collective-permute-start | bytes 442376 | tf_op jit(solution)/shard_map/ppermute | solution.py:307
  17.4 5.2 %collective-permute-start.7 = (bf16[384,256]{1,0:T(8,128)(2,1)S(1)}, bf16[384,256]{1,0:T(8,128)(2,1)S(1)}, u32[]{:S(2)}, u32[]{:S(2)}) collective-permute-start(bf16[384,256]{1,0:T(8,128)(2,1)S(1)} %collective-permute-done.1.mine_ref.refs_2_), channel_id=1, source_target_pairs={{0,1},{1,0},{2,3},{3,2},{4,5},{5,4},{6,7},{7,6},{8,9},{9,8},{10,11... | collective-permute-start | bytes 589832 | tf_op jit(solution)/shard_map/ppermute | solution.py:283
  18.2 7.4 %collective-permute-start.11 = (bf16[384,256]{1,0:T(8,128)(2,1)S(1)}, bf16[384,256]{1,0:T(8,128)(2,1)S(1)}, u32[]{:S(2)}, u32[]{:S(2)}) collective-permute-start(bf16[384,256]{1,0:T(8,128)(2,1)S(1)} %collective-permute-done.4.refs_5_), channel_id=1, source_target_pairs={{0,1},{1,0},{2,3},{3,2},{4,5},{5,4},{6,7},{7,6},{8,9},{9,8},{10,11... | collective-permute-start | bytes 589832 | tf_op jit(solution)/shard_map/ppermute | solution.py:283
  18.3 5.4 %collective-permute-start.6 = (bf16[320,256]{1,0:T(8,128)(2,1)S(1)}, bf16[320,256]{1,0:T(8,128)(2,1)S(1)}, u32[]{:S(2)}, u32[]{:S(2)}) collective-permute-start(bf16[320,256]{1,0:T(8,128)(2,1)S(1)} %slice.13), channel_id=1, source_target_pairs={{0,4},{1,3},{2,0},{3,7},{4,8},{5,1},{6,2},{7,11},{8,12},{9,5},{10,... | collective-permute-start | bytes 491528 | tf_op jit(solution)/shard_map/ppermute | solution.py:307
  20.5 5.1 %collective-permute-start.9 = (bf16[288,256]{1,0:T(8,128)(2,1)S(1)}, bf16[288,256]{1,0:T(8,128)(2,1)S(1)}, u32[]{:S(2)}, u32[]{:S(2)}) collective-permute-start(bf16[288,256]{1,0:T(8,128)(2,1)S(1)} %collective-permute-done.5.refs_6_), channel_id=1, source_target_pairs={{0,4},{1,3},{2,0},{3,7},{4,8},{5,1},{6,2},{7,11},{8,12},{9,5},{10,... | collective-permute-start | bytes 442376 | tf_op jit(solution)/shard_map/ppermute | solution.py:307
  22.5 3.1 %collective-permute-start.10 = (bf16[288,256]{1,0:T(8,128)(2,1)S(1)}, bf16[288,256]{1,0:T(8,128)(2,1)S(1)}, u32[]{:S(2)}, u32[]{:S(2)}) collective-permute-start(bf16[288,256]{1,0:T(8,128)(2,1)S(1)} %collective-permute-done.3.refs_4_), channel_id=1, source_target_pairs={{0,1},{1,0},{2,3},{3,2},{4,5},{5,4},{6,7},{7,6},{8,9},{9,8},{10,11... | collective-permute-start | bytes 442376 | tf_op jit(solution)/shard_map/ppermute | solution.py:283
  23.6 2.0 %collective-permute-start.13 = (bf16[320,256]{1,0:T(8,128)(2,1)S(1)}, bf16[320,256]{1,0:T(8,128)(2,1)S(1)}, u32[]{:S(2)}, u32[]{:S(2)}) collective-permute-start(bf16[320,256]{1,0:T(8,128)(2,1)S(1)} %collective-permute-done.6.refs_7_), channel_id=1, source_target_pairs={{0,1},{1,0},{2,3},{3,2},{4,5},{5,4},{6,7},{7,6},{8,9},{9,8},{10,11... | collective-permute-start | bytes 491528 | tf_op jit(solution)/shard_map/ppermute | solution.py:283
  23.6 2.0 %collective-permute-start.12 = (bf16[288,256]{1,0:T(8,128)(2,1)S(1)}, bf16[288,256]{1,0:T(8,128)(2,1)S(1)}, u32[]{:S(2)}, u32[]{:S(2)}) collective-permute-start(bf16[288,256]{1,0:T(8,128)(2,1)S(1)} %collective-permute-done.5.refs_6_), channel_id=1, source_target_pairs={{0,1},{1,0},{2,3},{3,2},{4,5},{5,4},{6,7},{7,6},{8,9},{9,8},{10,11... | collective-permute-start | bytes 442376 | tf_op jit(solution)/shard_map/ppermute | solution.py:283
  25.6 1.4 %collective-permute-start.14 = (bf16[288,256]{1,0:T(8,128)(2,1)S(1)}, bf16[288,256]{1,0:T(8,128)(2,1)S(1)}, u32[]{:S(2)}, u32[]{:S(2)}) collective-permute-start(bf16[288,256]{1,0:T(8,128)(2,1)S(1)} %collective-permute-done.9.refs_8_), channel_id=1, source_target_pairs={{0,1},{1,0},{2,3},{3,2},{4,5},{5,4},{6,7},{7,6},{8,9},{9,8},{10,11... | collective-permute-start | bytes 442376 | tf_op jit(solution)/shard_map/ppermute | solution.py:283

commit v15 on v13

--- a/solution.py
+++ b/solution.py
@@ -125,7 +125,7 @@
     per_chip = 2 * rows_here * hidden * samples // tile
     half = residues // rows_here // 4
     base = tiles * width
-    way = 1 - 2 * (device % 2)
+    way = 2 * (device % 2) - 1
     place = place_of(device, half)
     spots = [(keep_ref, base + n * per_chip, half - n) for n in range(half)]
     spots += [(give_ref, base + n * per_chip, n + 1 - half) for n in range(half)]
@@ -280,7 +280,7 @@
     )
     by_place = {(place_of(r, half), r % 2): r for r in range(size)}
     around = [
-        (r, by_place[(place_of(r, half) + 1 - 2 * (r % 2)) % (2 * half), r % 2]) for r in range(size)
+        (r, by_place[(place_of(r, half) + 2 * (r % 2) - 1) % (2 * half), r % 2]) for r in range(size)
     ]
 
     def swap(value):

time: 31.4 us -> 31.5 us (level)
  waiting for transfers between devices: 8.19 us -> 8.63 us
  starting transfers between devices: 14.9 us -> 14.5 us
    ppermute x7, waiting for transfers between devices: 6.82 us -> 7.27 us  [per_device(): landed = [lax.ppermute(x, 'row', around) for x in flying]]
    ppermute x7, starting transfers between devices: 13.9 us -> 13.5 us  [per_device(): landed = [lax.ppermute(x, 'row', around) for x in flying]]
where the time goes in v15:
time: 31.5 us; the launch traced here: 31.4 us
  starting transfers between devices  14.5 us (46%)
  waiting for transfers between devices  8.63 us (27%)
  Pallas kernels  8.07 us (26%)
    ppermute x7, starting transfers between devices, per_device(): landed = [lax.ppermute(x, 'row', around) for x in flying]  13.5 us
    ppermute x7, waiting for transfers between devices, per_device(): landed = [lax.ppermute(x, 'row', around) for x in flying]  7.27 us
    pallas_call x1, Pallas kernels, per_device(): pl.pallas_call(functools.partial(pair_kernel, places, gridded, rows_here,...  4.43 us
    pallas_call x1, Pallas kernels, per_device(): pl.pallas_call(functools.partial(project_kernel, rows_here), out_shape=[r...  3.22 us
    ppermute x8, waiting for transfers between devices, swap(): return lax.ppermute(value, 'row', [(r, r ^ 1) for r in range(size)])  1.36 us
    ppermute x8, starting transfers between devices, swap(): return lax.ppermute(value, 'row', [(r, r ^ 1) for r in range(size)])  1.04 us
  transfers between devices with their start and end apart: 15, of which 8 were waited for; matrix products, arithmetic and copies ran while one was open for 0% of the time, Pallas kernels for 1%

profile of v15, /device:TPU:0, one launch (start us, length us, event | category | flops | bytes accessed | tf_op | source)
XLA Modules:
  0.0 31.4 jit_solution(11672576294528476779)
XLA Ops:
  0.0 3.2 %shard_map.91 = (bf16[384,256]{1,0:T(8,128)(2,1)S(1)}, bf16[384,256]{1,0:T(8,128)(2,1)S(1)}) custom-call(bf16[8,256,256]{2,1,0:T(8,128)(2,1)} %x_hbm.1, f32[1,256]{1,0:T(1,128)} %bitcast.10, f32[1,256]{1,0:T(1,128)} %bitcast.11, bf16[32,256]{1,0:T(8,128)(2,1)} %bitcast.8, f32[1,32]{1,0:T(1,128)} %bitcast.12, bf16[32,256]{1,0:T(8,128)(2,1)} %bitcast.9, ...), custom_call_target="tpu_custom_call" | custom-call | flops 536870912 | bytes 1048576 | tf_op jit(solution)/shard_map/pallas_call | solution.py:245
  3.2 0.5 %collective-permute-start = (bf16[384,256]{1,0:T(8,128)(2,1)S(1)}, bf16[384,256]{1,0:T(8,128)(2,1)S(1)}, u32[]{:S(2)}, u32[]{:S(2)}) collective-permute-start(bf16[384,256]{1,0:T(8,128)(2,1)S(1)} %get-tuple-element.24.refs_0_), channel_id=1, source_target_pairs={{0,1},{1,0},{2,3},{3,2},{4,5},{5,4},{6,7},{7,6},{8,9},{9,8},{10,11... | collective-permute-start | bytes 589832 | tf_op jit(solution)/shard_map/ppermute | solution.py:287
  3.8 2.6 %collective-permute-start.1 = (bf16[384,256]{1,0:T(8,128)(2,1)S(1)}, bf16[384,256]{1,0:T(8,128)(2,1)S(1)}, u32[]{:S(2)}, u32[]{:S(2)}) collective-permute-start(bf16[384,256]{1,0:T(8,128)(2,1)S(1)} %get-tuple-element.28), channel_id=1, source_target_pairs={{0,2},{1,5},{2,6},{3,1},{4,0},{5,9},{6,10},{7,3},{8,4},{9,13},{10,... | collective-permute-start | bytes 589832 | tf_op jit(solution)/shard_map/ppermute | solution.py:311
  6.3 0.4 %shard_map.92 = (bf16[128,1024]{1,0:T(8,128)(2,1)S(1)}, f32[1,128]{1,0:T(1,128)S(1)}) custom-call(bf16[1024,128]{1,0:T(8,128)(2,1)S(1)} %copy-done, f32[1,128]{1,0:T(1,128)S(1)} %bitcast.7), custom_call_target="tpu_custom_call" | custom-call | flops 268435456 | bytes 1048576 | tf_op jit(solution)/shard_map/pallas_call | solution.py:289
  6.8 1.6 %collective-permute-start.2 = (bf16[352,256]{1,0:T(8,128)(2,1)S(1)}, bf16[352,256]{1,0:T(8,128)(2,1)S(1)}, u32[]{:S(2)}, u32[]{:S(2)}) collective-permute-start(bf16[352,256]{1,0:T(8,128)(2,1)S(1)} %slice.9), channel_id=1, source_target_pairs={{0,2},{1,5},{2,6},{3,1},{4,0},{5,9},{6,10},{7,3},{8,4},{9,13},{10,... | collective-permute-start | bytes 540680 | tf_op jit(solution)/shard_map/ppermute | solution.py:311
  8.4 1.6 %collective-permute-done.1.mine_ref.refs_2_ = bf16[384,256]{1,0:T(8,128)(2,1)S(1)} collective-permute-done((bf16[384,256]{1,0:T(8,128)(2,1)S(1)}, bf16[384,256]{1,0:T(8,128)(2,1)S(1)}, u32[]{:S(2)}, u32[]{:S(2)}) %collective-permute-start.1) | collective-permute-done | bytes 196640 | tf_op jit(solution)/shard_map/ppermute | solution.py:311
  10.1 2.0 %collective-permute-start.3 = (bf16[288,256]{1,0:T(8,128)(2,1)S(1)}, bf16[288,256]{1,0:T(8,128)(2,1)S(1)}, u32[]{:S(2)}, u32[]{:S(2)}) collective-permute-start(bf16[288,256]{1,0:T(8,128)(2,1)S(1)} %slice.12), channel_id=1, source_target_pairs={{0,2},{1,5},{2,6},{3,1},{4,0},{5,9},{6,10},{7,3},{8,4},{9,13},{10,... | collective-permute-start | bytes 442376 | tf_op jit(solution)/shard_map/ppermute | solution.py:311
  12.1 0.3 collective-permute-done.2.theirs_ref.refs_3_
  12.3 1.7 %collective-permute-start.4 = (bf16[384,256]{1,0:T(8,128)(2,1)S(1)}, bf16[384,256]{1,0:T(8,128)(2,1)S(1)}, u32[]{:S(2)}, u32[]{:S(2)}) collective-permute-start(bf16[384,256]{1,0:T(8,128)(2,1)S(1)} %shard_map.93), channel_id=1, source_target_pairs={{0,2},{1,5},{2,6},{3,1},{4,0},{5,9},{6,10},{7,3},{8,4},{9,13},{10,... | collective-permute-start | bytes 589832 | tf_op jit(solution)/shard_map/ppermute | solution.py:311
  14.0 0.0 collective-permute-start.8
  14.0 1.2 %collective-permute-done.3.refs_4_ = bf16[288,256]{1,0:T(8,128)(2,1)S(1)} collective-permute-done((bf16[288,256]{1,0:T(8,128)(2,1)S(1)}, bf16[288,256]{1,0:T(8,128)(2,1)S(1)}, u32[]{:S(2)}, u32[]{:S(2)}) %collective-permute-start.3) | collective-permute-done | bytes 147488 | tf_op jit(solution)/shard_map/ppermute | solution.py:311
  15.3 2.0 %collective-permute-start.5 = (bf16[288,256]{1,0:T(8,128)(2,1)S(1)}, bf16[288,256]{1,0:T(8,128)(2,1)S(1)}, u32[]{:S(2)}, u32[]{:S(2)}) collective-permute-start(bf16[288,256]{1,0:T(8,128)(2,1)S(1)} %collective-permute-done.3.refs_4_), channel_id=1, source_target_pairs={{0,2},{1,5},{2,6},{3,1},{4,0},{5,9},{6,10},{7,3},{8,4},{9,13},{10,... | collective-permute-start | bytes 442376 | tf_op jit(solution)/shard_map/ppermute | solution.py:311
  17.2 0.8 %collective-permute-done.4.refs_5_ = bf16[384,256]{1,0:T(8,128)(2,1)S(1)} collective-permute-done((bf16[384,256]{1,0:T(8,128)(2,1)S(1)}, bf16[384,256]{1,0:T(8,128)(2,1)S(1)}, u32[]{:S(2)}, u32[]{:S(2)}) %collective-permute-start.4) | collective-permute-done | bytes 196640 | tf_op jit(solution)/shard_map/ppermute | solution.py:311
  18.1 1.7 %collective-permute-start.6 = (bf16[320,256]{1,0:T(8,128)(2,1)S(1)}, bf16[320,256]{1,0:T(8,128)(2,1)S(1)}, u32[]{:S(2)}, u32[]{:S(2)}) collective-permute-start(bf16[320,256]{1,0:T(8,128)(2,1)S(1)} %slice.13), channel_id=1, source_target_pairs={{0,2},{1,5},{2,6},{3,1},{4,0},{5,9},{6,10},{7,3},{8,4},{9,13},{10,... | collective-permute-start | bytes 491528 | tf_op jit(solution)/shard_map/ppermute | solution.py:311
  19.8 0.6 %collective-permute-done.5.refs_6_ = bf16[288,256]{1,0:T(8,128)(2,1)S(1)} collective-permute-done((bf16[288,256]{1,0:T(8,128)(2,1)S(1)}, bf16[288,256]{1,0:T(8,128)(2,1)S(1)}, u32[]{:S(2)}, u32[]{:S(2)}) %collective-permute-start.5) | collective-permute-done | bytes 147488 | tf_op jit(solution)/shard_map/ppermute | solution.py:311
  20.4 2.0 %collective-permute-start.9 = (bf16[288,256]{1,0:T(8,128)(2,1)S(1)}, bf16[288,256]{1,0:T(8,128)(2,1)S(1)}, u32[]{:S(2)}, u32[]{:S(2)}) collective-permute-start(bf16[288,256]{1,0:T(8,128)(2,1)S(1)} %collective-permute-done.5.refs_6_), channel_id=1, source_target_pairs={{0,2},{1,5},{2,6},{3,1},{4,0},{5,9},{6,10},{7,3},{8,4},{9,13},{10,... | collective-permute-start | bytes 442376 | tf_op jit(solution)/shard_map/ppermute | solution.py:311
  22.4 0.0 collective-permute-done.8.refs_10_
  22.4 0.0 collective-permute-start.10
  22.4 1.1 %collective-permute-done.6.refs_7_ = bf16[320,256]{1,0:T(8,128)(2,1)S(1)} collective-permute-done((bf16[320,256]{1,0:T(8,128)(2,1)S(1)}, bf16[320,256]{1,0:T(8,128)(2,1)S(1)}, u32[]{:S(2)}, u32[]{:S(2)}) %collective-permute-start.6) | collective-permute-done | bytes 163872 | tf_op jit(solution)/shard_map/ppermute | solution.py:311
  23.5 0.5 %collective-permute-start.12 = (bf16[288,256]{1,0:T(8,128)(2,1)S(1)}, bf16[288,256]{1,0:T(8,128)(2,1)S(1)}, u32[]{:S(2)}, u32[]{:S(2)}) collective-permute-start(bf16[288,256]{1,0:T(8,128)(2,1)S(1)} %collective-permute-done.5.refs_6_), channel_id=1, source_target_pairs={{0,1},{1,0},{2,3},{3,2},{4,5},{5,4},{6,7},{7,6},{8,9},{9,8},{10,11... | collective-permute-start | bytes 442376 | tf_op jit(solution)/shard_map/ppermute | solution.py:287
  24.0 1.6 %collective-permute-done.9.refs_8_ = bf16[288,256]{1,0:T(8,128)(2,1)S(1)} collective-permute-done((bf16[288,256]{1,0:T(8,128)(2,1)S(1)}, bf16[288,256]{1,0:T(8,128)(2,1)S(1)}, u32[]{:S(2)}, u32[]{:S(2)}) %collective-permute-start.9) | collective-permute-done | bytes 147488 | tf_op jit(solution)/shard_map/ppermute | solution.py:311
  25.5 0.0 collective-permute-done.11.refs_12_
  25.6 1.3 %collective-permute-done.14.refs_15_ = bf16[288,256]{1,0:T(8,128)(2,1)S(1)} collective-permute-done((bf16[288,256]{1,0:T(8,128)(2,1)S(1)}, bf16[288,256]{1,0:T(8,128)(2,1)S(1)}, u32[]{:S(2)}, u32[]{:S(2)}) %collective-permute-start.14) | collective-permute-done | bytes 147488 | tf_op jit(solution)/shard_map/ppermute | solution.py:287
  26.9 4.4 %shard_map.94 = bf16[16,256,128]{2,1,0:T(8,128)(2,1)} custom-call(bf16[384,256]{1,0:T(8,128)(2,1)S(1)} %get-tuple-element.24.refs_0_, bf16[384,256]{1,0:T(8,128)(2,1)S(1)} %collective-permute-done.refs_1_, bf16[384,256]{1,0:T(8,128)(2,1)S(1)} %collective-permute-done.1.mine_ref.refs_2_, bf16[352,256]{1,0:T(8,128)(2,1)S(1)} %collective-permute-done.2.theirs_ref.refs_3_, ...), custom_call_target="tpu_custom_call" | custom-call | tf_op jit(solution)/shard_map/pallas_call | solution.py:359
  (17 shorter events, 0.1 us)
Async XLA Ops:
  0.0 6.3 %copy-start = (bf16[1024,128]{1,0:T(8,128)(2,1)S(1)}, bf16[1024,128]{1,0:T(8,128)(2,1)}, u32[]{:S(2)}) copy-start(bf16[1024,128]{1,0:T(8,128)(2,1)} %final_ref.1) | copy-start | bytes 786436
  3.2 3.5 %collective-permute-start = (bf16[384,256]{1,0:T(8,128)(2,1)S(1)}, bf16[384,256]{1,0:T(8,128)(2,1)S(1)}, u32[]{:S(2)}, u32[]{:S(2)}) collective-permute-start(bf16[384,256]{1,0:T(8,128)(2,1)S(1)} %get-tuple-element.24.refs_0_), channel_id=1, source_target_pairs={{0,1},{1,0},{2,3},{3,2},{4,5},{5,4},{6,7},{7,6},{8,9},{9,8},{10,11... | collective-permute-start | bytes 589832 | tf_op jit(solution)/shard_map/ppermute | solution.py:287
  3.8 2.6 %copy-start.1 = (f32[128]{0:T(128)S(1)}, f32[128]{0:T(128)}, u32[]{:S(2)}) copy-start(f32[128]{0:T(128)} %param.17) | copy-start | bytes 1540
  3.8 6.3 %collective-permute-start.1 = (bf16[384,256]{1,0:T(8,128)(2,1)S(1)}, bf16[384,256]{1,0:T(8,128)(2,1)S(1)}, u32[]{:S(2)}, u32[]{:S(2)}) collective-permute-start(bf16[384,256]{1,0:T(8,128)(2,1)S(1)} %get-tuple-element.28), channel_id=1, source_target_pairs={{0,2},{1,5},{2,6},{3,1},{4,0},{5,9},{6,10},{7,3},{8,4},{9,13},{10,... | collective-permute-start | bytes 589832 | tf_op jit(solution)/shard_map/ppermute | solution.py:311
  6.8 5.5 %collective-permute-start.2 = (bf16[352,256]{1,0:T(8,128)(2,1)S(1)}, bf16[352,256]{1,0:T(8,128)(2,1)S(1)}, u32[]{:S(2)}, u32[]{:S(2)}) collective-permute-start(bf16[352,256]{1,0:T(8,128)(2,1)S(1)} %slice.9), channel_id=1, source_target_pairs={{0,2},{1,5},{2,6},{3,1},{4,0},{5,9},{6,10},{7,3},{8,4},{9,13},{10,... | collective-permute-start | bytes 540680 | tf_op jit(solution)/shard_map/ppermute | solution.py:311
  10.1 5.2 %collective-permute-start.3 = (bf16[288,256]{1,0:T(8,128)(2,1)S(1)}, bf16[288,256]{1,0:T(8,128)(2,1)S(1)}, u32[]{:S(2)}, u32[]{:S(2)}) collective-permute-start(bf16[288,256]{1,0:T(8,128)(2,1)S(1)} %slice.12), channel_id=1, source_target_pairs={{0,2},{1,5},{2,6},{3,1},{4,0},{5,9},{6,10},{7,3},{8,4},{9,13},{10,... | collective-permute-start | bytes 442376 | tf_op jit(solution)/shard_map/ppermute | solution.py:311
  12.3 5.7 %collective-permute-start.4 = (bf16[384,256]{1,0:T(8,128)(2,1)S(1)}, bf16[384,256]{1,0:T(8,128)(2,1)S(1)}, u32[]{:S(2)}, u32[]{:S(2)}) collective-permute-start(bf16[384,256]{1,0:T(8,128)(2,1)S(1)} %shard_map.93), channel_id=1, source_target_pairs={{0,2},{1,5},{2,6},{3,1},{4,0},{5,9},{6,10},{7,3},{8,4},{9,13},{10,... | collective-permute-start | bytes 589832 | tf_op jit(solution)/shard_map/ppermute | solution.py:311
  14.0 8.4 %collective-permute-start.8 = (bf16[352,256]{1,0:T(8,128)(2,1)S(1)}, bf16[352,256]{1,0:T(8,128)(2,1)S(1)}, u32[]{:S(2)}, u32[]{:S(2)}) collective-permute-start(bf16[352,256]{1,0:T(8,128)(2,1)S(1)} %collective-permute-done.2.theirs_ref.refs_3_), channel_id=1, source_target_pairs={{0,1},{1,0},{2,3},{3,2},{4,5},{5,4},{6,7},{7,6},{8,9},{9,8},{10,11... | collective-permute-start | bytes 540680 | tf_op jit(solution)/shard_map/ppermute | solution.py:287
  15.3 5.1 %collective-permute-start.5 = (bf16[288,256]{1,0:T(8,128)(2,1)S(1)}, bf16[288,256]{1,0:T(8,128)(2,1)S(1)}, u32[]{:S(2)}, u32[]{:S(2)}) collective-permute-start(bf16[288,256]{1,0:T(8,128)(2,1)S(1)} %collective-permute-done.3.refs_4_), channel_id=1, source_target_pairs={{0,2},{1,5},{2,6},{3,1},{4,0},{5,9},{6,10},{7,3},{8,4},{9,13},{10,... | collective-permute-start | bytes 442376 | tf_op jit(solution)/shard_map/ppermute | solution.py:311
  17.2 5.2 %collective-permute-start.7 = (bf16[384,256]{1,0:T(8,128)(2,1)S(1)}, bf16[384,256]{1,0:T(8,128)(2,1)S(1)}, u32[]{:S(2)}, u32[]{:S(2)}) collective-permute-start(bf16[384,256]{1,0:T(8,128)(2,1)S(1)} %collective-permute-done.1.mine_ref.refs_2_), channel_id=1, source_target_pairs={{0,1},{1,0},{2,3},{3,2},{4,5},{5,4},{6,7},{7,6},{8,9},{9,8},{10,11... | collective-permute-start | bytes 589832 | tf_op jit(solution)/shard_map/ppermute | solution.py:287
  18.1 7.5 %collective-permute-start.11 = (bf16[384,256]{1,0:T(8,128)(2,1)S(1)}, bf16[384,256]{1,0:T(8,128)(2,1)S(1)}, u32[]{:S(2)}, u32[]{:S(2)}) collective-permute-start(bf16[384,256]{1,0:T(8,128)(2,1)S(1)} %collective-permute-done.4.refs_5_), channel_id=1, source_target_pairs={{0,1},{1,0},{2,3},{3,2},{4,5},{5,4},{6,7},{7,6},{8,9},{9,8},{10,11... | collective-permute-start | bytes 589832 | tf_op jit(solution)/shard_map/ppermute | solution.py:287
  18.1 5.4 %collective-permute-start.6 = (bf16[320,256]{1,0:T(8,128)(2,1)S(1)}, bf16[320,256]{1,0:T(8,128)(2,1)S(1)}, u32[]{:S(2)}, u32[]{:S(2)}) collective-permute-start(bf16[320,256]{1,0:T(8,128)(2,1)S(1)} %slice.13), channel_id=1, source_target_pairs={{0,2},{1,5},{2,6},{3,1},{4,0},{5,9},{6,10},{7,3},{8,4},{9,13},{10,... | collective-permute-start | bytes 491528 | tf_op jit(solution)/shard_map/ppermute | solution.py:311
  20.4 5.1 %collective-permute-start.9 = (bf16[288,256]{1,0:T(8,128)(2,1)S(1)}, bf16[288,256]{1,0:T(8,128)(2,1)S(1)}, u32[]{:S(2)}, u32[]{:S(2)}) collective-permute-start(bf16[288,256]{1,0:T(8,128)(2,1)S(1)} %collective-permute-done.5.refs_6_), channel_id=1, source_target_pairs={{0,2},{1,5},{2,6},{3,1},{4,0},{5,9},{6,10},{7,3},{8,4},{9,13},{10,... | collective-permute-start | bytes 442376 | tf_op jit(solution)/shard_map/ppermute | solution.py:311
  22.4 3.2 %collective-permute-start.10 = (bf16[288,256]{1,0:T(8,128)(2,1)S(1)}, bf16[288,256]{1,0:T(8,128)(2,1)S(1)}, u32[]{:S(2)}, u32[]{:S(2)}) collective-permute-start(bf16[288,256]{1,0:T(8,128)(2,1)S(1)} %collective-permute-done.3.refs_4_), channel_id=1, source_target_pairs={{0,1},{1,0},{2,3},{3,2},{4,5},{5,4},{6,7},{7,6},{8,9},{9,8},{10,11... | collective-permute-start | bytes 442376 | tf_op jit(solution)/shard_map/ppermute | solution.py:287
  23.5 2.1 %collective-permute-start.13 = (bf16[320,256]{1,0:T(8,128)(2,1)S(1)}, bf16[320,256]{1,0:T(8,128)(2,1)S(1)}, u32[]{:S(2)}, u32[]{:S(2)}) collective-permute-start(bf16[320,256]{1,0:T(8,128)(2,1)S(1)} %collective-permute-done.6.refs_7_), channel_id=1, source_target_pairs={{0,1},{1,0},{2,3},{3,2},{4,5},{5,4},{6,7},{7,6},{8,9},{9,8},{10,11... | collective-permute-start | bytes 491528 | tf_op jit(solution)/shard_map/ppermute | solution.py:287
  23.5 2.1 %collective-permute-start.12 = (bf16[288,256]{1,0:T(8,128)(2,1)S(1)}, bf16[288,256]{1,0:T(8,128)(2,1)S(1)}, u32[]{:S(2)}, u32[]{:S(2)}) collective-permute-start(bf16[288,256]{1,0:T(8,128)(2,1)S(1)} %collective-permute-done.5.refs_6_), channel_id=1, source_target_pairs={{0,1},{1,0},{2,3},{3,2},{4,5},{5,4},{6,7},{7,6},{8,9},{9,8},{10,11... | collective-permute-start | bytes 442376 | tf_op jit(solution)/shard_map/ppermute | solution.py:287
  25.5 1.4 %collective-permute-start.14 = (bf16[288,256]{1,0:T(8,128)(2,1)S(1)}, bf16[288,256]{1,0:T(8,128)(2,1)S(1)}, u32[]{:S(2)}, u32[]{:S(2)}) collective-permute-start(bf16[288,256]{1,0:T(8,128)(2,1)S(1)} %collective-permute-done.9.refs_8_), channel_id=1, source_target_pairs={{0,1},{1,0},{2,3},{3,2},{4,5},{5,4},{6,7},{7,6},{8,9},{9,8},{10,11... | collective-permute-start | bytes 442376 | tf_op jit(solution)/shard_map/ppermute | solution.py:287

commit v16 on v15

--- a/solution.py
+++ b/solution.py
@@ -12,6 +12,7 @@
 LANES = 128
 CHUNKS = 1
 BLOCK = 64
+EARLY = 4
 
 
 def repeat_rows(values, times):
@@ -148,7 +149,7 @@
         next_ref[at + per_chip : at + 2 * per_chip, :] = theirs_ref[low : low + per_chip, :]
 
 
-def weight_kernel(final_ref, offset_ref, out_ref, offset_out, wide_ref):
+def weight_kernel(final_ref, offset_ref, out_ref, mixing_out, offset_out, wide_ref):
     offset_out[...] = offset_ref[...]
     channels, columns = out_ref.shape
     hidden = math.isqrt(columns)
@@ -156,59 +157,112 @@
     step = LANES // hidden
     for e in range(0, hidden, step):
         rows = [wide_ref[pl.ds(e + n, hidden, stride=hidden), :] for n in range(step)]
+        mixing_out[:, e * channels : (e + step) * channels] = jnp.concatenate(rows, axis=1).astype(
+            jnp.bfloat16
+        )
         out_ref[:, e * hidden : (e + step) * hidden] = jnp.concatenate(rows, axis=0).T.astype(
             jnp.bfloat16
         )
 
 
-def pair_kernel(places, gridded, rows_here, hidden, samples, *refs):
+def left_pieces(shards, rows_here, hidden, here, low, high):
+    core = lax.rem(lax.axis_index("row"), 2)
+    span = rows_here * hidden
+    pieces = []
+    for _, _, ref, base in shards:
+        tile = ref.shape[1]
+        deep = span * here // tile
+        start = pl.multiple_of(base + core * deep, deep)
+        piece = ref[pl.ds(start, deep), :].astype(jnp.float32)
+        wide = jnp.concatenate([piece[n * here : (n + 1) * here] for n in range(span // tile)], axis=1)
+        pieces.append(wide[:, low * hidden : high * hidden])
+    return pieces
+
+
+def even(pieces):
+    return pieces + [jnp.zeros_like(pieces[0])] * (len(pieces) % 2)
+
+
+def outer_products(shards, left_ref, outer_ref, hidden, here):
+    left = left_ref[...]
+    for e in range(0, hidden, 2):
+        both = even(
+            [
+                ref[base + e * here : base + (e + 2) * here, :].astype(jnp.float32)
+                for ref, base, _, _ in shards
+            ]
+        )
+        for k in range(2):
+            right = jnp.concatenate([x[k * here : (k + 1) * here] for x in both], axis=0)
+            outer = jnp.dot(left, right.astype(jnp.bfloat16), preferred_element_type=jnp.float32)
+            outer = outer.astype(jnp.bfloat16)
+            for i in range(outer_ref.shape[0]):
+                outer_ref[i, (e + k) * hidden : (e + k + 1) * hidden, :] = outer[
+                    i * hidden : (i + 1) * hidden
+                ]
+
+
+def early_kernel(places, rows_here, hidden, here, *refs):
     refs = list(refs)
-    count = len(places)
+    messages = [refs.pop(0) for _ in range(1 + max(max(n, m) for n, _, m, _ in places))]
+    shards = [(messages[n], right, messages[m], left) for n, right, m, left in places]
+    weight_ref = refs.pop(0)
+    total_ref = refs.pop(0) if len(refs) == 4 else None
+    total_out, left_ref, outer_ref = refs
+    count = total_out.shape[0]
+    pieces = even(left_pieces(shards, rows_here, hidden, here, 0, count))
+    left_ref[...] = jnp.concatenate(pieces, axis=0).T.astype(jnp.bfloat16)
+    outer_products(shards, left_ref, outer_ref, hidden, here)
+    for i in range(count):
+        value = jnp.dot(weight_ref[...], outer_ref[i], preferred_element_type=jnp.float32).T
+        total_out[i] = value if total_ref is None else value + total_ref[i]
+
+
+def pair_kernel(places, gridded, early, rows_here, hidden, samples, *refs):
+    refs = list(refs)
+    here = samples // len(places)
     if gridded:
         shards = [(refs.pop(0), 0, refs.pop(0), 0) for _ in places]
     else:
         messages = [refs.pop(0) for _ in places]
         shards = [(messages[n], right, messages[m], left) for n, right, m, left in places]
-    weight_ref, offset_ref, out_hbm, left_ref, outer_ref, out_ref, sems = refs
+    weight_ref, offset_ref = refs.pop(0), refs.pop(0)
+    total_ref, mixing_ref = (refs.pop(0), refs.pop(0)) if early else (None, None)
+    out_hbm, left_ref, outer_ref, out_ref, sems = refs
     tile = shards[0][0].shape[1]
-    here = samples // count
-    span = rows_here * hidden
-    deep = span * here // tile
-    core = lax.rem(lax.axis_index("row"), 2)
-    pieces = []
-    for _, _, ref, base in shards:
-        start = pl.multiple_of(base + core * deep, deep)
-        piece = ref[pl.ds(start, deep), :].astype(jnp.float32)
-        pieces.append(
-            jnp.concatenate([piece[n * here : (n + 1) * here] for n in range(span // tile)], axis=1)
-        )
-    left_ref[...] = jnp.concatenate(pieces, axis=0).T.astype(jnp.bfloat16)
-
-    left = left_ref[...]
-    for e in range(0, hidden, 2):
-        both = [
-            ref[base + e * here : base + (e + 2) * here, :].astype(jnp.float32)
-            for ref, base, _, _ in shards
-        ]
-        for k in range(2):
-            right = jnp.concatenate([x[k * here : (k + 1) * here] for x in both], axis=0)
-            outer = jnp.dot(left, right.astype(jnp.bfloat16), preferred_element_type=jnp.float32)
-            outer = outer.astype(jnp.bfloat16)
-            for i in range(rows_here):
-                outer_ref[i, (e + k) * hidden : (e + k + 1) * hidden, :] = outer[
-                    i * hidden : (i + 1) * hidden
-                ]
-
+    channels = out_ref.shape[2]
     first = pl.program_id(0) * tile if gridded else 0
     copies = []
-    for i in range(rows_here):
-        value = jnp.dot(weight_ref[...], outer_ref[i], preferred_element_type=jnp.float32)
-        value = value.T * (1.0 / samples) + offset_ref[...]
-        out_ref[i] = value.astype(jnp.bfloat16)
+
+    def finish(i, value):
+        out_ref[i] = (value * (1.0 / samples) + offset_ref[...]).astype(jnp.bfloat16)
         copies.append(
             pltpu.make_async_copy(out_ref.at[i], out_hbm.at[i, pl.ds(first, tile)], sems.at[i])
         )
         copies[-1].start()
+
+    pieces = left_pieces(shards, rows_here, hidden, here, early, rows_here)
+    left_ref[...] = jnp.concatenate(pieces, axis=0).T.astype(jnp.bfloat16)
+    if early:
+        last = left_pieces(shards[-1:], rows_here, hidden, here, 0, early)[0]
+        last = [last[:, i * hidden : (i + 1) * hidden] for i in range(early)]
+        mixed = jnp.dot(
+            jnp.concatenate(last, axis=0).astype(jnp.bfloat16),
+            mixing_ref[...],
+            preferred_element_type=jnp.float32,
+        )
+        ref, base, _, _ = shards[-1]
+        right = ref[base : base + hidden * here, :].astype(jnp.float32).T.astype(jnp.bfloat16)
+        for i in range(early):
+            part = mixed[i * here : (i + 1) * here]
+            part = [part[:, e * channels : (e + 1) * channels] for e in range(hidden)]
+            part = jnp.concatenate(part, axis=0).astype(jnp.bfloat16)
+            value = jnp.dot(right, part, preferred_element_type=jnp.float32)
+            finish(i, value + total_ref[i])
+    outer_products(shards, left_ref, outer_ref, hidden, here)
+    for i in range(early, rows_here):
+        value = jnp.dot(weight_ref[...], outer_ref[i - early], preferred_element_type=jnp.float32)
+        finish(i, value.T)
     for copy in copies:
         copy.wait()
 
@@ -286,27 +340,50 @@
     def swap(value):
         return lax.ppermute(value, "row", [(r, r ^ 1) for r in range(size)])
 
-    weight, offset = pl.pallas_call(
+    weight, mixing, offset = pl.pallas_call(
         weight_kernel,
         out_shape=[
             jax.ShapeDtypeStruct((channels, hidden * hidden), jnp.bfloat16),
+            jax.ShapeDtypeStruct((hidden, hidden * channels), jnp.bfloat16),
             jax.ShapeDtypeStruct((1, channels), jnp.float32),
         ],
         in_specs=[vmem] * 2,
-        out_specs=[vmem] * 2,
+        out_specs=[vmem] * 3,
         scratch_shapes=[pltpu.VMEM((hidden * hidden, channels), jnp.float32)],
         compiler_params=pltpu.CompilerParams(vmem_limit_bytes=16 * MIB),
         cost_estimate=pl.CostEstimate(flops=2**28, bytes_accessed=2**20, transcendentals=0),
     )(final_projector_coefficients, final_projector_offset.reshape(1, channels))
-    theirs, weight, offset = lax.optimization_barrier((swap(give), weight, offset))
-    messages = [give, theirs]
-    places = [(n, 0, n, body + (half - 1) * per_chip) for n in range(2)]
-
-    def take(*lefts):
-        places.extend((len(messages) + n, 0, len(messages) + m, low) for n, (m, low) in enumerate(lefts))
-
+    theirs, weight, mixing, offset = lax.optimization_barrier((swap(give), weight, mixing, offset))
+    def lay_out(groups):
+        messages, places = [], []
+        for values, left in groups:
+            first = len(messages)
+            places += [(first + n, 0, first + m, low) for n, (m, low) in enumerate(left)]
+            messages += values
+        return messages, places
+
+    def early_sums(groups, total):
+        messages, places = lay_out(groups)
+        operands = messages + [weight] + ([] if total is None else [total])
+        deep = here * (len(places) + len(places) % 2)
+        return pl.pallas_call(
+            functools.partial(early_kernel, places, rows_here, hidden, here),
+            out_shape=jax.ShapeDtypeStruct((early, residues, channels), jnp.float32),
+            in_specs=[vmem] * len(operands),
+            out_specs=vmem,
+            scratch_shapes=[
+                pltpu.VMEM((early * hidden, deep), jnp.bfloat16),
+                pltpu.VMEM((early, hidden * hidden, tile), jnp.bfloat16),
+            ],
+            compiler_params=pltpu.CompilerParams(vmem_limit_bytes=24 * MIB),
+            cost_estimate=pl.CostEstimate(flops=2**30, bytes_accessed=2**21, transcendentals=0),
+        )(*operands)
+
+    gridded = tiles > 1
+    early = 0 if gridded else EARLY
+    own = ([give, theirs], [(n, body + (half - 1) * per_chip) for n in range(2)])
     flying = [keep, theirs[: body + (half - 1) * per_chip]]
-    swapped, lefts = [], []
+    arrived, swapped, lefts, total = [], [], [], None
     for step in range(1, half + 1):
         landed = [lax.ppermute(x, "row", around) for x in flying]
         if step >= 3:
@@ -331,14 +408,16 @@
         elif step < half - 1:
             flying.append(landed[1][: landed[1].shape[0] - 2 * per_chip])
         landed = lax.optimization_barrier(landed)
-        take(*lefts[-1])
-        messages += landed
+        arrived.append(landed)
+        if step == half - 1 and early:
+            groups = [own] + list(zip(arrived, lefts)) + list(zip(swapped, lefts))
+            turn, total = lax.optimization_barrier((landed[0], early_sums(groups, None)))
+            landed = [turn, landed[1]]
         swapped.append([swap(x) for x in landed])
-    for pair, left in zip(swapped, lefts):
-        take(*left)
-        messages += pair
-
-    gridded = tiles > 1
+    if early:
+        total = early_sums([(swapped[-2], lefts[-2]), (arrived[-1], lefts[-1])], total)
+
+    messages, places = lay_out([own] + list(zip(arrived, lefts)) + list(zip(swapped, lefts)))
     if gridded:
         operands, specs = [], []
         for n, right, m, left in places:
@@ -347,29 +426,30 @@
                 pl.BlockSpec((width, tile), lambda t, first=right // width: (first + t, 0)),
                 pl.BlockSpec((per_chip, tile), lambda t, at=left // per_chip: (at, 0)),
             ]
+        operands += [weight, offset]
         specs += [
             pl.BlockSpec((channels, hidden * hidden), lambda t: (0, 0)),
             pl.BlockSpec((1, channels), lambda t: (0, 0)),
         ]
         grid = (tiles,)
     else:
-        operands = messages
-        specs = [vmem] * (len(messages) + 2)
+        operands = messages + [weight, offset, total, mixing]
+        specs = [vmem] * len(operands)
         grid = ()
     return pl.pallas_call(
-        functools.partial(pair_kernel, places, gridded, rows_here, hidden, samples),
+        functools.partial(pair_kernel, places, gridded, early, rows_here, hidden, samples),
         out_shape=jax.ShapeDtypeStruct((rows_here, residues, channels), jnp.bfloat16),
         grid=grid,
         in_specs=specs,
         out_specs=hbm,
         scratch_shapes=[
-            pltpu.VMEM((rows_here * hidden, samples), jnp.bfloat16),
-            pltpu.VMEM((rows_here, hidden * hidden, tile), jnp.bfloat16),
+            pltpu.VMEM(((rows_here - early) * hidden, samples), jnp.bfloat16),
+            pltpu.VMEM((rows_here - early, hidden * hidden, tile), jnp.bfloat16),
             pltpu.VMEM((rows_here, tile, channels), jnp.bfloat16),
             pltpu.SemaphoreType.DMA((rows_here,)),
         ],
         compiler_params=pltpu.CompilerParams(vmem_limit_bytes=40 * MIB),
-    )(*operands, weight, offset)
+    )(*operands)
 
 
 def solution(mesh):

time: 31.5 us -> 32.1 us (1.019)
  waiting for transfers between devices: 8.63 us -> 6.66 us
  Pallas kernels: 8.07 us -> 9.98 us
  starting transfers between devices: 14.5 us -> 15.2 us
    pallas_call x1 -> x3, Pallas kernels: 4.43 us -> 6.34 us  [the longest x1 4 us: per_device(): pl.pallas_call(functools.partial(pair_kernel, places, gridded, early, row...]
    ppermute x7, waiting for transfers between devices: 7.27 us -> 5.72 us  [per_device(): landed = [lax.ppermute(x, 'row', around) for x in flying]]
    ppermute x8, starting transfers between devices: 1.04 us -> 1.69 us  [swap(): return lax.ppermute(value, 'row', [(r, r ^ 1) for r in range(size)])]
    ppermute x8, waiting for transfers between devices: 1.36 us -> 0.93 us  [swap(): return lax.ppermute(value, 'row', [(r, r ^ 1) for r in range(size)])]
  transfers between devices with their start and end apart: 15 -> 15, of which waited for: 8 -> 7; matrix products, arithmetic and copies ran while one was open for 0% -> 0% of each run, Pallas kernels for 1% -> 9%
where the time goes in v16:
time: 32.1 us; the launch traced here: 31.9 us
  starting transfers between devices  15.2 us (47%)
  Pallas kernels  9.98 us (31%)
  waiting for transfers between devices  6.66 us (21%)
    ppermute x7, starting transfers between devices, per_device(): landed = [lax.ppermute(x, 'row', around) for x in flying]  13.5 us
    ppermute x7, waiting for transfers between devices, per_device(): landed = [lax.ppermute(x, 'row', around) for x in flying]  5.72 us
    pallas_call x1, Pallas kernels, per_device(): pl.pallas_call(functools.partial(pair_kernel, places, gridded, early, row...  4 us
    pallas_call x1, Pallas kernels, per_device(): pl.pallas_call(functools.partial(project_kernel, rows_here), out_shape=[r...  3.22 us
    pallas_call x2, Pallas kernels, early_sums(): pl.pallas_call(functools.partial(early_kernel, places, rows_here, hidden,...  2.34 us
    ppermute x8, starting transfers between devices, swap(): return lax.ppermute(value, 'row', [(r, r ^ 1) for r in range(size)])  1.69 us
    ppermute x8, waiting for transfers between devices, swap(): return lax.ppermute(value, 'row', [(r, r ^ 1) for r in range(size)])  0.93 us
  transfers between devices with their start and end apart: 15, of which 7 were waited for; matrix products, arithmetic and copies ran while one was open for 0% of the time, Pallas kernels for 9%

profile of v16, /device:TPU:0, one launch (start us, length us, event | category | flops | bytes accessed | tf_op | source)
XLA Modules:
  0.0 31.9 jit_solution(1614217453981934607)
XLA Ops:
  0.0 3.2 %shard_map.91 = (bf16[384,256]{1,0:T(8,128)(2,1)S(1)}, bf16[384,256]{1,0:T(8,128)(2,1)S(1)}) custom-call(bf16[8,256,256]{2,1,0:T(8,128)(2,1)} %x_hbm.1, f32[1,256]{1,0:T(1,128)} %bitcast.10, f32[1,256]{1,0:T(1,128)} %bitcast.11, bf16[32,256]{1,0:T(8,128)(2,1)} %bitcast.8, f32[1,32]{1,0:T(1,128)} %bitcast.12, bf16[32,256]{1,0:T(8,128)(2,1)} %bitcast.9, ...), custom_call_target="tpu_custom_call" | custom-call | flops 536870912 | bytes 1048576 | tf_op jit(solution)/shard_map/pallas_call | solution.py:299
  3.2 0.5 %collective-permute-start = (bf16[384,256]{1,0:T(8,128)(2,1)S(1)}, bf16[384,256]{1,0:T(8,128)(2,1)S(1)}, u32[]{:S(2)}, u32[]{:S(2)}) collective-permute-start(bf16[384,256]{1,0:T(8,128)(2,1)S(1)} %get-tuple-element.28.refs_0_), channel_id=1, source_target_pairs={{0,1},{1,0},{2,3},{3,2},{4,5},{5,4},{6,7},{7,6},{8,9},{9,8},{10,11... | collective-permute-start | bytes 589832 | tf_op jit(solution)/shard_map/ppermute | solution.py:341
  3.8 2.6 %collective-permute-start.1 = (bf16[384,256]{1,0:T(8,128)(2,1)S(1)}, bf16[384,256]{1,0:T(8,128)(2,1)S(1)}, u32[]{:S(2)}, u32[]{:S(2)}) collective-permute-start(bf16[384,256]{1,0:T(8,128)(2,1)S(1)} %get-tuple-element.33), channel_id=1, source_target_pairs={{0,2},{1,5},{2,6},{3,1},{4,0},{5,9},{6,10},{7,3},{8,4},{9,13},{10,... | collective-permute-start | bytes 589832 | tf_op jit(solution)/shard_map/ppermute | solution.py:388
  6.3 0.4 %shard_map.92 = (bf16[128,1024]{1,0:T(8,128)(2,1)S(1)}, bf16[32,4096]{1,0:T(8,128)(2,1)S(1)}, f32[1,128]{1,0:T(1,128)S(1)}) custom-call(bf16[1024,128]{1,0:T(8,128)(2,1)S(1)} %copy-done, f32[1,128]{1,0:T(1,128)S(1)} %bitcast.7), custom_call_target="tpu_custom_call" | custom-call | flops 268435456 | bytes 1048576 | tf_op jit(solution)/shard_map/pallas_call | solution.py:343
  6.8 0.0 collective-permute-done.refs_1_
  6.8 1.6 %collective-permute-start.2 = (bf16[352,256]{1,0:T(8,128)(2,1)S(1)}, bf16[352,256]{1,0:T(8,128)(2,1)S(1)}, u32[]{:S(2)}, u32[]{:S(2)}) collective-permute-start(bf16[352,256]{1,0:T(8,128)(2,1)S(1)} %slice.9), channel_id=1, source_target_pairs={{0,2},{1,5},{2,6},{3,1},{4,0},{5,9},{6,10},{7,3},{8,4},{9,13},{10,... | collective-permute-start | bytes 540680 | tf_op jit(solution)/shard_map/ppermute | solution.py:388
  8.4 1.6 %collective-permute-done.1.mine_ref.refs_2_ = bf16[384,256]{1,0:T(8,128)(2,1)S(1)} collective-permute-done((bf16[384,256]{1,0:T(8,128)(2,1)S(1)}, bf16[384,256]{1,0:T(8,128)(2,1)S(1)}, u32[]{:S(2)}, u32[]{:S(2)}) %collective-permute-start.1) | collective-permute-done | bytes 196640 | tf_op jit(solution)/shard_map/ppermute | solution.py:388
  10.1 2.0 %collective-permute-start.3 = (bf16[288,256]{1,0:T(8,128)(2,1)S(1)}, bf16[288,256]{1,0:T(8,128)(2,1)S(1)}, u32[]{:S(2)}, u32[]{:S(2)}) collective-permute-start(bf16[288,256]{1,0:T(8,128)(2,1)S(1)} %slice.12), channel_id=1, source_target_pairs={{0,2},{1,5},{2,6},{3,1},{4,0},{5,9},{6,10},{7,3},{8,4},{9,13},{10,... | collective-permute-start | bytes 442376 | tf_op jit(solution)/shard_map/ppermute | solution.py:388
  12.1 0.3 collective-permute-done.2.theirs_ref.refs_3_
  12.4 1.7 %collective-permute-start.4 = (bf16[384,256]{1,0:T(8,128)(2,1)S(1)}, bf16[384,256]{1,0:T(8,128)(2,1)S(1)}, u32[]{:S(2)}, u32[]{:S(2)}) collective-permute-start(bf16[384,256]{1,0:T(8,128)(2,1)S(1)} %shard_map.93), channel_id=1, source_target_pairs={{0,2},{1,5},{2,6},{3,1},{4,0},{5,9},{6,10},{7,3},{8,4},{9,13},{10,... | collective-permute-start | bytes 589832 | tf_op jit(solution)/shard_map/ppermute | solution.py:388
  14.0 1.2 %collective-permute-done.3.refs_4_ = bf16[288,256]{1,0:T(8,128)(2,1)S(1)} collective-permute-done((bf16[288,256]{1,0:T(8,128)(2,1)S(1)}, bf16[288,256]{1,0:T(8,128)(2,1)S(1)}, u32[]{:S(2)}, u32[]{:S(2)}) %collective-permute-start.3) | collective-permute-done | bytes 147488 | tf_op jit(solution)/shard_map/ppermute | solution.py:388
  15.3 2.0 %collective-permute-start.5 = (bf16[288,256]{1,0:T(8,128)(2,1)S(1)}, bf16[288,256]{1,0:T(8,128)(2,1)S(1)}, u32[]{:S(2)}, u32[]{:S(2)}) collective-permute-start(bf16[288,256]{1,0:T(8,128)(2,1)S(1)} %collective-permute-done.3.refs_4_), channel_id=1, source_target_pairs={{0,2},{1,5},{2,6},{3,1},{4,0},{5,9},{6,10},{7,3},{8,4},{9,13},{10,... | collective-permute-start | bytes 442376 | tf_op jit(solution)/shard_map/ppermute | solution.py:388
  17.2 0.9 %collective-permute-done.4.refs_5_ = bf16[384,256]{1,0:T(8,128)(2,1)S(1)} collective-permute-done((bf16[384,256]{1,0:T(8,128)(2,1)S(1)}, bf16[384,256]{1,0:T(8,128)(2,1)S(1)}, u32[]{:S(2)}, u32[]{:S(2)}) %collective-permute-start.4) | collective-permute-done | bytes 196640 | tf_op jit(solution)/shard_map/ppermute | solution.py:388
  18.1 0.5 %collective-permute-start.8 = (bf16[352,256]{1,0:T(8,128)(2,1)S(1)}, bf16[352,256]{1,0:T(8,128)(2,1)S(1)}, u32[]{:S(2)}, u32[]{:S(2)}) collective-permute-start(bf16[352,256]{1,0:T(8,128)(2,1)S(1)} %collective-permute-done.2.theirs_ref.refs_3_), channel_id=1, source_target_pairs={{0,1},{1,0},{2,3},{3,2},{4,5},{5,4},{6,7},{7,6},{8,9},{9,8},{10,11... | collective-permute-start | bytes 540680 | tf_op jit(solution)/shard_map/ppermute | solution.py:341
  18.6 1.7 %collective-permute-start.6 = (bf16[320,256]{1,0:T(8,128)(2,1)S(1)}, bf16[320,256]{1,0:T(8,128)(2,1)S(1)}, u32[]{:S(2)}, u32[]{:S(2)}) collective-permute-start(bf16[320,256]{1,0:T(8,128)(2,1)S(1)} %slice.13), channel_id=1, source_target_pairs={{0,2},{1,5},{2,6},{3,1},{4,0},{5,9},{6,10},{7,3},{8,4},{9,13},{10,... | collective-permute-start | bytes 491528 | tf_op jit(solution)/shard_map/ppermute | solution.py:388
  20.3 0.1 collective-permute-done.5.refs_6_
  20.4 2.0 %collective-permute-start.9 = (bf16[288,256]{1,0:T(8,128)(2,1)S(1)}, bf16[288,256]{1,0:T(8,128)(2,1)S(1)}, u32[]{:S(2)}, u32[]{:S(2)}) collective-permute-start(bf16[288,256]{1,0:T(8,128)(2,1)S(1)} %collective-permute-done.5.refs_6_), channel_id=1, source_target_pairs={{0,2},{1,5},{2,6},{3,1},{4,0},{5,9},{6,10},{7,3},{8,4},{9,13},{10,... | collective-permute-start | bytes 442376 | tf_op jit(solution)/shard_map/ppermute | solution.py:388
  22.4 1.6 %collective-permute-done.6.refs_7_ = bf16[320,256]{1,0:T(8,128)(2,1)S(1)} collective-permute-done((bf16[320,256]{1,0:T(8,128)(2,1)S(1)}, bf16[320,256]{1,0:T(8,128)(2,1)S(1)}, u32[]{:S(2)}, u32[]{:S(2)}) %collective-permute-start.6) | collective-permute-done | bytes 163872 | tf_op jit(solution)/shard_map/ppermute | solution.py:388
  24.0 1.2 %shard_map.94.refs_4_ = f32[4,256,128]{2,1,0:T(8,128)S(1)} custom-call(bf16[384,256]{1,0:T(8,128)(2,1)S(1)} %get-tuple-element.28.refs_0_, bf16[384,256]{1,0:T(8,128)(2,1)S(1)} %collective-permute-done.refs_1_, bf16[384,256]{1,0:T(8,128)(2,1)S(1)} %collective-permute-done.1.mine_ref.refs_2_, bf16[352,256]{1,0:T(8,128)(2,1)S(1)} %collective-permute-done.2.theirs_ref.refs_3_, ...), custom_call_target="tpu_custom_call" | custom-call | flops 1073741824 | bytes 2097152 | tf_op jit(solution)/shard_map/pallas_call | solution.py:369
  25.2 0.6 %collective-permute-start.12 = (bf16[288,256]{1,0:T(8,128)(2,1)S(1)}, bf16[288,256]{1,0:T(8,128)(2,1)S(1)}, u32[]{:S(2)}, u32[]{:S(2)}) collective-permute-start(bf16[288,256]{1,0:T(8,128)(2,1)S(1)} %collective-permute-done.5.refs_6_), channel_id=1, source_target_pairs={{0,1},{1,0},{2,3},{3,2},{4,5},{5,4},{6,7},{7,6},{8,9},{9,8},{10,11... | collective-permute-start | bytes 442376 | tf_op jit(solution)/shard_map/ppermute | solution.py:341
  25.7 0.1 collective-permute-start.14
  25.8 0.9 %collective-permute-done.12.refs_0_.refs_13_ = bf16[288,256]{1,0:T(8,128)(2,1)S(1)} collective-permute-done((bf16[288,256]{1,0:T(8,128)(2,1)S(1)}, bf16[288,256]{1,0:T(8,128)(2,1)S(1)}, u32[]{:S(2)}, u32[]{:S(2)}) %collective-permute-start.12) | collective-permute-done | bytes 147488 | tf_op jit(solution)/shard_map/ppermute | solution.py:341
  26.8 1.2 %shard_map.95.refs_18_ = f32[4,256,128]{2,1,0:T(8,128)S(1)} custom-call(bf16[288,256]{1,0:T(8,128)(2,1)S(1)} %collective-permute-done.12.refs_0_.refs_13_, bf16[320,256]{1,0:T(8,128)(2,1)S(1)} %collective-permute-done.13.refs_1_.refs_14_, bf16[288,256]{1,0:T(8,128)(2,1)S(1)} %collective-permute-done.9.refs_2_.refs_8_, ...), custom_call_target="tpu_custom_call" | custom-call | flops 1073741824 | bytes 2097152 | tf_op jit(solution)/shard_map/pallas_call | solution.py:369
  27.9 4.0 %shard_map.96 = bf16[16,256,128]{2,1,0:T(8,128)(2,1)} custom-call(bf16[384,256]{1,0:T(8,128)(2,1)S(1)} %get-tuple-element.28.refs_0_, bf16[384,256]{1,0:T(8,128)(2,1)S(1)} %collective-permute-done.refs_1_, bf16[384,256]{1,0:T(8,128)(2,1)S(1)} %collective-permute-done.1.mine_ref.refs_2_, bf16[352,256]{1,0:T(8,128)(2,1)S(1)} %collective-permute-done.2.theirs_ref.refs_3_, ...), custom_call_target="tpu_custom_call" | custom-call | tf_op jit(solution)/shard_map/pallas_call | solution.py:439
  (19 shorter events, 0.1 us)
Async XLA Ops:
  0.0 6.3 %copy-start = (bf16[1024,128]{1,0:T(8,128)(2,1)S(1)}, bf16[1024,128]{1,0:T(8,128)(2,1)}, u32[]{:S(2)}) copy-start(bf16[1024,128]{1,0:T(8,128)(2,1)} %final_ref.1) | copy-start | bytes 786436
  3.2 3.5 %collective-permute-start = (bf16[384,256]{1,0:T(8,128)(2,1)S(1)}, bf16[384,256]{1,0:T(8,128)(2,1)S(1)}, u32[]{:S(2)}, u32[]{:S(2)}) collective-permute-start(bf16[384,256]{1,0:T(8,128)(2,1)S(1)} %get-tuple-element.28.refs_0_), channel_id=1, source_target_pairs={{0,1},{1,0},{2,3},{3,2},{4,5},{5,4},{6,7},{7,6},{8,9},{9,8},{10,11... | collective-permute-start | bytes 589832 | tf_op jit(solution)/shard_map/ppermute | solution.py:341
  3.8 2.6 %copy-start.1 = (f32[128]{0:T(128)S(1)}, f32[128]{0:T(128)}, u32[]{:S(2)}) copy-start(f32[128]{0:T(128)} %param.17) | copy-start | bytes 1540
  3.8 6.3 %collective-permute-start.1 = (bf16[384,256]{1,0:T(8,128)(2,1)S(1)}, bf16[384,256]{1,0:T(8,128)(2,1)S(1)}, u32[]{:S(2)}, u32[]{:S(2)}) collective-permute-start(bf16[384,256]{1,0:T(8,128)(2,1)S(1)} %get-tuple-element.33), channel_id=1, source_target_pairs={{0,2},{1,5},{2,6},{3,1},{4,0},{5,9},{6,10},{7,3},{8,4},{9,13},{10,... | collective-permute-start | bytes 589832 | tf_op jit(solution)/shard_map/ppermute | solution.py:388
  6.8 5.5 %collective-permute-start.2 = (bf16[352,256]{1,0:T(8,128)(2,1)S(1)}, bf16[352,256]{1,0:T(8,128)(2,1)S(1)}, u32[]{:S(2)}, u32[]{:S(2)}) collective-permute-start(bf16[352,256]{1,0:T(8,128)(2,1)S(1)} %slice.9), channel_id=1, source_target_pairs={{0,2},{1,5},{2,6},{3,1},{4,0},{5,9},{6,10},{7,3},{8,4},{9,13},{10,... | collective-permute-start | bytes 540680 | tf_op jit(solution)/shard_map/ppermute | solution.py:388
  10.1 5.2 %collective-permute-start.3 = (bf16[288,256]{1,0:T(8,128)(2,1)S(1)}, bf16[288,256]{1,0:T(8,128)(2,1)S(1)}, u32[]{:S(2)}, u32[]{:S(2)}) collective-permute-start(bf16[288,256]{1,0:T(8,128)(2,1)S(1)} %slice.12), channel_id=1, source_target_pairs={{0,2},{1,5},{2,6},{3,1},{4,0},{5,9},{6,10},{7,3},{8,4},{9,13},{10,... | collective-permute-start | bytes 442376 | tf_op jit(solution)/shard_map/ppermute | solution.py:388
  12.4 5.7 %collective-permute-start.4 = (bf16[384,256]{1,0:T(8,128)(2,1)S(1)}, bf16[384,256]{1,0:T(8,128)(2,1)S(1)}, u32[]{:S(2)}, u32[]{:S(2)}) collective-permute-start(bf16[384,256]{1,0:T(8,128)(2,1)S(1)} %shard_map.93), channel_id=1, source_target_pairs={{0,2},{1,5},{2,6},{3,1},{4,0},{5,9},{6,10},{7,3},{8,4},{9,13},{10,... | collective-permute-start | bytes 589832 | tf_op jit(solution)/shard_map/ppermute | solution.py:388
  15.3 5.1 %collective-permute-start.5 = (bf16[288,256]{1,0:T(8,128)(2,1)S(1)}, bf16[288,256]{1,0:T(8,128)(2,1)S(1)}, u32[]{:S(2)}, u32[]{:S(2)}) collective-permute-start(bf16[288,256]{1,0:T(8,128)(2,1)S(1)} %collective-permute-done.3.refs_4_), channel_id=1, source_target_pairs={{0,2},{1,5},{2,6},{3,1},{4,0},{5,9},{6,10},{7,3},{8,4},{9,13},{10,... | collective-permute-start | bytes 442376 | tf_op jit(solution)/shard_map/ppermute | solution.py:388
  17.2 5.2 %collective-permute-start.7 = (bf16[384,256]{1,0:T(8,128)(2,1)S(1)}, bf16[384,256]{1,0:T(8,128)(2,1)S(1)}, u32[]{:S(2)}, u32[]{:S(2)}) collective-permute-start(bf16[384,256]{1,0:T(8,128)(2,1)S(1)} %collective-permute-done.1.mine_ref.refs_2_), channel_id=1, source_target_pairs={{0,1},{1,0},{2,3},{3,2},{4,5},{5,4},{6,7},{7,6},{8,9},{9,8},{10,11... | collective-permute-start | bytes 589832 | tf_op jit(solution)/shard_map/ppermute | solution.py:341
  18.1 5.9 %collective-permute-start.11 = (bf16[384,256]{1,0:T(8,128)(2,1)S(1)}, bf16[384,256]{1,0:T(8,128)(2,1)S(1)}, u32[]{:S(2)}, u32[]{:S(2)}) collective-permute-start(bf16[384,256]{1,0:T(8,128)(2,1)S(1)} %collective-permute-done.4.refs_5_), channel_id=1, source_target_pairs={{0,1},{1,0},{2,3},{3,2},{4,5},{5,4},{6,7},{7,6},{8,9},{9,8},{10,11... | collective-permute-start | bytes 589832 | tf_op jit(solution)/shard_map/ppermute | solution.py:341
  18.1 2.3 %collective-permute-start.8 = (bf16[352,256]{1,0:T(8,128)(2,1)S(1)}, bf16[352,256]{1,0:T(8,128)(2,1)S(1)}, u32[]{:S(2)}, u32[]{:S(2)}) collective-permute-start(bf16[352,256]{1,0:T(8,128)(2,1)S(1)} %collective-permute-done.2.theirs_ref.refs_3_), channel_id=1, source_target_pairs={{0,1},{1,0},{2,3},{3,2},{4,5},{5,4},{6,7},{7,6},{8,9},{9,8},{10,11... | collective-permute-start | bytes 540680 | tf_op jit(solution)/shard_map/ppermute | solution.py:341
  18.6 5.4 %collective-permute-start.6 = (bf16[320,256]{1,0:T(8,128)(2,1)S(1)}, bf16[320,256]{1,0:T(8,128)(2,1)S(1)}, u32[]{:S(2)}, u32[]{:S(2)}) collective-permute-start(bf16[320,256]{1,0:T(8,128)(2,1)S(1)} %slice.13), channel_id=1, source_target_pairs={{0,2},{1,5},{2,6},{3,1},{4,0},{5,9},{6,10},{7,3},{8,4},{9,13},{10,... | collective-permute-start | bytes 491528 | tf_op jit(solution)/shard_map/ppermute | solution.py:388
  20.4 3.6 %collective-permute-start.10 = (bf16[288,256]{1,0:T(8,128)(2,1)S(1)}, bf16[288,256]{1,0:T(8,128)(2,1)S(1)}, u32[]{:S(2)}, u32[]{:S(2)}) collective-permute-start(bf16[288,256]{1,0:T(8,128)(2,1)S(1)} %collective-permute-done.3.refs_4_), channel_id=1, source_target_pairs={{0,1},{1,0},{2,3},{3,2},{4,5},{5,4},{6,7},{7,6},{8,9},{9,8},{10,11... | collective-permute-start | bytes 442376 | tf_op jit(solution)/shard_map/ppermute | solution.py:341
  20.4 5.3 %collective-permute-start.9 = (bf16[288,256]{1,0:T(8,128)(2,1)S(1)}, bf16[288,256]{1,0:T(8,128)(2,1)S(1)}, u32[]{:S(2)}, u32[]{:S(2)}) collective-permute-start(bf16[288,256]{1,0:T(8,128)(2,1)S(1)} %collective-permute-done.5.refs_6_), channel_id=1, source_target_pairs={{0,2},{1,5},{2,6},{3,1},{4,0},{5,9},{6,10},{7,3},{8,4},{9,13},{10,... | collective-permute-start | bytes 442376 | tf_op jit(solution)/shard_map/ppermute | solution.py:388
  24.0 1.9 %collective-permute-start.13 = (bf16[320,256]{1,0:T(8,128)(2,1)S(1)}, bf16[320,256]{1,0:T(8,128)(2,1)S(1)}, u32[]{:S(2)}, u32[]{:S(2)}) collective-permute-start(bf16[320,256]{1,0:T(8,128)(2,1)S(1)} %collective-permute-done.6.refs_7_), channel_id=1, source_target_pairs={{0,1},{1,0},{2,3},{3,2},{4,5},{5,4},{6,7},{7,6},{8,9},{9,8},{10,11... | collective-permute-start | bytes 491528 | tf_op jit(solution)/shard_map/ppermute | solution.py:341
  25.2 1.6 %collective-permute-start.12 = (bf16[288,256]{1,0:T(8,128)(2,1)S(1)}, bf16[288,256]{1,0:T(8,128)(2,1)S(1)}, u32[]{:S(2)}, u32[]{:S(2)}) collective-permute-start(bf16[288,256]{1,0:T(8,128)(2,1)S(1)} %collective-permute-done.5.refs_6_), channel_id=1, source_target_pairs={{0,1},{1,0},{2,3},{3,2},{4,5},{5,4},{6,7},{7,6},{8,9},{9,8},{10,11... | collective-permute-start | bytes 442376 | tf_op jit(solution)/shard_map/ppermute | solution.py:341
  25.7 2.2 %collective-permute-start.14 = (bf16[288,256]{1,0:T(8,128)(2,1)S(1)}, bf16[288,256]{1,0:T(8,128)(2,1)S(1)}, u32[]{:S(2)}, u32[]{:S(2)}) collective-permute-start(bf16[288,256]{1,0:T(8,128)(2,1)S(1)} %collective-permute-done.9.refs_2_.refs_8_), channel_id=1, source_target_pairs={{0,1},{1,0},{2,3},{3,2},{4,5},{5,4},{6,7},{7,6},{8,9},{9,8},{10,11... | collective-permute-start | bytes 442376 | tf_op jit(solution)/shard_map/ppermute | solution.py:341

commit v17 on v15

--- a/solution.py
+++ b/solution.py
@@ -38,6 +38,7 @@
     second_hbm,
     second_offset_hbm,
     keep_ref,
+    rest_ref,
     give_ref,
     x_ref,
     gain_ref,
@@ -127,7 +128,8 @@
     base = tiles * width
     way = 2 * (device % 2) - 1
     place = place_of(device, half)
-    spots = [(keep_ref, base + n * per_chip, half - n) for n in range(half)]
+    spots = [(keep_ref, base, half)]
+    spots += [(rest_ref, n * per_chip, half - 1 - n) for n in range(half - 1)]
     spots += [(give_ref, base + n * per_chip, n + 1 - half) for n in range(half)]
     for message, low, ahead in spots:
         chip = chip_at(lax.rem(place + way * ahead + 2 * half, 2 * half), half)
@@ -139,13 +141,20 @@
         message[low : low + per_chip, :] = jnp.concatenate(block, axis=0).astype(jnp.bfloat16)
 
 
-def join_kernel(base, per_chip, mine_ref, theirs_ref, next_ref):
-    next_ref[:base, :] = theirs_ref[:base, :]
-    for n in range((next_ref.shape[0] - base) // (2 * per_chip)):
-        low = base + n * per_chip
-        at = low + n * per_chip
-        next_ref[at : at + per_chip, :] = mine_ref[low + per_chip : low + 2 * per_chip, :]
-        next_ref[at + per_chip : at + 2 * per_chip, :] = theirs_ref[low : low + per_chip, :]
+def couple_kernel(base, per_chip, mine_ref, theirs_ref, out_ref):
+    for low in range(0, mine_ref.shape[0], per_chip):
+        out_ref[2 * low : 2 * low + per_chip, :] = mine_ref[low : low + per_chip, :]
+        out_ref[2 * low + per_chip : 2 * (low + per_chip), :] = theirs_ref[
+            base + low : base + low + per_chip, :
+        ]
+
+
+def join_kernel(per_chip, right_ref, left_ref, here_ref, next_ref):
+    base, count = right_ref.shape[0], left_ref.shape[0] - 2 * per_chip
+    here_ref[:base, :] = right_ref[...]
+    next_ref[:base, :] = right_ref[...]
+    here_ref[base:, :] = left_ref[count:, :]
+    next_ref[base:, :] = left_ref[:count, :]
 
 
 def weight_kernel(final_ref, offset_ref, out_ref, offset_out, wide_ref):
@@ -242,11 +251,11 @@
 
     vmem = pl.BlockSpec(memory_space=pltpu.VMEM)
     hbm = pl.BlockSpec(memory_space=pltpu.HBM)
-    keep, give = pl.pallas_call(
+    keep, rest, give = pl.pallas_call(
         functools.partial(project_kernel, rows_here),
-        out_shape=[rows(body + half * per_chip)] * 2,
+        out_shape=[rows(body + per_chip), rows((half - 1) * per_chip), rows(body + half * per_chip)],
         in_specs=[hbm] * 7,
-        out_specs=[vmem] * 2,
+        out_specs=[vmem] * 3,
         scratch_shapes=[
             pltpu.VMEM((here, residues, features), jnp.bfloat16),
             pltpu.VMEM((1, features), jnp.float32),
@@ -302,41 +311,47 @@
     messages = [give, theirs]
     places = [(n, 0, n, body + (half - 1) * per_chip) for n in range(2)]
 
-    def take(*lefts):
-        places.extend((len(messages) + n, 0, len(messages) + m, low) for n, (m, low) in enumerate(lefts))
-
-    flying = [keep, theirs[: body + (half - 1) * per_chip]]
-    swapped, lefts = [], []
+    def take(landed):
+        first, last = len(messages), len(landed) - 1
+        low = landed[last].shape[0] - len(landed) * per_chip
+        places.extend((first + n, 0, first + last, low + n * per_chip) for n in range(len(landed)))
+        messages.extend(landed)
+
+    small = dict(
+        compiler_params=pltpu.CompilerParams(vmem_limit_bytes=16 * MIB),
+        cost_estimate=pl.CostEstimate(flops=0, bytes_accessed=2**19, transcendentals=0),
+    )
+    couples = pl.pallas_call(
+        functools.partial(couple_kernel, body, per_chip),
+        out_shape=rows(2 * (half - 1) * per_chip),
+        in_specs=[vmem] * 2,
+        out_specs=vmem,
+        **small,
+    )(rest, theirs)
+    flying = [keep, theirs[:body], couples]
+    swapped = []
     for step in range(1, half + 1):
         landed = [lax.ppermute(x, "row", around) for x in flying]
         if step >= 3:
             landed[-1], swapped[step - 3] = lax.optimization_barrier((landed[-1], swapped[step - 3]))
-        low = [x.shape[0] - per_chip for x in landed]
+        flying = landed[:1]
         if step == 1:
-            lefts.append([(0, low[0]), (1, low[1])])
-        elif step < half:
-            lefts.append([(1, low[1] - per_chip), (1, low[1])])
-        else:
-            lefts.append([(0, low[0])])
-        flying = [landed[0][: body + per_chip]]
-        if step == 1:
-            flying += pl.pallas_call(
-                functools.partial(join_kernel, body, per_chip),
-                out_shape=[rows(body + 2 * (half - 2) * per_chip)],
+            here_rows, next_rows = pl.pallas_call(
+                functools.partial(join_kernel, per_chip),
+                out_shape=[rows(body + 2 * per_chip), rows(body + 2 * (half - 2) * per_chip)],
                 in_specs=[vmem] * 2,
-                out_specs=[vmem],
-                compiler_params=pltpu.CompilerParams(vmem_limit_bytes=16 * MIB),
-                cost_estimate=pl.CostEstimate(flops=0, bytes_accessed=2**19, transcendentals=0),
-            )(*landed)
+                out_specs=[vmem] * 2,
+                **small,
+            )(*landed[1:])
+            landed = [landed[0], here_rows]
+            flying.append(next_rows)
         elif step < half - 1:
             flying.append(landed[1][: landed[1].shape[0] - 2 * per_chip])
         landed = lax.optimization_barrier(landed)
-        take(*lefts[-1])
-        messages += landed
+        take(landed)
         swapped.append([swap(x) for x in landed])
-    for pair, left in zip(swapped, lefts):
-        take(*left)
-        messages += pair
+    for pair in swapped:
+        take(pair)
 
     gridded = tiles > 1
     if gridded:

time: 31.5 us -> 32.3 us (1.025)
  starting transfers between devices: 14.5 us -> 15.4 us
    ppermute x8, starting transfers between devices: 1.04 us -> 1.55 us  [swap(): return lax.ppermute(value, 'row', [(r, r ^ 1) for r in range(size)])]
    ppermute x7 -> x8, starting transfers between devices: 13.5 us -> 13.8 us  [per_device(): landed = [lax.ppermute(x, 'row', around) for x in flying]]
    ppermute x7 -> x8, waiting for transfers between devices: 7.27 us -> 7.2 us  [per_device(): landed = [lax.ppermute(x, 'row', around) for x in flying]]
  transfers between devices with their start and end apart: 15 -> 16, of which waited for: 8 -> 6; matrix products, arithmetic and copies ran while one was open for 0% -> 0% of each run, Pallas kernels for 1% -> 1%
where the time goes in v17:
time: 32.3 us; the launch traced here: 32.1 us
  starting transfers between devices  15.4 us (48%)
  waiting for transfers between devices  8.57 us (27%)
  Pallas kernels  8.09 us (25%)
    ppermute x8, starting transfers between devices, per_device(): landed = [lax.ppermute(x, 'row', around) for x in flying]  13.8 us
    ppermute x8, waiting for transfers between devices, per_device(): landed = [lax.ppermute(x, 'row', around) for x in flying]  7.2 us
    pallas_call x1, Pallas kernels, per_device(): pl.pallas_call(functools.partial(pair_kernel, places, gridded, rows_here,...  4.43 us
    pallas_call x1, Pallas kernels, per_device(): pl.pallas_call(functools.partial(project_kernel, rows_here), out_shape=[r...  3.22 us
    ppermute x8, starting transfers between devices, swap(): return lax.ppermute(value, 'row', [(r, r ^ 1) for r in range(size)])  1.55 us
    ppermute x8, waiting for transfers between devices, swap(): return lax.ppermute(value, 'row', [(r, r ^ 1) for r in range(size)])  1.37 us
  transfers between devices with their start and end apart: 16, of which 6 were waited for; matrix products, arithmetic and copies ran while one was open for 0% of the time, Pallas kernels for 1%

profile of v17, /device:TPU:0, one launch (start us, length us, event | category | flops | bytes accessed | tf_op | source)
XLA Modules:
  0.0 32.1 jit_solution(11656838472688380011)
XLA Ops:
  0.0 3.2 %shard_map.91 = (bf16[288,256]{1,0:T(8,128)(2,1)S(1)}, bf16[96,256]{1,0:T(8,128)(2,1)S(1)}, bf16[384,256]{1,0:T(8,128)(2,1)S(1)}) custom-call(bf16[8,256,256]{2,1,0:T(8,128)(2,1)} %x_hbm.1, f32[1,256]{1,0:T(1,128)} %bitcast.10, f32[1,256]{1,0:T(1,128)} %bitcast.11, bf16[32,256]{1,0:T(8,128)(2,1)} %bitcast.8, f32[1,32]{1,0:T(1,128)} %bitcast.12, ...), custom_call_target="tpu_custom_call" | custom-call | flops 536870912 | bytes 1048576 | tf_op jit(solution)/shard_map/pallas_call | solution.py:254
  3.2 0.5 %collective-permute-start = (bf16[384,256]{1,0:T(8,128)(2,1)S(1)}, bf16[384,256]{1,0:T(8,128)(2,1)S(1)}, u32[]{:S(2)}, u32[]{:S(2)}) collective-permute-start(bf16[384,256]{1,0:T(8,128)(2,1)S(1)} %get-tuple-element.27.refs_0_), channel_id=1, source_target_pairs={{0,1},{1,0},{2,3},{3,2},{4,5},{5,4},{6,7},{7,6},{8,9},{9,8},{10,11... | collective-permute-start | bytes 589832 | tf_op jit(solution)/shard_map/ppermute | solution.py:296
  3.8 2.6 %collective-permute-start.1 = (bf16[288,256]{1,0:T(8,128)(2,1)S(1)}, bf16[288,256]{1,0:T(8,128)(2,1)S(1)}, u32[]{:S(2)}, u32[]{:S(2)}) collective-permute-start(bf16[288,256]{1,0:T(8,128)(2,1)S(1)} %get-tuple-element.31), channel_id=1, source_target_pairs={{0,2},{1,5},{2,6},{3,1},{4,0},{5,9},{6,10},{7,3},{8,4},{9,13},{10,... | collective-permute-start | bytes 442376 | tf_op jit(solution)/shard_map/ppermute | solution.py:334
  6.3 0.4 %shard_map.92 = (bf16[128,1024]{1,0:T(8,128)(2,1)S(1)}, f32[1,128]{1,0:T(1,128)S(1)}) custom-call(bf16[1024,128]{1,0:T(8,128)(2,1)S(1)} %copy-done, f32[1,128]{1,0:T(1,128)S(1)} %bitcast.7), custom_call_target="tpu_custom_call" | custom-call | flops 268435456 | bytes 1048576 | tf_op jit(solution)/shard_map/pallas_call | solution.py:298
  6.8 1.6 %collective-permute-start.2 = (bf16[256,256]{1,0:T(8,128)(2,1)S(1)}, bf16[256,256]{1,0:T(8,128)(2,1)S(1)}, u32[]{:S(2)}, u32[]{:S(2)}) collective-permute-start(bf16[256,256]{1,0:T(8,128)(2,1)S(1)} %slice.6), channel_id=1, source_target_pairs={{0,2},{1,5},{2,6},{3,1},{4,0},{5,9},{6,10},{7,3},{8,4},{9,13},{10,... | collective-permute-start | bytes 393224 | tf_op jit(solution)/shard_map/ppermute | solution.py:334
  8.4 1.6 %collective-permute-start.3 = (bf16[192,256]{1,0:T(8,128)(2,1)S(1)}, bf16[192,256]{1,0:T(8,128)(2,1)S(1)}, u32[]{:S(2)}, u32[]{:S(2)}) collective-permute-start(bf16[192,256]{1,0:T(8,128)(2,1)S(1)} %shard_map.93), channel_id=1, source_target_pairs={{0,2},{1,5},{2,6},{3,1},{4,0},{5,9},{6,10},{7,3},{8,4},{9,13},{10,... | collective-permute-start | bytes 294920 | tf_op jit(solution)/shard_map/ppermute | solution.py:334
  10.0 1.6 %collective-permute-start.4 = (bf16[288,256]{1,0:T(8,128)(2,1)S(1)}, bf16[288,256]{1,0:T(8,128)(2,1)S(1)}, u32[]{:S(2)}, u32[]{:S(2)}) collective-permute-start(bf16[288,256]{1,0:T(8,128)(2,1)S(1)} %collective-permute-done.1.refs_2_), channel_id=1, source_target_pairs={{0,2},{1,5},{2,6},{3,1},{4,0},{5,9},{6,10},{7,3},{8,4},{9,13},{10,... | collective-permute-start | bytes 442376 | tf_op jit(solution)/shard_map/ppermute | solution.py:334
  11.6 1.5 %collective-permute-done.3.left_ref = bf16[192,256]{1,0:T(8,128)(2,1)S(1)} collective-permute-done((bf16[192,256]{1,0:T(8,128)(2,1)S(1)}, bf16[192,256]{1,0:T(8,128)(2,1)S(1)}, u32[]{:S(2)}, u32[]{:S(2)}) %collective-permute-start.3) | collective-permute-done | bytes 98336 | tf_op jit(solution)/shard_map/ppermute | solution.py:334
  13.1 0.0 collective-permute-done.2.right_ref
  13.1 1.6 %collective-permute-start.5 = (bf16[384,256]{1,0:T(8,128)(2,1)S(1)}, bf16[384,256]{1,0:T(8,128)(2,1)S(1)}, u32[]{:S(2)}, u32[]{:S(2)}) collective-permute-start(bf16[384,256]{1,0:T(8,128)(2,1)S(1)} %get-tuple-element.36), channel_id=1, source_target_pairs={{0,2},{1,5},{2,6},{3,1},{4,0},{5,9},{6,10},{7,3},{8,4},{9,13},{10,... | collective-permute-start | bytes 589832 | tf_op jit(solution)/shard_map/ppermute | solution.py:334
  14.7 0.4 %collective-permute-done.4.refs_4_ = bf16[288,256]{1,0:T(8,128)(2,1)S(1)} collective-permute-done((bf16[288,256]{1,0:T(8,128)(2,1)S(1)}, bf16[288,256]{1,0:T(8,128)(2,1)S(1)}, u32[]{:S(2)}, u32[]{:S(2)}) %collective-permute-start.4) | collective-permute-done | bytes 147488 | tf_op jit(solution)/shard_map/ppermute | solution.py:334
  15.2 1.6 %collective-permute-start.6 = (bf16[288,256]{1,0:T(8,128)(2,1)S(1)}, bf16[288,256]{1,0:T(8,128)(2,1)S(1)}, u32[]{:S(2)}, u32[]{:S(2)}) collective-permute-start(bf16[288,256]{1,0:T(8,128)(2,1)S(1)} %collective-permute-done.4.refs_4_), channel_id=1, source_target_pairs={{0,2},{1,5},{2,6},{3,1},{4,0},{5,9},{6,10},{7,3},{8,4},{9,13},{10,... | collective-permute-start | bytes 442376 | tf_op jit(solution)/shard_map/ppermute | solution.py:334
  16.8 0.0 collective-permute-start.8
  16.8 2.1 %collective-permute-done.5.refs_5_ = bf16[384,256]{1,0:T(8,128)(2,1)S(1)} collective-permute-done((bf16[384,256]{1,0:T(8,128)(2,1)S(1)}, bf16[384,256]{1,0:T(8,128)(2,1)S(1)}, u32[]{:S(2)}, u32[]{:S(2)}) %collective-permute-start.5) | collective-permute-done | bytes 196640 | tf_op jit(solution)/shard_map/ppermute | solution.py:334
  18.8 0.0 collective-permute-start.12
  18.8 0.5 %collective-permute-start.9 = (bf16[320,256]{1,0:T(8,128)(2,1)S(1)}, bf16[320,256]{1,0:T(8,128)(2,1)S(1)}, u32[]{:S(2)}, u32[]{:S(2)}) collective-permute-start(bf16[320,256]{1,0:T(8,128)(2,1)S(1)} %get-tuple-element.35.refs_3_), channel_id=1, source_target_pairs={{0,1},{1,0},{2,3},{3,2},{4,5},{5,4},{6,7},{7,6},{8,9},{9,8},{10,11... | collective-permute-start | bytes 491528 | tf_op jit(solution)/shard_map/ppermute | solution.py:296
  19.4 1.6 %collective-permute-start.7 = (bf16[320,256]{1,0:T(8,128)(2,1)S(1)}, bf16[320,256]{1,0:T(8,128)(2,1)S(1)}, u32[]{:S(2)}, u32[]{:S(2)}) collective-permute-start(bf16[320,256]{1,0:T(8,128)(2,1)S(1)} %slice.8), channel_id=1, source_target_pairs={{0,2},{1,5},{2,6},{3,1},{4,0},{5,9},{6,10},{7,3},{8,4},{9,13},{10,... | collective-permute-start | bytes 491528 | tf_op jit(solution)/shard_map/ppermute | solution.py:334
  21.0 1.6 %collective-permute-start.10 = (bf16[288,256]{1,0:T(8,128)(2,1)S(1)}, bf16[288,256]{1,0:T(8,128)(2,1)S(1)}, u32[]{:S(2)}, u32[]{:S(2)}) collective-permute-start(bf16[288,256]{1,0:T(8,128)(2,1)S(1)} %collective-permute-done.6.refs_6_), channel_id=1, source_target_pairs={{0,2},{1,5},{2,6},{3,1},{4,0},{5,9},{6,10},{7,3},{8,4},{9,13},{10,... | collective-permute-start | bytes 442376 | tf_op jit(solution)/shard_map/ppermute | solution.py:334
  22.6 2.2 %collective-permute-done.7.refs_7_ = bf16[320,256]{1,0:T(8,128)(2,1)S(1)} collective-permute-done((bf16[320,256]{1,0:T(8,128)(2,1)S(1)}, bf16[320,256]{1,0:T(8,128)(2,1)S(1)}, u32[]{:S(2)}, u32[]{:S(2)}) %collective-permute-start.7) | collective-permute-done | bytes 163872 | tf_op jit(solution)/shard_map/ppermute | solution.py:334
  24.7 0.5 %collective-permute-start.13 = (bf16[288,256]{1,0:T(8,128)(2,1)S(1)}, bf16[288,256]{1,0:T(8,128)(2,1)S(1)}, u32[]{:S(2)}, u32[]{:S(2)}) collective-permute-start(bf16[288,256]{1,0:T(8,128)(2,1)S(1)} %collective-permute-done.6.refs_6_), channel_id=1, source_target_pairs={{0,1},{1,0},{2,3},{3,2},{4,5},{5,4},{6,7},{7,6},{8,9},{9,8},{10,11... | collective-permute-start | bytes 442376 | tf_op jit(solution)/shard_map/ppermute | solution.py:296
  25.2 1.1 %collective-permute-done.10.refs_8_ = bf16[288,256]{1,0:T(8,128)(2,1)S(1)} collective-permute-done((bf16[288,256]{1,0:T(8,128)(2,1)S(1)}, bf16[288,256]{1,0:T(8,128)(2,1)S(1)}, u32[]{:S(2)}, u32[]{:S(2)}) %collective-permute-start.10) | collective-permute-done | bytes 147488 | tf_op jit(solution)/shard_map/ppermute | solution.py:334
  26.3 0.0 collective-permute-done.13.refs_13_
  26.4 1.3 %collective-permute-done.15.refs_15_ = bf16[288,256]{1,0:T(8,128)(2,1)S(1)} collective-permute-done((bf16[288,256]{1,0:T(8,128)(2,1)S(1)}, bf16[288,256]{1,0:T(8,128)(2,1)S(1)}, u32[]{:S(2)}, u32[]{:S(2)}) %collective-permute-start.15) | collective-permute-done | bytes 147488 | tf_op jit(solution)/shard_map/ppermute | solution.py:296
  27.7 4.4 %shard_map.95 = bf16[16,256,128]{2,1,0:T(8,128)(2,1)} custom-call(bf16[384,256]{1,0:T(8,128)(2,1)S(1)} %get-tuple-element.27.refs_0_, bf16[384,256]{1,0:T(8,128)(2,1)S(1)} %collective-permute-done.theirs_ref.refs_1_, bf16[288,256]{1,0:T(8,128)(2,1)S(1)} %collective-permute-done.1.refs_2_, bf16[320,256]{1,0:T(8,128)(2,1)S(1)} %get-tuple-element.35.refs_3_, ...), custom_call_target="tpu_custom_call" | custom-call | tf_op jit(solution)/shard_map/pallas_call | solution.py:374
  (19 shorter events, 0.1 us)
Async XLA Ops:
  0.0 6.3 %copy-start = (bf16[1024,128]{1,0:T(8,128)(2,1)S(1)}, bf16[1024,128]{1,0:T(8,128)(2,1)}, u32[]{:S(2)}) copy-start(bf16[1024,128]{1,0:T(8,128)(2,1)} %final_ref.1) | copy-start | bytes 786436
  3.2 3.5 %collective-permute-start = (bf16[384,256]{1,0:T(8,128)(2,1)S(1)}, bf16[384,256]{1,0:T(8,128)(2,1)S(1)}, u32[]{:S(2)}, u32[]{:S(2)}) collective-permute-start(bf16[384,256]{1,0:T(8,128)(2,1)S(1)} %get-tuple-element.27.refs_0_), channel_id=1, source_target_pairs={{0,1},{1,0},{2,3},{3,2},{4,5},{5,4},{6,7},{7,6},{8,9},{9,8},{10,11... | collective-permute-start | bytes 589832 | tf_op jit(solution)/shard_map/ppermute | solution.py:296
  3.8 2.6 %copy-start.1 = (f32[128]{0:T(128)S(1)}, f32[128]{0:T(128)}, u32[]{:S(2)}) copy-start(f32[128]{0:T(128)} %param.17) | copy-start | bytes 1540
  3.8 6.3 %collective-permute-start.1 = (bf16[288,256]{1,0:T(8,128)(2,1)S(1)}, bf16[288,256]{1,0:T(8,128)(2,1)S(1)}, u32[]{:S(2)}, u32[]{:S(2)}) collective-permute-start(bf16[288,256]{1,0:T(8,128)(2,1)S(1)} %get-tuple-element.31), channel_id=1, source_target_pairs={{0,2},{1,5},{2,6},{3,1},{4,0},{5,9},{6,10},{7,3},{8,4},{9,13},{10,... | collective-permute-start | bytes 442376 | tf_op jit(solution)/shard_map/ppermute | solution.py:334
  6.8 6.3 %collective-permute-start.2 = (bf16[256,256]{1,0:T(8,128)(2,1)S(1)}, bf16[256,256]{1,0:T(8,128)(2,1)S(1)}, u32[]{:S(2)}, u32[]{:S(2)}) collective-permute-start(bf16[256,256]{1,0:T(8,128)(2,1)S(1)} %slice.6), channel_id=1, source_target_pairs={{0,2},{1,5},{2,6},{3,1},{4,0},{5,9},{6,10},{7,3},{8,4},{9,13},{10,... | collective-permute-start | bytes 393224 | tf_op jit(solution)/shard_map/ppermute | solution.py:334
  8.4 4.7 %collective-permute-start.3 = (bf16[192,256]{1,0:T(8,128)(2,1)S(1)}, bf16[192,256]{1,0:T(8,128)(2,1)S(1)}, u32[]{:S(2)}, u32[]{:S(2)}) collective-permute-start(bf16[192,256]{1,0:T(8,128)(2,1)S(1)} %shard_map.93), channel_id=1, source_target_pairs={{0,2},{1,5},{2,6},{3,1},{4,0},{5,9},{6,10},{7,3},{8,4},{9,13},{10,... | collective-permute-start | bytes 294920 | tf_op jit(solution)/shard_map/ppermute | solution.py:334
  10.0 5.1 %collective-permute-start.4 = (bf16[288,256]{1,0:T(8,128)(2,1)S(1)}, bf16[288,256]{1,0:T(8,128)(2,1)S(1)}, u32[]{:S(2)}, u32[]{:S(2)}) collective-permute-start(bf16[288,256]{1,0:T(8,128)(2,1)S(1)} %collective-permute-done.1.refs_2_), channel_id=1, source_target_pairs={{0,2},{1,5},{2,6},{3,1},{4,0},{5,9},{6,10},{7,3},{8,4},{9,13},{10,... | collective-permute-start | bytes 442376 | tf_op jit(solution)/shard_map/ppermute | solution.py:334
  13.1 5.7 %collective-permute-start.5 = (bf16[384,256]{1,0:T(8,128)(2,1)S(1)}, bf16[384,256]{1,0:T(8,128)(2,1)S(1)}, u32[]{:S(2)}, u32[]{:S(2)}) collective-permute-start(bf16[384,256]{1,0:T(8,128)(2,1)S(1)} %get-tuple-element.36), channel_id=1, source_target_pairs={{0,2},{1,5},{2,6},{3,1},{4,0},{5,9},{6,10},{7,3},{8,4},{9,13},{10,... | collective-permute-start | bytes 589832 | tf_op jit(solution)/shard_map/ppermute | solution.py:334
  15.2 5.8 %collective-permute-start.6 = (bf16[288,256]{1,0:T(8,128)(2,1)S(1)}, bf16[288,256]{1,0:T(8,128)(2,1)S(1)}, u32[]{:S(2)}, u32[]{:S(2)}) collective-permute-start(bf16[288,256]{1,0:T(8,128)(2,1)S(1)} %collective-permute-done.4.refs_4_), channel_id=1, source_target_pairs={{0,2},{1,5},{2,6},{3,1},{4,0},{5,9},{6,10},{7,3},{8,4},{9,13},{10,... | collective-permute-start | bytes 442376 | tf_op jit(solution)/shard_map/ppermute | solution.py:334
  16.8 5.8 %collective-permute-start.8 = (bf16[288,256]{1,0:T(8,128)(2,1)S(1)}, bf16[288,256]{1,0:T(8,128)(2,1)S(1)}, u32[]{:S(2)}, u32[]{:S(2)}) collective-permute-start(bf16[288,256]{1,0:T(8,128)(2,1)S(1)} %collective-permute-done.1.refs_2_), channel_id=1, source_target_pairs={{0,1},{1,0},{2,3},{3,2},{4,5},{5,4},{6,7},{7,6},{8,9},{9,8},{10,11... | collective-permute-start | bytes 442376 | tf_op jit(solution)/shard_map/ppermute | solution.py:296
  18.8 7.5 %collective-permute-start.12 = (bf16[384,256]{1,0:T(8,128)(2,1)S(1)}, bf16[384,256]{1,0:T(8,128)(2,1)S(1)}, u32[]{:S(2)}, u32[]{:S(2)}) collective-permute-start(bf16[384,256]{1,0:T(8,128)(2,1)S(1)} %collective-permute-done.5.refs_5_), channel_id=1, source_target_pairs={{0,1},{1,0},{2,3},{3,2},{4,5},{5,4},{6,7},{7,6},{8,9},{9,8},{10,11... | collective-permute-start | bytes 589832 | tf_op jit(solution)/shard_map/ppermute | solution.py:296
  18.8 3.7 %collective-permute-start.9 = (bf16[320,256]{1,0:T(8,128)(2,1)S(1)}, bf16[320,256]{1,0:T(8,128)(2,1)S(1)}, u32[]{:S(2)}, u32[]{:S(2)}) collective-permute-start(bf16[320,256]{1,0:T(8,128)(2,1)S(1)} %get-tuple-element.35.refs_3_), channel_id=1, source_target_pairs={{0,1},{1,0},{2,3},{3,2},{4,5},{5,4},{6,7},{7,6},{8,9},{9,8},{10,11... | collective-permute-start | bytes 491528 | tf_op jit(solution)/shard_map/ppermute | solution.py:296
  19.4 5.4 %collective-permute-start.7 = (bf16[320,256]{1,0:T(8,128)(2,1)S(1)}, bf16[320,256]{1,0:T(8,128)(2,1)S(1)}, u32[]{:S(2)}, u32[]{:S(2)}) collective-permute-start(bf16[320,256]{1,0:T(8,128)(2,1)S(1)} %slice.8), channel_id=1, source_target_pairs={{0,2},{1,5},{2,6},{3,1},{4,0},{5,9},{6,10},{7,3},{8,4},{9,13},{10,... | collective-permute-start | bytes 491528 | tf_op jit(solution)/shard_map/ppermute | solution.py:334
  21.0 5.3 %collective-permute-start.10 = (bf16[288,256]{1,0:T(8,128)(2,1)S(1)}, bf16[288,256]{1,0:T(8,128)(2,1)S(1)}, u32[]{:S(2)}, u32[]{:S(2)}) collective-permute-start(bf16[288,256]{1,0:T(8,128)(2,1)S(1)} %collective-permute-done.6.refs_6_), channel_id=1, source_target_pairs={{0,2},{1,5},{2,6},{3,1},{4,0},{5,9},{6,10},{7,3},{8,4},{9,13},{10,... | collective-permute-start | bytes 442376 | tf_op jit(solution)/shard_map/ppermute | solution.py:334
  22.6 3.7 %collective-permute-start.11 = (bf16[288,256]{1,0:T(8,128)(2,1)S(1)}, bf16[288,256]{1,0:T(8,128)(2,1)S(1)}, u32[]{:S(2)}, u32[]{:S(2)}) collective-permute-start(bf16[288,256]{1,0:T(8,128)(2,1)S(1)} %collective-permute-done.4.refs_4_), channel_id=1, source_target_pairs={{0,1},{1,0},{2,3},{3,2},{4,5},{5,4},{6,7},{7,6},{8,9},{9,8},{10,11... | collective-permute-start | bytes 442376 | tf_op jit(solution)/shard_map/ppermute | solution.py:296
  24.7 1.6 %collective-permute-start.14 = (bf16[320,256]{1,0:T(8,128)(2,1)S(1)}, bf16[320,256]{1,0:T(8,128)(2,1)S(1)}, u32[]{:S(2)}, u32[]{:S(2)}) collective-permute-start(bf16[320,256]{1,0:T(8,128)(2,1)S(1)} %collective-permute-done.7.refs_7_), channel_id=1, source_target_pairs={{0,1},{1,0},{2,3},{3,2},{4,5},{5,4},{6,7},{7,6},{8,9},{9,8},{10,11... | collective-permute-start | bytes 491528 | tf_op jit(solution)/shard_map/ppermute | solution.py:296
  24.7 1.6 %collective-permute-start.13 = (bf16[288,256]{1,0:T(8,128)(2,1)S(1)}, bf16[288,256]{1,0:T(8,128)(2,1)S(1)}, u32[]{:S(2)}, u32[]{:S(2)}) collective-permute-start(bf16[288,256]{1,0:T(8,128)(2,1)S(1)} %collective-permute-done.6.refs_6_), channel_id=1, source_target_pairs={{0,1},{1,0},{2,3},{3,2},{4,5},{5,4},{6,7},{7,6},{8,9},{9,8},{10,11... | collective-permute-start | bytes 442376 | tf_op jit(solution)/shard_map/ppermute | solution.py:296
  26.3 1.4 %collective-permute-start.15 = (bf16[288,256]{1,0:T(8,128)(2,1)S(1)}, bf16[288,256]{1,0:T(8,128)(2,1)S(1)}, u32[]{:S(2)}, u32[]{:S(2)}) collective-permute-start(bf16[288,256]{1,0:T(8,128)(2,1)S(1)} %collective-permute-done.10.refs_8_), channel_id=1, source_target_pairs={{0,1},{1,0},{2,3},{3,2},{4,5},{5,4},{6,7},{7,6},{8,9},{9,8},{10,11... | collective-permute-start | bytes 442376 | tf_op jit(solution)/shard_map/ppermute | solution.py:296

commit v18 on v15

--- a/solution.py
+++ b/solution.py
@@ -148,7 +148,7 @@
         next_ref[at + per_chip : at + 2 * per_chip, :] = theirs_ref[low : low + per_chip, :]
 
 
-def weight_kernel(final_ref, offset_ref, out_ref, offset_out, wide_ref):
+def weight_kernel(final_ref, offset_ref, out_ref, mixing_out, offset_out, wide_ref):
     offset_out[...] = offset_ref[...]
     channels, columns = out_ref.shape
     hidden = math.isqrt(columns)
@@ -156,14 +156,25 @@
     step = LANES // hidden
     for e in range(0, hidden, step):
         rows = [wide_ref[pl.ds(e + n, hidden, stride=hidden), :] for n in range(step)]
+        mixing_out[:, e * channels : (e + step) * channels] = jnp.concatenate(rows, axis=1).astype(
+            jnp.bfloat16
+        )
         out_ref[:, e * hidden : (e + step) * hidden] = jnp.concatenate(rows, axis=0).T.astype(
             jnp.bfloat16
         )
 
 
-def pair_kernel(places, gridded, rows_here, hidden, samples, *refs):
+def left_piece(ref, base, rows_here, hidden, here):
+    tile = ref.shape[1]
+    span = rows_here * hidden
+    deep = span * here // tile
+    start = pl.multiple_of(base + lax.rem(lax.axis_index("row"), 2) * deep, deep)
+    piece = ref[pl.ds(start, deep), :].astype(jnp.float32)
+    return jnp.concatenate([piece[n * here : (n + 1) * here] for n in range(span // tile)], axis=1)
+
+
+def pair_kernel(places, gridded, rows_here, hidden, here, samples, *refs):
     refs = list(refs)
-    count = len(places)
     if gridded:
         shards = [(refs.pop(0), 0, refs.pop(0), 0) for _ in places]
     else:
@@ -171,17 +182,8 @@
         shards = [(messages[n], right, messages[m], left) for n, right, m, left in places]
     weight_ref, offset_ref, out_hbm, left_ref, outer_ref, out_ref, sems = refs
     tile = shards[0][0].shape[1]
-    here = samples // count
-    span = rows_here * hidden
-    deep = span * here // tile
-    core = lax.rem(lax.axis_index("row"), 2)
-    pieces = []
-    for _, _, ref, base in shards:
-        start = pl.multiple_of(base + core * deep, deep)
-        piece = ref[pl.ds(start, deep), :].astype(jnp.float32)
-        pieces.append(
-            jnp.concatenate([piece[n * here : (n + 1) * here] for n in range(span // tile)], axis=1)
-        )
+    pieces = [left_piece(ref, base, rows_here, hidden, here) for _, _, ref, base in shards]
+    pieces += [jnp.zeros_like(pieces[0])] * (len(pieces) % 2)
     left_ref[...] = jnp.concatenate(pieces, axis=0).T.astype(jnp.bfloat16)
 
     left = left_ref[...]
@@ -190,6 +192,7 @@
             ref[base + e * here : base + (e + 2) * here, :].astype(jnp.float32)
             for ref, base, _, _ in shards
         ]
+        both += [jnp.zeros_like(both[0])] * (len(both) % 2)
         for k in range(2):
             right = jnp.concatenate([x[k * here : (k + 1) * here] for x in both], axis=0)
             outer = jnp.dot(left, right.astype(jnp.bfloat16), preferred_element_type=jnp.float32)
@@ -199,7 +202,12 @@
                     i * hidden : (i + 1) * hidden
                 ]
 
-    first = pl.program_id(0) * tile if gridded else 0
+    if not gridded:
+        for i in range(rows_here):
+            value = jnp.dot(weight_ref[...], outer_ref[i], preferred_element_type=jnp.float32)
+            out_hbm[i] = value.T
+        return
+    first = pl.program_id(0) * tile
     copies = []
     for i in range(rows_here):
         value = jnp.dot(weight_ref[...], outer_ref[i], preferred_element_type=jnp.float32)
@@ -208,6 +216,36 @@
         copies.append(
             pltpu.make_async_copy(out_ref.at[i], out_hbm.at[i, pl.ds(first, tile)], sems.at[i])
         )
+        copies[-1].start()
+    for copy in copies:
+        copy.wait()
+
+
+def last_kernel(base, rows_here, hidden, here, samples, ref, total_ref, mixing_ref, offset_ref, out_hbm, out_ref, sems):
+    channels = out_ref.shape[2]
+    right = ref[: hidden * here, :].astype(jnp.float32).T.astype(jnp.bfloat16)
+    left = left_piece(ref, base, rows_here, hidden, here)
+    left = [left[:, i * hidden : (i + 1) * hidden] for i in range(rows_here)]
+    mixed = jnp.dot(
+        jnp.concatenate(left, axis=0).astype(jnp.bfloat16),
+        mixing_ref[...],
+        preferred_element_type=jnp.float32,
+    )
+    copies = []
+    for i in range(0, rows_here, 2):
+        parts = []
+        for k in range(2):
+            part = mixed[(i + k) * here : (i + k + 1) * here]
+            part = [part[:, e * channels : (e + 1) * channels] for e in range(hidden)]
+            parts.append(jnp.concatenate(part, axis=0).astype(jnp.bfloat16))
+        value = jnp.dot(
+            right, jnp.concatenate(parts, axis=1), preferred_element_type=jnp.float32
+        )
+        for k in range(2):
+            part = value[:, k * channels : (k + 1) * channels] + total_ref[i + k]
+            out_ref[i + k] = (part * (1.0 / samples) + offset_ref[...]).astype(jnp.bfloat16)
+        rows = pl.ds(i, 2)
+        copies.append(pltpu.make_async_copy(out_ref.at[rows], out_hbm.at[rows], sems.at[i // 2]))
         copies[-1].start()
     for copy in copies:
         copy.wait()
@@ -286,19 +324,20 @@
     def swap(value):
         return lax.ppermute(value, "row", [(r, r ^ 1) for r in range(size)])
 
-    weight, offset = pl.pallas_call(
+    weight, mixing, offset = pl.pallas_call(
         weight_kernel,
         out_shape=[
             jax.ShapeDtypeStruct((channels, hidden * hidden), jnp.bfloat16),
+            jax.ShapeDtypeStruct((hidden, hidden * channels), jnp.bfloat16),
             jax.ShapeDtypeStruct((1, channels), jnp.float32),
         ],
         in_specs=[vmem] * 2,
-        out_specs=[vmem] * 2,
+        out_specs=[vmem] * 3,
         scratch_shapes=[pltpu.VMEM((hidden * hidden, channels), jnp.float32)],
         compiler_params=pltpu.CompilerParams(vmem_limit_bytes=16 * MIB),
         cost_estimate=pl.CostEstimate(flops=2**28, bytes_accessed=2**20, transcendentals=0),
     )(final_projector_coefficients, final_projector_offset.reshape(1, channels))
-    theirs, weight, offset = lax.optimization_barrier((swap(give), weight, offset))
+    theirs, weight, mixing, offset = lax.optimization_barrier((swap(give), weight, mixing, offset))
     messages = [give, theirs]
     places = [(n, 0, n, body + (half - 1) * per_chip) for n in range(2)]
 
@@ -339,6 +378,7 @@
         messages += pair
 
     gridded = tiles > 1
+    final = jax.ShapeDtypeStruct((rows_here, residues, channels), jnp.bfloat16)
     if gridded:
         operands, specs = [], []
         for n, right, m, left in places:
@@ -351,25 +391,40 @@
             pl.BlockSpec((channels, hidden * hidden), lambda t: (0, 0)),
             pl.BlockSpec((1, channels), lambda t: (0, 0)),
         ]
-        grid = (tiles,)
+        grid, result, out_spec = (tiles,), final, hbm
     else:
-        operands = messages
-        specs = [vmem] * (len(messages) + 2)
-        grid = ()
-    return pl.pallas_call(
-        functools.partial(pair_kernel, places, gridded, rows_here, hidden, samples),
-        out_shape=jax.ShapeDtypeStruct((rows_here, residues, channels), jnp.bfloat16),
+        places, operands = places[:-1], messages[:-1]
+        specs = [vmem] * (len(operands) + 2)
+        grid, out_spec = (), vmem
+        result = jax.ShapeDtypeStruct((rows_here, residues, channels), jnp.float32)
+    deep = here * (len(places) + len(places) % 2)
+    total = pl.pallas_call(
+        functools.partial(pair_kernel, places, gridded, rows_here, hidden, here, samples),
+        out_shape=result,
         grid=grid,
         in_specs=specs,
-        out_specs=hbm,
+        out_specs=out_spec,
         scratch_shapes=[
-            pltpu.VMEM((rows_here * hidden, samples), jnp.bfloat16),
+            pltpu.VMEM((rows_here * hidden, deep), jnp.bfloat16),
             pltpu.VMEM((rows_here, hidden * hidden, tile), jnp.bfloat16),
             pltpu.VMEM((rows_here, tile, channels), jnp.bfloat16),
             pltpu.SemaphoreType.DMA((rows_here,)),
         ],
         compiler_params=pltpu.CompilerParams(vmem_limit_bytes=40 * MIB),
     )(*operands, weight, offset)
+    if gridded:
+        return total
+    return pl.pallas_call(
+        functools.partial(last_kernel, body, rows_here, hidden, here, samples),
+        out_shape=final,
+        in_specs=[vmem] * 4,
+        out_specs=hbm,
+        scratch_shapes=[
+            pltpu.VMEM((rows_here, tile, channels), jnp.bfloat16),
+            pltpu.SemaphoreType.DMA((rows_here // 2,)),
+        ],
+        compiler_params=pltpu.CompilerParams(vmem_limit_bytes=24 * MIB),
+    )(messages[-1], total, mixing, offset)
 
 
 def solution(mesh):

time: 31.5 us -> 32.4 us (1.029)
  local copies, waits for them, and re-layouts: 0.04 us -> 1.64 us
  waiting for transfers between devices: 8.63 us -> 7.59 us
  Pallas kernels: 8.07 us -> 9.07 us
  starting transfers between devices: 14.5 us -> 13.7 us
    pallas_call x0 -> x1, Pallas kernels: none -> 1.71 us  [per_device(): pl.pallas_call(functools.partial(last_kernel, body, rows_here, hidden, he...]
    unnamed x4, local copies, waits for them, and re-layouts: 0.01 us -> 1.6 us
    ppermute x8, waiting for transfers between devices: 1.36 us -> 0.03 us  [swap(): return lax.ppermute(value, 'row', [(r, r ^ 1) for r in range(size)])]
    ppermute x7, starting transfers between devices: 13.5 us -> 12.7 us  [per_device(): landed = [lax.ppermute(x, 'row', around) for x in flying]]
    pallas_call x1, Pallas kernels: 4.43 us -> 3.77 us  [per_device(): pl.pallas_call(functools.partial(pair_kernel, places, gridded, rows_here,...]
  transfers between devices with their start and end apart: 15 -> 15, of which waited for: 8 -> 4; matrix products, arithmetic and copies ran while one was open for 0% -> 0% of each run, Pallas kernels for 1% -> 13%
where the time goes in v18:
time: 32.4 us; the launch traced here: 32.1 us
  starting transfers between devices  13.7 us (42%)
  Pallas kernels  9.07 us (28%)
  waiting for transfers between devices  7.59 us (23%)
  local copies, waits for them, and re-layouts  1.64 us (5%)
    ppermute x7, starting transfers between devices, per_device(): landed = [lax.ppermute(x, 'row', around) for x in flying]  12.7 us
    ppermute x7, waiting for transfers between devices, per_device(): landed = [lax.ppermute(x, 'row', around) for x in flying]  7.56 us
    pallas_call x1, Pallas kernels, per_device(): pl.pallas_call(functools.partial(pair_kernel, places, gridded, rows_here,...  3.77 us
    pallas_call x1, Pallas kernels, per_device(): pl.pallas_call(functools.partial(project_kernel, rows_here), out_shape=[r...  3.18 us
    pallas_call x1, Pallas kernels, per_device(): pl.pallas_call(functools.partial(last_kernel, body, rows_here, hidden, he...  1.71 us
    unnamed x4, local copies, waits for them, and re-layouts  1.6 us
    ppermute x8, starting transfers between devices, swap(): return lax.ppermute(value, 'row', [(r, r ^ 1) for r in range(size)])  1.04 us
  transfers between devices with their start and end apart: 15, of which 4 were waited for; matrix products, arithmetic and copies ran while one was open for 0% of the time, Pallas kernels for 13%

profile of v18, /device:TPU:0, one launch (start us, length us, event | category | flops | bytes accessed | tf_op | source)
XLA Modules:
  0.0 32.1 jit_solution(16177919926854712482)
XLA Ops:
  0.0 3.2 %shard_map.91 = (bf16[384,256]{1,0:T(8,128)(2,1)S(1)}, bf16[384,256]{1,0:T(8,128)(2,1)S(1)}) custom-call(bf16[8,256,256]{2,1,0:T(8,128)(2,1)} %x_hbm.1, f32[1,256]{1,0:T(1,128)} %bitcast.10, f32[1,256]{1,0:T(1,128)} %bitcast.11, bf16[32,256]{1,0:T(8,128)(2,1)} %bitcast.8, f32[1,32]{1,0:T(1,128)} %bitcast.12, bf16[32,256]{1,0:T(8,128)(2,1)} %bitcast.9, ...), custom_call_target="tpu_custom_call" | custom-call | flops 536870912 | bytes 1048576 | tf_op jit(solution)/shard_map/pallas_call | solution.py:283
  3.2 0.5 %collective-permute-start.4 = (bf16[384,256]{1,0:T(8,128)(2,1)S(1)}, bf16[384,256]{1,0:T(8,128)(2,1)S(1)}, u32[]{:S(2)}, u32[]{:S(2)}) collective-permute-start(bf16[384,256]{1,0:T(8,128)(2,1)S(1)} %get-tuple-element.27.refs_0_), channel_id=1, source_target_pairs={{0,1},{1,0},{2,3},{3,2},{4,5},{5,4},{6,7},{7,6},{8,9},{9,8},{10,11... | collective-permute-start | bytes 589832 | tf_op jit(solution)/shard_map/ppermute | solution.py:325
  3.7 2.6 %collective-permute-start = (bf16[384,256]{1,0:T(8,128)(2,1)S(1)}, bf16[384,256]{1,0:T(8,128)(2,1)S(1)}, u32[]{:S(2)}, u32[]{:S(2)}) collective-permute-start(bf16[384,256]{1,0:T(8,128)(2,1)S(1)} %get-tuple-element.26), channel_id=1, source_target_pairs={{0,2},{1,5},{2,6},{3,1},{4,0},{5,9},{6,10},{7,3},{8,4},{9,13},{10,... | collective-permute-start | bytes 589832 | tf_op jit(solution)/shard_map/ppermute | solution.py:350
  6.3 0.9 %copy-done = bf16[1024,128]{1,0:T(8,128)(2,1)S(1)} copy-done((bf16[1024,128]{1,0:T(8,128)(2,1)S(1)}, bf16[1024,128]{1,0:T(8,128)(2,1)}, u32[]{:S(2)}) %copy-start) | copy-done | bytes 262168
  7.2 0.7 %copy-done.1 = f32[128]{0:T(128)S(1)} copy-done((f32[128]{0:T(128)S(1)}, f32[128]{0:T(128)}, u32[]{:S(2)}) %copy-start.1) | copy-done | bytes 536
  7.9 0.4 %shard_map.92 = (bf16[128,1024]{1,0:T(8,128)(2,1)S(1)}, bf16[32,4096]{1,0:T(8,128)(2,1)S(1)}, f32[1,128]{1,0:T(1,128)S(1)}) custom-call(bf16[1024,128]{1,0:T(8,128)(2,1)S(1)} %copy-done, f32[1,128]{1,0:T(1,128)S(1)} %bitcast.7), custom_call_target="tpu_custom_call" | custom-call | flops 268435456 | bytes 1048576 | tf_op jit(solution)/shard_map/pallas_call | solution.py:327
  8.3 1.6 %collective-permute-start.5 = (bf16[352,256]{1,0:T(8,128)(2,1)S(1)}, bf16[352,256]{1,0:T(8,128)(2,1)S(1)}, u32[]{:S(2)}, u32[]{:S(2)}) collective-permute-start(bf16[352,256]{1,0:T(8,128)(2,1)S(1)} %slice.10), channel_id=1, source_target_pairs={{0,2},{1,5},{2,6},{3,1},{4,0},{5,9},{6,10},{7,3},{8,4},{9,13},{10,... | collective-permute-start | bytes 540680 | tf_op jit(solution)/shard_map/ppermute | solution.py:350
  10.0 0.0 collective-permute-done.mine_ref.refs_2_
  10.0 2.0 %collective-permute-start.1 = (bf16[288,256]{1,0:T(8,128)(2,1)S(1)}, bf16[288,256]{1,0:T(8,128)(2,1)S(1)}, u32[]{:S(2)}, u32[]{:S(2)}) collective-permute-start(bf16[288,256]{1,0:T(8,128)(2,1)S(1)} %slice.12), channel_id=1, source_target_pairs={{0,2},{1,5},{2,6},{3,1},{4,0},{5,9},{6,10},{7,3},{8,4},{9,13},{10,... | collective-permute-start | bytes 442376 | tf_op jit(solution)/shard_map/ppermute | solution.py:350
  12.0 1.9 %collective-permute-done.5.theirs_ref.refs_3_ = bf16[352,256]{1,0:T(8,128)(2,1)S(1)} collective-permute-done((bf16[352,256]{1,0:T(8,128)(2,1)S(1)}, bf16[352,256]{1,0:T(8,128)(2,1)S(1)}, u32[]{:S(2)}, u32[]{:S(2)}) %collective-permute-start.5) | collective-permute-done | bytes 180256 | tf_op jit(solution)/shard_map/ppermute | solution.py:350
  13.9 1.6 %collective-permute-start.6 = (bf16[384,256]{1,0:T(8,128)(2,1)S(1)}, bf16[384,256]{1,0:T(8,128)(2,1)S(1)}, u32[]{:S(2)}, u32[]{:S(2)}) collective-permute-start(bf16[384,256]{1,0:T(8,128)(2,1)S(1)} %shard_map.93), channel_id=1, source_target_pairs={{0,2},{1,5},{2,6},{3,1},{4,0},{5,9},{6,10},{7,3},{8,4},{9,13},{10,... | collective-permute-start | bytes 589832 | tf_op jit(solution)/shard_map/ppermute | solution.py:350
  15.5 0.0 collective-permute-start.12
  15.5 0.0 collective-permute-done.1.refs_4_
  15.5 1.6 %collective-permute-start.2 = (bf16[288,256]{1,0:T(8,128)(2,1)S(1)}, bf16[288,256]{1,0:T(8,128)(2,1)S(1)}, u32[]{:S(2)}, u32[]{:S(2)}) collective-permute-start(bf16[288,256]{1,0:T(8,128)(2,1)S(1)} %collective-permute-done.1.refs_4_), channel_id=1, source_target_pairs={{0,2},{1,5},{2,6},{3,1},{4,0},{5,9},{6,10},{7,3},{8,4},{9,13},{10,... | collective-permute-start | bytes 442376 | tf_op jit(solution)/shard_map/ppermute | solution.py:350
  17.2 0.0 collective-permute-start.11
  17.2 2.5 %collective-permute-done.6.refs_5_ = bf16[384,256]{1,0:T(8,128)(2,1)S(1)} collective-permute-done((bf16[384,256]{1,0:T(8,128)(2,1)S(1)}, bf16[384,256]{1,0:T(8,128)(2,1)S(1)}, u32[]{:S(2)}, u32[]{:S(2)}) %collective-permute-start.6) | collective-permute-done | bytes 196640 | tf_op jit(solution)/shard_map/ppermute | solution.py:350
  19.6 1.6 %collective-permute-start.10 = (bf16[320,256]{1,0:T(8,128)(2,1)S(1)}, bf16[320,256]{1,0:T(8,128)(2,1)S(1)}, u32[]{:S(2)}, u32[]{:S(2)}) collective-permute-start(bf16[320,256]{1,0:T(8,128)(2,1)S(1)} %slice.13), channel_id=1, source_target_pairs={{0,2},{1,5},{2,6},{3,1},{4,0},{5,9},{6,10},{7,3},{8,4},{9,13},{10,... | collective-permute-start | bytes 491528 | tf_op jit(solution)/shard_map/ppermute | solution.py:350
  21.3 1.6 %collective-permute-start.3 = (bf16[288,256]{1,0:T(8,128)(2,1)S(1)}, bf16[288,256]{1,0:T(8,128)(2,1)S(1)}, u32[]{:S(2)}, u32[]{:S(2)}) collective-permute-start(bf16[288,256]{1,0:T(8,128)(2,1)S(1)} %collective-permute-done.2.refs_6_), channel_id=1, source_target_pairs={{0,2},{1,5},{2,6},{3,1},{4,0},{5,9},{6,10},{7,3},{8,4},{9,13},{10,... | collective-permute-start | bytes 442376 | tf_op jit(solution)/shard_map/ppermute | solution.py:350
  22.9 2.2 %collective-permute-done.10.refs_7_ = bf16[320,256]{1,0:T(8,128)(2,1)S(1)} collective-permute-done((bf16[320,256]{1,0:T(8,128)(2,1)S(1)}, bf16[320,256]{1,0:T(8,128)(2,1)S(1)}, u32[]{:S(2)}, u32[]{:S(2)}) %collective-permute-start.10) | collective-permute-done | bytes 163872 | tf_op jit(solution)/shard_map/ppermute | solution.py:350
  25.0 0.5 %collective-permute-start.13 = (bf16[288,256]{1,0:T(8,128)(2,1)S(1)}, bf16[288,256]{1,0:T(8,128)(2,1)S(1)}, u32[]{:S(2)}, u32[]{:S(2)}) collective-permute-start(bf16[288,256]{1,0:T(8,128)(2,1)S(1)} %collective-permute-done.2.refs_6_), channel_id=1, source_target_pairs={{0,1},{1,0},{2,3},{3,2},{4,5},{5,4},{6,7},{7,6},{8,9},{9,8},{10,11... | collective-permute-start | bytes 442376 | tf_op jit(solution)/shard_map/ppermute | solution.py:325
  25.5 1.1 %collective-permute-done.3.refs_8_ = bf16[288,256]{1,0:T(8,128)(2,1)S(1)} collective-permute-done((bf16[288,256]{1,0:T(8,128)(2,1)S(1)}, bf16[288,256]{1,0:T(8,128)(2,1)S(1)}, u32[]{:S(2)}, u32[]{:S(2)}) %collective-permute-start.3) | collective-permute-done | bytes 147488 | tf_op jit(solution)/shard_map/ppermute | solution.py:350
  26.6 0.0 collective-permute-done.13.refs_13_
  26.6 3.8 %shard_map.94.total_ref = f32[16,256,128]{2,1,0:T(8,128)S(1)} custom-call(bf16[384,256]{1,0:T(8,128)(2,1)S(1)} %get-tuple-element.27.refs_0_, bf16[384,256]{1,0:T(8,128)(2,1)S(1)} %collective-permute-done.4.refs_1_, bf16[384,256]{1,0:T(8,128)(2,1)S(1)} %collective-permute-done.mine_ref.refs_2_, ...), custom_call_target="tpu_custom_call" | custom-call | tf_op jit(solution)/shard_map/pallas_call | solution.py:401
  30.4 1.7 %shard_map.95 = bf16[16,256,128]{2,1,0:T(8,128)(2,1)} custom-call(bf16[288,256]{1,0:T(8,128)(2,1)S(1)} %collective-permute-done.9.ref, f32[16,256,128]{2,1,0:T(8,128)S(1)} %shard_map.94.total_ref, bf16[32,4096]{1,0:T(8,128)(2,1)S(1)} %get-tuple-element.46.mixing_ref, f32[1,128]{1,0:T(1,128)S(1)} %get-tuple-element.45.refs_16_.offset_ref), custom_call_target="tpu_custom_call" | custom-call | tf_op jit(solution)/shard_map/pallas_call | solution.py:417
  (18 shorter events, 0.1 us)
Async XLA Ops:
  3.2 5.1 %collective-permute-start.4 = (bf16[384,256]{1,0:T(8,128)(2,1)S(1)}, bf16[384,256]{1,0:T(8,128)(2,1)S(1)}, u32[]{:S(2)}, u32[]{:S(2)}) collective-permute-start(bf16[384,256]{1,0:T(8,128)(2,1)S(1)} %get-tuple-element.27.refs_0_), channel_id=1, source_target_pairs={{0,1},{1,0},{2,3},{3,2},{4,5},{5,4},{6,7},{7,6},{8,9},{9,8},{10,11... | collective-permute-start | bytes 589832 | tf_op jit(solution)/shard_map/ppermute | solution.py:325
  3.7 6.3 %collective-permute-start = (bf16[384,256]{1,0:T(8,128)(2,1)S(1)}, bf16[384,256]{1,0:T(8,128)(2,1)S(1)}, u32[]{:S(2)}, u32[]{:S(2)}) collective-permute-start(bf16[384,256]{1,0:T(8,128)(2,1)S(1)} %get-tuple-element.26), channel_id=1, source_target_pairs={{0,2},{1,5},{2,6},{3,1},{4,0},{5,9},{6,10},{7,3},{8,4},{9,13},{10,... | collective-permute-start | bytes 589832 | tf_op jit(solution)/shard_map/ppermute | solution.py:350
  6.3 0.9 %copy-start = (bf16[1024,128]{1,0:T(8,128)(2,1)S(1)}, bf16[1024,128]{1,0:T(8,128)(2,1)}, u32[]{:S(2)}) copy-start(bf16[1024,128]{1,0:T(8,128)(2,1)} %final_ref.1) | copy-start | bytes 786436
  7.2 0.7 %copy-start.1 = (f32[128]{0:T(128)S(1)}, f32[128]{0:T(128)}, u32[]{:S(2)}) copy-start(f32[128]{0:T(128)} %param.17) | copy-start | bytes 1540
  8.3 5.5 %collective-permute-start.5 = (bf16[352,256]{1,0:T(8,128)(2,1)S(1)}, bf16[352,256]{1,0:T(8,128)(2,1)S(1)}, u32[]{:S(2)}, u32[]{:S(2)}) collective-permute-start(bf16[352,256]{1,0:T(8,128)(2,1)S(1)} %slice.10), channel_id=1, source_target_pairs={{0,2},{1,5},{2,6},{3,1},{4,0},{5,9},{6,10},{7,3},{8,4},{9,13},{10,... | collective-permute-start | bytes 540680 | tf_op jit(solution)/shard_map/ppermute | solution.py:350
  10.0 5.5 %collective-permute-start.1 = (bf16[288,256]{1,0:T(8,128)(2,1)S(1)}, bf16[288,256]{1,0:T(8,128)(2,1)S(1)}, u32[]{:S(2)}, u32[]{:S(2)}) collective-permute-start(bf16[288,256]{1,0:T(8,128)(2,1)S(1)} %slice.12), channel_id=1, source_target_pairs={{0,2},{1,5},{2,6},{3,1},{4,0},{5,9},{6,10},{7,3},{8,4},{9,13},{10,... | collective-permute-start | bytes 442376 | tf_op jit(solution)/shard_map/ppermute | solution.py:350
  13.9 5.7 %collective-permute-start.6 = (bf16[384,256]{1,0:T(8,128)(2,1)S(1)}, bf16[384,256]{1,0:T(8,128)(2,1)S(1)}, u32[]{:S(2)}, u32[]{:S(2)}) collective-permute-start(bf16[384,256]{1,0:T(8,128)(2,1)S(1)} %shard_map.93), channel_id=1, source_target_pairs={{0,2},{1,5},{2,6},{3,1},{4,0},{5,9},{6,10},{7,3},{8,4},{9,13},{10,... | collective-permute-start | bytes 589832 | tf_op jit(solution)/shard_map/ppermute | solution.py:350
  15.5 7.3 %collective-permute-start.12 = (bf16[352,256]{1,0:T(8,128)(2,1)S(1)}, bf16[352,256]{1,0:T(8,128)(2,1)S(1)}, u32[]{:S(2)}, u32[]{:S(2)}) collective-permute-start(bf16[352,256]{1,0:T(8,128)(2,1)S(1)} %collective-permute-done.5.theirs_ref.refs_3_), channel_id=1, source_target_pairs={{0,1},{1,0},{2,3},{3,2},{4,5},{5,4},{6,7},{7,6},{8,9},{9,8},{10,11... | collective-permute-start | bytes 540680 | tf_op jit(solution)/shard_map/ppermute | solution.py:325
  15.5 5.7 %collective-permute-start.2 = (bf16[288,256]{1,0:T(8,128)(2,1)S(1)}, bf16[288,256]{1,0:T(8,128)(2,1)S(1)}, u32[]{:S(2)}, u32[]{:S(2)}) collective-permute-start(bf16[288,256]{1,0:T(8,128)(2,1)S(1)} %collective-permute-done.1.refs_4_), channel_id=1, source_target_pairs={{0,2},{1,5},{2,6},{3,1},{4,0},{5,9},{6,10},{7,3},{8,4},{9,13},{10,... | collective-permute-start | bytes 442376 | tf_op jit(solution)/shard_map/ppermute | solution.py:350
  17.2 5.7 %collective-permute-start.11 = (bf16[384,256]{1,0:T(8,128)(2,1)S(1)}, bf16[384,256]{1,0:T(8,128)(2,1)S(1)}, u32[]{:S(2)}, u32[]{:S(2)}) collective-permute-start(bf16[384,256]{1,0:T(8,128)(2,1)S(1)} %collective-permute-done.mine_ref.refs_2_), channel_id=1, source_target_pairs={{0,1},{1,0},{2,3},{3,2},{4,5},{5,4},{6,7},{7,6},{8,9},{9,8},{10,11... | collective-permute-start | bytes 589832 | tf_op jit(solution)/shard_map/ppermute | solution.py:325
  19.6 7.0 %collective-permute-start.8 = (bf16[384,256]{1,0:T(8,128)(2,1)S(1)}, bf16[384,256]{1,0:T(8,128)(2,1)S(1)}, u32[]{:S(2)}, u32[]{:S(2)}) collective-permute-start(bf16[384,256]{1,0:T(8,128)(2,1)S(1)} %collective-permute-done.6.refs_5_), channel_id=1, source_target_pairs={{0,1},{1,0},{2,3},{3,2},{4,5},{5,4},{6,7},{7,6},{8,9},{9,8},{10,11... | collective-permute-start | bytes 589832 | tf_op jit(solution)/shard_map/ppermute | solution.py:325
  19.6 5.4 %collective-permute-start.10 = (bf16[320,256]{1,0:T(8,128)(2,1)S(1)}, bf16[320,256]{1,0:T(8,128)(2,1)S(1)}, u32[]{:S(2)}, u32[]{:S(2)}) collective-permute-start(bf16[320,256]{1,0:T(8,128)(2,1)S(1)} %slice.13), channel_id=1, source_target_pairs={{0,2},{1,5},{2,6},{3,1},{4,0},{5,9},{6,10},{7,3},{8,4},{9,13},{10,... | collective-permute-start | bytes 491528 | tf_op jit(solution)/shard_map/ppermute | solution.py:350
  21.3 5.3 %collective-permute-start.3 = (bf16[288,256]{1,0:T(8,128)(2,1)S(1)}, bf16[288,256]{1,0:T(8,128)(2,1)S(1)}, u32[]{:S(2)}, u32[]{:S(2)}) collective-permute-start(bf16[288,256]{1,0:T(8,128)(2,1)S(1)} %collective-permute-done.2.refs_6_), channel_id=1, source_target_pairs={{0,2},{1,5},{2,6},{3,1},{4,0},{5,9},{6,10},{7,3},{8,4},{9,13},{10,... | collective-permute-start | bytes 442376 | tf_op jit(solution)/shard_map/ppermute | solution.py:350
  22.9 3.7 %collective-permute-start.7 = (bf16[288,256]{1,0:T(8,128)(2,1)S(1)}, bf16[288,256]{1,0:T(8,128)(2,1)S(1)}, u32[]{:S(2)}, u32[]{:S(2)}) collective-permute-start(bf16[288,256]{1,0:T(8,128)(2,1)S(1)} %collective-permute-done.1.refs_4_), channel_id=1, source_target_pairs={{0,1},{1,0},{2,3},{3,2},{4,5},{5,4},{6,7},{7,6},{8,9},{9,8},{10,11... | collective-permute-start | bytes 442376 | tf_op jit(solution)/shard_map/ppermute | solution.py:325
  25.0 1.6 %collective-permute-start.14 = (bf16[320,256]{1,0:T(8,128)(2,1)S(1)}, bf16[320,256]{1,0:T(8,128)(2,1)S(1)}, u32[]{:S(2)}, u32[]{:S(2)}) collective-permute-start(bf16[320,256]{1,0:T(8,128)(2,1)S(1)} %collective-permute-done.10.refs_7_), channel_id=1, source_target_pairs={{0,1},{1,0},{2,3},{3,2},{4,5},{5,4},{6,7},{7,6},{8,9},{9,8},{10,11... | collective-permute-start | bytes 491528 | tf_op jit(solution)/shard_map/ppermute | solution.py:325
  25.0 1.6 %collective-permute-start.13 = (bf16[288,256]{1,0:T(8,128)(2,1)S(1)}, bf16[288,256]{1,0:T(8,128)(2,1)S(1)}, u32[]{:S(2)}, u32[]{:S(2)}) collective-permute-start(bf16[288,256]{1,0:T(8,128)(2,1)S(1)} %collective-permute-done.2.refs_6_), channel_id=1, source_target_pairs={{0,1},{1,0},{2,3},{3,2},{4,5},{5,4},{6,7},{7,6},{8,9},{9,8},{10,11... | collective-permute-start | bytes 442376 | tf_op jit(solution)/shard_map/ppermute | solution.py:325
  26.6 3.8 %collective-permute-start.9 = (bf16[288,256]{1,0:T(8,128)(2,1)S(1)}, bf16[288,256]{1,0:T(8,128)(2,1)S(1)}, u32[]{:S(2)}, u32[]{:S(2)}) collective-permute-start(bf16[288,256]{1,0:T(8,128)(2,1)S(1)} %collective-permute-done.3.refs_8_), channel_id=1, source_target_pairs={{0,1},{1,0},{2,3},{3,2},{4,5},{5,4},{6,7},{7,6},{8,9},{9,8},{10,11... | collective-permute-start | bytes 442376 | tf_op jit(solution)/shard_map/ppermute | solution.py:325

commit v19 on v18

--- a/solution.py
+++ b/solution.py
@@ -37,8 +37,12 @@
     first_offset_hbm,
     second_hbm,
     second_offset_hbm,
+    final_hbm,
+    final_offset_hbm,
     keep_ref,
     give_ref,
+    final_ref,
+    final_offset_ref,
     x_ref,
     gain_ref,
     shift_ref,
@@ -74,6 +78,12 @@
         rows = pl.ds(n * some, some)
         large.append(pltpu.make_async_copy(x_hbm.at[rows], x_ref.at[rows], sems.at[n]))
         large[-1].start()
+    later = [
+        pltpu.make_async_copy(final_hbm, final_ref, sems.at[CHUNKS + len(small)]),
+        pltpu.make_async_copy(final_offset_hbm, final_offset_ref, sems.at[CHUNKS + len(small) + 1]),
+    ]
+    for copy in later:
+        copy.start()
     for copy in copies:
         copy.wait()
 
@@ -121,6 +131,8 @@
         value = (right[t].T + second_offset).astype(jnp.bfloat16)
         keep_ref[t * width : (t + 1) * width, :] = value
         give_ref[t * width : (t + 1) * width, :] = value
+    for copy in later:
+        copy.wait()
     device = lax.axis_index("row")
     per_chip = 2 * rows_here * hidden * samples // tile
     half = residues // rows_here // 4
@@ -148,8 +160,7 @@
         next_ref[at + per_chip : at + 2 * per_chip, :] = theirs_ref[low : low + per_chip, :]
 
 
-def weight_kernel(final_ref, offset_ref, out_ref, mixing_out, offset_out, wide_ref):
-    offset_out[...] = offset_ref[...]
+def weight_kernel(final_ref, out_ref, mixing_out, wide_ref):
     channels, columns = out_ref.shape
     hidden = math.isqrt(columns)
     wide_ref[...] = final_ref[...].astype(jnp.float32)
@@ -225,27 +236,26 @@
     channels = out_ref.shape[2]
     right = ref[: hidden * here, :].astype(jnp.float32).T.astype(jnp.bfloat16)
     left = left_piece(ref, base, rows_here, hidden, here)
-    left = [left[:, i * hidden : (i + 1) * hidden] for i in range(rows_here)]
-    mixed = jnp.dot(
-        jnp.concatenate(left, axis=0).astype(jnp.bfloat16),
-        mixing_ref[...],
-        preferred_element_type=jnp.float32,
-    )
     copies = []
-    for i in range(0, rows_here, 2):
+    some = 4
+    for low in range(0, rows_here, some):
+        block = [left[:, i * hidden : (i + 1) * hidden] for i in range(low, low + some)]
+        mixed = jnp.dot(
+            jnp.concatenate(block, axis=0).astype(jnp.bfloat16),
+            mixing_ref[...],
+            preferred_element_type=jnp.float32,
+        )
         parts = []
-        for k in range(2):
-            part = mixed[(i + k) * here : (i + k + 1) * here]
+        for k in range(some):
+            part = mixed[k * here : (k + 1) * here]
             part = [part[:, e * channels : (e + 1) * channels] for e in range(hidden)]
             parts.append(jnp.concatenate(part, axis=0).astype(jnp.bfloat16))
-        value = jnp.dot(
-            right, jnp.concatenate(parts, axis=1), preferred_element_type=jnp.float32
-        )
-        for k in range(2):
-            part = value[:, k * channels : (k + 1) * channels] + total_ref[i + k]
-            out_ref[i + k] = (part * (1.0 / samples) + offset_ref[...]).astype(jnp.bfloat16)
-        rows = pl.ds(i, 2)
-        copies.append(pltpu.make_async_copy(out_ref.at[rows], out_hbm.at[rows], sems.at[i // 2]))
+        value = jnp.dot(right, jnp.concatenate(parts, axis=1), preferred_element_type=jnp.float32)
+        for k in range(some):
+            part = value[:, k * channels : (k + 1) * channels] + total_ref[low + k]
+            out_ref[low + k] = (part * (1.0 / samples) + offset_ref[...]).astype(jnp.bfloat16)
+        rows = pl.ds(low, some)
+        copies.append(pltpu.make_async_copy(out_ref.at[rows], out_hbm.at[rows], sems.at[low // some]))
         copies[-1].start()
     for copy in copies:
         copy.wait()
@@ -280,11 +290,15 @@
 
     vmem = pl.BlockSpec(memory_space=pltpu.VMEM)
     hbm = pl.BlockSpec(memory_space=pltpu.HBM)
-    keep, give = pl.pallas_call(
+    keep, give, final, offset = pl.pallas_call(
         functools.partial(project_kernel, rows_here),
-        out_shape=[rows(body + half * per_chip)] * 2,
-        in_specs=[hbm] * 7,
-        out_specs=[vmem] * 2,
+        out_shape=[rows(body + half * per_chip)] * 2
+        + [
+            jax.ShapeDtypeStruct(final_projector_coefficients.shape, jnp.bfloat16),
+            jax.ShapeDtypeStruct((1, channels), jnp.float32),
+        ],
+        in_specs=[hbm] * 9,
+        out_specs=[vmem] * 4,
         scratch_shapes=[
             pltpu.VMEM((here, residues, features), jnp.bfloat16),
             pltpu.VMEM((1, features), jnp.float32),
@@ -294,7 +308,7 @@
             pltpu.VMEM((hidden, features), jnp.bfloat16),
             pltpu.VMEM((1, hidden), jnp.float32),
             pltpu.VMEM((residues * width // LANES, LANES), jnp.float32),
-            pltpu.SemaphoreType.DMA((CHUNKS + 6,)),
+            pltpu.SemaphoreType.DMA((CHUNKS + 8,)),
         ],
         compiler_params=pltpu.CompilerParams(vmem_limit_bytes=32 * MIB),
         cost_estimate=pl.CostEstimate(
@@ -313,6 +327,8 @@
                 first_side_offset.reshape(1, hidden),
                 second_side_coefficients.T,
                 second_side_offset.reshape(1, hidden),
+                final_projector_coefficients,
+                final_projector_offset.reshape(1, channels),
             )
         ]
     )
@@ -324,20 +340,19 @@
     def swap(value):
         return lax.ppermute(value, "row", [(r, r ^ 1) for r in range(size)])
 
-    weight, mixing, offset = pl.pallas_call(
+    weight, mixing = pl.pallas_call(
         weight_kernel,
         out_shape=[
             jax.ShapeDtypeStruct((channels, hidden * hidden), jnp.bfloat16),
             jax.ShapeDtypeStruct((hidden, hidden * channels), jnp.bfloat16),
-            jax.ShapeDtypeStruct((1, channels), jnp.float32),
         ],
-        in_specs=[vmem] * 2,
-        out_specs=[vmem] * 3,
+        in_specs=[vmem],
+        out_specs=[vmem] * 2,
         scratch_shapes=[pltpu.VMEM((hidden * hidden, channels), jnp.float32)],
         compiler_params=pltpu.CompilerParams(vmem_limit_bytes=16 * MIB),
         cost_estimate=pl.CostEstimate(flops=2**28, bytes_accessed=2**20, transcendentals=0),
-    )(final_projector_coefficients, final_projector_offset.reshape(1, channels))
-    theirs, weight, mixing, offset = lax.optimization_barrier((swap(give), weight, mixing, offset))
+    )(final)
+    theirs, weight, mixing = lax.optimization_barrier((swap(give), weight, mixing))
     messages = [give, theirs]
     places = [(n, 0, n, body + (half - 1) * per_chip) for n in range(2)]
 
@@ -378,7 +393,7 @@
         messages += pair
 
     gridded = tiles > 1
-    final = jax.ShapeDtypeStruct((rows_here, residues, channels), jnp.bfloat16)
+    outcome = jax.ShapeDtypeStruct((rows_here, residues, channels), jnp.bfloat16)
     if gridded:
         operands, specs = [], []
         for n, right, m, left in places:
@@ -391,7 +406,7 @@
             pl.BlockSpec((channels, hidden * hidden), lambda t: (0, 0)),
             pl.BlockSpec((1, channels), lambda t: (0, 0)),
         ]
-        grid, result, out_spec = (tiles,), final, hbm
+        grid, result, out_spec = (tiles,), outcome, hbm
     else:
         places, operands = places[:-1], messages[:-1]
         specs = [vmem] * (len(operands) + 2)
@@ -416,12 +431,12 @@
         return total
     return pl.pallas_call(
         functools.partial(last_kernel, body, rows_here, hidden, here, samples),
-        out_shape=final,
+        out_shape=outcome,
         in_specs=[vmem] * 4,
         out_specs=hbm,
         scratch_shapes=[
             pltpu.VMEM((rows_here, tile, channels), jnp.bfloat16),
-            pltpu.SemaphoreType.DMA((rows_here // 2,)),
+            pltpu.SemaphoreType.DMA((rows_here // 4,)),
         ],
         compiler_params=pltpu.CompilerParams(vmem_limit_bytes=24 * MIB),
     )(messages[-1], total, mixing, offset)

time: 32.4 us -> 31.7 us (0.978)
  local copies, waits for them, and re-layouts: 1.64 us -> 0.04 us
  starting transfers between devices: 13.7 us -> 14.5 us
  Pallas kernels: 9.07 us -> 9.54 us
    unnamed x4 -> x0, local copies, waits for them, and re-layouts: 1.6 us -> none
    ppermute x7, starting transfers between devices: 12.7 us -> 13.5 us  [per_device(): landed = [lax.ppermute(x, 'row', around) for x in flying]]
  transfers between devices with their start and end apart: 15 -> 15, of which waited for: 4 -> 7; matrix products, arithmetic and copies ran while one was open for 0% -> 0% of each run, Pallas kernels for 13% -> 14%
where the time goes in v19:
time: 31.7 us; the launch traced here: 31.5 us
  starting transfers between devices  14.5 us (46%)
  Pallas kernels  9.54 us (30%)
  waiting for transfers between devices  7.3 us (23%)
    ppermute x7, starting transfers between devices, per_device(): landed = [lax.ppermute(x, 'row', around) for x in flying]  13.5 us
    ppermute x7, waiting for transfers between devices, per_device(): landed = [lax.ppermute(x, 'row', around) for x in flying]  7.28 us
    pallas_call x1, Pallas kernels, per_device(): pl.pallas_call(functools.partial(pair_kernel, places, gridded, rows_here,...  3.89 us
    pallas_call x1, Pallas kernels, per_device(): pl.pallas_call(functools.partial(project_kernel, rows_here), out_shape=[r...  3.24 us
    pallas_call x1, Pallas kernels, per_device(): pl.pallas_call(functools.partial(last_kernel, body, rows_here, hidden, he...  2 us
    ppermute x8, starting transfers between devices, swap(): return lax.ppermute(value, 'row', [(r, r ^ 1) for r in range(size)])  1.04 us
  transfers between devices with their start and end apart: 15, of which 7 were waited for; matrix products, arithmetic and copies ran while one was open for 0% of the time, Pallas kernels for 14%

profile of v19, /device:TPU:0, one launch (start us, length us, event | category | flops | bytes accessed | tf_op | source)
XLA Modules:
  0.0 31.5 jit_solution(18435268662004819217)
XLA Ops:
  0.0 3.2 %shard_map.91 = (bf16[384,256]{1,0:T(8,128)(2,1)S(1)}, bf16[384,256]{1,0:T(8,128)(2,1)S(1)}, bf16[1024,128]{1,0:T(8,128)(2,1)S(1)}, f32[1,128]{1,0:T(1,128)S(1)}) custom-call(bf16[8,256,256]{2,1,0:T(8,128)(2,1)} %x_hbm.1, f32[1,256]{1,0:T(1,128)} %bitcast.9, f32[1,256]{1,0:T(1,128)} %bitcast.10, bf16[32,256]{1,0:T(8,128)(2,1)} %bitcast.7, f32[1,32]{1,0:T(1,128)} %bitcast.11, ...), custom_call_target="tpu_custom_call" | custom-call | flops 536870912 | bytes 1048576 | tf_op jit(solution)/shard_map/pallas_call | solution.py:293
  3.2 0.5 %collective-permute-start.4 = (bf16[384,256]{1,0:T(8,128)(2,1)S(1)}, bf16[384,256]{1,0:T(8,128)(2,1)S(1)}, u32[]{:S(2)}, u32[]{:S(2)}) collective-permute-start(bf16[384,256]{1,0:T(8,128)(2,1)S(1)} %get-tuple-element.27.refs_0_), channel_id=1, source_target_pairs={{0,1},{1,0},{2,3},{3,2},{4,5},{5,4},{6,7},{7,6},{8,9},{9,8},{10,11... | collective-permute-start | bytes 589832 | tf_op jit(solution)/shard_map/ppermute | solution.py:341
  3.8 2.6 %collective-permute-start = (bf16[384,256]{1,0:T(8,128)(2,1)S(1)}, bf16[384,256]{1,0:T(8,128)(2,1)S(1)}, u32[]{:S(2)}, u32[]{:S(2)}) collective-permute-start(bf16[384,256]{1,0:T(8,128)(2,1)S(1)} %get-tuple-element.26), channel_id=1, source_target_pairs={{0,2},{1,5},{2,6},{3,1},{4,0},{5,9},{6,10},{7,3},{8,4},{9,13},{10,... | collective-permute-start | bytes 589832 | tf_op jit(solution)/shard_map/ppermute | solution.py:365
  6.3 0.4 %shard_map.92 = (bf16[128,1024]{1,0:T(8,128)(2,1)S(1)}, bf16[32,4096]{1,0:T(8,128)(2,1)S(1)}) custom-call(bf16[1024,128]{1,0:T(8,128)(2,1)S(1)} %get-tuple-element.28.final_ref), custom_call_target="tpu_custom_call" | custom-call | flops 268435456 | bytes 1048576 | tf_op jit(solution)/shard_map/pallas_call | solution.py:343
  6.8 1.6 %collective-permute-start.5 = (bf16[352,256]{1,0:T(8,128)(2,1)S(1)}, bf16[352,256]{1,0:T(8,128)(2,1)S(1)}, u32[]{:S(2)}, u32[]{:S(2)}) collective-permute-start(bf16[352,256]{1,0:T(8,128)(2,1)S(1)} %slice.10), channel_id=1, source_target_pairs={{0,2},{1,5},{2,6},{3,1},{4,0},{5,9},{6,10},{7,3},{8,4},{9,13},{10,... | collective-permute-start | bytes 540680 | tf_op jit(solution)/shard_map/ppermute | solution.py:365
  8.4 1.6 %collective-permute-done.mine_ref.refs_2_ = bf16[384,256]{1,0:T(8,128)(2,1)S(1)} collective-permute-done((bf16[384,256]{1,0:T(8,128)(2,1)S(1)}, bf16[384,256]{1,0:T(8,128)(2,1)S(1)}, u32[]{:S(2)}, u32[]{:S(2)}) %collective-permute-start) | collective-permute-done | bytes 196640 | tf_op jit(solution)/shard_map/ppermute | solution.py:365
  10.1 2.0 %collective-permute-start.1 = (bf16[288,256]{1,0:T(8,128)(2,1)S(1)}, bf16[288,256]{1,0:T(8,128)(2,1)S(1)}, u32[]{:S(2)}, u32[]{:S(2)}) collective-permute-start(bf16[288,256]{1,0:T(8,128)(2,1)S(1)} %slice.12), channel_id=1, source_target_pairs={{0,2},{1,5},{2,6},{3,1},{4,0},{5,9},{6,10},{7,3},{8,4},{9,13},{10,... | collective-permute-start | bytes 442376 | tf_op jit(solution)/shard_map/ppermute | solution.py:365
  12.1 0.3 collective-permute-done.5.theirs_ref.refs_3_
  12.4 1.7 %collective-permute-start.6 = (bf16[384,256]{1,0:T(8,128)(2,1)S(1)}, bf16[384,256]{1,0:T(8,128)(2,1)S(1)}, u32[]{:S(2)}, u32[]{:S(2)}) collective-permute-start(bf16[384,256]{1,0:T(8,128)(2,1)S(1)} %shard_map.93), channel_id=1, source_target_pairs={{0,2},{1,5},{2,6},{3,1},{4,0},{5,9},{6,10},{7,3},{8,4},{9,13},{10,... | collective-permute-start | bytes 589832 | tf_op jit(solution)/shard_map/ppermute | solution.py:365
  14.0 1.2 %collective-permute-done.1.refs_4_ = bf16[288,256]{1,0:T(8,128)(2,1)S(1)} collective-permute-done((bf16[288,256]{1,0:T(8,128)(2,1)S(1)}, bf16[288,256]{1,0:T(8,128)(2,1)S(1)}, u32[]{:S(2)}, u32[]{:S(2)}) %collective-permute-start.1) | collective-permute-done | bytes 147488 | tf_op jit(solution)/shard_map/ppermute | solution.py:365
  15.3 2.0 %collective-permute-start.2 = (bf16[288,256]{1,0:T(8,128)(2,1)S(1)}, bf16[288,256]{1,0:T(8,128)(2,1)S(1)}, u32[]{:S(2)}, u32[]{:S(2)}) collective-permute-start(bf16[288,256]{1,0:T(8,128)(2,1)S(1)} %collective-permute-done.1.refs_4_), channel_id=1, source_target_pairs={{0,2},{1,5},{2,6},{3,1},{4,0},{5,9},{6,10},{7,3},{8,4},{9,13},{10,... | collective-permute-start | bytes 442376 | tf_op jit(solution)/shard_map/ppermute | solution.py:365
  17.2 0.0 collective-permute-start.11
  17.2 0.9 %collective-permute-done.6.refs_5_ = bf16[384,256]{1,0:T(8,128)(2,1)S(1)} collective-permute-done((bf16[384,256]{1,0:T(8,128)(2,1)S(1)}, bf16[384,256]{1,0:T(8,128)(2,1)S(1)}, u32[]{:S(2)}, u32[]{:S(2)}) %collective-permute-start.6) | collective-permute-done | bytes 196640 | tf_op jit(solution)/shard_map/ppermute | solution.py:365
  18.1 0.0 collective-permute-start.8
  18.1 1.7 %collective-permute-start.10 = (bf16[320,256]{1,0:T(8,128)(2,1)S(1)}, bf16[320,256]{1,0:T(8,128)(2,1)S(1)}, u32[]{:S(2)}, u32[]{:S(2)}) collective-permute-start(bf16[320,256]{1,0:T(8,128)(2,1)S(1)} %slice.13), channel_id=1, source_target_pairs={{0,2},{1,5},{2,6},{3,1},{4,0},{5,9},{6,10},{7,3},{8,4},{9,13},{10,... | collective-permute-start | bytes 491528 | tf_op jit(solution)/shard_map/ppermute | solution.py:365
  19.8 0.6 %collective-permute-done.2.refs_6_ = bf16[288,256]{1,0:T(8,128)(2,1)S(1)} collective-permute-done((bf16[288,256]{1,0:T(8,128)(2,1)S(1)}, bf16[288,256]{1,0:T(8,128)(2,1)S(1)}, u32[]{:S(2)}, u32[]{:S(2)}) %collective-permute-start.2) | collective-permute-done | bytes 147488 | tf_op jit(solution)/shard_map/ppermute | solution.py:365
  20.4 2.0 %collective-permute-start.3 = (bf16[288,256]{1,0:T(8,128)(2,1)S(1)}, bf16[288,256]{1,0:T(8,128)(2,1)S(1)}, u32[]{:S(2)}, u32[]{:S(2)}) collective-permute-start(bf16[288,256]{1,0:T(8,128)(2,1)S(1)} %collective-permute-done.2.refs_6_), channel_id=1, source_target_pairs={{0,2},{1,5},{2,6},{3,1},{4,0},{5,9},{6,10},{7,3},{8,4},{9,13},{10,... | collective-permute-start | bytes 442376 | tf_op jit(solution)/shard_map/ppermute | solution.py:365
  22.4 0.0 collective-permute-done.11.refs_9_
  22.4 1.1 %collective-permute-done.10.refs_7_ = bf16[320,256]{1,0:T(8,128)(2,1)S(1)} collective-permute-done((bf16[320,256]{1,0:T(8,128)(2,1)S(1)}, bf16[320,256]{1,0:T(8,128)(2,1)S(1)}, u32[]{:S(2)}, u32[]{:S(2)}) %collective-permute-start.10) | collective-permute-done | bytes 163872 | tf_op jit(solution)/shard_map/ppermute | solution.py:365
  23.5 0.5 %collective-permute-start.13 = (bf16[288,256]{1,0:T(8,128)(2,1)S(1)}, bf16[288,256]{1,0:T(8,128)(2,1)S(1)}, u32[]{:S(2)}, u32[]{:S(2)}) collective-permute-start(bf16[288,256]{1,0:T(8,128)(2,1)S(1)} %collective-permute-done.2.refs_6_), channel_id=1, source_target_pairs={{0,1},{1,0},{2,3},{3,2},{4,5},{5,4},{6,7},{7,6},{8,9},{9,8},{10,11... | collective-permute-start | bytes 442376 | tf_op jit(solution)/shard_map/ppermute | solution.py:341
  24.0 1.6 %collective-permute-done.3.refs_8_ = bf16[288,256]{1,0:T(8,128)(2,1)S(1)} collective-permute-done((bf16[288,256]{1,0:T(8,128)(2,1)S(1)}, bf16[288,256]{1,0:T(8,128)(2,1)S(1)}, u32[]{:S(2)}, u32[]{:S(2)}) %collective-permute-start.3) | collective-permute-done | bytes 147488 | tf_op jit(solution)/shard_map/ppermute | solution.py:365
  25.6 0.0 collective-permute-done.13.refs_13_
  25.6 3.9 %shard_map.94.total_ref = f32[16,256,128]{2,1,0:T(8,128)S(1)} custom-call(bf16[384,256]{1,0:T(8,128)(2,1)S(1)} %get-tuple-element.27.refs_0_, bf16[384,256]{1,0:T(8,128)(2,1)S(1)} %collective-permute-done.4.refs_1_, bf16[384,256]{1,0:T(8,128)(2,1)S(1)} %collective-permute-done.mine_ref.refs_2_, ...), custom_call_target="tpu_custom_call" | custom-call | tf_op jit(solution)/shard_map/pallas_call | solution.py:416
  29.5 2.0 %shard_map.95 = bf16[16,256,128]{2,1,0:T(8,128)(2,1)} custom-call(bf16[288,256]{1,0:T(8,128)(2,1)S(1)} %collective-permute-done.9.ref, f32[16,256,128]{2,1,0:T(8,128)S(1)} %shard_map.94.total_ref, bf16[32,4096]{1,0:T(8,128)(2,1)S(1)} %get-tuple-element.46.mixing_ref, f32[1,128]{1,0:T(1,128)S(1)} %get-tuple-element.45.refs_16_.offset_ref), custom_call_target="tpu_custom_call" | custom-call | tf_op jit(solution)/shard_map/pallas_call | solution.py:432
  (14 shorter events, 0.1 us)
Async XLA Ops:
  3.2 3.5 %collective-permute-start.4 = (bf16[384,256]{1,0:T(8,128)(2,1)S(1)}, bf16[384,256]{1,0:T(8,128)(2,1)S(1)}, u32[]{:S(2)}, u32[]{:S(2)}) collective-permute-start(bf16[384,256]{1,0:T(8,128)(2,1)S(1)} %get-tuple-element.27.refs_0_), channel_id=1, source_target_pairs={{0,1},{1,0},{2,3},{3,2},{4,5},{5,4},{6,7},{7,6},{8,9},{9,8},{10,11... | collective-permute-start | bytes 589832 | tf_op jit(solution)/shard_map/ppermute | solution.py:341
  3.8 6.3 %collective-permute-start = (bf16[384,256]{1,0:T(8,128)(2,1)S(1)}, bf16[384,256]{1,0:T(8,128)(2,1)S(1)}, u32[]{:S(2)}, u32[]{:S(2)}) collective-permute-start(bf16[384,256]{1,0:T(8,128)(2,1)S(1)} %get-tuple-element.26), channel_id=1, source_target_pairs={{0,2},{1,5},{2,6},{3,1},{4,0},{5,9},{6,10},{7,3},{8,4},{9,13},{10,... | collective-permute-start | bytes 589832 | tf_op jit(solution)/shard_map/ppermute | solution.py:365
  6.8 5.5 %collective-permute-start.5 = (bf16[352,256]{1,0:T(8,128)(2,1)S(1)}, bf16[352,256]{1,0:T(8,128)(2,1)S(1)}, u32[]{:S(2)}, u32[]{:S(2)}) collective-permute-start(bf16[352,256]{1,0:T(8,128)(2,1)S(1)} %slice.10), channel_id=1, source_target_pairs={{0,2},{1,5},{2,6},{3,1},{4,0},{5,9},{6,10},{7,3},{8,4},{9,13},{10,... | collective-permute-start | bytes 540680 | tf_op jit(solution)/shard_map/ppermute | solution.py:365
  10.1 5.2 %collective-permute-start.1 = (bf16[288,256]{1,0:T(8,128)(2,1)S(1)}, bf16[288,256]{1,0:T(8,128)(2,1)S(1)}, u32[]{:S(2)}, u32[]{:S(2)}) collective-permute-start(bf16[288,256]{1,0:T(8,128)(2,1)S(1)} %slice.12), channel_id=1, source_target_pairs={{0,2},{1,5},{2,6},{3,1},{4,0},{5,9},{6,10},{7,3},{8,4},{9,13},{10,... | collective-permute-start | bytes 442376 | tf_op jit(solution)/shard_map/ppermute | solution.py:365
  12.4 5.7 %collective-permute-start.6 = (bf16[384,256]{1,0:T(8,128)(2,1)S(1)}, bf16[384,256]{1,0:T(8,128)(2,1)S(1)}, u32[]{:S(2)}, u32[]{:S(2)}) collective-permute-start(bf16[384,256]{1,0:T(8,128)(2,1)S(1)} %shard_map.93), channel_id=1, source_target_pairs={{0,2},{1,5},{2,6},{3,1},{4,0},{5,9},{6,10},{7,3},{8,4},{9,13},{10,... | collective-permute-start | bytes 589832 | tf_op jit(solution)/shard_map/ppermute | solution.py:365
  14.0 8.4 %collective-permute-start.12 = (bf16[352,256]{1,0:T(8,128)(2,1)S(1)}, bf16[352,256]{1,0:T(8,128)(2,1)S(1)}, u32[]{:S(2)}, u32[]{:S(2)}) collective-permute-start(bf16[352,256]{1,0:T(8,128)(2,1)S(1)} %collective-permute-done.5.theirs_ref.refs_3_), channel_id=1, source_target_pairs={{0,1},{1,0},{2,3},{3,2},{4,5},{5,4},{6,7},{7,6},{8,9},{9,8},{10,11... | collective-permute-start | bytes 540680 | tf_op jit(solution)/shard_map/ppermute | solution.py:341
  15.3 5.1 %collective-permute-start.2 = (bf16[288,256]{1,0:T(8,128)(2,1)S(1)}, bf16[288,256]{1,0:T(8,128)(2,1)S(1)}, u32[]{:S(2)}, u32[]{:S(2)}) collective-permute-start(bf16[288,256]{1,0:T(8,128)(2,1)S(1)} %collective-permute-done.1.refs_4_), channel_id=1, source_target_pairs={{0,2},{1,5},{2,6},{3,1},{4,0},{5,9},{6,10},{7,3},{8,4},{9,13},{10,... | collective-permute-start | bytes 442376 | tf_op jit(solution)/shard_map/ppermute | solution.py:365
  17.2 5.2 %collective-permute-start.11 = (bf16[384,256]{1,0:T(8,128)(2,1)S(1)}, bf16[384,256]{1,0:T(8,128)(2,1)S(1)}, u32[]{:S(2)}, u32[]{:S(2)}) collective-permute-start(bf16[384,256]{1,0:T(8,128)(2,1)S(1)} %collective-permute-done.mine_ref.refs_2_), channel_id=1, source_target_pairs={{0,1},{1,0},{2,3},{3,2},{4,5},{5,4},{6,7},{7,6},{8,9},{9,8},{10,11... | collective-permute-start | bytes 589832 | tf_op jit(solution)/shard_map/ppermute | solution.py:341
  18.1 7.5 %collective-permute-start.8 = (bf16[384,256]{1,0:T(8,128)(2,1)S(1)}, bf16[384,256]{1,0:T(8,128)(2,1)S(1)}, u32[]{:S(2)}, u32[]{:S(2)}) collective-permute-start(bf16[384,256]{1,0:T(8,128)(2,1)S(1)} %collective-permute-done.6.refs_5_), channel_id=1, source_target_pairs={{0,1},{1,0},{2,3},{3,2},{4,5},{5,4},{6,7},{7,6},{8,9},{9,8},{10,11... | collective-permute-start | bytes 589832 | tf_op jit(solution)/shard_map/ppermute | solution.py:341
  18.1 5.4 %collective-permute-start.10 = (bf16[320,256]{1,0:T(8,128)(2,1)S(1)}, bf16[320,256]{1,0:T(8,128)(2,1)S(1)}, u32[]{:S(2)}, u32[]{:S(2)}) collective-permute-start(bf16[320,256]{1,0:T(8,128)(2,1)S(1)} %slice.13), channel_id=1, source_target_pairs={{0,2},{1,5},{2,6},{3,1},{4,0},{5,9},{6,10},{7,3},{8,4},{9,13},{10,... | collective-permute-start | bytes 491528 | tf_op jit(solution)/shard_map/ppermute | solution.py:365
  20.4 5.1 %collective-permute-start.3 = (bf16[288,256]{1,0:T(8,128)(2,1)S(1)}, bf16[288,256]{1,0:T(8,128)(2,1)S(1)}, u32[]{:S(2)}, u32[]{:S(2)}) collective-permute-start(bf16[288,256]{1,0:T(8,128)(2,1)S(1)} %collective-permute-done.2.refs_6_), channel_id=1, source_target_pairs={{0,2},{1,5},{2,6},{3,1},{4,0},{5,9},{6,10},{7,3},{8,4},{9,13},{10,... | collective-permute-start | bytes 442376 | tf_op jit(solution)/shard_map/ppermute | solution.py:365
  22.4 3.2 %collective-permute-start.7 = (bf16[288,256]{1,0:T(8,128)(2,1)S(1)}, bf16[288,256]{1,0:T(8,128)(2,1)S(1)}, u32[]{:S(2)}, u32[]{:S(2)}) collective-permute-start(bf16[288,256]{1,0:T(8,128)(2,1)S(1)} %collective-permute-done.1.refs_4_), channel_id=1, source_target_pairs={{0,1},{1,0},{2,3},{3,2},{4,5},{5,4},{6,7},{7,6},{8,9},{9,8},{10,11... | collective-permute-start | bytes 442376 | tf_op jit(solution)/shard_map/ppermute | solution.py:341
  23.5 2.1 %collective-permute-start.14 = (bf16[320,256]{1,0:T(8,128)(2,1)S(1)}, bf16[320,256]{1,0:T(8,128)(2,1)S(1)}, u32[]{:S(2)}, u32[]{:S(2)}) collective-permute-start(bf16[320,256]{1,0:T(8,128)(2,1)S(1)} %collective-permute-done.10.refs_7_), channel_id=1, source_target_pairs={{0,1},{1,0},{2,3},{3,2},{4,5},{5,4},{6,7},{7,6},{8,9},{9,8},{10,11... | collective-permute-start | bytes 491528 | tf_op jit(solution)/shard_map/ppermute | solution.py:341
  23.5 2.1 %collective-permute-start.13 = (bf16[288,256]{1,0:T(8,128)(2,1)S(1)}, bf16[288,256]{1,0:T(8,128)(2,1)S(1)}, u32[]{:S(2)}, u32[]{:S(2)}) collective-permute-start(bf16[288,256]{1,0:T(8,128)(2,1)S(1)} %collective-permute-done.2.refs_6_), channel_id=1, source_target_pairs={{0,1},{1,0},{2,3},{3,2},{4,5},{5,4},{6,7},{7,6},{8,9},{9,8},{10,11... | collective-permute-start | bytes 442376 | tf_op jit(solution)/shard_map/ppermute | solution.py:341
  25.6 3.9 %collective-permute-start.9 = (bf16[288,256]{1,0:T(8,128)(2,1)S(1)}, bf16[288,256]{1,0:T(8,128)(2,1)S(1)}, u32[]{:S(2)}, u32[]{:S(2)}) collective-permute-start(bf16[288,256]{1,0:T(8,128)(2,1)S(1)} %collective-permute-done.3.refs_8_), channel_id=1, source_target_pairs={{0,1},{1,0},{2,3},{3,2},{4,5},{5,4},{6,7},{7,6},{8,9},{9,8},{10,11... | collective-permute-start | bytes 442376 | tf_op jit(solution)/shard_map/ppermute | solution.py:341

commit v20 on v15

--- a/solution.py
+++ b/solution.py
@@ -37,8 +37,12 @@
     first_offset_hbm,
     second_hbm,
     second_offset_hbm,
+    final_hbm,
+    final_offset_hbm,
     keep_ref,
     give_ref,
+    final_ref,
+    final_offset_ref,
     x_ref,
     gain_ref,
     shift_ref,
@@ -74,6 +78,12 @@
         rows = pl.ds(n * some, some)
         large.append(pltpu.make_async_copy(x_hbm.at[rows], x_ref.at[rows], sems.at[n]))
         large[-1].start()
+    later = [
+        pltpu.make_async_copy(final_hbm, final_ref, sems.at[CHUNKS + len(small)]),
+        pltpu.make_async_copy(final_offset_hbm, final_offset_ref, sems.at[CHUNKS + len(small) + 1]),
+    ]
+    for copy in later:
+        copy.start()
     for copy in copies:
         copy.wait()
 
@@ -121,6 +131,8 @@
         value = (right[t].T + second_offset).astype(jnp.bfloat16)
         keep_ref[t * width : (t + 1) * width, :] = value
         give_ref[t * width : (t + 1) * width, :] = value
+    for copy in later:
+        copy.wait()
     device = lax.axis_index("row")
     per_chip = 2 * rows_here * hidden * samples // tile
     half = residues // rows_here // 4
@@ -148,8 +160,7 @@
         next_ref[at + per_chip : at + 2 * per_chip, :] = theirs_ref[low : low + per_chip, :]
 
 
-def weight_kernel(final_ref, offset_ref, out_ref, offset_out, wide_ref):
-    offset_out[...] = offset_ref[...]
+def weight_kernel(final_ref, out_ref, wide_ref):
     channels, columns = out_ref.shape
     hidden = math.isqrt(columns)
     wide_ref[...] = final_ref[...].astype(jnp.float32)
@@ -242,11 +253,15 @@
 
     vmem = pl.BlockSpec(memory_space=pltpu.VMEM)
     hbm = pl.BlockSpec(memory_space=pltpu.HBM)
-    keep, give = pl.pallas_call(
+    keep, give, final, offset = pl.pallas_call(
         functools.partial(project_kernel, rows_here),
-        out_shape=[rows(body + half * per_chip)] * 2,
-        in_specs=[hbm] * 7,
-        out_specs=[vmem] * 2,
+        out_shape=[rows(body + half * per_chip)] * 2
+        + [
+            jax.ShapeDtypeStruct(final_projector_coefficients.shape, jnp.bfloat16),
+            jax.ShapeDtypeStruct((1, channels), jnp.float32),
+        ],
+        in_specs=[hbm] * 9,
+        out_specs=[vmem] * 4,
         scratch_shapes=[
             pltpu.VMEM((here, residues, features), jnp.bfloat16),
             pltpu.VMEM((1, features), jnp.float32),
@@ -256,7 +271,7 @@
             pltpu.VMEM((hidden, features), jnp.bfloat16),
             pltpu.VMEM((1, hidden), jnp.float32),
             pltpu.VMEM((residues * width // LANES, LANES), jnp.float32),
-            pltpu.SemaphoreType.DMA((CHUNKS + 6,)),
+            pltpu.SemaphoreType.DMA((CHUNKS + 8,)),
         ],
         compiler_params=pltpu.CompilerParams(vmem_limit_bytes=32 * MIB),
         cost_estimate=pl.CostEstimate(
@@ -275,6 +290,8 @@
                 first_side_offset.reshape(1, hidden),
                 second_side_coefficients.T,
                 second_side_offset.reshape(1, hidden),
+                final_projector_coefficients,
+                final_projector_offset.reshape(1, channels),
             )
         ]
     )
@@ -286,19 +303,16 @@
     def swap(value):
         return lax.ppermute(value, "row", [(r, r ^ 1) for r in range(size)])
 
-    weight, offset = pl.pallas_call(
+    weight = pl.pallas_call(
         weight_kernel,
-        out_shape=[
-            jax.ShapeDtypeStruct((channels, hidden * hidden), jnp.bfloat16),
-            jax.ShapeDtypeStruct((1, channels), jnp.float32),
-        ],
-        in_specs=[vmem] * 2,
-        out_specs=[vmem] * 2,
+        out_shape=jax.ShapeDtypeStruct((channels, hidden * hidden), jnp.bfloat16),
+        in_specs=[vmem],
+        out_specs=vmem,
         scratch_shapes=[pltpu.VMEM((hidden * hidden, channels), jnp.float32)],
         compiler_params=pltpu.CompilerParams(vmem_limit_bytes=16 * MIB),
         cost_estimate=pl.CostEstimate(flops=2**28, bytes_accessed=2**20, transcendentals=0),
-    )(final_projector_coefficients, final_projector_offset.reshape(1, channels))
-    theirs, weight, offset = lax.optimization_barrier((swap(give), weight, offset))
+    )(final)
+    theirs, weight = lax.optimization_barrier((swap(give), weight))
     messages = [give, theirs]
     places = [(n, 0, n, body + (half - 1) * per_chip) for n in range(2)]
 

time: 31.5 us -> 31.7 us (level)
  no operation moved by 1% of the time
where the time goes in v20:
time: 31.7 us; the launch traced here: 31.5 us
  starting transfers between devices  14.5 us (46%)
  waiting for transfers between devices  8.63 us (27%)
  Pallas kernels  8.22 us (26%)
    ppermute x7, starting transfers between devices, per_device(): landed = [lax.ppermute(x, 'row', around) for x in flying]  13.5 us
    ppermute x7, waiting for transfers between devices, per_device(): landed = [lax.ppermute(x, 'row', around) for x in flying]  7.27 us
    pallas_call x1, Pallas kernels, per_device(): pl.pallas_call(functools.partial(pair_kernel, places, gridded, rows_here,...  4.57 us
    pallas_call x1, Pallas kernels, per_device(): pl.pallas_call(functools.partial(project_kernel, rows_here), out_shape=[r...  3.24 us
    ppermute x8, waiting for transfers between devices, swap(): return lax.ppermute(value, 'row', [(r, r ^ 1) for r in range(size)])  1.36 us
    ppermute x8, starting transfers between devices, swap(): return lax.ppermute(value, 'row', [(r, r ^ 1) for r in range(size)])  1.04 us
  transfers between devices with their start and end apart: 15, of which 8 were waited for; matrix products, arithmetic and copies ran while one was open for 0% of the time, Pallas kernels for 1%

profile of v20, /device:TPU:0, one launch (start us, length us, event | category | flops | bytes accessed | tf_op | source)
XLA Modules:
  0.0 31.5 jit_solution(8886698280379993678)
XLA Ops:
  0.0 3.2 %shard_map.91 = (bf16[384,256]{1,0:T(8,128)(2,1)S(1)}, bf16[384,256]{1,0:T(8,128)(2,1)S(1)}, bf16[1024,128]{1,0:T(8,128)(2,1)S(1)}, f32[1,128]{1,0:T(1,128)S(1)}) custom-call(bf16[8,256,256]{2,1,0:T(8,128)(2,1)} %x_hbm.1, f32[1,256]{1,0:T(1,128)} %bitcast.9, f32[1,256]{1,0:T(1,128)} %bitcast.10, bf16[32,256]{1,0:T(8,128)(2,1)} %bitcast.7, f32[1,32]{1,0:T(1,128)} %bitcast.11, ...), custom_call_target="tpu_custom_call" | custom-call | flops 536870912 | bytes 1048576 | tf_op jit(solution)/shard_map/pallas_call | solution.py:256
  3.2 0.5 %collective-permute-start = (bf16[384,256]{1,0:T(8,128)(2,1)S(1)}, bf16[384,256]{1,0:T(8,128)(2,1)S(1)}, u32[]{:S(2)}, u32[]{:S(2)}) collective-permute-start(bf16[384,256]{1,0:T(8,128)(2,1)S(1)} %get-tuple-element.23.refs_0_), channel_id=1, source_target_pairs={{0,1},{1,0},{2,3},{3,2},{4,5},{5,4},{6,7},{7,6},{8,9},{9,8},{10,11... | collective-permute-start | bytes 589832 | tf_op jit(solution)/shard_map/ppermute | solution.py:304
  3.8 2.6 %collective-permute-start.1 = (bf16[384,256]{1,0:T(8,128)(2,1)S(1)}, bf16[384,256]{1,0:T(8,128)(2,1)S(1)}, u32[]{:S(2)}, u32[]{:S(2)}) collective-permute-start(bf16[384,256]{1,0:T(8,128)(2,1)S(1)} %get-tuple-element.26), channel_id=1, source_target_pairs={{0,2},{1,5},{2,6},{3,1},{4,0},{5,9},{6,10},{7,3},{8,4},{9,13},{10,... | collective-permute-start | bytes 589832 | tf_op jit(solution)/shard_map/ppermute | solution.py:325
  6.3 0.4 %shard_map.92.refs_16_ = bf16[128,1024]{1,0:T(8,128)(2,1)S(1)} custom-call(bf16[1024,128]{1,0:T(8,128)(2,1)S(1)} %get-tuple-element.24.final_ref), custom_call_target="tpu_custom_call" | custom-call | flops 268435456 | bytes 1048576 | tf_op jit(solution)/shard_map/pallas_call | solution.py:306
  6.7 0.0 collective-permute-done.refs_1_
  6.8 1.6 %collective-permute-start.2 = (bf16[352,256]{1,0:T(8,128)(2,1)S(1)}, bf16[352,256]{1,0:T(8,128)(2,1)S(1)}, u32[]{:S(2)}, u32[]{:S(2)}) collective-permute-start(bf16[352,256]{1,0:T(8,128)(2,1)S(1)} %slice.9), channel_id=1, source_target_pairs={{0,2},{1,5},{2,6},{3,1},{4,0},{5,9},{6,10},{7,3},{8,4},{9,13},{10,... | collective-permute-start | bytes 540680 | tf_op jit(solution)/shard_map/ppermute | solution.py:325
  8.4 1.6 %collective-permute-done.1.mine_ref.refs_2_ = bf16[384,256]{1,0:T(8,128)(2,1)S(1)} collective-permute-done((bf16[384,256]{1,0:T(8,128)(2,1)S(1)}, bf16[384,256]{1,0:T(8,128)(2,1)S(1)}, u32[]{:S(2)}, u32[]{:S(2)}) %collective-permute-start.1) | collective-permute-done | bytes 196640 | tf_op jit(solution)/shard_map/ppermute | solution.py:325
  10.1 2.0 %collective-permute-start.3 = (bf16[288,256]{1,0:T(8,128)(2,1)S(1)}, bf16[288,256]{1,0:T(8,128)(2,1)S(1)}, u32[]{:S(2)}, u32[]{:S(2)}) collective-permute-start(bf16[288,256]{1,0:T(8,128)(2,1)S(1)} %slice.12), channel_id=1, source_target_pairs={{0,2},{1,5},{2,6},{3,1},{4,0},{5,9},{6,10},{7,3},{8,4},{9,13},{10,... | collective-permute-start | bytes 442376 | tf_op jit(solution)/shard_map/ppermute | solution.py:325
  12.1 0.2 collective-permute-done.2.theirs_ref.refs_3_
  12.3 1.7 %collective-permute-start.4 = (bf16[384,256]{1,0:T(8,128)(2,1)S(1)}, bf16[384,256]{1,0:T(8,128)(2,1)S(1)}, u32[]{:S(2)}, u32[]{:S(2)}) collective-permute-start(bf16[384,256]{1,0:T(8,128)(2,1)S(1)} %shard_map.93), channel_id=1, source_target_pairs={{0,2},{1,5},{2,6},{3,1},{4,0},{5,9},{6,10},{7,3},{8,4},{9,13},{10,... | collective-permute-start | bytes 589832 | tf_op jit(solution)/shard_map/ppermute | solution.py:325
  14.0 0.0 collective-permute-start.8
  14.0 1.2 %collective-permute-done.3.refs_4_ = bf16[288,256]{1,0:T(8,128)(2,1)S(1)} collective-permute-done((bf16[288,256]{1,0:T(8,128)(2,1)S(1)}, bf16[288,256]{1,0:T(8,128)(2,1)S(1)}, u32[]{:S(2)}, u32[]{:S(2)}) %collective-permute-start.3) | collective-permute-done | bytes 147488 | tf_op jit(solution)/shard_map/ppermute | solution.py:325
  15.3 2.0 %collective-permute-start.5 = (bf16[288,256]{1,0:T(8,128)(2,1)S(1)}, bf16[288,256]{1,0:T(8,128)(2,1)S(1)}, u32[]{:S(2)}, u32[]{:S(2)}) collective-permute-start(bf16[288,256]{1,0:T(8,128)(2,1)S(1)} %collective-permute-done.3.refs_4_), channel_id=1, source_target_pairs={{0,2},{1,5},{2,6},{3,1},{4,0},{5,9},{6,10},{7,3},{8,4},{9,13},{10,... | collective-permute-start | bytes 442376 | tf_op jit(solution)/shard_map/ppermute | solution.py:325
  17.2 0.8 %collective-permute-done.4.refs_5_ = bf16[384,256]{1,0:T(8,128)(2,1)S(1)} collective-permute-done((bf16[384,256]{1,0:T(8,128)(2,1)S(1)}, bf16[384,256]{1,0:T(8,128)(2,1)S(1)}, u32[]{:S(2)}, u32[]{:S(2)}) %collective-permute-start.4) | collective-permute-done | bytes 196640 | tf_op jit(solution)/shard_map/ppermute | solution.py:325
  18.1 1.7 %collective-permute-start.6 = (bf16[320,256]{1,0:T(8,128)(2,1)S(1)}, bf16[320,256]{1,0:T(8,128)(2,1)S(1)}, u32[]{:S(2)}, u32[]{:S(2)}) collective-permute-start(bf16[320,256]{1,0:T(8,128)(2,1)S(1)} %slice.13), channel_id=1, source_target_pairs={{0,2},{1,5},{2,6},{3,1},{4,0},{5,9},{6,10},{7,3},{8,4},{9,13},{10,... | collective-permute-start | bytes 491528 | tf_op jit(solution)/shard_map/ppermute | solution.py:325
  19.8 0.6 %collective-permute-done.5.refs_6_ = bf16[288,256]{1,0:T(8,128)(2,1)S(1)} collective-permute-done((bf16[288,256]{1,0:T(8,128)(2,1)S(1)}, bf16[288,256]{1,0:T(8,128)(2,1)S(1)}, u32[]{:S(2)}, u32[]{:S(2)}) %collective-permute-start.5) | collective-permute-done | bytes 147488 | tf_op jit(solution)/shard_map/ppermute | solution.py:325
  20.4 2.0 %collective-permute-start.9 = (bf16[288,256]{1,0:T(8,128)(2,1)S(1)}, bf16[288,256]{1,0:T(8,128)(2,1)S(1)}, u32[]{:S(2)}, u32[]{:S(2)}) collective-permute-start(bf16[288,256]{1,0:T(8,128)(2,1)S(1)} %collective-permute-done.5.refs_6_), channel_id=1, source_target_pairs={{0,2},{1,5},{2,6},{3,1},{4,0},{5,9},{6,10},{7,3},{8,4},{9,13},{10,... | collective-permute-start | bytes 442376 | tf_op jit(solution)/shard_map/ppermute | solution.py:325
  22.4 1.1 %collective-permute-done.6.refs_7_ = bf16[320,256]{1,0:T(8,128)(2,1)S(1)} collective-permute-done((bf16[320,256]{1,0:T(8,128)(2,1)S(1)}, bf16[320,256]{1,0:T(8,128)(2,1)S(1)}, u32[]{:S(2)}, u32[]{:S(2)}) %collective-permute-start.6) | collective-permute-done | bytes 163872 | tf_op jit(solution)/shard_map/ppermute | solution.py:325
  23.5 0.0 collective-permute-start.13
  23.5 0.5 %collective-permute-start.12 = (bf16[288,256]{1,0:T(8,128)(2,1)S(1)}, bf16[288,256]{1,0:T(8,128)(2,1)S(1)}, u32[]{:S(2)}, u32[]{:S(2)}) collective-permute-start(bf16[288,256]{1,0:T(8,128)(2,1)S(1)} %collective-permute-done.5.refs_6_), channel_id=1, source_target_pairs={{0,1},{1,0},{2,3},{3,2},{4,5},{5,4},{6,7},{7,6},{8,9},{9,8},{10,11... | collective-permute-start | bytes 442376 | tf_op jit(solution)/shard_map/ppermute | solution.py:304
  24.0 1.6 %collective-permute-done.9.refs_8_ = bf16[288,256]{1,0:T(8,128)(2,1)S(1)} collective-permute-done((bf16[288,256]{1,0:T(8,128)(2,1)S(1)}, bf16[288,256]{1,0:T(8,128)(2,1)S(1)}, u32[]{:S(2)}, u32[]{:S(2)}) %collective-permute-start.9) | collective-permute-done | bytes 147488 | tf_op jit(solution)/shard_map/ppermute | solution.py:325
  25.6 0.0 collective-permute-done.12.refs_13_
  25.6 1.3 %collective-permute-done.14.refs_15_ = bf16[288,256]{1,0:T(8,128)(2,1)S(1)} collective-permute-done((bf16[288,256]{1,0:T(8,128)(2,1)S(1)}, bf16[288,256]{1,0:T(8,128)(2,1)S(1)}, u32[]{:S(2)}, u32[]{:S(2)}) %collective-permute-start.14) | collective-permute-done | bytes 147488 | tf_op jit(solution)/shard_map/ppermute | solution.py:304
  26.9 4.6 %shard_map.94 = bf16[16,256,128]{2,1,0:T(8,128)(2,1)} custom-call(bf16[384,256]{1,0:T(8,128)(2,1)S(1)} %get-tuple-element.23.refs_0_, bf16[384,256]{1,0:T(8,128)(2,1)S(1)} %collective-permute-done.refs_1_, bf16[384,256]{1,0:T(8,128)(2,1)S(1)} %collective-permute-done.1.mine_ref.refs_2_, bf16[352,256]{1,0:T(8,128)(2,1)S(1)} %collective-permute-done.2.theirs_ref.refs_3_, ...), custom_call_target="tpu_custom_call" | custom-call | tf_op jit(solution)/shard_map/pallas_call | solution.py:373
  (13 shorter events, 0.1 us)
Async XLA Ops:
  3.2 3.5 %collective-permute-start = (bf16[384,256]{1,0:T(8,128)(2,1)S(1)}, bf16[384,256]{1,0:T(8,128)(2,1)S(1)}, u32[]{:S(2)}, u32[]{:S(2)}) collective-permute-start(bf16[384,256]{1,0:T(8,128)(2,1)S(1)} %get-tuple-element.23.refs_0_), channel_id=1, source_target_pairs={{0,1},{1,0},{2,3},{3,2},{4,5},{5,4},{6,7},{7,6},{8,9},{9,8},{10,11... | collective-permute-start | bytes 589832 | tf_op jit(solution)/shard_map/ppermute | solution.py:304
  3.8 6.3 %collective-permute-start.1 = (bf16[384,256]{1,0:T(8,128)(2,1)S(1)}, bf16[384,256]{1,0:T(8,128)(2,1)S(1)}, u32[]{:S(2)}, u32[]{:S(2)}) collective-permute-start(bf16[384,256]{1,0:T(8,128)(2,1)S(1)} %get-tuple-element.26), channel_id=1, source_target_pairs={{0,2},{1,5},{2,6},{3,1},{4,0},{5,9},{6,10},{7,3},{8,4},{9,13},{10,... | collective-permute-start | bytes 589832 | tf_op jit(solution)/shard_map/ppermute | solution.py:325
  6.8 5.5 %collective-permute-start.2 = (bf16[352,256]{1,0:T(8,128)(2,1)S(1)}, bf16[352,256]{1,0:T(8,128)(2,1)S(1)}, u32[]{:S(2)}, u32[]{:S(2)}) collective-permute-start(bf16[352,256]{1,0:T(8,128)(2,1)S(1)} %slice.9), channel_id=1, source_target_pairs={{0,2},{1,5},{2,6},{3,1},{4,0},{5,9},{6,10},{7,3},{8,4},{9,13},{10,... | collective-permute-start | bytes 540680 | tf_op jit(solution)/shard_map/ppermute | solution.py:325
  10.1 5.2 %collective-permute-start.3 = (bf16[288,256]{1,0:T(8,128)(2,1)S(1)}, bf16[288,256]{1,0:T(8,128)(2,1)S(1)}, u32[]{:S(2)}, u32[]{:S(2)}) collective-permute-start(bf16[288,256]{1,0:T(8,128)(2,1)S(1)} %slice.12), channel_id=1, source_target_pairs={{0,2},{1,5},{2,6},{3,1},{4,0},{5,9},{6,10},{7,3},{8,4},{9,13},{10,... | collective-permute-start | bytes 442376 | tf_op jit(solution)/shard_map/ppermute | solution.py:325
  12.3 5.7 %collective-permute-start.4 = (bf16[384,256]{1,0:T(8,128)(2,1)S(1)}, bf16[384,256]{1,0:T(8,128)(2,1)S(1)}, u32[]{:S(2)}, u32[]{:S(2)}) collective-permute-start(bf16[384,256]{1,0:T(8,128)(2,1)S(1)} %shard_map.93), channel_id=1, source_target_pairs={{0,2},{1,5},{2,6},{3,1},{4,0},{5,9},{6,10},{7,3},{8,4},{9,13},{10,... | collective-permute-start | bytes 589832 | tf_op jit(solution)/shard_map/ppermute | solution.py:325
  14.0 8.4 %collective-permute-start.8 = (bf16[352,256]{1,0:T(8,128)(2,1)S(1)}, bf16[352,256]{1,0:T(8,128)(2,1)S(1)}, u32[]{:S(2)}, u32[]{:S(2)}) collective-permute-start(bf16[352,256]{1,0:T(8,128)(2,1)S(1)} %collective-permute-done.2.theirs_ref.refs_3_), channel_id=1, source_target_pairs={{0,1},{1,0},{2,3},{3,2},{4,5},{5,4},{6,7},{7,6},{8,9},{9,8},{10,11... | collective-permute-start | bytes 540680 | tf_op jit(solution)/shard_map/ppermute | solution.py:304
  15.3 5.1 %collective-permute-start.5 = (bf16[288,256]{1,0:T(8,128)(2,1)S(1)}, bf16[288,256]{1,0:T(8,128)(2,1)S(1)}, u32[]{:S(2)}, u32[]{:S(2)}) collective-permute-start(bf16[288,256]{1,0:T(8,128)(2,1)S(1)} %collective-permute-done.3.refs_4_), channel_id=1, source_target_pairs={{0,2},{1,5},{2,6},{3,1},{4,0},{5,9},{6,10},{7,3},{8,4},{9,13},{10,... | collective-permute-start | bytes 442376 | tf_op jit(solution)/shard_map/ppermute | solution.py:325
  17.2 5.2 %collective-permute-start.7 = (bf16[384,256]{1,0:T(8,128)(2,1)S(1)}, bf16[384,256]{1,0:T(8,128)(2,1)S(1)}, u32[]{:S(2)}, u32[]{:S(2)}) collective-permute-start(bf16[384,256]{1,0:T(8,128)(2,1)S(1)} %collective-permute-done.1.mine_ref.refs_2_), channel_id=1, source_target_pairs={{0,1},{1,0},{2,3},{3,2},{4,5},{5,4},{6,7},{7,6},{8,9},{9,8},{10,11... | collective-permute-start | bytes 589832 | tf_op jit(solution)/shard_map/ppermute | solution.py:304
  18.1 7.5 %collective-permute-start.11 = (bf16[384,256]{1,0:T(8,128)(2,1)S(1)}, bf16[384,256]{1,0:T(8,128)(2,1)S(1)}, u32[]{:S(2)}, u32[]{:S(2)}) collective-permute-start(bf16[384,256]{1,0:T(8,128)(2,1)S(1)} %collective-permute-done.4.refs_5_), channel_id=1, source_target_pairs={{0,1},{1,0},{2,3},{3,2},{4,5},{5,4},{6,7},{7,6},{8,9},{9,8},{10,11... | collective-permute-start | bytes 589832 | tf_op jit(solution)/shard_map/ppermute | solution.py:304
  18.1 5.4 %collective-permute-start.6 = (bf16[320,256]{1,0:T(8,128)(2,1)S(1)}, bf16[320,256]{1,0:T(8,128)(2,1)S(1)}, u32[]{:S(2)}, u32[]{:S(2)}) collective-permute-start(bf16[320,256]{1,0:T(8,128)(2,1)S(1)} %slice.13), channel_id=1, source_target_pairs={{0,2},{1,5},{2,6},{3,1},{4,0},{5,9},{6,10},{7,3},{8,4},{9,13},{10,... | collective-permute-start | bytes 491528 | tf_op jit(solution)/shard_map/ppermute | solution.py:325
  20.4 5.1 %collective-permute-start.9 = (bf16[288,256]{1,0:T(8,128)(2,1)S(1)}, bf16[288,256]{1,0:T(8,128)(2,1)S(1)}, u32[]{:S(2)}, u32[]{:S(2)}) collective-permute-start(bf16[288,256]{1,0:T(8,128)(2,1)S(1)} %collective-permute-done.5.refs_6_), channel_id=1, source_target_pairs={{0,2},{1,5},{2,6},{3,1},{4,0},{5,9},{6,10},{7,3},{8,4},{9,13},{10,... | collective-permute-start | bytes 442376 | tf_op jit(solution)/shard_map/ppermute | solution.py:325
  22.4 3.2 %collective-permute-start.10 = (bf16[288,256]{1,0:T(8,128)(2,1)S(1)}, bf16[288,256]{1,0:T(8,128)(2,1)S(1)}, u32[]{:S(2)}, u32[]{:S(2)}) collective-permute-start(bf16[288,256]{1,0:T(8,128)(2,1)S(1)} %collective-permute-done.3.refs_4_), channel_id=1, source_target_pairs={{0,1},{1,0},{2,3},{3,2},{4,5},{5,4},{6,7},{7,6},{8,9},{9,8},{10,11... | collective-permute-start | bytes 442376 | tf_op jit(solution)/shard_map/ppermute | solution.py:304
  23.5 2.1 %collective-permute-start.13 = (bf16[320,256]{1,0:T(8,128)(2,1)S(1)}, bf16[320,256]{1,0:T(8,128)(2,1)S(1)}, u32[]{:S(2)}, u32[]{:S(2)}) collective-permute-start(bf16[320,256]{1,0:T(8,128)(2,1)S(1)} %collective-permute-done.6.refs_7_), channel_id=1, source_target_pairs={{0,1},{1,0},{2,3},{3,2},{4,5},{5,4},{6,7},{7,6},{8,9},{9,8},{10,11... | collective-permute-start | bytes 491528 | tf_op jit(solution)/shard_map/ppermute | solution.py:304
  23.5 2.1 %collective-permute-start.12 = (bf16[288,256]{1,0:T(8,128)(2,1)S(1)}, bf16[288,256]{1,0:T(8,128)(2,1)S(1)}, u32[]{:S(2)}, u32[]{:S(2)}) collective-permute-start(bf16[288,256]{1,0:T(8,128)(2,1)S(1)} %collective-permute-done.5.refs_6_), channel_id=1, source_target_pairs={{0,1},{1,0},{2,3},{3,2},{4,5},{5,4},{6,7},{7,6},{8,9},{9,8},{10,11... | collective-permute-start | bytes 442376 | tf_op jit(solution)/shard_map/ppermute | solution.py:304
  25.6 1.4 %collective-permute-start.14 = (bf16[288,256]{1,0:T(8,128)(2,1)S(1)}, bf16[288,256]{1,0:T(8,128)(2,1)S(1)}, u32[]{:S(2)}, u32[]{:S(2)}) collective-permute-start(bf16[288,256]{1,0:T(8,128)(2,1)S(1)} %collective-permute-done.9.refs_8_), channel_id=1, source_target_pairs={{0,1},{1,0},{2,3},{3,2},{4,5},{5,4},{6,7},{7,6},{8,9},{9,8},{10,11... | collective-permute-start | bytes 442376 | tf_op jit(solution)/shard_map/ppermute | solution.py:304

commit v21 on v15

--- a/solution.py
+++ b/solution.py
@@ -152,7 +152,7 @@
     offset_out[...] = offset_ref[...]
     channels, columns = out_ref.shape
     hidden = math.isqrt(columns)
-    wide_ref[...] = final_ref[...].astype(jnp.float32)
+    wide_ref[: hidden * hidden, :] = final_ref[...].astype(jnp.float32)
     step = LANES // hidden
     for e in range(0, hidden, step):
         rows = [wide_ref[pl.ds(e + n, hidden, stride=hidden), :] for n in range(step)]
@@ -255,7 +255,7 @@
             pltpu.VMEM((1, hidden), jnp.float32),
             pltpu.VMEM((hidden, features), jnp.bfloat16),
             pltpu.VMEM((1, hidden), jnp.float32),
-            pltpu.VMEM((residues * width // LANES, LANES), jnp.float32),
+            pltpu.VMEM((residues * width // LANES + here, LANES), jnp.float32),
             pltpu.SemaphoreType.DMA((CHUNKS + 6,)),
         ],
         compiler_params=pltpu.CompilerParams(vmem_limit_bytes=32 * MIB),
@@ -294,7 +294,7 @@
         ],
         in_specs=[vmem] * 2,
         out_specs=[vmem] * 2,
-        scratch_shapes=[pltpu.VMEM((hidden * hidden, channels), jnp.float32)],
+        scratch_shapes=[pltpu.VMEM(((hidden + 1) * hidden, channels), jnp.float32)],
         compiler_params=pltpu.CompilerParams(vmem_limit_bytes=16 * MIB),
         cost_estimate=pl.CostEstimate(flops=2**28, bytes_accessed=2**20, transcendentals=0),
     )(final_projector_coefficients, final_projector_offset.reshape(1, channels))

time: 31.5 us -> 31.5 us (level)
  no operation moved by 1% of the time
where the time goes in v21:
time: 31.5 us; the launch traced here: 31.4 us
  starting transfers between devices  14.5 us (46%)
  waiting for transfers between devices  8.63 us (27%)
  Pallas kernels  8.07 us (26%)
    ppermute x7, starting transfers between devices, per_device(): landed = [lax.ppermute(x, 'row', around) for x in flying]  13.5 us
    ppermute x7, waiting for transfers between devices, per_device(): landed = [lax.ppermute(x, 'row', around) for x in flying]  7.26 us
    pallas_call x1, Pallas kernels, per_device(): pl.pallas_call(functools.partial(pair_kernel, places, gridded, rows_here,...  4.43 us
    pallas_call x1, Pallas kernels, per_device(): pl.pallas_call(functools.partial(project_kernel, rows_here), out_shape=[r...  3.22 us
    ppermute x8, waiting for transfers between devices, swap(): return lax.ppermute(value, 'row', [(r, r ^ 1) for r in range(size)])  1.36 us
    ppermute x8, starting transfers between devices, swap(): return lax.ppermute(value, 'row', [(r, r ^ 1) for r in range(size)])  1.04 us
  transfers between devices with their start and end apart: 15, of which 8 were waited for; matrix products, arithmetic and copies ran while one was open for 0% of the time, Pallas kernels for 1%

profile of v21, /device:TPU:0, one launch (start us, length us, event | category | flops | bytes accessed | tf_op | source)
XLA Modules:
  0.0 31.4 jit_solution(7988686406288213173)
XLA Ops:
  0.0 3.2 %shard_map.91 = (bf16[384,256]{1,0:T(8,128)(2,1)S(1)}, bf16[384,256]{1,0:T(8,128)(2,1)S(1)}) custom-call(bf16[8,256,256]{2,1,0:T(8,128)(2,1)} %x_hbm.1, f32[1,256]{1,0:T(1,128)} %bitcast.10, f32[1,256]{1,0:T(1,128)} %bitcast.11, bf16[32,256]{1,0:T(8,128)(2,1)} %bitcast.8, f32[1,32]{1,0:T(1,128)} %bitcast.12, bf16[32,256]{1,0:T(8,128)(2,1)} %bitcast.9, ...), custom_call_target="tpu_custom_call" | custom-call | flops 536870912 | bytes 1048576 | tf_op jit(solution)/shard_map/pallas_call | solution.py:245
  3.2 0.5 %collective-permute-start = (bf16[384,256]{1,0:T(8,128)(2,1)S(1)}, bf16[384,256]{1,0:T(8,128)(2,1)S(1)}, u32[]{:S(2)}, u32[]{:S(2)}) collective-permute-start(bf16[384,256]{1,0:T(8,128)(2,1)S(1)} %get-tuple-element.24.refs_0_), channel_id=1, source_target_pairs={{0,1},{1,0},{2,3},{3,2},{4,5},{5,4},{6,7},{7,6},{8,9},{9,8},{10,11... | collective-permute-start | bytes 589832 | tf_op jit(solution)/shard_map/ppermute | solution.py:287
  3.8 2.6 %collective-permute-start.1 = (bf16[384,256]{1,0:T(8,128)(2,1)S(1)}, bf16[384,256]{1,0:T(8,128)(2,1)S(1)}, u32[]{:S(2)}, u32[]{:S(2)}) collective-permute-start(bf16[384,256]{1,0:T(8,128)(2,1)S(1)} %get-tuple-element.28), channel_id=1, source_target_pairs={{0,2},{1,5},{2,6},{3,1},{4,0},{5,9},{6,10},{7,3},{8,4},{9,13},{10,... | collective-permute-start | bytes 589832 | tf_op jit(solution)/shard_map/ppermute | solution.py:311
  6.3 0.4 %shard_map.92 = (bf16[128,1024]{1,0:T(8,128)(2,1)S(1)}, f32[1,128]{1,0:T(1,128)S(1)}) custom-call(bf16[1024,128]{1,0:T(8,128)(2,1)S(1)} %copy-done, f32[1,128]{1,0:T(1,128)S(1)} %bitcast.7), custom_call_target="tpu_custom_call" | custom-call | flops 268435456 | bytes 1048576 | tf_op jit(solution)/shard_map/pallas_call | solution.py:289
  6.8 0.0 collective-permute-done.refs_1_
  6.8 1.6 %collective-permute-start.2 = (bf16[352,256]{1,0:T(8,128)(2,1)S(1)}, bf16[352,256]{1,0:T(8,128)(2,1)S(1)}, u32[]{:S(2)}, u32[]{:S(2)}) collective-permute-start(bf16[352,256]{1,0:T(8,128)(2,1)S(1)} %slice.9), channel_id=1, source_target_pairs={{0,2},{1,5},{2,6},{3,1},{4,0},{5,9},{6,10},{7,3},{8,4},{9,13},{10,... | collective-permute-start | bytes 540680 | tf_op jit(solution)/shard_map/ppermute | solution.py:311
  8.4 1.6 %collective-permute-done.1.mine_ref.refs_2_ = bf16[384,256]{1,0:T(8,128)(2,1)S(1)} collective-permute-done((bf16[384,256]{1,0:T(8,128)(2,1)S(1)}, bf16[384,256]{1,0:T(8,128)(2,1)S(1)}, u32[]{:S(2)}, u32[]{:S(2)}) %collective-permute-start.1) | collective-permute-done | bytes 196640 | tf_op jit(solution)/shard_map/ppermute | solution.py:311
  10.1 2.0 %collective-permute-start.3 = (bf16[288,256]{1,0:T(8,128)(2,1)S(1)}, bf16[288,256]{1,0:T(8,128)(2,1)S(1)}, u32[]{:S(2)}, u32[]{:S(2)}) collective-permute-start(bf16[288,256]{1,0:T(8,128)(2,1)S(1)} %slice.12), channel_id=1, source_target_pairs={{0,2},{1,5},{2,6},{3,1},{4,0},{5,9},{6,10},{7,3},{8,4},{9,13},{10,... | collective-permute-start | bytes 442376 | tf_op jit(solution)/shard_map/ppermute | solution.py:311
  12.1 0.3 collective-permute-done.2.theirs_ref.refs_3_
  12.4 1.7 %collective-permute-start.4 = (bf16[384,256]{1,0:T(8,128)(2,1)S(1)}, bf16[384,256]{1,0:T(8,128)(2,1)S(1)}, u32[]{:S(2)}, u32[]{:S(2)}) collective-permute-start(bf16[384,256]{1,0:T(8,128)(2,1)S(1)} %shard_map.93), channel_id=1, source_target_pairs={{0,2},{1,5},{2,6},{3,1},{4,0},{5,9},{6,10},{7,3},{8,4},{9,13},{10,... | collective-permute-start | bytes 589832 | tf_op jit(solution)/shard_map/ppermute | solution.py:311
  14.0 1.2 %collective-permute-done.3.refs_4_ = bf16[288,256]{1,0:T(8,128)(2,1)S(1)} collective-permute-done((bf16[288,256]{1,0:T(8,128)(2,1)S(1)}, bf16[288,256]{1,0:T(8,128)(2,1)S(1)}, u32[]{:S(2)}, u32[]{:S(2)}) %collective-permute-start.3) | collective-permute-done | bytes 147488 | tf_op jit(solution)/shard_map/ppermute | solution.py:311
  15.3 2.0 %collective-permute-start.5 = (bf16[288,256]{1,0:T(8,128)(2,1)S(1)}, bf16[288,256]{1,0:T(8,128)(2,1)S(1)}, u32[]{:S(2)}, u32[]{:S(2)}) collective-permute-start(bf16[288,256]{1,0:T(8,128)(2,1)S(1)} %collective-permute-done.3.refs_4_), channel_id=1, source_target_pairs={{0,2},{1,5},{2,6},{3,1},{4,0},{5,9},{6,10},{7,3},{8,4},{9,13},{10,... | collective-permute-start | bytes 442376 | tf_op jit(solution)/shard_map/ppermute | solution.py:311
  17.2 0.0 collective-permute-start.7
  17.2 0.8 %collective-permute-done.4.refs_5_ = bf16[384,256]{1,0:T(8,128)(2,1)S(1)} collective-permute-done((bf16[384,256]{1,0:T(8,128)(2,1)S(1)}, bf16[384,256]{1,0:T(8,128)(2,1)S(1)}, u32[]{:S(2)}, u32[]{:S(2)}) %collective-permute-start.4) | collective-permute-done | bytes 196640 | tf_op jit(solution)/shard_map/ppermute | solution.py:311
  18.1 0.0 collective-permute-start.11
  18.1 1.7 %collective-permute-start.6 = (bf16[320,256]{1,0:T(8,128)(2,1)S(1)}, bf16[320,256]{1,0:T(8,128)(2,1)S(1)}, u32[]{:S(2)}, u32[]{:S(2)}) collective-permute-start(bf16[320,256]{1,0:T(8,128)(2,1)S(1)} %slice.13), channel_id=1, source_target_pairs={{0,2},{1,5},{2,6},{3,1},{4,0},{5,9},{6,10},{7,3},{8,4},{9,13},{10,... | collective-permute-start | bytes 491528 | tf_op jit(solution)/shard_map/ppermute | solution.py:311
  19.8 0.6 %collective-permute-done.5.refs_6_ = bf16[288,256]{1,0:T(8,128)(2,1)S(1)} collective-permute-done((bf16[288,256]{1,0:T(8,128)(2,1)S(1)}, bf16[288,256]{1,0:T(8,128)(2,1)S(1)}, u32[]{:S(2)}, u32[]{:S(2)}) %collective-permute-start.5) | collective-permute-done | bytes 147488 | tf_op jit(solution)/shard_map/ppermute | solution.py:311
  20.4 2.0 %collective-permute-start.9 = (bf16[288,256]{1,0:T(8,128)(2,1)S(1)}, bf16[288,256]{1,0:T(8,128)(2,1)S(1)}, u32[]{:S(2)}, u32[]{:S(2)}) collective-permute-start(bf16[288,256]{1,0:T(8,128)(2,1)S(1)} %collective-permute-done.5.refs_6_), channel_id=1, source_target_pairs={{0,2},{1,5},{2,6},{3,1},{4,0},{5,9},{6,10},{7,3},{8,4},{9,13},{10,... | collective-permute-start | bytes 442376 | tf_op jit(solution)/shard_map/ppermute | solution.py:311
  22.4 0.0 collective-permute-start.10
  22.4 1.1 %collective-permute-done.6.refs_7_ = bf16[320,256]{1,0:T(8,128)(2,1)S(1)} collective-permute-done((bf16[320,256]{1,0:T(8,128)(2,1)S(1)}, bf16[320,256]{1,0:T(8,128)(2,1)S(1)}, u32[]{:S(2)}, u32[]{:S(2)}) %collective-permute-start.6) | collective-permute-done | bytes 163872 | tf_op jit(solution)/shard_map/ppermute | solution.py:311
  23.5 0.5 %collective-permute-start.12 = (bf16[288,256]{1,0:T(8,128)(2,1)S(1)}, bf16[288,256]{1,0:T(8,128)(2,1)S(1)}, u32[]{:S(2)}, u32[]{:S(2)}) collective-permute-start(bf16[288,256]{1,0:T(8,128)(2,1)S(1)} %collective-permute-done.5.refs_6_), channel_id=1, source_target_pairs={{0,1},{1,0},{2,3},{3,2},{4,5},{5,4},{6,7},{7,6},{8,9},{9,8},{10,11... | collective-permute-start | bytes 442376 | tf_op jit(solution)/shard_map/ppermute | solution.py:287
  24.0 1.6 %collective-permute-done.9.refs_8_ = bf16[288,256]{1,0:T(8,128)(2,1)S(1)} collective-permute-done((bf16[288,256]{1,0:T(8,128)(2,1)S(1)}, bf16[288,256]{1,0:T(8,128)(2,1)S(1)}, u32[]{:S(2)}, u32[]{:S(2)}) %collective-permute-start.9) | collective-permute-done | bytes 147488 | tf_op jit(solution)/shard_map/ppermute | solution.py:311
  25.6 1.3 %collective-permute-done.14.refs_15_ = bf16[288,256]{1,0:T(8,128)(2,1)S(1)} collective-permute-done((bf16[288,256]{1,0:T(8,128)(2,1)S(1)}, bf16[288,256]{1,0:T(8,128)(2,1)S(1)}, u32[]{:S(2)}, u32[]{:S(2)}) %collective-permute-start.14) | collective-permute-done | bytes 147488 | tf_op jit(solution)/shard_map/ppermute | solution.py:287
  26.9 4.4 %shard_map.94 = bf16[16,256,128]{2,1,0:T(8,128)(2,1)} custom-call(bf16[384,256]{1,0:T(8,128)(2,1)S(1)} %get-tuple-element.24.refs_0_, bf16[384,256]{1,0:T(8,128)(2,1)S(1)} %collective-permute-done.refs_1_, bf16[384,256]{1,0:T(8,128)(2,1)S(1)} %collective-permute-done.1.mine_ref.refs_2_, bf16[352,256]{1,0:T(8,128)(2,1)S(1)} %collective-permute-done.2.theirs_ref.refs_3_, ...), custom_call_target="tpu_custom_call" | custom-call | tf_op jit(solution)/shard_map/pallas_call | solution.py:359
  (17 shorter events, 0.1 us)
Async XLA Ops:
  0.0 6.3 %copy-start = (bf16[1024,128]{1,0:T(8,128)(2,1)S(1)}, bf16[1024,128]{1,0:T(8,128)(2,1)}, u32[]{:S(2)}) copy-start(bf16[1024,128]{1,0:T(8,128)(2,1)} %final_ref.1) | copy-start | bytes 786436
  3.2 3.5 %collective-permute-start = (bf16[384,256]{1,0:T(8,128)(2,1)S(1)}, bf16[384,256]{1,0:T(8,128)(2,1)S(1)}, u32[]{:S(2)}, u32[]{:S(2)}) collective-permute-start(bf16[384,256]{1,0:T(8,128)(2,1)S(1)} %get-tuple-element.24.refs_0_), channel_id=1, source_target_pairs={{0,1},{1,0},{2,3},{3,2},{4,5},{5,4},{6,7},{7,6},{8,9},{9,8},{10,11... | collective-permute-start | bytes 589832 | tf_op jit(solution)/shard_map/ppermute | solution.py:287
  3.8 2.6 %copy-start.1 = (f32[128]{0:T(128)S(1)}, f32[128]{0:T(128)}, u32[]{:S(2)}) copy-start(f32[128]{0:T(128)} %param.17) | copy-start | bytes 1540
  3.8 6.3 %collective-permute-start.1 = (bf16[384,256]{1,0:T(8,128)(2,1)S(1)}, bf16[384,256]{1,0:T(8,128)(2,1)S(1)}, u32[]{:S(2)}, u32[]{:S(2)}) collective-permute-start(bf16[384,256]{1,0:T(8,128)(2,1)S(1)} %get-tuple-element.28), channel_id=1, source_target_pairs={{0,2},{1,5},{2,6},{3,1},{4,0},{5,9},{6,10},{7,3},{8,4},{9,13},{10,... | collective-permute-start | bytes 589832 | tf_op jit(solution)/shard_map/ppermute | solution.py:311
  6.8 5.5 %collective-permute-start.2 = (bf16[352,256]{1,0:T(8,128)(2,1)S(1)}, bf16[352,256]{1,0:T(8,128)(2,1)S(1)}, u32[]{:S(2)}, u32[]{:S(2)}) collective-permute-start(bf16[352,256]{1,0:T(8,128)(2,1)S(1)} %slice.9), channel_id=1, source_target_pairs={{0,2},{1,5},{2,6},{3,1},{4,0},{5,9},{6,10},{7,3},{8,4},{9,13},{10,... | collective-permute-start | bytes 540680 | tf_op jit(solution)/shard_map/ppermute | solution.py:311
  10.1 5.2 %collective-permute-start.3 = (bf16[288,256]{1,0:T(8,128)(2,1)S(1)}, bf16[288,256]{1,0:T(8,128)(2,1)S(1)}, u32[]{:S(2)}, u32[]{:S(2)}) collective-permute-start(bf16[288,256]{1,0:T(8,128)(2,1)S(1)} %slice.12), channel_id=1, source_target_pairs={{0,2},{1,5},{2,6},{3,1},{4,0},{5,9},{6,10},{7,3},{8,4},{9,13},{10,... | collective-permute-start | bytes 442376 | tf_op jit(solution)/shard_map/ppermute | solution.py:311
  12.4 5.7 %collective-permute-start.4 = (bf16[384,256]{1,0:T(8,128)(2,1)S(1)}, bf16[384,256]{1,0:T(8,128)(2,1)S(1)}, u32[]{:S(2)}, u32[]{:S(2)}) collective-permute-start(bf16[384,256]{1,0:T(8,128)(2,1)S(1)} %shard_map.93), channel_id=1, source_target_pairs={{0,2},{1,5},{2,6},{3,1},{4,0},{5,9},{6,10},{7,3},{8,4},{9,13},{10,... | collective-permute-start | bytes 589832 | tf_op jit(solution)/shard_map/ppermute | solution.py:311
  14.0 8.4 %collective-permute-start.8 = (bf16[352,256]{1,0:T(8,128)(2,1)S(1)}, bf16[352,256]{1,0:T(8,128)(2,1)S(1)}, u32[]{:S(2)}, u32[]{:S(2)}) collective-permute-start(bf16[352,256]{1,0:T(8,128)(2,1)S(1)} %collective-permute-done.2.theirs_ref.refs_3_), channel_id=1, source_target_pairs={{0,1},{1,0},{2,3},{3,2},{4,5},{5,4},{6,7},{7,6},{8,9},{9,8},{10,11... | collective-permute-start | bytes 540680 | tf_op jit(solution)/shard_map/ppermute | solution.py:287
  15.3 5.1 %collective-permute-start.5 = (bf16[288,256]{1,0:T(8,128)(2,1)S(1)}, bf16[288,256]{1,0:T(8,128)(2,1)S(1)}, u32[]{:S(2)}, u32[]{:S(2)}) collective-permute-start(bf16[288,256]{1,0:T(8,128)(2,1)S(1)} %collective-permute-done.3.refs_4_), channel_id=1, source_target_pairs={{0,2},{1,5},{2,6},{3,1},{4,0},{5,9},{6,10},{7,3},{8,4},{9,13},{10,... | collective-permute-start | bytes 442376 | tf_op jit(solution)/shard_map/ppermute | solution.py:311
  17.2 5.2 %collective-permute-start.7 = (bf16[384,256]{1,0:T(8,128)(2,1)S(1)}, bf16[384,256]{1,0:T(8,128)(2,1)S(1)}, u32[]{:S(2)}, u32[]{:S(2)}) collective-permute-start(bf16[384,256]{1,0:T(8,128)(2,1)S(1)} %collective-permute-done.1.mine_ref.refs_2_), channel_id=1, source_target_pairs={{0,1},{1,0},{2,3},{3,2},{4,5},{5,4},{6,7},{7,6},{8,9},{9,8},{10,11... | collective-permute-start | bytes 589832 | tf_op jit(solution)/shard_map/ppermute | solution.py:287
  18.1 7.5 %collective-permute-start.11 = (bf16[384,256]{1,0:T(8,128)(2,1)S(1)}, bf16[384,256]{1,0:T(8,128)(2,1)S(1)}, u32[]{:S(2)}, u32[]{:S(2)}) collective-permute-start(bf16[384,256]{1,0:T(8,128)(2,1)S(1)} %collective-permute-done.4.refs_5_), channel_id=1, source_target_pairs={{0,1},{1,0},{2,3},{3,2},{4,5},{5,4},{6,7},{7,6},{8,9},{9,8},{10,11... | collective-permute-start | bytes 589832 | tf_op jit(solution)/shard_map/ppermute | solution.py:287
  18.1 5.4 %collective-permute-start.6 = (bf16[320,256]{1,0:T(8,128)(2,1)S(1)}, bf16[320,256]{1,0:T(8,128)(2,1)S(1)}, u32[]{:S(2)}, u32[]{:S(2)}) collective-permute-start(bf16[320,256]{1,0:T(8,128)(2,1)S(1)} %slice.13), channel_id=1, source_target_pairs={{0,2},{1,5},{2,6},{3,1},{4,0},{5,9},{6,10},{7,3},{8,4},{9,13},{10,... | collective-permute-start | bytes 491528 | tf_op jit(solution)/shard_map/ppermute | solution.py:311
  20.4 5.1 %collective-permute-start.9 = (bf16[288,256]{1,0:T(8,128)(2,1)S(1)}, bf16[288,256]{1,0:T(8,128)(2,1)S(1)}, u32[]{:S(2)}, u32[]{:S(2)}) collective-permute-start(bf16[288,256]{1,0:T(8,128)(2,1)S(1)} %collective-permute-done.5.refs_6_), channel_id=1, source_target_pairs={{0,2},{1,5},{2,6},{3,1},{4,0},{5,9},{6,10},{7,3},{8,4},{9,13},{10,... | collective-permute-start | bytes 442376 | tf_op jit(solution)/shard_map/ppermute | solution.py:311
  22.4 3.2 %collective-permute-start.10 = (bf16[288,256]{1,0:T(8,128)(2,1)S(1)}, bf16[288,256]{1,0:T(8,128)(2,1)S(1)}, u32[]{:S(2)}, u32[]{:S(2)}) collective-permute-start(bf16[288,256]{1,0:T(8,128)(2,1)S(1)} %collective-permute-done.3.refs_4_), channel_id=1, source_target_pairs={{0,1},{1,0},{2,3},{3,2},{4,5},{5,4},{6,7},{7,6},{8,9},{9,8},{10,11... | collective-permute-start | bytes 442376 | tf_op jit(solution)/shard_map/ppermute | solution.py:287
  23.5 2.1 %collective-permute-start.13 = (bf16[320,256]{1,0:T(8,128)(2,1)S(1)}, bf16[320,256]{1,0:T(8,128)(2,1)S(1)}, u32[]{:S(2)}, u32[]{:S(2)}) collective-permute-start(bf16[320,256]{1,0:T(8,128)(2,1)S(1)} %collective-permute-done.6.refs_7_), channel_id=1, source_target_pairs={{0,1},{1,0},{2,3},{3,2},{4,5},{5,4},{6,7},{7,6},{8,9},{9,8},{10,11... | collective-permute-start | bytes 491528 | tf_op jit(solution)/shard_map/ppermute | solution.py:287
  23.5 2.1 %collective-permute-start.12 = (bf16[288,256]{1,0:T(8,128)(2,1)S(1)}, bf16[288,256]{1,0:T(8,128)(2,1)S(1)}, u32[]{:S(2)}, u32[]{:S(2)}) collective-permute-start(bf16[288,256]{1,0:T(8,128)(2,1)S(1)} %collective-permute-done.5.refs_6_), channel_id=1, source_target_pairs={{0,1},{1,0},{2,3},{3,2},{4,5},{5,4},{6,7},{7,6},{8,9},{9,8},{10,11... | collective-permute-start | bytes 442376 | tf_op jit(solution)/shard_map/ppermute | solution.py:287
  25.6 1.4 %collective-permute-start.14 = (bf16[288,256]{1,0:T(8,128)(2,1)S(1)}, bf16[288,256]{1,0:T(8,128)(2,1)S(1)}, u32[]{:S(2)}, u32[]{:S(2)}) collective-permute-start(bf16[288,256]{1,0:T(8,128)(2,1)S(1)} %collective-permute-done.9.refs_8_), channel_id=1, source_target_pairs={{0,1},{1,0},{2,3},{3,2},{4,5},{5,4},{6,7},{7,6},{8,9},{9,8},{10,11... | collective-permute-start | bytes 442376 | tf_op jit(solution)/shard_map/ppermute | solution.py:287

commit v22 on v21

--- a/solution.py
+++ b/solution.py
@@ -94,15 +94,16 @@
     member = lax.broadcasted_iota(jnp.int32, (tile // fold, tile), 1)
     gather = (member // fold == group).astype(jnp.bfloat16)
 
+    ones = jnp.ones((features, LANES), jnp.bfloat16)
     right = [jnp.zeros((tile, width), jnp.float32) for _ in range(tiles)]
     for s in range(samples):
         if s % some == 0:
             large[s // some].wait()
+        center = jnp.dot(x_ref[s], ones, preferred_element_type=jnp.float32) * (1.0 / features)
         normed = []
         for low in range(0, residues, BLOCK):
             values = x_ref[s, low : low + BLOCK, :].astype(jnp.float32)
-            center = jnp.mean(values, axis=-1, keepdims=True)
-            values = values - center
+            values = values - jnp.concatenate([center[low : low + BLOCK]] * (features // LANES), axis=1)
             variance = jnp.mean(jnp.square(values), axis=-1, keepdims=True)
             values = values * lax.rsqrt(variance + 1e-05) * gain_ref[...] + shift_ref[...]
             normed.append(values.astype(jnp.bfloat16))

time: 31.5 us -> 33.2 us (1.054)
  Pallas kernels: 8.07 us -> 9.76 us
    pallas_call x1, Pallas kernels: 3.22 us -> 4.92 us  [per_device(): pl.pallas_call(functools.partial(project_kernel, rows_here), out_shape=[r...]
where the time goes in v22:
time: 33.2 us; the launch traced here: 33 us
  starting transfers between devices  14.5 us (44%)
  Pallas kernels  9.76 us (29%)
  waiting for transfers between devices  8.61 us (26%)
    ppermute x7, starting transfers between devices, per_device(): landed = [lax.ppermute(x, 'row', around) for x in flying]  13.5 us
    ppermute x7, waiting for transfers between devices, per_device(): landed = [lax.ppermute(x, 'row', around) for x in flying]  7.25 us
    pallas_call x1, Pallas kernels, per_device(): pl.pallas_call(functools.partial(project_kernel, rows_here), out_shape=[r...  4.92 us
    pallas_call x1, Pallas kernels, per_device(): pl.pallas_call(functools.partial(pair_kernel, places, gridded, rows_here,...  4.43 us
    ppermute x8, waiting for transfers between devices, swap(): return lax.ppermute(value, 'row', [(r, r ^ 1) for r in range(size)])  1.36 us
    ppermute x8, starting transfers between devices, swap(): return lax.ppermute(value, 'row', [(r, r ^ 1) for r in range(size)])  1.04 us
  transfers between devices with their start and end apart: 15, of which 8 were waited for; matrix products, arithmetic and copies ran while one was open for 0% of the time, Pallas kernels for 1%

profile of v22, /device:TPU:0, one launch (start us, length us, event | category | flops | bytes accessed | tf_op | source)
XLA Modules:
  0.0 33.0 jit_solution(1787350336704458960)
XLA Ops:
  0.0 4.9 %shard_map.91 = (bf16[384,256]{1,0:T(8,128)(2,1)S(1)}, bf16[384,256]{1,0:T(8,128)(2,1)S(1)}) custom-call(bf16[8,256,256]{2,1,0:T(8,128)(2,1)} %x_hbm.1, f32[1,256]{1,0:T(1,128)} %bitcast.10, f32[1,256]{1,0:T(1,128)} %bitcast.11, bf16[32,256]{1,0:T(8,128)(2,1)} %bitcast.8, f32[1,32]{1,0:T(1,128)} %bitcast.12, bf16[32,256]{1,0:T(8,128)(2,1)} %bitcast.9, ...), custom_call_target="tpu_custom_call" | custom-call | flops 536870912 | bytes 1048576 | tf_op jit(solution)/shard_map/pallas_call | solution.py:246
  4.9 0.5 %collective-permute-start = (bf16[384,256]{1,0:T(8,128)(2,1)S(1)}, bf16[384,256]{1,0:T(8,128)(2,1)S(1)}, u32[]{:S(2)}, u32[]{:S(2)}) collective-permute-start(bf16[384,256]{1,0:T(8,128)(2,1)S(1)} %get-tuple-element.24.refs_0_), channel_id=1, source_target_pairs={{0,1},{1,0},{2,3},{3,2},{4,5},{5,4},{6,7},{7,6},{8,9},{9,8},{10,11... | collective-permute-start | bytes 589832 | tf_op jit(solution)/shard_map/ppermute | solution.py:288
  5.4 2.6 %collective-permute-start.1 = (bf16[384,256]{1,0:T(8,128)(2,1)S(1)}, bf16[384,256]{1,0:T(8,128)(2,1)S(1)}, u32[]{:S(2)}, u32[]{:S(2)}) collective-permute-start(bf16[384,256]{1,0:T(8,128)(2,1)S(1)} %get-tuple-element.28), channel_id=1, source_target_pairs={{0,2},{1,5},{2,6},{3,1},{4,0},{5,9},{6,10},{7,3},{8,4},{9,13},{10,... | collective-permute-start | bytes 589832 | tf_op jit(solution)/shard_map/ppermute | solution.py:312
  8.0 0.4 %shard_map.92 = (bf16[128,1024]{1,0:T(8,128)(2,1)S(1)}, f32[1,128]{1,0:T(1,128)S(1)}) custom-call(bf16[1024,128]{1,0:T(8,128)(2,1)S(1)} %copy-done, f32[1,128]{1,0:T(1,128)S(1)} %bitcast.7), custom_call_target="tpu_custom_call" | custom-call | flops 268435456 | bytes 1048576 | tf_op jit(solution)/shard_map/pallas_call | solution.py:290
  8.4 0.0 collective-permute-done.refs_1_
  8.5 1.6 %collective-permute-start.2 = (bf16[352,256]{1,0:T(8,128)(2,1)S(1)}, bf16[352,256]{1,0:T(8,128)(2,1)S(1)}, u32[]{:S(2)}, u32[]{:S(2)}) collective-permute-start(bf16[352,256]{1,0:T(8,128)(2,1)S(1)} %slice.9), channel_id=1, source_target_pairs={{0,2},{1,5},{2,6},{3,1},{4,0},{5,9},{6,10},{7,3},{8,4},{9,13},{10,... | collective-permute-start | bytes 540680 | tf_op jit(solution)/shard_map/ppermute | solution.py:312
  10.1 1.6 %collective-permute-done.1.mine_ref.refs_2_ = bf16[384,256]{1,0:T(8,128)(2,1)S(1)} collective-permute-done((bf16[384,256]{1,0:T(8,128)(2,1)S(1)}, bf16[384,256]{1,0:T(8,128)(2,1)S(1)}, u32[]{:S(2)}, u32[]{:S(2)}) %collective-permute-start.1) | collective-permute-done | bytes 196640 | tf_op jit(solution)/shard_map/ppermute | solution.py:312
  11.7 2.0 %collective-permute-start.3 = (bf16[288,256]{1,0:T(8,128)(2,1)S(1)}, bf16[288,256]{1,0:T(8,128)(2,1)S(1)}, u32[]{:S(2)}, u32[]{:S(2)}) collective-permute-start(bf16[288,256]{1,0:T(8,128)(2,1)S(1)} %slice.12), channel_id=1, source_target_pairs={{0,2},{1,5},{2,6},{3,1},{4,0},{5,9},{6,10},{7,3},{8,4},{9,13},{10,... | collective-permute-start | bytes 442376 | tf_op jit(solution)/shard_map/ppermute | solution.py:312
  13.8 0.3 collective-permute-done.2.theirs_ref.refs_3_
  14.0 1.7 %collective-permute-start.4 = (bf16[384,256]{1,0:T(8,128)(2,1)S(1)}, bf16[384,256]{1,0:T(8,128)(2,1)S(1)}, u32[]{:S(2)}, u32[]{:S(2)}) collective-permute-start(bf16[384,256]{1,0:T(8,128)(2,1)S(1)} %shard_map.93), channel_id=1, source_target_pairs={{0,2},{1,5},{2,6},{3,1},{4,0},{5,9},{6,10},{7,3},{8,4},{9,13},{10,... | collective-permute-start | bytes 589832 | tf_op jit(solution)/shard_map/ppermute | solution.py:312
  15.7 0.0 collective-permute-start.8
  15.7 1.2 %collective-permute-done.3.refs_4_ = bf16[288,256]{1,0:T(8,128)(2,1)S(1)} collective-permute-done((bf16[288,256]{1,0:T(8,128)(2,1)S(1)}, bf16[288,256]{1,0:T(8,128)(2,1)S(1)}, u32[]{:S(2)}, u32[]{:S(2)}) %collective-permute-start.3) | collective-permute-done | bytes 147488 | tf_op jit(solution)/shard_map/ppermute | solution.py:312
  16.9 2.0 %collective-permute-start.5 = (bf16[288,256]{1,0:T(8,128)(2,1)S(1)}, bf16[288,256]{1,0:T(8,128)(2,1)S(1)}, u32[]{:S(2)}, u32[]{:S(2)}) collective-permute-start(bf16[288,256]{1,0:T(8,128)(2,1)S(1)} %collective-permute-done.3.refs_4_), channel_id=1, source_target_pairs={{0,2},{1,5},{2,6},{3,1},{4,0},{5,9},{6,10},{7,3},{8,4},{9,13},{10,... | collective-permute-start | bytes 442376 | tf_op jit(solution)/shard_map/ppermute | solution.py:312
  18.9 0.0 collective-permute-start.7
  18.9 0.8 %collective-permute-done.4.refs_5_ = bf16[384,256]{1,0:T(8,128)(2,1)S(1)} collective-permute-done((bf16[384,256]{1,0:T(8,128)(2,1)S(1)}, bf16[384,256]{1,0:T(8,128)(2,1)S(1)}, u32[]{:S(2)}, u32[]{:S(2)}) %collective-permute-start.4) | collective-permute-done | bytes 196640 | tf_op jit(solution)/shard_map/ppermute | solution.py:312
  19.8 1.7 %collective-permute-start.6 = (bf16[320,256]{1,0:T(8,128)(2,1)S(1)}, bf16[320,256]{1,0:T(8,128)(2,1)S(1)}, u32[]{:S(2)}, u32[]{:S(2)}) collective-permute-start(bf16[320,256]{1,0:T(8,128)(2,1)S(1)} %slice.13), channel_id=1, source_target_pairs={{0,2},{1,5},{2,6},{3,1},{4,0},{5,9},{6,10},{7,3},{8,4},{9,13},{10,... | collective-permute-start | bytes 491528 | tf_op jit(solution)/shard_map/ppermute | solution.py:312
  21.4 0.6 %collective-permute-done.5.refs_6_ = bf16[288,256]{1,0:T(8,128)(2,1)S(1)} collective-permute-done((bf16[288,256]{1,0:T(8,128)(2,1)S(1)}, bf16[288,256]{1,0:T(8,128)(2,1)S(1)}, u32[]{:S(2)}, u32[]{:S(2)}) %collective-permute-start.5) | collective-permute-done | bytes 147488 | tf_op jit(solution)/shard_map/ppermute | solution.py:312
  22.1 2.0 %collective-permute-start.9 = (bf16[288,256]{1,0:T(8,128)(2,1)S(1)}, bf16[288,256]{1,0:T(8,128)(2,1)S(1)}, u32[]{:S(2)}, u32[]{:S(2)}) collective-permute-start(bf16[288,256]{1,0:T(8,128)(2,1)S(1)} %collective-permute-done.5.refs_6_), channel_id=1, source_target_pairs={{0,2},{1,5},{2,6},{3,1},{4,0},{5,9},{6,10},{7,3},{8,4},{9,13},{10,... | collective-permute-start | bytes 442376 | tf_op jit(solution)/shard_map/ppermute | solution.py:312
  24.1 0.0 collective-permute-done.8.refs_10_
  24.1 1.1 %collective-permute-done.6.refs_7_ = bf16[320,256]{1,0:T(8,128)(2,1)S(1)} collective-permute-done((bf16[320,256]{1,0:T(8,128)(2,1)S(1)}, bf16[320,256]{1,0:T(8,128)(2,1)S(1)}, u32[]{:S(2)}, u32[]{:S(2)}) %collective-permute-start.6) | collective-permute-done | bytes 163872 | tf_op jit(solution)/shard_map/ppermute | solution.py:312
  25.2 0.5 %collective-permute-start.12 = (bf16[288,256]{1,0:T(8,128)(2,1)S(1)}, bf16[288,256]{1,0:T(8,128)(2,1)S(1)}, u32[]{:S(2)}, u32[]{:S(2)}) collective-permute-start(bf16[288,256]{1,0:T(8,128)(2,1)S(1)} %collective-permute-done.5.refs_6_), channel_id=1, source_target_pairs={{0,1},{1,0},{2,3},{3,2},{4,5},{5,4},{6,7},{7,6},{8,9},{9,8},{10,11... | collective-permute-start | bytes 442376 | tf_op jit(solution)/shard_map/ppermute | solution.py:288
  25.7 1.6 %collective-permute-done.9.refs_8_ = bf16[288,256]{1,0:T(8,128)(2,1)S(1)} collective-permute-done((bf16[288,256]{1,0:T(8,128)(2,1)S(1)}, bf16[288,256]{1,0:T(8,128)(2,1)S(1)}, u32[]{:S(2)}, u32[]{:S(2)}) %collective-permute-start.9) | collective-permute-done | bytes 147488 | tf_op jit(solution)/shard_map/ppermute | solution.py:312
  27.3 1.3 %collective-permute-done.14.refs_15_ = bf16[288,256]{1,0:T(8,128)(2,1)S(1)} collective-permute-done((bf16[288,256]{1,0:T(8,128)(2,1)S(1)}, bf16[288,256]{1,0:T(8,128)(2,1)S(1)}, u32[]{:S(2)}, u32[]{:S(2)}) %collective-permute-start.14) | collective-permute-done | bytes 147488 | tf_op jit(solution)/shard_map/ppermute | solution.py:288
  28.6 4.4 %shard_map.94 = bf16[16,256,128]{2,1,0:T(8,128)(2,1)} custom-call(bf16[384,256]{1,0:T(8,128)(2,1)S(1)} %get-tuple-element.24.refs_0_, bf16[384,256]{1,0:T(8,128)(2,1)S(1)} %collective-permute-done.refs_1_, bf16[384,256]{1,0:T(8,128)(2,1)S(1)} %collective-permute-done.1.mine_ref.refs_2_, bf16[352,256]{1,0:T(8,128)(2,1)S(1)} %collective-permute-done.2.theirs_ref.refs_3_, ...), custom_call_target="tpu_custom_call" | custom-call | tf_op jit(solution)/shard_map/pallas_call | solution.py:360
  (17 shorter events, 0.1 us)
Async XLA Ops:
  0.0 8.0 %copy-start = (bf16[1024,128]{1,0:T(8,128)(2,1)S(1)}, bf16[1024,128]{1,0:T(8,128)(2,1)}, u32[]{:S(2)}) copy-start(bf16[1024,128]{1,0:T(8,128)(2,1)} %final_ref.1) | copy-start | bytes 786436
  4.9 3.5 %collective-permute-start = (bf16[384,256]{1,0:T(8,128)(2,1)S(1)}, bf16[384,256]{1,0:T(8,128)(2,1)S(1)}, u32[]{:S(2)}, u32[]{:S(2)}) collective-permute-start(bf16[384,256]{1,0:T(8,128)(2,1)S(1)} %get-tuple-element.24.refs_0_), channel_id=1, source_target_pairs={{0,1},{1,0},{2,3},{3,2},{4,5},{5,4},{6,7},{7,6},{8,9},{9,8},{10,11... | collective-permute-start | bytes 589832 | tf_op jit(solution)/shard_map/ppermute | solution.py:288
  5.4 2.6 %copy-start.1 = (f32[128]{0:T(128)S(1)}, f32[128]{0:T(128)}, u32[]{:S(2)}) copy-start(f32[128]{0:T(128)} %param.17) | copy-start | bytes 1540
  5.4 6.3 %collective-permute-start.1 = (bf16[384,256]{1,0:T(8,128)(2,1)S(1)}, bf16[384,256]{1,0:T(8,128)(2,1)S(1)}, u32[]{:S(2)}, u32[]{:S(2)}) collective-permute-start(bf16[384,256]{1,0:T(8,128)(2,1)S(1)} %get-tuple-element.28), channel_id=1, source_target_pairs={{0,2},{1,5},{2,6},{3,1},{4,0},{5,9},{6,10},{7,3},{8,4},{9,13},{10,... | collective-permute-start | bytes 589832 | tf_op jit(solution)/shard_map/ppermute | solution.py:312
  8.5 5.5 %collective-permute-start.2 = (bf16[352,256]{1,0:T(8,128)(2,1)S(1)}, bf16[352,256]{1,0:T(8,128)(2,1)S(1)}, u32[]{:S(2)}, u32[]{:S(2)}) collective-permute-start(bf16[352,256]{1,0:T(8,128)(2,1)S(1)} %slice.9), channel_id=1, source_target_pairs={{0,2},{1,5},{2,6},{3,1},{4,0},{5,9},{6,10},{7,3},{8,4},{9,13},{10,... | collective-permute-start | bytes 540680 | tf_op jit(solution)/shard_map/ppermute | solution.py:312
  11.7 5.2 %collective-permute-start.3 = (bf16[288,256]{1,0:T(8,128)(2,1)S(1)}, bf16[288,256]{1,0:T(8,128)(2,1)S(1)}, u32[]{:S(2)}, u32[]{:S(2)}) collective-permute-start(bf16[288,256]{1,0:T(8,128)(2,1)S(1)} %slice.12), channel_id=1, source_target_pairs={{0,2},{1,5},{2,6},{3,1},{4,0},{5,9},{6,10},{7,3},{8,4},{9,13},{10,... | collective-permute-start | bytes 442376 | tf_op jit(solution)/shard_map/ppermute | solution.py:312
  14.0 5.7 %collective-permute-start.4 = (bf16[384,256]{1,0:T(8,128)(2,1)S(1)}, bf16[384,256]{1,0:T(8,128)(2,1)S(1)}, u32[]{:S(2)}, u32[]{:S(2)}) collective-permute-start(bf16[384,256]{1,0:T(8,128)(2,1)S(1)} %shard_map.93), channel_id=1, source_target_pairs={{0,2},{1,5},{2,6},{3,1},{4,0},{5,9},{6,10},{7,3},{8,4},{9,13},{10,... | collective-permute-start | bytes 589832 | tf_op jit(solution)/shard_map/ppermute | solution.py:312
  15.7 8.4 %collective-permute-start.8 = (bf16[352,256]{1,0:T(8,128)(2,1)S(1)}, bf16[352,256]{1,0:T(8,128)(2,1)S(1)}, u32[]{:S(2)}, u32[]{:S(2)}) collective-permute-start(bf16[352,256]{1,0:T(8,128)(2,1)S(1)} %collective-permute-done.2.theirs_ref.refs_3_), channel_id=1, source_target_pairs={{0,1},{1,0},{2,3},{3,2},{4,5},{5,4},{6,7},{7,6},{8,9},{9,8},{10,11... | collective-permute-start | bytes 540680 | tf_op jit(solution)/shard_map/ppermute | solution.py:288
  16.9 5.1 %collective-permute-start.5 = (bf16[288,256]{1,0:T(8,128)(2,1)S(1)}, bf16[288,256]{1,0:T(8,128)(2,1)S(1)}, u32[]{:S(2)}, u32[]{:S(2)}) collective-permute-start(bf16[288,256]{1,0:T(8,128)(2,1)S(1)} %collective-permute-done.3.refs_4_), channel_id=1, source_target_pairs={{0,2},{1,5},{2,6},{3,1},{4,0},{5,9},{6,10},{7,3},{8,4},{9,13},{10,... | collective-permute-start | bytes 442376 | tf_op jit(solution)/shard_map/ppermute | solution.py:312
  18.9 5.2 %collective-permute-start.7 = (bf16[384,256]{1,0:T(8,128)(2,1)S(1)}, bf16[384,256]{1,0:T(8,128)(2,1)S(1)}, u32[]{:S(2)}, u32[]{:S(2)}) collective-permute-start(bf16[384,256]{1,0:T(8,128)(2,1)S(1)} %collective-permute-done.1.mine_ref.refs_2_), channel_id=1, source_target_pairs={{0,1},{1,0},{2,3},{3,2},{4,5},{5,4},{6,7},{7,6},{8,9},{9,8},{10,11... | collective-permute-start | bytes 589832 | tf_op jit(solution)/shard_map/ppermute | solution.py:288
  19.8 7.5 %collective-permute-start.11 = (bf16[384,256]{1,0:T(8,128)(2,1)S(1)}, bf16[384,256]{1,0:T(8,128)(2,1)S(1)}, u32[]{:S(2)}, u32[]{:S(2)}) collective-permute-start(bf16[384,256]{1,0:T(8,128)(2,1)S(1)} %collective-permute-done.4.refs_5_), channel_id=1, source_target_pairs={{0,1},{1,0},{2,3},{3,2},{4,5},{5,4},{6,7},{7,6},{8,9},{9,8},{10,11... | collective-permute-start | bytes 589832 | tf_op jit(solution)/shard_map/ppermute | solution.py:288
  19.8 5.4 %collective-permute-start.6 = (bf16[320,256]{1,0:T(8,128)(2,1)S(1)}, bf16[320,256]{1,0:T(8,128)(2,1)S(1)}, u32[]{:S(2)}, u32[]{:S(2)}) collective-permute-start(bf16[320,256]{1,0:T(8,128)(2,1)S(1)} %slice.13), channel_id=1, source_target_pairs={{0,2},{1,5},{2,6},{3,1},{4,0},{5,9},{6,10},{7,3},{8,4},{9,13},{10,... | collective-permute-start | bytes 491528 | tf_op jit(solution)/shard_map/ppermute | solution.py:312
  22.1 5.1 %collective-permute-start.9 = (bf16[288,256]{1,0:T(8,128)(2,1)S(1)}, bf16[288,256]{1,0:T(8,128)(2,1)S(1)}, u32[]{:S(2)}, u32[]{:S(2)}) collective-permute-start(bf16[288,256]{1,0:T(8,128)(2,1)S(1)} %collective-permute-done.5.refs_6_), channel_id=1, source_target_pairs={{0,2},{1,5},{2,6},{3,1},{4,0},{5,9},{6,10},{7,3},{8,4},{9,13},{10,... | collective-permute-start | bytes 442376 | tf_op jit(solution)/shard_map/ppermute | solution.py:312
  24.1 3.2 %collective-permute-start.10 = (bf16[288,256]{1,0:T(8,128)(2,1)S(1)}, bf16[288,256]{1,0:T(8,128)(2,1)S(1)}, u32[]{:S(2)}, u32[]{:S(2)}) collective-permute-start(bf16[288,256]{1,0:T(8,128)(2,1)S(1)} %collective-permute-done.3.refs_4_), channel_id=1, source_target_pairs={{0,1},{1,0},{2,3},{3,2},{4,5},{5,4},{6,7},{7,6},{8,9},{9,8},{10,11... | collective-permute-start | bytes 442376 | tf_op jit(solution)/shard_map/ppermute | solution.py:288
  25.2 2.1 %collective-permute-start.13 = (bf16[320,256]{1,0:T(8,128)(2,1)S(1)}, bf16[320,256]{1,0:T(8,128)(2,1)S(1)}, u32[]{:S(2)}, u32[]{:S(2)}) collective-permute-start(bf16[320,256]{1,0:T(8,128)(2,1)S(1)} %collective-permute-done.6.refs_7_), channel_id=1, source_target_pairs={{0,1},{1,0},{2,3},{3,2},{4,5},{5,4},{6,7},{7,6},{8,9},{9,8},{10,11... | collective-permute-start | bytes 491528 | tf_op jit(solution)/shard_map/ppermute | solution.py:288
  25.2 2.1 %collective-permute-start.12 = (bf16[288,256]{1,0:T(8,128)(2,1)S(1)}, bf16[288,256]{1,0:T(8,128)(2,1)S(1)}, u32[]{:S(2)}, u32[]{:S(2)}) collective-permute-start(bf16[288,256]{1,0:T(8,128)(2,1)S(1)} %collective-permute-done.5.refs_6_), channel_id=1, source_target_pairs={{0,1},{1,0},{2,3},{3,2},{4,5},{5,4},{6,7},{7,6},{8,9},{9,8},{10,11... | collective-permute-start | bytes 442376 | tf_op jit(solution)/shard_map/ppermute | solution.py:288
  27.2 1.4 %collective-permute-start.14 = (bf16[288,256]{1,0:T(8,128)(2,1)S(1)}, bf16[288,256]{1,0:T(8,128)(2,1)S(1)}, u32[]{:S(2)}, u32[]{:S(2)}) collective-permute-start(bf16[288,256]{1,0:T(8,128)(2,1)S(1)} %collective-permute-done.9.refs_8_), channel_id=1, source_target_pairs={{0,1},{1,0},{2,3},{3,2},{4,5},{5,4},{6,7},{7,6},{8,9},{9,8},{10,11... | collective-permute-start | bytes 442376 | tf_op jit(solution)/shard_map/ppermute | solution.py:288

commit v23 on v21

--- a/solution.py
+++ b/solution.py
@@ -95,28 +95,43 @@
     gather = (member // fold == group).astype(jnp.bfloat16)
 
     right = [jnp.zeros((tile, width), jnp.float32) for _ in range(tiles)]
-    for s in range(samples):
-        if s % some == 0:
-            large[s // some].wait()
-        normed = []
+    for copy in large:
+        copy.wait()
+
+    def normalise(s):
+        pieces = []
         for low in range(0, residues, BLOCK):
             values = x_ref[s, low : low + BLOCK, :].astype(jnp.float32)
             center = jnp.mean(values, axis=-1, keepdims=True)
             values = values - center
             variance = jnp.mean(jnp.square(values), axis=-1, keepdims=True)
             values = values * lax.rsqrt(variance + 1e-05) * gain_ref[...] + shift_ref[...]
-            normed.append(values.astype(jnp.bfloat16))
-        normed = jnp.concatenate(normed, axis=0)
-        second_here = jnp.where(column % samples == s, second, 0.0).astype(jnp.bfloat16)
-        for t in range(tiles):
-            part = normed[t * tile : (t + 1) * tile]
-            left = jnp.dot(part, first, preferred_element_type=jnp.float32)
-            right[t] += jnp.dot(part, second_here, preferred_element_type=jnp.float32)
-            left = jnp.where(own, left + first_offset, 0.0).astype(jnp.bfloat16)
-            low = t * (tile // fold) * samples + s
-            packed_ref[pl.ds(low, tile // fold, stride=samples), :] = jnp.dot(
-                gather, left, preferred_element_type=jnp.float32
-            )
+            pieces.append(values.astype(jnp.bfloat16))
+        return jnp.concatenate(pieces, axis=0)
+
+    def pack(s, t, left):
+        left = jnp.where(own, left + first_offset, 0.0).astype(jnp.bfloat16)
+        low = t * (tile // fold) * samples + s
+        packed_ref[pl.ds(low, tile // fold, stride=samples), :] = jnp.dot(
+            gather, left, preferred_element_type=jnp.float32
+        )
+
+    normed, lefts = {}, {}
+    for step in range(samples + 2):
+        s = step - 1
+        if 0 <= s < samples:
+            second_here = jnp.where(column % samples == s, second, 0.0).astype(jnp.bfloat16)
+            parts = [normed[s][t * tile : (t + 1) * tile] for t in range(tiles)]
+            lefts[s] = [jnp.dot(x, first, preferred_element_type=jnp.float32) for x in parts]
+            right = [
+                total + jnp.dot(x, second_here, preferred_element_type=jnp.float32)
+                for total, x in zip(right, parts)
+            ]
+        if step < samples:
+            normed[step] = normalise(step)
+        if step >= 2:
+            for t in range(tiles):
+                pack(step - 2, t, lefts[step - 2][t])
     for t in range(tiles):
         value = (right[t].T + second_offset).astype(jnp.bfloat16)
         keep_ref[t * width : (t + 1) * width, :] = value

time: 31.5 us -> 31.6 us (level)
  no operation moved by 1% of the time
where the time goes in v23:
time: 31.6 us; the launch traced here: 31.4 us
  starting transfers between devices  14.5 us (46%)
  waiting for transfers between devices  8.63 us (27%)
  Pallas kernels  8.16 us (26%)
    ppermute x7, starting transfers between devices, per_device(): landed = [lax.ppermute(x, 'row', around) for x in flying]  13.5 us
    ppermute x7, waiting for transfers between devices, per_device(): landed = [lax.ppermute(x, 'row', around) for x in flying]  7.27 us
    pallas_call x1, Pallas kernels, per_device(): pl.pallas_call(functools.partial(pair_kernel, places, gridded, rows_here,...  4.43 us
    pallas_call x1, Pallas kernels, per_device(): pl.pallas_call(functools.partial(project_kernel, rows_here), out_shape=[r...  3.31 us
    ppermute x8, waiting for transfers between devices, swap(): return lax.ppermute(value, 'row', [(r, r ^ 1) for r in range(size)])  1.36 us
    ppermute x8, starting transfers between devices, swap(): return lax.ppermute(value, 'row', [(r, r ^ 1) for r in range(size)])  1.04 us
  transfers between devices with their start and end apart: 15, of which 8 were waited for; matrix products, arithmetic and copies ran while one was open for 0% of the time, Pallas kernels for 1%

profile of v23, /device:TPU:0, one launch (start us, length us, event | category | flops | bytes accessed | tf_op | source)
XLA Modules:
  0.0 31.4 jit_solution(12237863862670205989)
XLA Ops:
  0.0 3.3 %shard_map.91 = (bf16[384,256]{1,0:T(8,128)(2,1)S(1)}, bf16[384,256]{1,0:T(8,128)(2,1)S(1)}) custom-call(bf16[8,256,256]{2,1,0:T(8,128)(2,1)} %x_hbm.1, f32[1,256]{1,0:T(1,128)} %bitcast.10, f32[1,256]{1,0:T(1,128)} %bitcast.11, bf16[32,256]{1,0:T(8,128)(2,1)} %bitcast.8, f32[1,32]{1,0:T(1,128)} %bitcast.12, bf16[32,256]{1,0:T(8,128)(2,1)} %bitcast.9, ...), custom_call_target="tpu_custom_call" | custom-call | flops 536870912 | bytes 1048576 | tf_op jit(solution)/shard_map/pallas_call | solution.py:260
  3.3 0.5 %collective-permute-start = (bf16[384,256]{1,0:T(8,128)(2,1)S(1)}, bf16[384,256]{1,0:T(8,128)(2,1)S(1)}, u32[]{:S(2)}, u32[]{:S(2)}) collective-permute-start(bf16[384,256]{1,0:T(8,128)(2,1)S(1)} %get-tuple-element.24.refs_0_), channel_id=1, source_target_pairs={{0,1},{1,0},{2,3},{3,2},{4,5},{5,4},{6,7},{7,6},{8,9},{9,8},{10,11... | collective-permute-start | bytes 589832 | tf_op jit(solution)/shard_map/ppermute | solution.py:302
  3.8 2.6 %collective-permute-start.1 = (bf16[384,256]{1,0:T(8,128)(2,1)S(1)}, bf16[384,256]{1,0:T(8,128)(2,1)S(1)}, u32[]{:S(2)}, u32[]{:S(2)}) collective-permute-start(bf16[384,256]{1,0:T(8,128)(2,1)S(1)} %get-tuple-element.28), channel_id=1, source_target_pairs={{0,2},{1,5},{2,6},{3,1},{4,0},{5,9},{6,10},{7,3},{8,4},{9,13},{10,... | collective-permute-start | bytes 589832 | tf_op jit(solution)/shard_map/ppermute | solution.py:326
  6.4 0.4 %shard_map.92 = (bf16[128,1024]{1,0:T(8,128)(2,1)S(1)}, f32[1,128]{1,0:T(1,128)S(1)}) custom-call(bf16[1024,128]{1,0:T(8,128)(2,1)S(1)} %copy-done, f32[1,128]{1,0:T(1,128)S(1)} %bitcast.7), custom_call_target="tpu_custom_call" | custom-call | flops 268435456 | bytes 1048576 | tf_op jit(solution)/shard_map/pallas_call | solution.py:304
  6.8 0.0 collective-permute-done.refs_1_
  6.9 1.6 %collective-permute-start.2 = (bf16[352,256]{1,0:T(8,128)(2,1)S(1)}, bf16[352,256]{1,0:T(8,128)(2,1)S(1)}, u32[]{:S(2)}, u32[]{:S(2)}) collective-permute-start(bf16[352,256]{1,0:T(8,128)(2,1)S(1)} %slice.9), channel_id=1, source_target_pairs={{0,2},{1,5},{2,6},{3,1},{4,0},{5,9},{6,10},{7,3},{8,4},{9,13},{10,... | collective-permute-start | bytes 540680 | tf_op jit(solution)/shard_map/ppermute | solution.py:326
  8.5 1.6 %collective-permute-done.1.mine_ref.refs_2_ = bf16[384,256]{1,0:T(8,128)(2,1)S(1)} collective-permute-done((bf16[384,256]{1,0:T(8,128)(2,1)S(1)}, bf16[384,256]{1,0:T(8,128)(2,1)S(1)}, u32[]{:S(2)}, u32[]{:S(2)}) %collective-permute-start.1) | collective-permute-done | bytes 196640 | tf_op jit(solution)/shard_map/ppermute | solution.py:326
  10.1 2.0 %collective-permute-start.3 = (bf16[288,256]{1,0:T(8,128)(2,1)S(1)}, bf16[288,256]{1,0:T(8,128)(2,1)S(1)}, u32[]{:S(2)}, u32[]{:S(2)}) collective-permute-start(bf16[288,256]{1,0:T(8,128)(2,1)S(1)} %slice.12), channel_id=1, source_target_pairs={{0,2},{1,5},{2,6},{3,1},{4,0},{5,9},{6,10},{7,3},{8,4},{9,13},{10,... | collective-permute-start | bytes 442376 | tf_op jit(solution)/shard_map/ppermute | solution.py:326
  12.2 0.3 collective-permute-done.2.theirs_ref.refs_3_
  12.4 1.7 %collective-permute-start.4 = (bf16[384,256]{1,0:T(8,128)(2,1)S(1)}, bf16[384,256]{1,0:T(8,128)(2,1)S(1)}, u32[]{:S(2)}, u32[]{:S(2)}) collective-permute-start(bf16[384,256]{1,0:T(8,128)(2,1)S(1)} %shard_map.93), channel_id=1, source_target_pairs={{0,2},{1,5},{2,6},{3,1},{4,0},{5,9},{6,10},{7,3},{8,4},{9,13},{10,... | collective-permute-start | bytes 589832 | tf_op jit(solution)/shard_map/ppermute | solution.py:326
  14.1 0.0 collective-permute-start.8
  14.1 1.2 %collective-permute-done.3.refs_4_ = bf16[288,256]{1,0:T(8,128)(2,1)S(1)} collective-permute-done((bf16[288,256]{1,0:T(8,128)(2,1)S(1)}, bf16[288,256]{1,0:T(8,128)(2,1)S(1)}, u32[]{:S(2)}, u32[]{:S(2)}) %collective-permute-start.3) | collective-permute-done | bytes 147488 | tf_op jit(solution)/shard_map/ppermute | solution.py:326
  15.3 2.0 %collective-permute-start.5 = (bf16[288,256]{1,0:T(8,128)(2,1)S(1)}, bf16[288,256]{1,0:T(8,128)(2,1)S(1)}, u32[]{:S(2)}, u32[]{:S(2)}) collective-permute-start(bf16[288,256]{1,0:T(8,128)(2,1)S(1)} %collective-permute-done.3.refs_4_), channel_id=1, source_target_pairs={{0,2},{1,5},{2,6},{3,1},{4,0},{5,9},{6,10},{7,3},{8,4},{9,13},{10,... | collective-permute-start | bytes 442376 | tf_op jit(solution)/shard_map/ppermute | solution.py:326
  17.3 0.0 collective-permute-start.7
  17.3 0.8 %collective-permute-done.4.refs_5_ = bf16[384,256]{1,0:T(8,128)(2,1)S(1)} collective-permute-done((bf16[384,256]{1,0:T(8,128)(2,1)S(1)}, bf16[384,256]{1,0:T(8,128)(2,1)S(1)}, u32[]{:S(2)}, u32[]{:S(2)}) %collective-permute-start.4) | collective-permute-done | bytes 196640 | tf_op jit(solution)/shard_map/ppermute | solution.py:326
  18.2 1.7 %collective-permute-start.6 = (bf16[320,256]{1,0:T(8,128)(2,1)S(1)}, bf16[320,256]{1,0:T(8,128)(2,1)S(1)}, u32[]{:S(2)}, u32[]{:S(2)}) collective-permute-start(bf16[320,256]{1,0:T(8,128)(2,1)S(1)} %slice.13), channel_id=1, source_target_pairs={{0,2},{1,5},{2,6},{3,1},{4,0},{5,9},{6,10},{7,3},{8,4},{9,13},{10,... | collective-permute-start | bytes 491528 | tf_op jit(solution)/shard_map/ppermute | solution.py:326
  19.8 0.6 %collective-permute-done.5.refs_6_ = bf16[288,256]{1,0:T(8,128)(2,1)S(1)} collective-permute-done((bf16[288,256]{1,0:T(8,128)(2,1)S(1)}, bf16[288,256]{1,0:T(8,128)(2,1)S(1)}, u32[]{:S(2)}, u32[]{:S(2)}) %collective-permute-start.5) | collective-permute-done | bytes 147488 | tf_op jit(solution)/shard_map/ppermute | solution.py:326
  20.5 2.0 %collective-permute-start.9 = (bf16[288,256]{1,0:T(8,128)(2,1)S(1)}, bf16[288,256]{1,0:T(8,128)(2,1)S(1)}, u32[]{:S(2)}, u32[]{:S(2)}) collective-permute-start(bf16[288,256]{1,0:T(8,128)(2,1)S(1)} %collective-permute-done.5.refs_6_), channel_id=1, source_target_pairs={{0,2},{1,5},{2,6},{3,1},{4,0},{5,9},{6,10},{7,3},{8,4},{9,13},{10,... | collective-permute-start | bytes 442376 | tf_op jit(solution)/shard_map/ppermute | solution.py:326
  22.5 0.0 collective-permute-done.8.refs_10_
  22.5 1.1 %collective-permute-done.6.refs_7_ = bf16[320,256]{1,0:T(8,128)(2,1)S(1)} collective-permute-done((bf16[320,256]{1,0:T(8,128)(2,1)S(1)}, bf16[320,256]{1,0:T(8,128)(2,1)S(1)}, u32[]{:S(2)}, u32[]{:S(2)}) %collective-permute-start.6) | collective-permute-done | bytes 163872 | tf_op jit(solution)/shard_map/ppermute | solution.py:326
  23.6 0.5 %collective-permute-start.12 = (bf16[288,256]{1,0:T(8,128)(2,1)S(1)}, bf16[288,256]{1,0:T(8,128)(2,1)S(1)}, u32[]{:S(2)}, u32[]{:S(2)}) collective-permute-start(bf16[288,256]{1,0:T(8,128)(2,1)S(1)} %collective-permute-done.5.refs_6_), channel_id=1, source_target_pairs={{0,1},{1,0},{2,3},{3,2},{4,5},{5,4},{6,7},{7,6},{8,9},{9,8},{10,11... | collective-permute-start | bytes 442376 | tf_op jit(solution)/shard_map/ppermute | solution.py:302
  24.1 1.6 %collective-permute-done.9.refs_8_ = bf16[288,256]{1,0:T(8,128)(2,1)S(1)} collective-permute-done((bf16[288,256]{1,0:T(8,128)(2,1)S(1)}, bf16[288,256]{1,0:T(8,128)(2,1)S(1)}, u32[]{:S(2)}, u32[]{:S(2)}) %collective-permute-start.9) | collective-permute-done | bytes 147488 | tf_op jit(solution)/shard_map/ppermute | solution.py:326
  25.7 1.3 %collective-permute-done.14.refs_15_ = bf16[288,256]{1,0:T(8,128)(2,1)S(1)} collective-permute-done((bf16[288,256]{1,0:T(8,128)(2,1)S(1)}, bf16[288,256]{1,0:T(8,128)(2,1)S(1)}, u32[]{:S(2)}, u32[]{:S(2)}) %collective-permute-start.14) | collective-permute-done | bytes 147488 | tf_op jit(solution)/shard_map/ppermute | solution.py:302
  27.0 4.4 %shard_map.94 = bf16[16,256,128]{2,1,0:T(8,128)(2,1)} custom-call(bf16[384,256]{1,0:T(8,128)(2,1)S(1)} %get-tuple-element.24.refs_0_, bf16[384,256]{1,0:T(8,128)(2,1)S(1)} %collective-permute-done.refs_1_, bf16[384,256]{1,0:T(8,128)(2,1)S(1)} %collective-permute-done.1.mine_ref.refs_2_, bf16[352,256]{1,0:T(8,128)(2,1)S(1)} %collective-permute-done.2.theirs_ref.refs_3_, ...), custom_call_target="tpu_custom_call" | custom-call | tf_op jit(solution)/shard_map/pallas_call | solution.py:374
  (17 shorter events, 0.1 us)
Async XLA Ops:
  0.0 6.4 %copy-start = (bf16[1024,128]{1,0:T(8,128)(2,1)S(1)}, bf16[1024,128]{1,0:T(8,128)(2,1)}, u32[]{:S(2)}) copy-start(bf16[1024,128]{1,0:T(8,128)(2,1)} %final_ref.1) | copy-start | bytes 786436
  3.3 3.5 %collective-permute-start = (bf16[384,256]{1,0:T(8,128)(2,1)S(1)}, bf16[384,256]{1,0:T(8,128)(2,1)S(1)}, u32[]{:S(2)}, u32[]{:S(2)}) collective-permute-start(bf16[384,256]{1,0:T(8,128)(2,1)S(1)} %get-tuple-element.24.refs_0_), channel_id=1, source_target_pairs={{0,1},{1,0},{2,3},{3,2},{4,5},{5,4},{6,7},{7,6},{8,9},{9,8},{10,11... | collective-permute-start | bytes 589832 | tf_op jit(solution)/shard_map/ppermute | solution.py:302
  3.8 2.6 %copy-start.1 = (f32[128]{0:T(128)S(1)}, f32[128]{0:T(128)}, u32[]{:S(2)}) copy-start(f32[128]{0:T(128)} %param.17) | copy-start | bytes 1540
  3.8 6.3 %collective-permute-start.1 = (bf16[384,256]{1,0:T(8,128)(2,1)S(1)}, bf16[384,256]{1,0:T(8,128)(2,1)S(1)}, u32[]{:S(2)}, u32[]{:S(2)}) collective-permute-start(bf16[384,256]{1,0:T(8,128)(2,1)S(1)} %get-tuple-element.28), channel_id=1, source_target_pairs={{0,2},{1,5},{2,6},{3,1},{4,0},{5,9},{6,10},{7,3},{8,4},{9,13},{10,... | collective-permute-start | bytes 589832 | tf_op jit(solution)/shard_map/ppermute | solution.py:326
  6.9 5.5 %collective-permute-start.2 = (bf16[352,256]{1,0:T(8,128)(2,1)S(1)}, bf16[352,256]{1,0:T(8,128)(2,1)S(1)}, u32[]{:S(2)}, u32[]{:S(2)}) collective-permute-start(bf16[352,256]{1,0:T(8,128)(2,1)S(1)} %slice.9), channel_id=1, source_target_pairs={{0,2},{1,5},{2,6},{3,1},{4,0},{5,9},{6,10},{7,3},{8,4},{9,13},{10,... | collective-permute-start | bytes 540680 | tf_op jit(solution)/shard_map/ppermute | solution.py:326
  10.1 5.2 %collective-permute-start.3 = (bf16[288,256]{1,0:T(8,128)(2,1)S(1)}, bf16[288,256]{1,0:T(8,128)(2,1)S(1)}, u32[]{:S(2)}, u32[]{:S(2)}) collective-permute-start(bf16[288,256]{1,0:T(8,128)(2,1)S(1)} %slice.12), channel_id=1, source_target_pairs={{0,2},{1,5},{2,6},{3,1},{4,0},{5,9},{6,10},{7,3},{8,4},{9,13},{10,... | collective-permute-start | bytes 442376 | tf_op jit(solution)/shard_map/ppermute | solution.py:326
  12.4 5.7 %collective-permute-start.4 = (bf16[384,256]{1,0:T(8,128)(2,1)S(1)}, bf16[384,256]{1,0:T(8,128)(2,1)S(1)}, u32[]{:S(2)}, u32[]{:S(2)}) collective-permute-start(bf16[384,256]{1,0:T(8,128)(2,1)S(1)} %shard_map.93), channel_id=1, source_target_pairs={{0,2},{1,5},{2,6},{3,1},{4,0},{5,9},{6,10},{7,3},{8,4},{9,13},{10,... | collective-permute-start | bytes 589832 | tf_op jit(solution)/shard_map/ppermute | solution.py:326
  14.1 8.4 %collective-permute-start.8 = (bf16[352,256]{1,0:T(8,128)(2,1)S(1)}, bf16[352,256]{1,0:T(8,128)(2,1)S(1)}, u32[]{:S(2)}, u32[]{:S(2)}) collective-permute-start(bf16[352,256]{1,0:T(8,128)(2,1)S(1)} %collective-permute-done.2.theirs_ref.refs_3_), channel_id=1, source_target_pairs={{0,1},{1,0},{2,3},{3,2},{4,5},{5,4},{6,7},{7,6},{8,9},{9,8},{10,11... | collective-permute-start | bytes 540680 | tf_op jit(solution)/shard_map/ppermute | solution.py:302
  15.3 5.1 %collective-permute-start.5 = (bf16[288,256]{1,0:T(8,128)(2,1)S(1)}, bf16[288,256]{1,0:T(8,128)(2,1)S(1)}, u32[]{:S(2)}, u32[]{:S(2)}) collective-permute-start(bf16[288,256]{1,0:T(8,128)(2,1)S(1)} %collective-permute-done.3.refs_4_), channel_id=1, source_target_pairs={{0,2},{1,5},{2,6},{3,1},{4,0},{5,9},{6,10},{7,3},{8,4},{9,13},{10,... | collective-permute-start | bytes 442376 | tf_op jit(solution)/shard_map/ppermute | solution.py:326
  17.3 5.2 %collective-permute-start.7 = (bf16[384,256]{1,0:T(8,128)(2,1)S(1)}, bf16[384,256]{1,0:T(8,128)(2,1)S(1)}, u32[]{:S(2)}, u32[]{:S(2)}) collective-permute-start(bf16[384,256]{1,0:T(8,128)(2,1)S(1)} %collective-permute-done.1.mine_ref.refs_2_), channel_id=1, source_target_pairs={{0,1},{1,0},{2,3},{3,2},{4,5},{5,4},{6,7},{7,6},{8,9},{9,8},{10,11... | collective-permute-start | bytes 589832 | tf_op jit(solution)/shard_map/ppermute | solution.py:302
  18.2 7.5 %collective-permute-start.11 = (bf16[384,256]{1,0:T(8,128)(2,1)S(1)}, bf16[384,256]{1,0:T(8,128)(2,1)S(1)}, u32[]{:S(2)}, u32[]{:S(2)}) collective-permute-start(bf16[384,256]{1,0:T(8,128)(2,1)S(1)} %collective-permute-done.4.refs_5_), channel_id=1, source_target_pairs={{0,1},{1,0},{2,3},{3,2},{4,5},{5,4},{6,7},{7,6},{8,9},{9,8},{10,11... | collective-permute-start | bytes 589832 | tf_op jit(solution)/shard_map/ppermute | solution.py:302
  18.2 5.4 %collective-permute-start.6 = (bf16[320,256]{1,0:T(8,128)(2,1)S(1)}, bf16[320,256]{1,0:T(8,128)(2,1)S(1)}, u32[]{:S(2)}, u32[]{:S(2)}) collective-permute-start(bf16[320,256]{1,0:T(8,128)(2,1)S(1)} %slice.13), channel_id=1, source_target_pairs={{0,2},{1,5},{2,6},{3,1},{4,0},{5,9},{6,10},{7,3},{8,4},{9,13},{10,... | collective-permute-start | bytes 491528 | tf_op jit(solution)/shard_map/ppermute | solution.py:326
  20.5 5.1 %collective-permute-start.9 = (bf16[288,256]{1,0:T(8,128)(2,1)S(1)}, bf16[288,256]{1,0:T(8,128)(2,1)S(1)}, u32[]{:S(2)}, u32[]{:S(2)}) collective-permute-start(bf16[288,256]{1,0:T(8,128)(2,1)S(1)} %collective-permute-done.5.refs_6_), channel_id=1, source_target_pairs={{0,2},{1,5},{2,6},{3,1},{4,0},{5,9},{6,10},{7,3},{8,4},{9,13},{10,... | collective-permute-start | bytes 442376 | tf_op jit(solution)/shard_map/ppermute | solution.py:326
  22.5 3.2 %collective-permute-start.10 = (bf16[288,256]{1,0:T(8,128)(2,1)S(1)}, bf16[288,256]{1,0:T(8,128)(2,1)S(1)}, u32[]{:S(2)}, u32[]{:S(2)}) collective-permute-start(bf16[288,256]{1,0:T(8,128)(2,1)S(1)} %collective-permute-done.3.refs_4_), channel_id=1, source_target_pairs={{0,1},{1,0},{2,3},{3,2},{4,5},{5,4},{6,7},{7,6},{8,9},{9,8},{10,11... | collective-permute-start | bytes 442376 | tf_op jit(solution)/shard_map/ppermute | solution.py:302
  23.6 2.1 %collective-permute-start.13 = (bf16[320,256]{1,0:T(8,128)(2,1)S(1)}, bf16[320,256]{1,0:T(8,128)(2,1)S(1)}, u32[]{:S(2)}, u32[]{:S(2)}) collective-permute-start(bf16[320,256]{1,0:T(8,128)(2,1)S(1)} %collective-permute-done.6.refs_7_), channel_id=1, source_target_pairs={{0,1},{1,0},{2,3},{3,2},{4,5},{5,4},{6,7},{7,6},{8,9},{9,8},{10,11... | collective-permute-start | bytes 491528 | tf_op jit(solution)/shard_map/ppermute | solution.py:302
  23.6 2.1 %collective-permute-start.12 = (bf16[288,256]{1,0:T(8,128)(2,1)S(1)}, bf16[288,256]{1,0:T(8,128)(2,1)S(1)}, u32[]{:S(2)}, u32[]{:S(2)}) collective-permute-start(bf16[288,256]{1,0:T(8,128)(2,1)S(1)} %collective-permute-done.5.refs_6_), channel_id=1, source_target_pairs={{0,1},{1,0},{2,3},{3,2},{4,5},{5,4},{6,7},{7,6},{8,9},{9,8},{10,11... | collective-permute-start | bytes 442376 | tf_op jit(solution)/shard_map/ppermute | solution.py:302
  25.6 1.4 %collective-permute-start.14 = (bf16[288,256]{1,0:T(8,128)(2,1)S(1)}, bf16[288,256]{1,0:T(8,128)(2,1)S(1)}, u32[]{:S(2)}, u32[]{:S(2)}) collective-permute-start(bf16[288,256]{1,0:T(8,128)(2,1)S(1)} %collective-permute-done.9.refs_8_), channel_id=1, source_target_pairs={{0,1},{1,0},{2,3},{3,2},{4,5},{5,4},{6,7},{7,6},{8,9},{9,8},{10,11... | collective-permute-start | bytes 442376 | tf_op jit(solution)/shard_map/ppermute | solution.py:302

commit v24 on v23

--- a/solution.py
+++ b/solution.py
@@ -47,6 +47,7 @@
     second_ref,
     second_offset_ref,
     packed_ref,
+    placed_ref,
     sems,
 ):
     samples, residues, features = x_ref.shape
@@ -95,6 +96,10 @@
     gather = (member // fold == group).astype(jnp.bfloat16)
 
     right = [jnp.zeros((tile, width), jnp.float32) for _ in range(tiles)]
+    for s in range(samples):
+        placed_ref[s * features : (s + 1) * features, :] = jnp.where(
+            column % samples == s, second, 0.0
+        ).astype(jnp.bfloat16)
     for copy in large:
         copy.wait()
 
@@ -120,7 +125,7 @@
     for step in range(samples + 2):
         s = step - 1
         if 0 <= s < samples:
-            second_here = jnp.where(column % samples == s, second, 0.0).astype(jnp.bfloat16)
+            second_here = placed_ref[s * features : (s + 1) * features, :]
             parts = [normed[s][t * tile : (t + 1) * tile] for t in range(tiles)]
             lefts[s] = [jnp.dot(x, first, preferred_element_type=jnp.float32) for x in parts]
             right = [
@@ -271,6 +276,7 @@
             pltpu.VMEM((hidden, features), jnp.bfloat16),
             pltpu.VMEM((1, hidden), jnp.float32),
             pltpu.VMEM((residues * width // LANES + here, LANES), jnp.float32),
+            pltpu.VMEM((here * features, width), jnp.bfloat16),
             pltpu.SemaphoreType.DMA((CHUNKS + 6,)),
         ],
         compiler_params=pltpu.CompilerParams(vmem_limit_bytes=32 * MIB),

time: 31.6 us -> 31.6 us (level)
  no operation moved by 1% of the time
where the time goes in v24:
time: 31.6 us; the launch traced here: 31.4 us
  starting transfers between devices  14.5 us (46%)
  waiting for transfers between devices  8.63 us (27%)
  Pallas kernels  8.16 us (26%)
    ppermute x7, starting transfers between devices, per_device(): landed = [lax.ppermute(x, 'row', around) for x in flying]  13.5 us
    ppermute x7, waiting for transfers between devices, per_device(): landed = [lax.ppermute(x, 'row', around) for x in flying]  7.27 us
    pallas_call x1, Pallas kernels, per_device(): pl.pallas_call(functools.partial(pair_kernel, places, gridded, rows_here,...  4.43 us
    pallas_call x1, Pallas kernels, per_device(): pl.pallas_call(functools.partial(project_kernel, rows_here), out_shape=[r...  3.31 us
    ppermute x8, waiting for transfers between devices, swap(): return lax.ppermute(value, 'row', [(r, r ^ 1) for r in range(size)])  1.36 us
    ppermute x8, starting transfers between devices, swap(): return lax.ppermute(value, 'row', [(r, r ^ 1) for r in range(size)])  1.04 us
  transfers between devices with their start and end apart: 15, of which 8 were waited for; matrix products, arithmetic and copies ran while one was open for 0% of the time, Pallas kernels for 1%

profile of v24, /device:TPU:0, one launch (start us, length us, event | category | flops | bytes accessed | tf_op | source)
XLA Modules:
  0.0 31.4 jit_solution(14854238628300998688)
XLA Ops:
  0.0 3.3 %shard_map.91 = (bf16[384,256]{1,0:T(8,128)(2,1)S(1)}, bf16[384,256]{1,0:T(8,128)(2,1)S(1)}) custom-call(bf16[8,256,256]{2,1,0:T(8,128)(2,1)} %x_hbm.1, f32[1,256]{1,0:T(1,128)} %bitcast.10, f32[1,256]{1,0:T(1,128)} %bitcast.11, bf16[32,256]{1,0:T(8,128)(2,1)} %bitcast.8, f32[1,32]{1,0:T(1,128)} %bitcast.12, bf16[32,256]{1,0:T(8,128)(2,1)} %bitcast.9, ...), custom_call_target="tpu_custom_call" | custom-call | flops 536870912 | bytes 1048576 | tf_op jit(solution)/shard_map/pallas_call | solution.py:265
  3.3 0.5 %collective-permute-start = (bf16[384,256]{1,0:T(8,128)(2,1)S(1)}, bf16[384,256]{1,0:T(8,128)(2,1)S(1)}, u32[]{:S(2)}, u32[]{:S(2)}) collective-permute-start(bf16[384,256]{1,0:T(8,128)(2,1)S(1)} %get-tuple-element.24.refs_0_), channel_id=1, source_target_pairs={{0,1},{1,0},{2,3},{3,2},{4,5},{5,4},{6,7},{7,6},{8,9},{9,8},{10,11... | collective-permute-start | bytes 589832 | tf_op jit(solution)/shard_map/ppermute | solution.py:308
  3.8 2.6 %collective-permute-start.1 = (bf16[384,256]{1,0:T(8,128)(2,1)S(1)}, bf16[384,256]{1,0:T(8,128)(2,1)S(1)}, u32[]{:S(2)}, u32[]{:S(2)}) collective-permute-start(bf16[384,256]{1,0:T(8,128)(2,1)S(1)} %get-tuple-element.28), channel_id=1, source_target_pairs={{0,2},{1,5},{2,6},{3,1},{4,0},{5,9},{6,10},{7,3},{8,4},{9,13},{10,... | collective-permute-start | bytes 589832 | tf_op jit(solution)/shard_map/ppermute | solution.py:332
  6.4 0.4 %shard_map.92 = (bf16[128,1024]{1,0:T(8,128)(2,1)S(1)}, f32[1,128]{1,0:T(1,128)S(1)}) custom-call(bf16[1024,128]{1,0:T(8,128)(2,1)S(1)} %copy-done, f32[1,128]{1,0:T(1,128)S(1)} %bitcast.7), custom_call_target="tpu_custom_call" | custom-call | flops 268435456 | bytes 1048576 | tf_op jit(solution)/shard_map/pallas_call | solution.py:310
  6.8 0.0 collective-permute-done.refs_1_
  6.9 1.6 %collective-permute-start.2 = (bf16[352,256]{1,0:T(8,128)(2,1)S(1)}, bf16[352,256]{1,0:T(8,128)(2,1)S(1)}, u32[]{:S(2)}, u32[]{:S(2)}) collective-permute-start(bf16[352,256]{1,0:T(8,128)(2,1)S(1)} %slice.9), channel_id=1, source_target_pairs={{0,2},{1,5},{2,6},{3,1},{4,0},{5,9},{6,10},{7,3},{8,4},{9,13},{10,... | collective-permute-start | bytes 540680 | tf_op jit(solution)/shard_map/ppermute | solution.py:332
  8.5 1.6 %collective-permute-done.1.mine_ref.refs_2_ = bf16[384,256]{1,0:T(8,128)(2,1)S(1)} collective-permute-done((bf16[384,256]{1,0:T(8,128)(2,1)S(1)}, bf16[384,256]{1,0:T(8,128)(2,1)S(1)}, u32[]{:S(2)}, u32[]{:S(2)}) %collective-permute-start.1) | collective-permute-done | bytes 196640 | tf_op jit(solution)/shard_map/ppermute | solution.py:332
  10.1 2.0 %collective-permute-start.3 = (bf16[288,256]{1,0:T(8,128)(2,1)S(1)}, bf16[288,256]{1,0:T(8,128)(2,1)S(1)}, u32[]{:S(2)}, u32[]{:S(2)}) collective-permute-start(bf16[288,256]{1,0:T(8,128)(2,1)S(1)} %slice.12), channel_id=1, source_target_pairs={{0,2},{1,5},{2,6},{3,1},{4,0},{5,9},{6,10},{7,3},{8,4},{9,13},{10,... | collective-permute-start | bytes 442376 | tf_op jit(solution)/shard_map/ppermute | solution.py:332
  12.2 0.3 collective-permute-done.2.theirs_ref.refs_3_
  12.4 1.7 %collective-permute-start.4 = (bf16[384,256]{1,0:T(8,128)(2,1)S(1)}, bf16[384,256]{1,0:T(8,128)(2,1)S(1)}, u32[]{:S(2)}, u32[]{:S(2)}) collective-permute-start(bf16[384,256]{1,0:T(8,128)(2,1)S(1)} %shard_map.93), channel_id=1, source_target_pairs={{0,2},{1,5},{2,6},{3,1},{4,0},{5,9},{6,10},{7,3},{8,4},{9,13},{10,... | collective-permute-start | bytes 589832 | tf_op jit(solution)/shard_map/ppermute | solution.py:332
  14.1 1.2 %collective-permute-done.3.refs_4_ = bf16[288,256]{1,0:T(8,128)(2,1)S(1)} collective-permute-done((bf16[288,256]{1,0:T(8,128)(2,1)S(1)}, bf16[288,256]{1,0:T(8,128)(2,1)S(1)}, u32[]{:S(2)}, u32[]{:S(2)}) %collective-permute-start.3) | collective-permute-done | bytes 147488 | tf_op jit(solution)/shard_map/ppermute | solution.py:332
  15.3 2.0 %collective-permute-start.5 = (bf16[288,256]{1,0:T(8,128)(2,1)S(1)}, bf16[288,256]{1,0:T(8,128)(2,1)S(1)}, u32[]{:S(2)}, u32[]{:S(2)}) collective-permute-start(bf16[288,256]{1,0:T(8,128)(2,1)S(1)} %collective-permute-done.3.refs_4_), channel_id=1, source_target_pairs={{0,2},{1,5},{2,6},{3,1},{4,0},{5,9},{6,10},{7,3},{8,4},{9,13},{10,... | collective-permute-start | bytes 442376 | tf_op jit(solution)/shard_map/ppermute | solution.py:332
  17.3 0.0 collective-permute-start.7
  17.3 0.8 %collective-permute-done.4.refs_5_ = bf16[384,256]{1,0:T(8,128)(2,1)S(1)} collective-permute-done((bf16[384,256]{1,0:T(8,128)(2,1)S(1)}, bf16[384,256]{1,0:T(8,128)(2,1)S(1)}, u32[]{:S(2)}, u32[]{:S(2)}) %collective-permute-start.4) | collective-permute-done | bytes 196640 | tf_op jit(solution)/shard_map/ppermute | solution.py:332
  18.2 0.0 collective-permute-start.11
  18.2 1.7 %collective-permute-start.6 = (bf16[320,256]{1,0:T(8,128)(2,1)S(1)}, bf16[320,256]{1,0:T(8,128)(2,1)S(1)}, u32[]{:S(2)}, u32[]{:S(2)}) collective-permute-start(bf16[320,256]{1,0:T(8,128)(2,1)S(1)} %slice.13), channel_id=1, source_target_pairs={{0,2},{1,5},{2,6},{3,1},{4,0},{5,9},{6,10},{7,3},{8,4},{9,13},{10,... | collective-permute-start | bytes 491528 | tf_op jit(solution)/shard_map/ppermute | solution.py:332
  19.8 0.6 %collective-permute-done.5.refs_6_ = bf16[288,256]{1,0:T(8,128)(2,1)S(1)} collective-permute-done((bf16[288,256]{1,0:T(8,128)(2,1)S(1)}, bf16[288,256]{1,0:T(8,128)(2,1)S(1)}, u32[]{:S(2)}, u32[]{:S(2)}) %collective-permute-start.5) | collective-permute-done | bytes 147488 | tf_op jit(solution)/shard_map/ppermute | solution.py:332
  20.5 2.0 %collective-permute-start.9 = (bf16[288,256]{1,0:T(8,128)(2,1)S(1)}, bf16[288,256]{1,0:T(8,128)(2,1)S(1)}, u32[]{:S(2)}, u32[]{:S(2)}) collective-permute-start(bf16[288,256]{1,0:T(8,128)(2,1)S(1)} %collective-permute-done.5.refs_6_), channel_id=1, source_target_pairs={{0,2},{1,5},{2,6},{3,1},{4,0},{5,9},{6,10},{7,3},{8,4},{9,13},{10,... | collective-permute-start | bytes 442376 | tf_op jit(solution)/shard_map/ppermute | solution.py:332
  22.5 0.0 collective-permute-done.7.refs_9_
  22.5 1.1 %collective-permute-done.6.refs_7_ = bf16[320,256]{1,0:T(8,128)(2,1)S(1)} collective-permute-done((bf16[320,256]{1,0:T(8,128)(2,1)S(1)}, bf16[320,256]{1,0:T(8,128)(2,1)S(1)}, u32[]{:S(2)}, u32[]{:S(2)}) %collective-permute-start.6) | collective-permute-done | bytes 163872 | tf_op jit(solution)/shard_map/ppermute | solution.py:332
  23.6 0.5 %collective-permute-start.12 = (bf16[288,256]{1,0:T(8,128)(2,1)S(1)}, bf16[288,256]{1,0:T(8,128)(2,1)S(1)}, u32[]{:S(2)}, u32[]{:S(2)}) collective-permute-start(bf16[288,256]{1,0:T(8,128)(2,1)S(1)} %collective-permute-done.5.refs_6_), channel_id=1, source_target_pairs={{0,1},{1,0},{2,3},{3,2},{4,5},{5,4},{6,7},{7,6},{8,9},{9,8},{10,11... | collective-permute-start | bytes 442376 | tf_op jit(solution)/shard_map/ppermute | solution.py:308
  24.1 1.6 %collective-permute-done.9.refs_8_ = bf16[288,256]{1,0:T(8,128)(2,1)S(1)} collective-permute-done((bf16[288,256]{1,0:T(8,128)(2,1)S(1)}, bf16[288,256]{1,0:T(8,128)(2,1)S(1)}, u32[]{:S(2)}, u32[]{:S(2)}) %collective-permute-start.9) | collective-permute-done | bytes 147488 | tf_op jit(solution)/shard_map/ppermute | solution.py:332
  25.7 1.3 %collective-permute-done.14.refs_15_ = bf16[288,256]{1,0:T(8,128)(2,1)S(1)} collective-permute-done((bf16[288,256]{1,0:T(8,128)(2,1)S(1)}, bf16[288,256]{1,0:T(8,128)(2,1)S(1)}, u32[]{:S(2)}, u32[]{:S(2)}) %collective-permute-start.14) | collective-permute-done | bytes 147488 | tf_op jit(solution)/shard_map/ppermute | solution.py:308
  27.0 4.4 %shard_map.94 = bf16[16,256,128]{2,1,0:T(8,128)(2,1)} custom-call(bf16[384,256]{1,0:T(8,128)(2,1)S(1)} %get-tuple-element.24.refs_0_, bf16[384,256]{1,0:T(8,128)(2,1)S(1)} %collective-permute-done.refs_1_, bf16[384,256]{1,0:T(8,128)(2,1)S(1)} %collective-permute-done.1.mine_ref.refs_2_, bf16[352,256]{1,0:T(8,128)(2,1)S(1)} %collective-permute-done.2.theirs_ref.refs_3_, ...), custom_call_target="tpu_custom_call" | custom-call | tf_op jit(solution)/shard_map/pallas_call | solution.py:380
  (17 shorter events, 0.1 us)
Async XLA Ops:
  0.0 6.4 %copy-start = (bf16[1024,128]{1,0:T(8,128)(2,1)S(1)}, bf16[1024,128]{1,0:T(8,128)(2,1)}, u32[]{:S(2)}) copy-start(bf16[1024,128]{1,0:T(8,128)(2,1)} %final_ref.1) | copy-start | bytes 786436
  3.3 3.5 %collective-permute-start = (bf16[384,256]{1,0:T(8,128)(2,1)S(1)}, bf16[384,256]{1,0:T(8,128)(2,1)S(1)}, u32[]{:S(2)}, u32[]{:S(2)}) collective-permute-start(bf16[384,256]{1,0:T(8,128)(2,1)S(1)} %get-tuple-element.24.refs_0_), channel_id=1, source_target_pairs={{0,1},{1,0},{2,3},{3,2},{4,5},{5,4},{6,7},{7,6},{8,9},{9,8},{10,11... | collective-permute-start | bytes 589832 | tf_op jit(solution)/shard_map/ppermute | solution.py:308
  3.8 2.6 %copy-start.1 = (f32[128]{0:T(128)S(1)}, f32[128]{0:T(128)}, u32[]{:S(2)}) copy-start(f32[128]{0:T(128)} %param.17) | copy-start | bytes 1540
  3.8 6.3 %collective-permute-start.1 = (bf16[384,256]{1,0:T(8,128)(2,1)S(1)}, bf16[384,256]{1,0:T(8,128)(2,1)S(1)}, u32[]{:S(2)}, u32[]{:S(2)}) collective-permute-start(bf16[384,256]{1,0:T(8,128)(2,1)S(1)} %get-tuple-element.28), channel_id=1, source_target_pairs={{0,2},{1,5},{2,6},{3,1},{4,0},{5,9},{6,10},{7,3},{8,4},{9,13},{10,... | collective-permute-start | bytes 589832 | tf_op jit(solution)/shard_map/ppermute | solution.py:332
  6.9 5.5 %collective-permute-start.2 = (bf16[352,256]{1,0:T(8,128)(2,1)S(1)}, bf16[352,256]{1,0:T(8,128)(2,1)S(1)}, u32[]{:S(2)}, u32[]{:S(2)}) collective-permute-start(bf16[352,256]{1,0:T(8,128)(2,1)S(1)} %slice.9), channel_id=1, source_target_pairs={{0,2},{1,5},{2,6},{3,1},{4,0},{5,9},{6,10},{7,3},{8,4},{9,13},{10,... | collective-permute-start | bytes 540680 | tf_op jit(solution)/shard_map/ppermute | solution.py:332
  10.1 5.2 %collective-permute-start.3 = (bf16[288,256]{1,0:T(8,128)(2,1)S(1)}, bf16[288,256]{1,0:T(8,128)(2,1)S(1)}, u32[]{:S(2)}, u32[]{:S(2)}) collective-permute-start(bf16[288,256]{1,0:T(8,128)(2,1)S(1)} %slice.12), channel_id=1, source_target_pairs={{0,2},{1,5},{2,6},{3,1},{4,0},{5,9},{6,10},{7,3},{8,4},{9,13},{10,... | collective-permute-start | bytes 442376 | tf_op jit(solution)/shard_map/ppermute | solution.py:332
  12.4 5.7 %collective-permute-start.4 = (bf16[384,256]{1,0:T(8,128)(2,1)S(1)}, bf16[384,256]{1,0:T(8,128)(2,1)S(1)}, u32[]{:S(2)}, u32[]{:S(2)}) collective-permute-start(bf16[384,256]{1,0:T(8,128)(2,1)S(1)} %shard_map.93), channel_id=1, source_target_pairs={{0,2},{1,5},{2,6},{3,1},{4,0},{5,9},{6,10},{7,3},{8,4},{9,13},{10,... | collective-permute-start | bytes 589832 | tf_op jit(solution)/shard_map/ppermute | solution.py:332
  14.1 8.4 %collective-permute-start.8 = (bf16[352,256]{1,0:T(8,128)(2,1)S(1)}, bf16[352,256]{1,0:T(8,128)(2,1)S(1)}, u32[]{:S(2)}, u32[]{:S(2)}) collective-permute-start(bf16[352,256]{1,0:T(8,128)(2,1)S(1)} %collective-permute-done.2.theirs_ref.refs_3_), channel_id=1, source_target_pairs={{0,1},{1,0},{2,3},{3,2},{4,5},{5,4},{6,7},{7,6},{8,9},{9,8},{10,11... | collective-permute-start | bytes 540680 | tf_op jit(solution)/shard_map/ppermute | solution.py:308
  15.3 5.1 %collective-permute-start.5 = (bf16[288,256]{1,0:T(8,128)(2,1)S(1)}, bf16[288,256]{1,0:T(8,128)(2,1)S(1)}, u32[]{:S(2)}, u32[]{:S(2)}) collective-permute-start(bf16[288,256]{1,0:T(8,128)(2,1)S(1)} %collective-permute-done.3.refs_4_), channel_id=1, source_target_pairs={{0,2},{1,5},{2,6},{3,1},{4,0},{5,9},{6,10},{7,3},{8,4},{9,13},{10,... | collective-permute-start | bytes 442376 | tf_op jit(solution)/shard_map/ppermute | solution.py:332
  17.3 5.2 %collective-permute-start.7 = (bf16[384,256]{1,0:T(8,128)(2,1)S(1)}, bf16[384,256]{1,0:T(8,128)(2,1)S(1)}, u32[]{:S(2)}, u32[]{:S(2)}) collective-permute-start(bf16[384,256]{1,0:T(8,128)(2,1)S(1)} %collective-permute-done.1.mine_ref.refs_2_), channel_id=1, source_target_pairs={{0,1},{1,0},{2,3},{3,2},{4,5},{5,4},{6,7},{7,6},{8,9},{9,8},{10,11... | collective-permute-start | bytes 589832 | tf_op jit(solution)/shard_map/ppermute | solution.py:308
  18.2 7.5 %collective-permute-start.11 = (bf16[384,256]{1,0:T(8,128)(2,1)S(1)}, bf16[384,256]{1,0:T(8,128)(2,1)S(1)}, u32[]{:S(2)}, u32[]{:S(2)}) collective-permute-start(bf16[384,256]{1,0:T(8,128)(2,1)S(1)} %collective-permute-done.4.refs_5_), channel_id=1, source_target_pairs={{0,1},{1,0},{2,3},{3,2},{4,5},{5,4},{6,7},{7,6},{8,9},{9,8},{10,11... | collective-permute-start | bytes 589832 | tf_op jit(solution)/shard_map/ppermute | solution.py:308
  18.2 5.4 %collective-permute-start.6 = (bf16[320,256]{1,0:T(8,128)(2,1)S(1)}, bf16[320,256]{1,0:T(8,128)(2,1)S(1)}, u32[]{:S(2)}, u32[]{:S(2)}) collective-permute-start(bf16[320,256]{1,0:T(8,128)(2,1)S(1)} %slice.13), channel_id=1, source_target_pairs={{0,2},{1,5},{2,6},{3,1},{4,0},{5,9},{6,10},{7,3},{8,4},{9,13},{10,... | collective-permute-start | bytes 491528 | tf_op jit(solution)/shard_map/ppermute | solution.py:332
  20.5 5.1 %collective-permute-start.9 = (bf16[288,256]{1,0:T(8,128)(2,1)S(1)}, bf16[288,256]{1,0:T(8,128)(2,1)S(1)}, u32[]{:S(2)}, u32[]{:S(2)}) collective-permute-start(bf16[288,256]{1,0:T(8,128)(2,1)S(1)} %collective-permute-done.5.refs_6_), channel_id=1, source_target_pairs={{0,2},{1,5},{2,6},{3,1},{4,0},{5,9},{6,10},{7,3},{8,4},{9,13},{10,... | collective-permute-start | bytes 442376 | tf_op jit(solution)/shard_map/ppermute | solution.py:332
  22.5 3.2 %collective-permute-start.10 = (bf16[288,256]{1,0:T(8,128)(2,1)S(1)}, bf16[288,256]{1,0:T(8,128)(2,1)S(1)}, u32[]{:S(2)}, u32[]{:S(2)}) collective-permute-start(bf16[288,256]{1,0:T(8,128)(2,1)S(1)} %collective-permute-done.3.refs_4_), channel_id=1, source_target_pairs={{0,1},{1,0},{2,3},{3,2},{4,5},{5,4},{6,7},{7,6},{8,9},{9,8},{10,11... | collective-permute-start | bytes 442376 | tf_op jit(solution)/shard_map/ppermute | solution.py:308
  23.6 2.1 %collective-permute-start.13 = (bf16[320,256]{1,0:T(8,128)(2,1)S(1)}, bf16[320,256]{1,0:T(8,128)(2,1)S(1)}, u32[]{:S(2)}, u32[]{:S(2)}) collective-permute-start(bf16[320,256]{1,0:T(8,128)(2,1)S(1)} %collective-permute-done.6.refs_7_), channel_id=1, source_target_pairs={{0,1},{1,0},{2,3},{3,2},{4,5},{5,4},{6,7},{7,6},{8,9},{9,8},{10,11... | collective-permute-start | bytes 491528 | tf_op jit(solution)/shard_map/ppermute | solution.py:308
  23.6 2.1 %collective-permute-start.12 = (bf16[288,256]{1,0:T(8,128)(2,1)S(1)}, bf16[288,256]{1,0:T(8,128)(2,1)S(1)}, u32[]{:S(2)}, u32[]{:S(2)}) collective-permute-start(bf16[288,256]{1,0:T(8,128)(2,1)S(1)} %collective-permute-done.5.refs_6_), channel_id=1, source_target_pairs={{0,1},{1,0},{2,3},{3,2},{4,5},{5,4},{6,7},{7,6},{8,9},{9,8},{10,11... | collective-permute-start | bytes 442376 | tf_op jit(solution)/shard_map/ppermute | solution.py:308
  25.6 1.4 %collective-permute-start.14 = (bf16[288,256]{1,0:T(8,128)(2,1)S(1)}, bf16[288,256]{1,0:T(8,128)(2,1)S(1)}, u32[]{:S(2)}, u32[]{:S(2)}) collective-permute-start(bf16[288,256]{1,0:T(8,128)(2,1)S(1)} %collective-permute-done.9.refs_8_), channel_id=1, source_target_pairs={{0,1},{1,0},{2,3},{3,2},{4,5},{5,4},{6,7},{7,6},{8,9},{9,8},{10,11... | collective-permute-start | bytes 442376 | tf_op jit(solution)/shard_map/ppermute | solution.py:308

commit v25 on v24

--- a/solution.py
+++ b/solution.py
@@ -189,7 +189,7 @@
     else:
         messages = [refs.pop(0) for _ in places]
         shards = [(messages[n], right, messages[m], left) for n, right, m, left in places]
-    weight_ref, offset_ref, out_hbm, left_ref, outer_ref, out_ref, sems = refs
+    weight_ref, offset_ref, out_hbm, outer_ref, out_ref, sems = refs
     tile = shards[0][0].shape[1]
     here = samples // count
     span = rows_here * hidden
@@ -202,9 +202,8 @@
         pieces.append(
             jnp.concatenate([piece[n * here : (n + 1) * here] for n in range(span // tile)], axis=1)
         )
-    left_ref[...] = jnp.concatenate(pieces, axis=0).T.astype(jnp.bfloat16)
-
-    left = left_ref[...]
+    left = jnp.concatenate(pieces, axis=0).T.astype(jnp.bfloat16)
+
     for e in range(0, hidden, 2):
         both = [
             ref[base + e * here : base + (e + 2) * here, :].astype(jnp.float32)
@@ -225,10 +224,14 @@
         value = jnp.dot(weight_ref[...], outer_ref[i], preferred_element_type=jnp.float32)
         value = value.T * (1.0 / samples) + offset_ref[...]
         out_ref[i] = value.astype(jnp.bfloat16)
-        copies.append(
-            pltpu.make_async_copy(out_ref.at[i], out_hbm.at[i, pl.ds(first, tile)], sems.at[i])
-        )
-        copies[-1].start()
+        if i % 2:
+            rows = pl.ds(i - 1, 2)
+            copies.append(
+                pltpu.make_async_copy(
+                    out_ref.at[rows], out_hbm.at[rows, pl.ds(first, tile)], sems.at[i // 2]
+                )
+            )
+            copies[-1].start()
     for copy in copies:
         copy.wait()
 
@@ -384,7 +387,6 @@
         in_specs=specs,
         out_specs=hbm,
         scratch_shapes=[
-            pltpu.VMEM((rows_here * hidden, samples), jnp.bfloat16),
             pltpu.VMEM((rows_here, hidden * hidden, tile), jnp.bfloat16),
             pltpu.VMEM((rows_here, tile, channels), jnp.bfloat16),
             pltpu.SemaphoreType.DMA((rows_here,)),

time: 31.6 us -> 31.6 us (level)
  no operation moved by 1% of the time
where the time goes in v25:
time: 31.6 us; the launch traced here: 31.5 us
  starting transfers between devices  14.5 us (46%)
  waiting for transfers between devices  8.63 us (27%)
  Pallas kernels  8.17 us (26%)
    ppermute x7, starting transfers between devices, per_device(): landed = [lax.ppermute(x, 'row', around) for x in flying]  13.5 us
    ppermute x7, waiting for transfers between devices, per_device(): landed = [lax.ppermute(x, 'row', around) for x in flying]  7.27 us
    pallas_call x1, Pallas kernels, per_device(): pl.pallas_call(functools.partial(pair_kernel, places, gridded, rows_here,...  4.44 us
    pallas_call x1, Pallas kernels, per_device(): pl.pallas_call(functools.partial(project_kernel, rows_here), out_shape=[r...  3.31 us
    ppermute x8, waiting for transfers between devices, swap(): return lax.ppermute(value, 'row', [(r, r ^ 1) for r in range(size)])  1.36 us
    ppermute x8, starting transfers between devices, swap(): return lax.ppermute(value, 'row', [(r, r ^ 1) for r in range(size)])  1.04 us
  transfers between devices with their start and end apart: 15, of which 8 were waited for; matrix products, arithmetic and copies ran while one was open for 0% of the time, Pallas kernels for 1%

profile of v25, /device:TPU:0, one launch (start us, length us, event | category | flops | bytes accessed | tf_op | source)
XLA Modules:
  0.0 31.5 jit_solution(14029431307068191578)
XLA Ops:
  0.0 3.3 %shard_map.91 = (bf16[384,256]{1,0:T(8,128)(2,1)S(1)}, bf16[384,256]{1,0:T(8,128)(2,1)S(1)}) custom-call(bf16[8,256,256]{2,1,0:T(8,128)(2,1)} %x_hbm.1, f32[1,256]{1,0:T(1,128)} %bitcast.10, f32[1,256]{1,0:T(1,128)} %bitcast.11, bf16[32,256]{1,0:T(8,128)(2,1)} %bitcast.8, f32[1,32]{1,0:T(1,128)} %bitcast.12, bf16[32,256]{1,0:T(8,128)(2,1)} %bitcast.9, ...), custom_call_target="tpu_custom_call" | custom-call | flops 536870912 | bytes 1048576 | tf_op jit(solution)/shard_map/pallas_call | solution.py:268
  3.3 0.5 %collective-permute-start = (bf16[384,256]{1,0:T(8,128)(2,1)S(1)}, bf16[384,256]{1,0:T(8,128)(2,1)S(1)}, u32[]{:S(2)}, u32[]{:S(2)}) collective-permute-start(bf16[384,256]{1,0:T(8,128)(2,1)S(1)} %get-tuple-element.24.refs_0_), channel_id=1, source_target_pairs={{0,1},{1,0},{2,3},{3,2},{4,5},{5,4},{6,7},{7,6},{8,9},{9,8},{10,11... | collective-permute-start | bytes 589832 | tf_op jit(solution)/shard_map/ppermute | solution.py:311
  3.8 2.6 %collective-permute-start.1 = (bf16[384,256]{1,0:T(8,128)(2,1)S(1)}, bf16[384,256]{1,0:T(8,128)(2,1)S(1)}, u32[]{:S(2)}, u32[]{:S(2)}) collective-permute-start(bf16[384,256]{1,0:T(8,128)(2,1)S(1)} %get-tuple-element.28), channel_id=1, source_target_pairs={{0,2},{1,5},{2,6},{3,1},{4,0},{5,9},{6,10},{7,3},{8,4},{9,13},{10,... | collective-permute-start | bytes 589832 | tf_op jit(solution)/shard_map/ppermute | solution.py:335
  6.4 0.4 %shard_map.92 = (bf16[128,1024]{1,0:T(8,128)(2,1)S(1)}, f32[1,128]{1,0:T(1,128)S(1)}) custom-call(bf16[1024,128]{1,0:T(8,128)(2,1)S(1)} %copy-done, f32[1,128]{1,0:T(1,128)S(1)} %bitcast.7), custom_call_target="tpu_custom_call" | custom-call | flops 268435456 | bytes 1048576 | tf_op jit(solution)/shard_map/pallas_call | solution.py:313
  6.9 1.6 %collective-permute-start.2 = (bf16[352,256]{1,0:T(8,128)(2,1)S(1)}, bf16[352,256]{1,0:T(8,128)(2,1)S(1)}, u32[]{:S(2)}, u32[]{:S(2)}) collective-permute-start(bf16[352,256]{1,0:T(8,128)(2,1)S(1)} %slice.9), channel_id=1, source_target_pairs={{0,2},{1,5},{2,6},{3,1},{4,0},{5,9},{6,10},{7,3},{8,4},{9,13},{10,... | collective-permute-start | bytes 540680 | tf_op jit(solution)/shard_map/ppermute | solution.py:335
  8.5 1.6 %collective-permute-done.1.mine_ref.refs_2_ = bf16[384,256]{1,0:T(8,128)(2,1)S(1)} collective-permute-done((bf16[384,256]{1,0:T(8,128)(2,1)S(1)}, bf16[384,256]{1,0:T(8,128)(2,1)S(1)}, u32[]{:S(2)}, u32[]{:S(2)}) %collective-permute-start.1) | collective-permute-done | bytes 196640 | tf_op jit(solution)/shard_map/ppermute | solution.py:335
  10.1 2.0 %collective-permute-start.3 = (bf16[288,256]{1,0:T(8,128)(2,1)S(1)}, bf16[288,256]{1,0:T(8,128)(2,1)S(1)}, u32[]{:S(2)}, u32[]{:S(2)}) collective-permute-start(bf16[288,256]{1,0:T(8,128)(2,1)S(1)} %slice.12), channel_id=1, source_target_pairs={{0,2},{1,5},{2,6},{3,1},{4,0},{5,9},{6,10},{7,3},{8,4},{9,13},{10,... | collective-permute-start | bytes 442376 | tf_op jit(solution)/shard_map/ppermute | solution.py:335
  12.2 0.3 collective-permute-done.2.theirs_ref.refs_3_
  12.4 1.7 %collective-permute-start.4 = (bf16[384,256]{1,0:T(8,128)(2,1)S(1)}, bf16[384,256]{1,0:T(8,128)(2,1)S(1)}, u32[]{:S(2)}, u32[]{:S(2)}) collective-permute-start(bf16[384,256]{1,0:T(8,128)(2,1)S(1)} %shard_map.93), channel_id=1, source_target_pairs={{0,2},{1,5},{2,6},{3,1},{4,0},{5,9},{6,10},{7,3},{8,4},{9,13},{10,... | collective-permute-start | bytes 589832 | tf_op jit(solution)/shard_map/ppermute | solution.py:335
  14.1 0.0 collective-permute-start.8
  14.1 1.2 %collective-permute-done.3.refs_4_ = bf16[288,256]{1,0:T(8,128)(2,1)S(1)} collective-permute-done((bf16[288,256]{1,0:T(8,128)(2,1)S(1)}, bf16[288,256]{1,0:T(8,128)(2,1)S(1)}, u32[]{:S(2)}, u32[]{:S(2)}) %collective-permute-start.3) | collective-permute-done | bytes 147488 | tf_op jit(solution)/shard_map/ppermute | solution.py:335
  15.3 2.0 %collective-permute-start.5 = (bf16[288,256]{1,0:T(8,128)(2,1)S(1)}, bf16[288,256]{1,0:T(8,128)(2,1)S(1)}, u32[]{:S(2)}, u32[]{:S(2)}) collective-permute-start(bf16[288,256]{1,0:T(8,128)(2,1)S(1)} %collective-permute-done.3.refs_4_), channel_id=1, source_target_pairs={{0,2},{1,5},{2,6},{3,1},{4,0},{5,9},{6,10},{7,3},{8,4},{9,13},{10,... | collective-permute-start | bytes 442376 | tf_op jit(solution)/shard_map/ppermute | solution.py:335
  17.3 0.8 %collective-permute-done.4.refs_5_ = bf16[384,256]{1,0:T(8,128)(2,1)S(1)} collective-permute-done((bf16[384,256]{1,0:T(8,128)(2,1)S(1)}, bf16[384,256]{1,0:T(8,128)(2,1)S(1)}, u32[]{:S(2)}, u32[]{:S(2)}) %collective-permute-start.4) | collective-permute-done | bytes 196640 | tf_op jit(solution)/shard_map/ppermute | solution.py:335
  18.2 0.0 collective-permute-start.11
  18.2 1.7 %collective-permute-start.6 = (bf16[320,256]{1,0:T(8,128)(2,1)S(1)}, bf16[320,256]{1,0:T(8,128)(2,1)S(1)}, u32[]{:S(2)}, u32[]{:S(2)}) collective-permute-start(bf16[320,256]{1,0:T(8,128)(2,1)S(1)} %slice.13), channel_id=1, source_target_pairs={{0,2},{1,5},{2,6},{3,1},{4,0},{5,9},{6,10},{7,3},{8,4},{9,13},{10,... | collective-permute-start | bytes 491528 | tf_op jit(solution)/shard_map/ppermute | solution.py:335
  19.8 0.6 %collective-permute-done.5.refs_6_ = bf16[288,256]{1,0:T(8,128)(2,1)S(1)} collective-permute-done((bf16[288,256]{1,0:T(8,128)(2,1)S(1)}, bf16[288,256]{1,0:T(8,128)(2,1)S(1)}, u32[]{:S(2)}, u32[]{:S(2)}) %collective-permute-start.5) | collective-permute-done | bytes 147488 | tf_op jit(solution)/shard_map/ppermute | solution.py:335
  20.5 2.0 %collective-permute-start.9 = (bf16[288,256]{1,0:T(8,128)(2,1)S(1)}, bf16[288,256]{1,0:T(8,128)(2,1)S(1)}, u32[]{:S(2)}, u32[]{:S(2)}) collective-permute-start(bf16[288,256]{1,0:T(8,128)(2,1)S(1)} %collective-permute-done.5.refs_6_), channel_id=1, source_target_pairs={{0,2},{1,5},{2,6},{3,1},{4,0},{5,9},{6,10},{7,3},{8,4},{9,13},{10,... | collective-permute-start | bytes 442376 | tf_op jit(solution)/shard_map/ppermute | solution.py:335
  22.5 1.1 %collective-permute-done.6.refs_7_ = bf16[320,256]{1,0:T(8,128)(2,1)S(1)} collective-permute-done((bf16[320,256]{1,0:T(8,128)(2,1)S(1)}, bf16[320,256]{1,0:T(8,128)(2,1)S(1)}, u32[]{:S(2)}, u32[]{:S(2)}) %collective-permute-start.6) | collective-permute-done | bytes 163872 | tf_op jit(solution)/shard_map/ppermute | solution.py:335
  23.6 0.5 %collective-permute-start.12 = (bf16[288,256]{1,0:T(8,128)(2,1)S(1)}, bf16[288,256]{1,0:T(8,128)(2,1)S(1)}, u32[]{:S(2)}, u32[]{:S(2)}) collective-permute-start(bf16[288,256]{1,0:T(8,128)(2,1)S(1)} %collective-permute-done.5.refs_6_), channel_id=1, source_target_pairs={{0,1},{1,0},{2,3},{3,2},{4,5},{5,4},{6,7},{7,6},{8,9},{9,8},{10,11... | collective-permute-start | bytes 442376 | tf_op jit(solution)/shard_map/ppermute | solution.py:311
  24.1 1.6 %collective-permute-done.9.refs_8_ = bf16[288,256]{1,0:T(8,128)(2,1)S(1)} collective-permute-done((bf16[288,256]{1,0:T(8,128)(2,1)S(1)}, bf16[288,256]{1,0:T(8,128)(2,1)S(1)}, u32[]{:S(2)}, u32[]{:S(2)}) %collective-permute-start.9) | collective-permute-done | bytes 147488 | tf_op jit(solution)/shard_map/ppermute | solution.py:335
  25.6 0.0 collective-permute-done.10.refs_11_
  25.6 0.0 collective-permute-done.12.refs_13_
  25.7 1.3 %collective-permute-done.14.refs_15_ = bf16[288,256]{1,0:T(8,128)(2,1)S(1)} collective-permute-done((bf16[288,256]{1,0:T(8,128)(2,1)S(1)}, bf16[288,256]{1,0:T(8,128)(2,1)S(1)}, u32[]{:S(2)}, u32[]{:S(2)}) %collective-permute-start.14) | collective-permute-done | bytes 147488 | tf_op jit(solution)/shard_map/ppermute | solution.py:311
  27.0 4.4 %shard_map.94 = bf16[16,256,128]{2,1,0:T(8,128)(2,1)} custom-call(bf16[384,256]{1,0:T(8,128)(2,1)S(1)} %get-tuple-element.24.refs_0_, bf16[384,256]{1,0:T(8,128)(2,1)S(1)} %collective-permute-done.refs_1_, bf16[384,256]{1,0:T(8,128)(2,1)S(1)} %collective-permute-done.1.mine_ref.refs_2_, bf16[352,256]{1,0:T(8,128)(2,1)S(1)} %collective-permute-done.2.theirs_ref.refs_3_, ...), custom_call_target="tpu_custom_call" | custom-call | tf_op jit(solution)/shard_map/pallas_call | solution.py:383
  (17 shorter events, 0.1 us)
Async XLA Ops:
  0.0 6.4 %copy-start = (bf16[1024,128]{1,0:T(8,128)(2,1)S(1)}, bf16[1024,128]{1,0:T(8,128)(2,1)}, u32[]{:S(2)}) copy-start(bf16[1024,128]{1,0:T(8,128)(2,1)} %final_ref.1) | copy-start | bytes 786436
  3.3 3.5 %collective-permute-start = (bf16[384,256]{1,0:T(8,128)(2,1)S(1)}, bf16[384,256]{1,0:T(8,128)(2,1)S(1)}, u32[]{:S(2)}, u32[]{:S(2)}) collective-permute-start(bf16[384,256]{1,0:T(8,128)(2,1)S(1)} %get-tuple-element.24.refs_0_), channel_id=1, source_target_pairs={{0,1},{1,0},{2,3},{3,2},{4,5},{5,4},{6,7},{7,6},{8,9},{9,8},{10,11... | collective-permute-start | bytes 589832 | tf_op jit(solution)/shard_map/ppermute | solution.py:311
  3.8 2.6 %copy-start.1 = (f32[128]{0:T(128)S(1)}, f32[128]{0:T(128)}, u32[]{:S(2)}) copy-start(f32[128]{0:T(128)} %param.17) | copy-start | bytes 1540
  3.8 6.3 %collective-permute-start.1 = (bf16[384,256]{1,0:T(8,128)(2,1)S(1)}, bf16[384,256]{1,0:T(8,128)(2,1)S(1)}, u32[]{:S(2)}, u32[]{:S(2)}) collective-permute-start(bf16[384,256]{1,0:T(8,128)(2,1)S(1)} %get-tuple-element.28), channel_id=1, source_target_pairs={{0,2},{1,5},{2,6},{3,1},{4,0},{5,9},{6,10},{7,3},{8,4},{9,13},{10,... | collective-permute-start | bytes 589832 | tf_op jit(solution)/shard_map/ppermute | solution.py:335
  6.9 5.5 %collective-permute-start.2 = (bf16[352,256]{1,0:T(8,128)(2,1)S(1)}, bf16[352,256]{1,0:T(8,128)(2,1)S(1)}, u32[]{:S(2)}, u32[]{:S(2)}) collective-permute-start(bf16[352,256]{1,0:T(8,128)(2,1)S(1)} %slice.9), channel_id=1, source_target_pairs={{0,2},{1,5},{2,6},{3,1},{4,0},{5,9},{6,10},{7,3},{8,4},{9,13},{10,... | collective-permute-start | bytes 540680 | tf_op jit(solution)/shard_map/ppermute | solution.py:335
  10.1 5.2 %collective-permute-start.3 = (bf16[288,256]{1,0:T(8,128)(2,1)S(1)}, bf16[288,256]{1,0:T(8,128)(2,1)S(1)}, u32[]{:S(2)}, u32[]{:S(2)}) collective-permute-start(bf16[288,256]{1,0:T(8,128)(2,1)S(1)} %slice.12), channel_id=1, source_target_pairs={{0,2},{1,5},{2,6},{3,1},{4,0},{5,9},{6,10},{7,3},{8,4},{9,13},{10,... | collective-permute-start | bytes 442376 | tf_op jit(solution)/shard_map/ppermute | solution.py:335
  12.4 5.7 %collective-permute-start.4 = (bf16[384,256]{1,0:T(8,128)(2,1)S(1)}, bf16[384,256]{1,0:T(8,128)(2,1)S(1)}, u32[]{:S(2)}, u32[]{:S(2)}) collective-permute-start(bf16[384,256]{1,0:T(8,128)(2,1)S(1)} %shard_map.93), channel_id=1, source_target_pairs={{0,2},{1,5},{2,6},{3,1},{4,0},{5,9},{6,10},{7,3},{8,4},{9,13},{10,... | collective-permute-start | bytes 589832 | tf_op jit(solution)/shard_map/ppermute | solution.py:335
  14.1 8.4 %collective-permute-start.8 = (bf16[352,256]{1,0:T(8,128)(2,1)S(1)}, bf16[352,256]{1,0:T(8,128)(2,1)S(1)}, u32[]{:S(2)}, u32[]{:S(2)}) collective-permute-start(bf16[352,256]{1,0:T(8,128)(2,1)S(1)} %collective-permute-done.2.theirs_ref.refs_3_), channel_id=1, source_target_pairs={{0,1},{1,0},{2,3},{3,2},{4,5},{5,4},{6,7},{7,6},{8,9},{9,8},{10,11... | collective-permute-start | bytes 540680 | tf_op jit(solution)/shard_map/ppermute | solution.py:311
  15.3 5.1 %collective-permute-start.5 = (bf16[288,256]{1,0:T(8,128)(2,1)S(1)}, bf16[288,256]{1,0:T(8,128)(2,1)S(1)}, u32[]{:S(2)}, u32[]{:S(2)}) collective-permute-start(bf16[288,256]{1,0:T(8,128)(2,1)S(1)} %collective-permute-done.3.refs_4_), channel_id=1, source_target_pairs={{0,2},{1,5},{2,6},{3,1},{4,0},{5,9},{6,10},{7,3},{8,4},{9,13},{10,... | collective-permute-start | bytes 442376 | tf_op jit(solution)/shard_map/ppermute | solution.py:335
  17.3 5.2 %collective-permute-start.7 = (bf16[384,256]{1,0:T(8,128)(2,1)S(1)}, bf16[384,256]{1,0:T(8,128)(2,1)S(1)}, u32[]{:S(2)}, u32[]{:S(2)}) collective-permute-start(bf16[384,256]{1,0:T(8,128)(2,1)S(1)} %collective-permute-done.1.mine_ref.refs_2_), channel_id=1, source_target_pairs={{0,1},{1,0},{2,3},{3,2},{4,5},{5,4},{6,7},{7,6},{8,9},{9,8},{10,11... | collective-permute-start | bytes 589832 | tf_op jit(solution)/shard_map/ppermute | solution.py:311
  18.2 7.5 %collective-permute-start.11 = (bf16[384,256]{1,0:T(8,128)(2,1)S(1)}, bf16[384,256]{1,0:T(8,128)(2,1)S(1)}, u32[]{:S(2)}, u32[]{:S(2)}) collective-permute-start(bf16[384,256]{1,0:T(8,128)(2,1)S(1)} %collective-permute-done.4.refs_5_), channel_id=1, source_target_pairs={{0,1},{1,0},{2,3},{3,2},{4,5},{5,4},{6,7},{7,6},{8,9},{9,8},{10,11... | collective-permute-start | bytes 589832 | tf_op jit(solution)/shard_map/ppermute | solution.py:311
  18.2 5.4 %collective-permute-start.6 = (bf16[320,256]{1,0:T(8,128)(2,1)S(1)}, bf16[320,256]{1,0:T(8,128)(2,1)S(1)}, u32[]{:S(2)}, u32[]{:S(2)}) collective-permute-start(bf16[320,256]{1,0:T(8,128)(2,1)S(1)} %slice.13), channel_id=1, source_target_pairs={{0,2},{1,5},{2,6},{3,1},{4,0},{5,9},{6,10},{7,3},{8,4},{9,13},{10,... | collective-permute-start | bytes 491528 | tf_op jit(solution)/shard_map/ppermute | solution.py:335
  20.5 5.1 %collective-permute-start.9 = (bf16[288,256]{1,0:T(8,128)(2,1)S(1)}, bf16[288,256]{1,0:T(8,128)(2,1)S(1)}, u32[]{:S(2)}, u32[]{:S(2)}) collective-permute-start(bf16[288,256]{1,0:T(8,128)(2,1)S(1)} %collective-permute-done.5.refs_6_), channel_id=1, source_target_pairs={{0,2},{1,5},{2,6},{3,1},{4,0},{5,9},{6,10},{7,3},{8,4},{9,13},{10,... | collective-permute-start | bytes 442376 | tf_op jit(solution)/shard_map/ppermute | solution.py:335
  22.5 3.2 %collective-permute-start.10 = (bf16[288,256]{1,0:T(8,128)(2,1)S(1)}, bf16[288,256]{1,0:T(8,128)(2,1)S(1)}, u32[]{:S(2)}, u32[]{:S(2)}) collective-permute-start(bf16[288,256]{1,0:T(8,128)(2,1)S(1)} %collective-permute-done.3.refs_4_), channel_id=1, source_target_pairs={{0,1},{1,0},{2,3},{3,2},{4,5},{5,4},{6,7},{7,6},{8,9},{9,8},{10,11... | collective-permute-start | bytes 442376 | tf_op jit(solution)/shard_map/ppermute | solution.py:311
  23.6 2.1 %collective-permute-start.13 = (bf16[320,256]{1,0:T(8,128)(2,1)S(1)}, bf16[320,256]{1,0:T(8,128)(2,1)S(1)}, u32[]{:S(2)}, u32[]{:S(2)}) collective-permute-start(bf16[320,256]{1,0:T(8,128)(2,1)S(1)} %collective-permute-done.6.refs_7_), channel_id=1, source_target_pairs={{0,1},{1,0},{2,3},{3,2},{4,5},{5,4},{6,7},{7,6},{8,9},{9,8},{10,11... | collective-permute-start | bytes 491528 | tf_op jit(solution)/shard_map/ppermute | solution.py:311
  23.6 2.1 %collective-permute-start.12 = (bf16[288,256]{1,0:T(8,128)(2,1)S(1)}, bf16[288,256]{1,0:T(8,128)(2,1)S(1)}, u32[]{:S(2)}, u32[]{:S(2)}) collective-permute-start(bf16[288,256]{1,0:T(8,128)(2,1)S(1)} %collective-permute-done.5.refs_6_), channel_id=1, source_target_pairs={{0,1},{1,0},{2,3},{3,2},{4,5},{5,4},{6,7},{7,6},{8,9},{9,8},{10,11... | collective-permute-start | bytes 442376 | tf_op jit(solution)/shard_map/ppermute | solution.py:311
  25.6 1.4 %collective-permute-start.14 = (bf16[288,256]{1,0:T(8,128)(2,1)S(1)}, bf16[288,256]{1,0:T(8,128)(2,1)S(1)}, u32[]{:S(2)}, u32[]{:S(2)}) collective-permute-start(bf16[288,256]{1,0:T(8,128)(2,1)S(1)} %collective-permute-done.9.refs_8_), channel_id=1, source_target_pairs={{0,1},{1,0},{2,3},{3,2},{4,5},{5,4},{6,7},{7,6},{8,9},{9,8},{10,11... | collective-permute-start | bytes 442376 | tf_op jit(solution)/shard_map/ppermute | solution.py:311

commit v26 on v23

--- a/solution.py
+++ b/solution.py
@@ -10,7 +10,7 @@
 
 MIB = 1024 * 1024
 LANES = 128
-CHUNKS = 1
+CHUNKS = 2
 BLOCK = 64
 
 
@@ -95,9 +95,6 @@
     gather = (member // fold == group).astype(jnp.bfloat16)
 
     right = [jnp.zeros((tile, width), jnp.float32) for _ in range(tiles)]
-    for copy in large:
-        copy.wait()
-
     def normalise(s):
         pieces = []
         for low in range(0, residues, BLOCK):
@@ -128,6 +125,8 @@
                 for total, x in zip(right, parts)
             ]
         if step < samples:
+            if step % some == 0:
+                large[step // some].wait()
             normed[step] = normalise(step)
         if step >= 2:
             for t in range(tiles):

time: 31.6 us -> 31.6 us (level)
  no operation moved by 1% of the time
where the time goes in v26:
time: 31.6 us; the launch traced here: 31.4 us
  starting transfers between devices  14.5 us (46%)
  waiting for transfers between devices  8.64 us (27%)
  Pallas kernels  8.14 us (26%)
    ppermute x7, starting transfers between devices, per_device(): landed = [lax.ppermute(x, 'row', around) for x in flying]  13.5 us
    ppermute x7, waiting for transfers between devices, per_device(): landed = [lax.ppermute(x, 'row', around) for x in flying]  7.28 us
    pallas_call x1, Pallas kernels, per_device(): pl.pallas_call(functools.partial(pair_kernel, places, gridded, rows_here,...  4.43 us
    pallas_call x1, Pallas kernels, per_device(): pl.pallas_call(functools.partial(project_kernel, rows_here), out_shape=[r...  3.29 us
    ppermute x8, waiting for transfers between devices, swap(): return lax.ppermute(value, 'row', [(r, r ^ 1) for r in range(size)])  1.36 us
    ppermute x8, starting transfers between devices, swap(): return lax.ppermute(value, 'row', [(r, r ^ 1) for r in range(size)])  1.05 us
  transfers between devices with their start and end apart: 15, of which 8 were waited for; matrix products, arithmetic and copies ran while one was open for 0% of the time, Pallas kernels for 1%

profile of v26, /device:TPU:0, one launch (start us, length us, event | category | flops | bytes accessed | tf_op | source)
XLA Modules:
  0.0 31.4 jit_solution(16784683907868943466)
XLA Ops:
  0.0 3.3 %shard_map.91 = (bf16[384,256]{1,0:T(8,128)(2,1)S(1)}, bf16[384,256]{1,0:T(8,128)(2,1)S(1)}) custom-call(bf16[8,256,256]{2,1,0:T(8,128)(2,1)} %x_hbm.1, f32[1,256]{1,0:T(1,128)} %bitcast.10, f32[1,256]{1,0:T(1,128)} %bitcast.11, bf16[32,256]{1,0:T(8,128)(2,1)} %bitcast.8, f32[1,32]{1,0:T(1,128)} %bitcast.12, bf16[32,256]{1,0:T(8,128)(2,1)} %bitcast.9, ...), custom_call_target="tpu_custom_call" | custom-call | flops 536870912 | bytes 1048576 | tf_op jit(solution)/shard_map/pallas_call | solution.py:259
  3.3 0.5 %collective-permute-start = (bf16[384,256]{1,0:T(8,128)(2,1)S(1)}, bf16[384,256]{1,0:T(8,128)(2,1)S(1)}, u32[]{:S(2)}, u32[]{:S(2)}) collective-permute-start(bf16[384,256]{1,0:T(8,128)(2,1)S(1)} %get-tuple-element.24.refs_0_), channel_id=1, source_target_pairs={{0,1},{1,0},{2,3},{3,2},{4,5},{5,4},{6,7},{7,6},{8,9},{9,8},{10,11... | collective-permute-start | bytes 589832 | tf_op jit(solution)/shard_map/ppermute | solution.py:301
  3.8 2.6 %collective-permute-start.1 = (bf16[384,256]{1,0:T(8,128)(2,1)S(1)}, bf16[384,256]{1,0:T(8,128)(2,1)S(1)}, u32[]{:S(2)}, u32[]{:S(2)}) collective-permute-start(bf16[384,256]{1,0:T(8,128)(2,1)S(1)} %get-tuple-element.28), channel_id=1, source_target_pairs={{0,2},{1,5},{2,6},{3,1},{4,0},{5,9},{6,10},{7,3},{8,4},{9,13},{10,... | collective-permute-start | bytes 589832 | tf_op jit(solution)/shard_map/ppermute | solution.py:325
  6.4 0.4 %shard_map.92 = (bf16[128,1024]{1,0:T(8,128)(2,1)S(1)}, f32[1,128]{1,0:T(1,128)S(1)}) custom-call(bf16[1024,128]{1,0:T(8,128)(2,1)S(1)} %copy-done, f32[1,128]{1,0:T(1,128)S(1)} %bitcast.7), custom_call_target="tpu_custom_call" | custom-call | flops 268435456 | bytes 1048576 | tf_op jit(solution)/shard_map/pallas_call | solution.py:303
  6.8 0.0 collective-permute-done.refs_1_
  6.9 1.6 %collective-permute-start.2 = (bf16[352,256]{1,0:T(8,128)(2,1)S(1)}, bf16[352,256]{1,0:T(8,128)(2,1)S(1)}, u32[]{:S(2)}, u32[]{:S(2)}) collective-permute-start(bf16[352,256]{1,0:T(8,128)(2,1)S(1)} %slice.9), channel_id=1, source_target_pairs={{0,2},{1,5},{2,6},{3,1},{4,0},{5,9},{6,10},{7,3},{8,4},{9,13},{10,... | collective-permute-start | bytes 540680 | tf_op jit(solution)/shard_map/ppermute | solution.py:325
  8.5 1.6 %collective-permute-done.1.mine_ref.refs_2_ = bf16[384,256]{1,0:T(8,128)(2,1)S(1)} collective-permute-done((bf16[384,256]{1,0:T(8,128)(2,1)S(1)}, bf16[384,256]{1,0:T(8,128)(2,1)S(1)}, u32[]{:S(2)}, u32[]{:S(2)}) %collective-permute-start.1) | collective-permute-done | bytes 196640 | tf_op jit(solution)/shard_map/ppermute | solution.py:325
  10.1 2.0 %collective-permute-start.3 = (bf16[288,256]{1,0:T(8,128)(2,1)S(1)}, bf16[288,256]{1,0:T(8,128)(2,1)S(1)}, u32[]{:S(2)}, u32[]{:S(2)}) collective-permute-start(bf16[288,256]{1,0:T(8,128)(2,1)S(1)} %slice.12), channel_id=1, source_target_pairs={{0,2},{1,5},{2,6},{3,1},{4,0},{5,9},{6,10},{7,3},{8,4},{9,13},{10,... | collective-permute-start | bytes 442376 | tf_op jit(solution)/shard_map/ppermute | solution.py:325
  12.2 0.3 collective-permute-done.2.theirs_ref.refs_3_
  12.4 1.7 %collective-permute-start.4 = (bf16[384,256]{1,0:T(8,128)(2,1)S(1)}, bf16[384,256]{1,0:T(8,128)(2,1)S(1)}, u32[]{:S(2)}, u32[]{:S(2)}) collective-permute-start(bf16[384,256]{1,0:T(8,128)(2,1)S(1)} %shard_map.93), channel_id=1, source_target_pairs={{0,2},{1,5},{2,6},{3,1},{4,0},{5,9},{6,10},{7,3},{8,4},{9,13},{10,... | collective-permute-start | bytes 589832 | tf_op jit(solution)/shard_map/ppermute | solution.py:325
  14.1 1.2 %collective-permute-done.3.refs_4_ = bf16[288,256]{1,0:T(8,128)(2,1)S(1)} collective-permute-done((bf16[288,256]{1,0:T(8,128)(2,1)S(1)}, bf16[288,256]{1,0:T(8,128)(2,1)S(1)}, u32[]{:S(2)}, u32[]{:S(2)}) %collective-permute-start.3) | collective-permute-done | bytes 147488 | tf_op jit(solution)/shard_map/ppermute | solution.py:325
  15.3 2.0 %collective-permute-start.5 = (bf16[288,256]{1,0:T(8,128)(2,1)S(1)}, bf16[288,256]{1,0:T(8,128)(2,1)S(1)}, u32[]{:S(2)}, u32[]{:S(2)}) collective-permute-start(bf16[288,256]{1,0:T(8,128)(2,1)S(1)} %collective-permute-done.3.refs_4_), channel_id=1, source_target_pairs={{0,2},{1,5},{2,6},{3,1},{4,0},{5,9},{6,10},{7,3},{8,4},{9,13},{10,... | collective-permute-start | bytes 442376 | tf_op jit(solution)/shard_map/ppermute | solution.py:325
  17.3 0.0 collective-permute-start.7
  17.3 0.8 %collective-permute-done.4.refs_5_ = bf16[384,256]{1,0:T(8,128)(2,1)S(1)} collective-permute-done((bf16[384,256]{1,0:T(8,128)(2,1)S(1)}, bf16[384,256]{1,0:T(8,128)(2,1)S(1)}, u32[]{:S(2)}, u32[]{:S(2)}) %collective-permute-start.4) | collective-permute-done | bytes 196640 | tf_op jit(solution)/shard_map/ppermute | solution.py:325
  18.1 0.0 collective-permute-start.11
  18.2 1.7 %collective-permute-start.6 = (bf16[320,256]{1,0:T(8,128)(2,1)S(1)}, bf16[320,256]{1,0:T(8,128)(2,1)S(1)}, u32[]{:S(2)}, u32[]{:S(2)}) collective-permute-start(bf16[320,256]{1,0:T(8,128)(2,1)S(1)} %slice.13), channel_id=1, source_target_pairs={{0,2},{1,5},{2,6},{3,1},{4,0},{5,9},{6,10},{7,3},{8,4},{9,13},{10,... | collective-permute-start | bytes 491528 | tf_op jit(solution)/shard_map/ppermute | solution.py:325
  19.8 0.6 %collective-permute-done.5.refs_6_ = bf16[288,256]{1,0:T(8,128)(2,1)S(1)} collective-permute-done((bf16[288,256]{1,0:T(8,128)(2,1)S(1)}, bf16[288,256]{1,0:T(8,128)(2,1)S(1)}, u32[]{:S(2)}, u32[]{:S(2)}) %collective-permute-start.5) | collective-permute-done | bytes 147488 | tf_op jit(solution)/shard_map/ppermute | solution.py:325
  20.5 2.0 %collective-permute-start.9 = (bf16[288,256]{1,0:T(8,128)(2,1)S(1)}, bf16[288,256]{1,0:T(8,128)(2,1)S(1)}, u32[]{:S(2)}, u32[]{:S(2)}) collective-permute-start(bf16[288,256]{1,0:T(8,128)(2,1)S(1)} %collective-permute-done.5.refs_6_), channel_id=1, source_target_pairs={{0,2},{1,5},{2,6},{3,1},{4,0},{5,9},{6,10},{7,3},{8,4},{9,13},{10,... | collective-permute-start | bytes 442376 | tf_op jit(solution)/shard_map/ppermute | solution.py:325
  22.4 0.0 collective-permute-done.7.refs_9_
  22.5 1.1 %collective-permute-done.6.refs_7_ = bf16[320,256]{1,0:T(8,128)(2,1)S(1)} collective-permute-done((bf16[320,256]{1,0:T(8,128)(2,1)S(1)}, bf16[320,256]{1,0:T(8,128)(2,1)S(1)}, u32[]{:S(2)}, u32[]{:S(2)}) %collective-permute-start.6) | collective-permute-done | bytes 163872 | tf_op jit(solution)/shard_map/ppermute | solution.py:325
  23.5 0.5 %collective-permute-start.12 = (bf16[288,256]{1,0:T(8,128)(2,1)S(1)}, bf16[288,256]{1,0:T(8,128)(2,1)S(1)}, u32[]{:S(2)}, u32[]{:S(2)}) collective-permute-start(bf16[288,256]{1,0:T(8,128)(2,1)S(1)} %collective-permute-done.5.refs_6_), channel_id=1, source_target_pairs={{0,1},{1,0},{2,3},{3,2},{4,5},{5,4},{6,7},{7,6},{8,9},{9,8},{10,11... | collective-permute-start | bytes 442376 | tf_op jit(solution)/shard_map/ppermute | solution.py:301
  24.0 1.6 %collective-permute-done.9.refs_8_ = bf16[288,256]{1,0:T(8,128)(2,1)S(1)} collective-permute-done((bf16[288,256]{1,0:T(8,128)(2,1)S(1)}, bf16[288,256]{1,0:T(8,128)(2,1)S(1)}, u32[]{:S(2)}, u32[]{:S(2)}) %collective-permute-start.9) | collective-permute-done | bytes 147488 | tf_op jit(solution)/shard_map/ppermute | solution.py:325
  25.7 1.3 %collective-permute-done.14.refs_15_ = bf16[288,256]{1,0:T(8,128)(2,1)S(1)} collective-permute-done((bf16[288,256]{1,0:T(8,128)(2,1)S(1)}, bf16[288,256]{1,0:T(8,128)(2,1)S(1)}, u32[]{:S(2)}, u32[]{:S(2)}) %collective-permute-start.14) | collective-permute-done | bytes 147488 | tf_op jit(solution)/shard_map/ppermute | solution.py:301
  27.0 4.4 %shard_map.94 = bf16[16,256,128]{2,1,0:T(8,128)(2,1)} custom-call(bf16[384,256]{1,0:T(8,128)(2,1)S(1)} %get-tuple-element.24.refs_0_, bf16[384,256]{1,0:T(8,128)(2,1)S(1)} %collective-permute-done.refs_1_, bf16[384,256]{1,0:T(8,128)(2,1)S(1)} %collective-permute-done.1.mine_ref.refs_2_, bf16[352,256]{1,0:T(8,128)(2,1)S(1)} %collective-permute-done.2.theirs_ref.refs_3_, ...), custom_call_target="tpu_custom_call" | custom-call | tf_op jit(solution)/shard_map/pallas_call | solution.py:373
  (17 shorter events, 0.1 us)
Async XLA Ops:
  0.0 6.4 %copy-start = (bf16[1024,128]{1,0:T(8,128)(2,1)S(1)}, bf16[1024,128]{1,0:T(8,128)(2,1)}, u32[]{:S(2)}) copy-start(bf16[1024,128]{1,0:T(8,128)(2,1)} %final_ref.1) | copy-start | bytes 786436
  3.3 3.5 %collective-permute-start = (bf16[384,256]{1,0:T(8,128)(2,1)S(1)}, bf16[384,256]{1,0:T(8,128)(2,1)S(1)}, u32[]{:S(2)}, u32[]{:S(2)}) collective-permute-start(bf16[384,256]{1,0:T(8,128)(2,1)S(1)} %get-tuple-element.24.refs_0_), channel_id=1, source_target_pairs={{0,1},{1,0},{2,3},{3,2},{4,5},{5,4},{6,7},{7,6},{8,9},{9,8},{10,11... | collective-permute-start | bytes 589832 | tf_op jit(solution)/shard_map/ppermute | solution.py:301
  3.8 2.6 %copy-start.1 = (f32[128]{0:T(128)S(1)}, f32[128]{0:T(128)}, u32[]{:S(2)}) copy-start(f32[128]{0:T(128)} %param.17) | copy-start | bytes 1540
  3.8 6.3 %collective-permute-start.1 = (bf16[384,256]{1,0:T(8,128)(2,1)S(1)}, bf16[384,256]{1,0:T(8,128)(2,1)S(1)}, u32[]{:S(2)}, u32[]{:S(2)}) collective-permute-start(bf16[384,256]{1,0:T(8,128)(2,1)S(1)} %get-tuple-element.28), channel_id=1, source_target_pairs={{0,2},{1,5},{2,6},{3,1},{4,0},{5,9},{6,10},{7,3},{8,4},{9,13},{10,... | collective-permute-start | bytes 589832 | tf_op jit(solution)/shard_map/ppermute | solution.py:325
  6.9 5.5 %collective-permute-start.2 = (bf16[352,256]{1,0:T(8,128)(2,1)S(1)}, bf16[352,256]{1,0:T(8,128)(2,1)S(1)}, u32[]{:S(2)}, u32[]{:S(2)}) collective-permute-start(bf16[352,256]{1,0:T(8,128)(2,1)S(1)} %slice.9), channel_id=1, source_target_pairs={{0,2},{1,5},{2,6},{3,1},{4,0},{5,9},{6,10},{7,3},{8,4},{9,13},{10,... | collective-permute-start | bytes 540680 | tf_op jit(solution)/shard_map/ppermute | solution.py:325
  10.1 5.2 %collective-permute-start.3 = (bf16[288,256]{1,0:T(8,128)(2,1)S(1)}, bf16[288,256]{1,0:T(8,128)(2,1)S(1)}, u32[]{:S(2)}, u32[]{:S(2)}) collective-permute-start(bf16[288,256]{1,0:T(8,128)(2,1)S(1)} %slice.12), channel_id=1, source_target_pairs={{0,2},{1,5},{2,6},{3,1},{4,0},{5,9},{6,10},{7,3},{8,4},{9,13},{10,... | collective-permute-start | bytes 442376 | tf_op jit(solution)/shard_map/ppermute | solution.py:325
  12.4 5.7 %collective-permute-start.4 = (bf16[384,256]{1,0:T(8,128)(2,1)S(1)}, bf16[384,256]{1,0:T(8,128)(2,1)S(1)}, u32[]{:S(2)}, u32[]{:S(2)}) collective-permute-start(bf16[384,256]{1,0:T(8,128)(2,1)S(1)} %shard_map.93), channel_id=1, source_target_pairs={{0,2},{1,5},{2,6},{3,1},{4,0},{5,9},{6,10},{7,3},{8,4},{9,13},{10,... | collective-permute-start | bytes 589832 | tf_op jit(solution)/shard_map/ppermute | solution.py:325
  14.1 8.4 %collective-permute-start.8 = (bf16[352,256]{1,0:T(8,128)(2,1)S(1)}, bf16[352,256]{1,0:T(8,128)(2,1)S(1)}, u32[]{:S(2)}, u32[]{:S(2)}) collective-permute-start(bf16[352,256]{1,0:T(8,128)(2,1)S(1)} %collective-permute-done.2.theirs_ref.refs_3_), channel_id=1, source_target_pairs={{0,1},{1,0},{2,3},{3,2},{4,5},{5,4},{6,7},{7,6},{8,9},{9,8},{10,11... | collective-permute-start | bytes 540680 | tf_op jit(solution)/shard_map/ppermute | solution.py:301
  15.3 5.1 %collective-permute-start.5 = (bf16[288,256]{1,0:T(8,128)(2,1)S(1)}, bf16[288,256]{1,0:T(8,128)(2,1)S(1)}, u32[]{:S(2)}, u32[]{:S(2)}) collective-permute-start(bf16[288,256]{1,0:T(8,128)(2,1)S(1)} %collective-permute-done.3.refs_4_), channel_id=1, source_target_pairs={{0,2},{1,5},{2,6},{3,1},{4,0},{5,9},{6,10},{7,3},{8,4},{9,13},{10,... | collective-permute-start | bytes 442376 | tf_op jit(solution)/shard_map/ppermute | solution.py:325
  17.3 5.2 %collective-permute-start.7 = (bf16[384,256]{1,0:T(8,128)(2,1)S(1)}, bf16[384,256]{1,0:T(8,128)(2,1)S(1)}, u32[]{:S(2)}, u32[]{:S(2)}) collective-permute-start(bf16[384,256]{1,0:T(8,128)(2,1)S(1)} %collective-permute-done.1.mine_ref.refs_2_), channel_id=1, source_target_pairs={{0,1},{1,0},{2,3},{3,2},{4,5},{5,4},{6,7},{7,6},{8,9},{9,8},{10,11... | collective-permute-start | bytes 589832 | tf_op jit(solution)/shard_map/ppermute | solution.py:301
  18.1 7.5 %collective-permute-start.11 = (bf16[384,256]{1,0:T(8,128)(2,1)S(1)}, bf16[384,256]{1,0:T(8,128)(2,1)S(1)}, u32[]{:S(2)}, u32[]{:S(2)}) collective-permute-start(bf16[384,256]{1,0:T(8,128)(2,1)S(1)} %collective-permute-done.4.refs_5_), channel_id=1, source_target_pairs={{0,1},{1,0},{2,3},{3,2},{4,5},{5,4},{6,7},{7,6},{8,9},{9,8},{10,11... | collective-permute-start | bytes 589832 | tf_op jit(solution)/shard_map/ppermute | solution.py:301
  18.2 5.4 %collective-permute-start.6 = (bf16[320,256]{1,0:T(8,128)(2,1)S(1)}, bf16[320,256]{1,0:T(8,128)(2,1)S(1)}, u32[]{:S(2)}, u32[]{:S(2)}) collective-permute-start(bf16[320,256]{1,0:T(8,128)(2,1)S(1)} %slice.13), channel_id=1, source_target_pairs={{0,2},{1,5},{2,6},{3,1},{4,0},{5,9},{6,10},{7,3},{8,4},{9,13},{10,... | collective-permute-start | bytes 491528 | tf_op jit(solution)/shard_map/ppermute | solution.py:325
  20.5 5.1 %collective-permute-start.9 = (bf16[288,256]{1,0:T(8,128)(2,1)S(1)}, bf16[288,256]{1,0:T(8,128)(2,1)S(1)}, u32[]{:S(2)}, u32[]{:S(2)}) collective-permute-start(bf16[288,256]{1,0:T(8,128)(2,1)S(1)} %collective-permute-done.5.refs_6_), channel_id=1, source_target_pairs={{0,2},{1,5},{2,6},{3,1},{4,0},{5,9},{6,10},{7,3},{8,4},{9,13},{10,... | collective-permute-start | bytes 442376 | tf_op jit(solution)/shard_map/ppermute | solution.py:325
  22.4 3.2 %collective-permute-start.10 = (bf16[288,256]{1,0:T(8,128)(2,1)S(1)}, bf16[288,256]{1,0:T(8,128)(2,1)S(1)}, u32[]{:S(2)}, u32[]{:S(2)}) collective-permute-start(bf16[288,256]{1,0:T(8,128)(2,1)S(1)} %collective-permute-done.3.refs_4_), channel_id=1, source_target_pairs={{0,1},{1,0},{2,3},{3,2},{4,5},{5,4},{6,7},{7,6},{8,9},{9,8},{10,11... | collective-permute-start | bytes 442376 | tf_op jit(solution)/shard_map/ppermute | solution.py:301
  23.5 2.1 %collective-permute-start.13 = (bf16[320,256]{1,0:T(8,128)(2,1)S(1)}, bf16[320,256]{1,0:T(8,128)(2,1)S(1)}, u32[]{:S(2)}, u32[]{:S(2)}) collective-permute-start(bf16[320,256]{1,0:T(8,128)(2,1)S(1)} %collective-permute-done.6.refs_7_), channel_id=1, source_target_pairs={{0,1},{1,0},{2,3},{3,2},{4,5},{5,4},{6,7},{7,6},{8,9},{9,8},{10,11... | collective-permute-start | bytes 491528 | tf_op jit(solution)/shard_map/ppermute | solution.py:301
  23.5 2.1 %collective-permute-start.12 = (bf16[288,256]{1,0:T(8,128)(2,1)S(1)}, bf16[288,256]{1,0:T(8,128)(2,1)S(1)}, u32[]{:S(2)}, u32[]{:S(2)}) collective-permute-start(bf16[288,256]{1,0:T(8,128)(2,1)S(1)} %collective-permute-done.5.refs_6_), channel_id=1, source_target_pairs={{0,1},{1,0},{2,3},{3,2},{4,5},{5,4},{6,7},{7,6},{8,9},{9,8},{10,11... | collective-permute-start | bytes 442376 | tf_op jit(solution)/shard_map/ppermute | solution.py:301
  25.6 1.4 %collective-permute-start.14 = (bf16[288,256]{1,0:T(8,128)(2,1)S(1)}, bf16[288,256]{1,0:T(8,128)(2,1)S(1)}, u32[]{:S(2)}, u32[]{:S(2)}) collective-permute-start(bf16[288,256]{1,0:T(8,128)(2,1)S(1)} %collective-permute-done.9.refs_8_), channel_id=1, source_target_pairs={{0,1},{1,0},{2,3},{3,2},{4,5},{5,4},{6,7},{7,6},{8,9},{9,8},{10,11... | collective-permute-start | bytes 442376 | tf_op jit(solution)/shard_map/ppermute | solution.py:301
